TPU v7x, 32 devices: a whole 2x2x4 slice. The times are simulated.
32 devices in a mesh: row: 8 (over y, x, core), col: 4 (over z).
Axes of the slice: x: 2, y: 2, z: 4, core: 2. Of those that a mesh axis runs over, the one named last changes fastest.
Arguments:
- nodes: bfloat16 [8192, 256], P(('row', 'col')), may hold values from -6 to 6
- weight: bfloat16 [256, 256], replicated, may hold values from -0.375 to 0.375
- adjacency: bfloat16 [8192, 8192], P('row', 'col'), may hold values from -0.09375 to 0.09375
- history: bfloat16 [32768, 256], P(('row', 'col')), may hold values from -6 to 6
- pull_owner: int32 [1024, 1], P(('row', 'col')), may hold values from 0 to 7; in each aligned block of 32 rows (0 to 31, 32 to 63, ...) at most 4 rows name the same one
- pull_slot: int32 [1024], P(('row', 'col')), may hold values from 0 to 7
- pull_target: int32 [1024], P(('row', 'col')), may hold values from 0 to 7
- hist_tiles: bfloat16 [1024, 128, 128], P(('row', 'col')), may hold values from -0.375 to 0.375
- cotangent: bfloat16 [8192, 256], P(('row', 'col')), may hold values from -6 to 6
Outputs:
- activated: bfloat16 [8192, 256], P(('row', 'col'))
- grad_nodes: bfloat16 [8192, 256], P(('row', 'col'))
- grad_weight: float32 [256, 256], replicated
Inputs may be any that keep to these rules, and one draw needn't show every extreme that they name: `pull_owner`: among the 32 pulls of one device no owner is named more than 4 times, a bound that some block reaches.
All inputs are finite; a program needn't handle non-finite values.
Results may differ from a plain program's by a relative error of at most 0.029.
Values may be sent and summed in bfloat16 or wider, within the bound.
No kernel may reach another device: no remote copies, remote signals or barrier semaphores. Data moves between devices by JAX's collectives and lax.ppermute only.
A program may use at most 128 MiB of HBM per device.

v0:
```python
import math

import jax
import jax.numpy as jnp
from jax import lax
from jax.sharding import PartitionSpec as P

HID = 256
BLK = 128


def local(
    nodes, weight, adjacency, history, pull_owner, pull_slot, pull_target, hist_tiles, cotangent
):
    projected = jnp.dot(nodes, weight, preferred_element_type=jnp.float32).astype(jnp.bfloat16)
    gathered = lax.all_gather(projected, "row", axis=0, tiled=True)
    owners = pull_owner[:, 0]
    blocks = history.reshape(-1, BLK, HID)
    everything = lax.all_gather(blocks, "row", axis=0, tiled=True)
    pulled = everything[owners * blocks.shape[0] + pull_slot]
    products = jnp.einsum("kab,kbf->kaf", hist_tiles, pulled, preferred_element_type=jnp.float32)
    row_count = adjacency.shape[0] // BLK
    placing = (pull_target[None, :] == jnp.arange(row_count, dtype=jnp.int32)[:, None]).astype(
        jnp.float32
    )
    history_term = jnp.einsum(
        "jk,kaf->jaf", placing, products, precision=lax.Precision.HIGHEST
    ).reshape(-1, HID)
    in_batch = jnp.dot(adjacency, gathered, preferred_element_type=jnp.float32)
    mixed = lax.psum_scatter(
        (in_batch + history_term).astype(jnp.bfloat16), "col", scatter_dimension=0, tiled=True
    ).astype(jnp.float32)
    activated = jax.nn.silu(mixed).astype(jnp.bfloat16)
    sigmoid_z = jax.nn.sigmoid(mixed)
    grad_pre = (
        cotangent.astype(jnp.float32) * sigmoid_z * (1.0 + mixed * (1.0 - sigmoid_z))
    ).astype(jnp.bfloat16)
    grad_panel = lax.all_gather(grad_pre, "col", axis=0, tiled=True)
    grad_proj = lax.psum_scatter(
        lax.dot_general(
            adjacency, grad_panel, (((0,), (0,)), ((), ())), preferred_element_type=jnp.float32
        ).astype(jnp.bfloat16),
        "row",
        scatter_dimension=0,
        tiled=True,
    )
    grad_nodes = jnp.dot(grad_proj, weight.T, preferred_element_type=jnp.float32).astype(
        jnp.bfloat16
    )
    partial_grad = lax.dot_general(
        nodes, grad_proj, (((0,), (0,)), ((), ())), preferred_element_type=jnp.float32
    )
    all_nodes = nodes.shape[0] * lax.axis_size("row") * lax.axis_size("col")
    grad_weight = lax.psum(partial_grad, ("row", "col")) * (1.0 / math.sqrt(all_nodes))
    return (activated, grad_nodes, grad_weight)


def solution(mesh):
    return jax.shard_map(
        local,
        mesh=mesh,
        in_specs=(
            P(("row", "col"), None),
            P(),
            P("row", "col"),
            P(("row", "col"), None),
            P(("row", "col"), None),
            P(("row", "col")),
            P(("row", "col")),
            P(("row", "col"), None, None),
            P(("row", "col"), None),
        ),
        out_specs=(P(("row", "col"), None), P(("row", "col"), None), P()),
        check_vma=False,
    )
```

profile of v0, /device:TPU:0, one launch (start us, length us, event | category | flops | bytes accessed | tf_op | source)
XLA Modules:
  0.0 297.0 jit_solution(4547305703324849508)
XLA Ops:
  7.2 0.0 copy-start
  7.2 0.0 all-gather.5.cloned.1.call-start
  7.2 0.7 all-gather.5.cloned.1.call-update
  7.9 0.0 all-gather.3.cloned.1.call-start
  8.0 1.8 convolution_convert_fusion.2
  9.8 0.0 all-gather.3.cloned.1.call-update
  9.8 0.0 reduce-scatter.3.cloned.1.call-start
  9.8 0.7 compare_select_fusion
  10.5 38.8 %all-gather.5.cloned.1.call-done = bf16[64,128,256]{2,1,0:T(8,128)(2,1)} async-done(((bf16[8,128,256]{2,1,0:T(8,128)(2,1)}), bf16[64,128,256]{2,1,0:T(8,128)(2,1)}) %all-gather.5.cloned.1.call-update) | async-done | bytes 4194320 | tf_op jit(solution)/shard_map/all_gather | solution.py:19
  49.4 2.9 gather_fusion
  52.2 0.0 copy-done
  52.2 0.0 copy-start.4
  52.2 0.8 convolution_bitcast_fusion
  53.0 0.0 copy-done.4
  53.0 3.8 %fusion = f32[8,128,256]{1,0,2:T(8,128)S(1)} fusion(f32[32,128,256]{1,2,0:T(8,128)S(1)} %convolution_bitcast_fusion, s32[32]{0:T(128)S(1)} %copy-done.4), kind=kOutput, calls=%fused_computation.1 | convolution fusion | flops 100663552 | bytes 5243008 | tf_op jit(solution)/shard_map/jk,kaf->jaf/dot_general | solution.py:26
  56.8 18.5 %all-gather.3.cloned.1.call-done = bf16[2048,256]{1,0:T(8,128)(2,1)} async-done(((bf16[256,256]{1,0:T(8,128)(2,1)}), bf16[2048,256]{1,0:T(8,128)(2,1)}) %all-gather.3.cloned.1.call-update) | async-done | bytes 1048592 | tf_op jit(solution)/shard_map/all_gather | solution.py:16
  75.3 0.0 copy-start.3
  75.3 4.7 %fusion.4 = bf16[1024,256]{0,1:T(8,128)(2,1)} fusion(bf16[2048,256]{1,0:T(8,128)(2,1)} %all-gather.3.cloned.1.call-done, bf16[1024,2048]{1,0:T(8,128)(2,1)} %param.11, f32[32,8,8,128]{3,2,1,0:T(8,128)S(1)} %bitcast.38), kind=kOutput, calls=%fused_computation.8 | convolution fusion | flops 1074266112 | bytes 6815744 | tf_op jit(solution)/shard_map/dot_general | solution.py:29
  80.1 0.0 reduce-scatter.3.cloned.1.call-update
  80.1 0.0 reduce-scatter.5.cloned.1.call-start
  80.1 0.0 copy-done.3
  80.2 0.1 copy.17
  80.3 21.6 %reduce-scatter.3.cloned.1.call-done = bf16[256,256]{0,1:T(8,128)(2,1)} async-done(((bf16[1024,256]{0,1:T(8,128)(2,1)}), bf16[256,256]{0,1:T(8,128)(2,1)}) %reduce-scatter.3.cloned.1.call-update) | async-done | bytes 131088 | tf_op jit(solution)/shard_map/reduce_scatter | solution.py:30
  101.9 1.0 fusion.11
  102.9 15.9 %all_gather.11 = bf16[1024,256]{0,1:T(8,128)(2,1)S(1)} all-gather(bf16[256,256]{0,1:T(8,128)(2,1)S(1)} %get-tuple-element.9), channel_id=1, replica_groups=mesh['row'=8,'col'=4] {'col'}, dimensions={0}, use_global_device_ids=true | all-gather | bytes 655360 | tf_op jit(solution)/shard_map/all_gather | solution.py:38
  118.8 0.0 copy-start.2
  118.8 0.0 copy-start.1
  118.8 4.5 %fusion.2 = bf16[2048,256]{0,1:T(8,128)(2,1)} fusion(bf16[1024,256]{0,1:T(8,128)(2,1)S(1)} %all_gather.11, bf16[1024,2048]{1,0:T(8,128)(2,1)} %param.11), kind=kOutput, calls=%fused_computation.4 | convolution fusion | flops 1074266112 | bytes 5767168 | tf_op jit(solution)/shard_map/dot_general | solution.py:40
  123.3 0.0 reduce-scatter.5.cloned.1.call-update
  123.3 0.0 all-reduce.2.cloned.1.call-start
  123.4 0.8 copy.18
  124.1 33.6 %reduce-scatter.5.cloned.1.call-done = bf16[256,256]{0,1:T(8,128)(2,1)} async-done(((bf16[2048,256]{0,1:T(8,128)(2,1)}), bf16[256,256]{0,1:T(8,128)(2,1)}) %reduce-scatter.5.cloned.1.call-update) | async-done | bytes 131088 | tf_op jit(solution)/shard_map/reduce_scatter | solution.py:39
  157.7 0.0 copy-done.2
  157.7 1.8 convolution_bitcast_fusion.2
  159.5 0.0 all-reduce.2.cloned.1.call-update
  159.5 0.0 copy-done.1
  159.5 1.8 convolution_convert_fusion.1
  161.3 127.3 %all-reduce.2.cloned.1.call-done = f32[256,256]{0,1:T(8,128)} async-done(((f32[256,256]{0,1:T(8,128)}), f32[256,256]{0,1:T(8,128)}) %all-reduce.2.cloned.1.call-update) | async-done | bytes 262160 | tf_op jit(solution)/shard_map/psum | solution.py:54
  288.6 1.0 broadcast_multiply_fusion
  289.6 0.8 copy.19
  (1 shorter events, 0.0 us)
Async XLA Ops:
  7.2 45.1 %copy-start = (bf16[32,128,128]{2,1,0:T(8,128)(2,1)S(1)}, bf16[32,128,128]{2,1,0:T(8,128)(2,1)}, u32[]{:S(2)}) copy-start(bf16[32,128,128]{2,1,0:T(8,128)(2,1)} %param.16) | copy-start | bytes 3145732
  7.2 42.2 %all-gather.5.cloned.1.call-start = ((), (), s32[]{:S(2)}) async-start(), calls=%async_computation.3 | async-start | bytes 4718592 | tf_op jit(solution)/shard_map/all_gather | solution.py:19
  7.9 67.4 %all-gather.3.cloned.1.call-start = ((), (), s32[]{:S(2)}) async-start(), calls=%async_computation.2 | async-start | bytes 1179648 | tf_op jit(solution)/shard_map/all_gather | solution.py:16
  9.8 92.1 %reduce-scatter.3.cloned.1.call-start = ((), (), s32[]{:S(2)}) async-start(), calls=%async_computation.4 | async-start | bytes 655360 | tf_op jit(solution)/shard_map/reduce_scatter | solution.py:30
  52.2 0.8 copy-start.4
  75.3 4.8 %copy-start.3 = (bf16[256,256]{1,0:T(8,128)(2,1)S(1)}, bf16[256,256]{1,0:T(8,128)(2,1)}, u32[]{:S(2)}) copy-start(bf16[256,256]{1,0:T(8,128)(2,1)} %param.17) | copy-start | bytes 393220
  80.1 77.6 %reduce-scatter.5.cloned.1.call-start = ((), (), s32[]{:S(2)}) async-start(), calls=%async_computation.5 | async-start | bytes 1179648 | tf_op jit(solution)/shard_map/reduce_scatter | solution.py:39
  118.8 38.9 %copy-start.2 = (bf16[256,256]{1,0:T(8,128)(2,1)S(1)}, bf16[256,256]{1,0:T(8,128)(2,1)}, u32[]{:S(2)}) copy-start(bf16[256,256]{1,0:T(8,128)(2,1)} %param.9) | copy-start | bytes 393220
  118.8 40.7 %copy-start.1 = (bf16[256,256]{1,0:T(8,128)(2,1)S(1)}, bf16[256,256]{1,0:T(8,128)(2,1)}, u32[]{:S(2)}) copy-start(bf16[256,256]{1,0:T(8,128)(2,1)} %param.10) | copy-start | bytes 393220
  123.3 165.3 %all-reduce.2.cloned.1.call-start = ((), (), s32[]{:S(2)}) async-start(), calls=%async_computation.6 | async-start | bytes 524288 | tf_op jit(solution)/shard_map/psum | solution.py:54
Sparse Core Ops, SparseCore 0:
  9.9 39.4 all-gather.4
  51.8 23.4 all-gather.2
  80.2 21.6 reduce-scatter.2
  123.4 34.2 reduce-scatter.4
  163.6 124.9 all-reduce.1
where the time goes:
time: 297 us
  waiting for transfers between devices  241 us (81%)
  matrix products  19.2 us (6%)
  blocking collectives  15.9 us (5%)
  between operations  13.9 us (5%)
  local copies, waits for them, and re-layouts  4.59 us (2%)
    psum x1, waiting for transfers between devices, local(): lax.psum(partial_grad, ('row', 'col')) * (1.0 / math.sqrt(all_nodes))  127 us
    all_gather x1, waiting for transfers between devices, local(): everything = lax.all_gather(blocks, 'row', axis=0, tiled=True)  38.8 us
    reduce_scatter x1, waiting for transfers between devices, local(): lax.psum_scatter(lax.dot_general(adjacency, grad_panel, (((0,), (0,)), ((...  33.6 us
    reduce_scatter x1, waiting for transfers between devices, local(): lax.psum_scatter((in_batch + history_term).astype(jnp.bfloat16), 'col', s...  21.6 us
    all_gather x1, waiting for transfers between devices, local(): gathered = lax.all_gather(projected, 'row', axis=0, tiled=True)  18.5 us
    all_gather x1, blocking collectives, local(): grad_panel = lax.all_gather(grad_pre, 'col', axis=0, tiled=True)  15.9 us
  transfers between devices with their start and end apart: 5, of which 5 were waited for; matrix products, arithmetic and copies ran while one was open for 4% of the time, Pallas kernels for 0%

commit v1 on v0

v1 whole, which is shorter than its diff:
```python
import functools
import math

import jax
import jax.numpy as jnp
from jax import lax
from jax.experimental import pallas as pl
from jax.experimental.pallas import tpu as pltpu
from jax.sharding import PartitionSpec as P

BLK = 128
CAP = 4
BF16 = jnp.bfloat16
F32 = jnp.float32
WHOLE = pl.BlockSpec(memory_space=pltpu.VMEM)
SCALARS = pl.BlockSpec(memory_space=pltpu.SMEM)


def swap(x, axis, offset):
    size = lax.axis_size(axis)
    return lax.ppermute(x, axis, [(i, i ^ offset) for i in range(size)])


def nbytes(*arrays):
    return sum(math.prod(a.shape) * jnp.dtype(a.dtype).itemsize for a in arrays)


def call(kernel, outs, scratch, flops, *operands, specs=None):
    held = nbytes(*operands, *outs) + nbytes(*scratch)
    return pl.pallas_call(
        kernel,
        out_shape=outs,
        in_specs=specs or [WHOLE] * len(operands),
        out_specs=[WHOLE] * len(outs),
        scratch_shapes=[pltpu.VMEM(s.shape, s.dtype) for s in scratch],
        compiler_params=pltpu.CompilerParams(vmem_limit_bytes=held + (8 << 20)),
        cost_estimate=pl.CostEstimate(flops=flops, bytes_accessed=held, transcendentals=0),
    )(*operands)


def aggregate_kernel(n_row, n_col, a_ref, *refs):
    pieces, outs, x_ref = refs[:n_row], refs[n_row:-1], refs[-1]
    span = pieces[0].shape[0]
    r, c = lax.axis_index("row"), lax.axis_index("col")
    for t in range(n_row):
        x_ref[pl.ds(pl.multiple_of((r ^ t) * span, span), span), :] = pieces[t][...]
    for s in range(n_col):
        rows = pl.ds(pl.multiple_of((c ^ s) * span, span), span)
        part = jnp.dot(a_ref[rows, :], x_ref[...], preferred_element_type=F32)
        outs[s][...] = part.astype(outs[s].dtype)


def history_kernel(n_row, n_col, which, slot, target, tiles, *refs):
    low, high = refs[:n_row], refs[n_row : 2 * n_row]
    outs, acc = refs[2 * n_row : -1], refs[-1]
    span = outs[0].shape[0]
    half = low[0].shape[0] // BLK
    c = lax.axis_index("col")
    acc[...] = jnp.zeros_like(acc)
    for t in range(n_row):
        for m in range(CAP):
            i = t * CAP + m
            at = slot[i]
            inside = pl.ds(pl.multiple_of((at % half) * BLK, BLK), BLK)
            block = jnp.where(at < half, low[t][inside, :], high[t][inside, :])
            rows = pl.ds(pl.multiple_of(target[i] * BLK, BLK), BLK)
            acc[rows, :] += jnp.dot(tiles[which[i]], block, preferred_element_type=F32)
    for s in range(n_col):
        rows = pl.ds(pl.multiple_of((c ^ s) * span, span), span)
        outs[s][...] = acc[rows, :].astype(outs[s].dtype)


def transposed_kernel(n_col, offsets, a_ref, *refs):
    pieces, outs, g_ref = refs[:n_col], refs[n_col:-1], refs[-1]
    span = pieces[0].shape[1]
    r, c = lax.axis_index("row"), lax.axis_index("col")
    for s in range(n_col):
        g_ref[:, pl.ds(pl.multiple_of((c ^ s) * span, span), span)] = pieces[s][...]
    for t, out in zip(offsets, outs, strict=True):
        columns = pl.ds(pl.multiple_of((r ^ t) * span, span), span)
        part = jnp.dot(g_ref[...], a_ref[:, columns], preferred_element_type=F32)
        out[...] = part.astype(out.dtype)


def spread_sum(x, axis, offsets):
    narrow = x.astype(BF16)
    terms = [(swap(narrow, axis, s) if s else narrow).astype(F32) for s in offsets]
    while len(terms) > 1:
        terms = [a + b for a, b in zip(terms[::2], terms[1::2], strict=True)]
    return terms[0]


def shape(*dims, dtype=BF16):
    return jax.ShapeDtypeStruct(dims, dtype)


def pull_lists(owner, slot, target, n_row, row_count):
    pulls = owner.shape[0]
    offset = owner ^ lax.axis_index("row")
    order = jnp.arange(pulls, dtype=jnp.int32)
    earlier = (offset[None, :] == offset[:, None]) & (order[None, :] < order[:, None])
    place = offset * CAP + jnp.sum(earlier, axis=1, dtype=jnp.int32)
    chosen = place[None, :] == jnp.arange(n_row * CAP, dtype=jnp.int32)[:, None]

    def pick(values):
        return jnp.sum(jnp.where(chosen, values[None, :], 0), axis=1, dtype=jnp.int32)

    used = jnp.any(chosen, axis=1)
    return pick(order), pick(slot), jnp.where(used, pick(target), row_count)


def local(
    nodes, weight, adjacency, history, pull_owner, pull_slot, pull_target, hist_tiles, cotangent
):
    n_row, n_col = lax.axis_size("row"), lax.axis_size("col")
    span, hid = nodes.shape
    panel, columns = adjacency.shape
    row_count = panel // BLK
    chips = list(range(2, n_row, 2))

    near = {0: nodes, **{t: swap(nodes, "row", t) for t in chips}}
    near.update({t ^ 1: swap(x, "row", 1) for t, x in list(near.items())})

    middle = history.shape[0] // 2
    bits = [1 << b for b in range(1, n_row.bit_length() - 1)]
    halves = []
    for half, order in ((history[:middle], bits), (history[middle:], bits[::-1])):
        held = {0: half}
        for bit in order:
            held.update({t ^ bit: swap(x, "row", bit) for t, x in list(held.items())})
        held.update({t ^ 1: swap(x, "row", 1) for t, x in list(held.items())})
        halves += [held[t] for t in range(n_row)]

    parts = call(
        functools.partial(aggregate_kernel, n_row, n_col),
        [shape(span, hid, dtype=BF16 if s else F32) for s in range(n_col)],
        [shape(columns, hid)],
        2 * panel * columns * hid,
        adjacency,
        *[near[t] for t in range(n_row)],
    )
    mixing = parts[0]
    for s in range(1, n_col):
        mixing = mixing + swap(parts[s], "col", s).astype(F32)
    in_batch = jnp.dot(mixing, weight.astype(F32), precision=lax.Precision.HIGHEST)

    lists = pull_lists(pull_owner[:, 0], pull_slot, pull_target, n_row, row_count)
    terms = call(
        functools.partial(history_kernel, n_row, n_col),
        [shape(span, hid, dtype=BF16 if s else F32) for s in range(n_col)],
        [shape(panel + BLK, hid, dtype=F32)],
        2 * n_row * CAP * BLK * BLK * hid,
        *lists,
        hist_tiles,
        *halves,
        specs=[SCALARS] * 3 + [WHOLE] * (1 + 2 * n_row),
    )
    mixed = in_batch + terms[0]
    for s in range(1, n_col):
        mixed = mixed + swap(terms[s], "col", s).astype(F32)

    activated = jax.nn.silu(mixed).astype(BF16)
    sigmoid_z = jax.nn.sigmoid(mixed)
    grad_pre = cotangent.astype(F32) * sigmoid_z * (1.0 + mixed * (1.0 - sigmoid_z))
    flipped = grad_pre.T.astype(BF16)
    pieces = [flipped] + [swap(flipped, "col", s) for s in range(1, n_col)]

    partial_grad = lax.dot_general(
        mixing.astype(BF16), flipped, (((0,), (1,)), ((), ())), preferred_element_type=F32
    )
    mine = lax.axis_index("row") % 2
    split = partial_grad.reshape(2, hid // 2, hid)
    kept = lax.dynamic_index_in_dim(split, mine, 0, keepdims=False)
    given = lax.dynamic_index_in_dim(split, 1 - mine, 0, keepdims=False).astype(BF16)
    kept = kept + swap(given, "row", 1).astype(F32)
    kept = spread_sum(kept, "row", [0] + chips)
    kept = spread_sum(kept, "col", range(n_col))
    kept = kept * (1.0 / math.sqrt(span * n_row * n_col))
    other = swap(kept, "row", 1)
    grad_weight = jnp.where(
        mine == 0,
        jnp.concatenate([kept, other], axis=0),
        jnp.concatenate([other, kept], axis=0),
    )

    flops = panel * columns * hid
    given = call(
        functools.partial(transposed_kernel, n_col, [t ^ 1 for t in chips] + [1]),
        [shape(hid, span)] * (n_row // 2),
        [shape(hid, panel)],
        flops,
        adjacency,
        *pieces,
    )
    kept = call(
        functools.partial(transposed_kernel, n_col, chips + [0]),
        [shape(hid, span, dtype=F32)] * (n_row // 2),
        [shape(hid, panel)],
        flops,
        adjacency,
        *pieces,
    )
    sums = [k + swap(g, "row", 1).astype(F32) for k, g in zip(kept, given, strict=True)]
    total = sums[-1]
    for t, part in zip(chips, sums[:-1], strict=True):
        total = total + swap(part.astype(BF16), "row", t).astype(F32)
    grad_proj = total.astype(BF16)
    grad_nodes = lax.dot_general(
        grad_proj, weight, (((0,), (1,)), ((), ())), preferred_element_type=F32
    ).astype(BF16)
    return (activated, grad_nodes, grad_weight)


def solution(mesh):
    return jax.shard_map(
        local,
        mesh=mesh,
        in_specs=(
            P(("row", "col"), None),
            P(),
            P("row", "col"),
            P(("row", "col"), None),
            P(("row", "col"), None),
            P(("row", "col")),
            P(("row", "col")),
            P(("row", "col"), None, None),
            P(("row", "col"), None),
        ),
        out_specs=(P(("row", "col"), None), P(("row", "col"), None), P()),
        check_vma=False,
    )
```

time: 297 us -> 119 us (0.40)
  waiting for transfers between devices: 241 us -> 34.7 us
  starting transfers between devices: 0.2 us -> 43.6 us
  local copies, waits for them, and re-layouts: 4.59 us -> 24.5 us
  blocking collectives: 15.9 us -> 0 us
  matrix products: 19.2 us -> 3.61 us
  between operations: 13.9 us -> 0.93 us
  Pallas kernels: 0 us -> 6.73 us
    psum x1 -> x0, waiting for transfers between devices: 127 us -> none  [local(): lax.psum(partial_grad, ('row', 'col')) * (1.0 / math.sqrt(all_nodes))]
    all_gather x2 -> x0, waiting for transfers between devices: 57.3 us -> none  [the longest x1 38.8 us: local(): everything = lax.all_gather(blocks, 'row', axis=0, tiled=True)]
    reduce_scatter x2 -> x0, waiting for transfers between devices: 55.2 us -> none  [the longest x1 33.6 us: local(): lax.psum_scatter(lax.dot_general(adjacency, grad_panel, (((0,), (0,)), ((...]
    ppermute x0 -> x45, starting transfers between devices: none -> 43.6 us  [swap(): return lax.ppermute(x, axis, [(i, i ^ offset) for i in range(size)])]
    ppermute x0 -> x45, waiting for transfers between devices: none -> 34.7 us  [swap(): return lax.ppermute(x, axis, [(i, i ^ offset) for i in range(size)])]
    unnamed x13 -> x42, local copies, waits for them, and re-layouts: 1.72 us -> 19.3 us
    all_gather x1 -> x0, blocking collectives: 15.9 us -> none  [local(): grad_panel = lax.all_gather(grad_pre, 'col', axis=0, tiled=True)]
    dot_general x7 -> x3, matrix products: 19.2 us -> 3.61 us  [the longest x1 1.4 us: local(): jnp.dot(mixing, weight.astype(F32), precision=lax.Precision.HIGHEST)]
  transfers between devices with their start and end apart: 5 -> 45, of which waited for: 5 -> 9; matrix products, arithmetic and copies ran while one was open for 4% -> 10% of each run, Pallas kernels for 0% -> 6%
where the time goes in v1:
time: 119 us; the launch traced here: 118 us
  starting transfers between devices  43.6 us (37%)
  waiting for transfers between devices  34.7 us (29%)
  local copies, waits for them, and re-layouts  24.5 us (21%)
  Pallas kernels  6.73 us (6%)
  other arithmetic  4.47 us (4%)
  matrix products  3.61 us (3%)
    ppermute x45, starting transfers between devices, swap(): return lax.ppermute(x, axis, [(i, i ^ offset) for i in range(size)])  43.6 us
    ppermute x45, waiting for transfers between devices, swap(): return lax.ppermute(x, axis, [(i, i ^ offset) for i in range(size)])  34.7 us
    unnamed x42, local copies, waits for them, and re-layouts  19.3 us
    pallas_call x4, Pallas kernels, call(): pl.pallas_call(kernel, out_shape=outs, in_specs=specs or [WHOLE] * len(op...  6.73 us
    pallas_call x4, local copies, waits for them, and re-layouts, call(): pl.pallas_call(kernel, out_shape=outs, in_specs=specs or [WHOLE] * len(op...  4.08 us
  transfers between devices with their start and end apart: 45, of which 9 were waited for; matrix products, arithmetic and copies ran while one was open for 10% of the time, Pallas kernels for 6%

profile of v1, /device:TPU:0, one launch (start us, length us, event | category | flops | bytes accessed | tf_op | source)
XLA Modules:
  0.0 118.5 jit_solution(15175158712569330750)
XLA Ops:
  0.7 3.0 %collective-permute-start.1 = (bf16[256,256]{1,0:T(8,128)(2,1)}, bf16[256,256]{1,0:T(8,128)(2,1)}, u32[]{:S(2)}, u32[]{:S(2)}) collective-permute-start(bf16[256,256]{1,0:T(8,128)(2,1)} %refs_0_.1), channel_id=1, source_target_pairs={{0,8},{4,12},{8,0},{12,4},{16,24},{20,28},{24,16},{28,20},{1,9},{5... | collective-permute-start | bytes 393224 | tf_op jit(solution)/shard_map/ppermute | solution.py:21
  3.7 1.1 fusion.7
  4.9 1.9 %collective-permute-start.20 = (bf16[512,256]{1,0:T(8,128)(2,1)S(1)}, bf16[512,256]{1,0:T(8,128)(2,1)S(1)}, u32[]{:S(2)}, u32[]{:S(2)}) collective-permute-start(bf16[512,256]{1,0:T(8,128)(2,1)S(1)} %get-tuple-element.46.refs_8_), channel_id=1, source_target_pairs={{0,16},{4,20},{8,24},{12,28},{16,0},{20,4},{24,8},{28,12},{1,17},{... | collective-permute-start | bytes 786440 | tf_op jit(solution)/shard_map/ppermute | solution.py:21
  6.9 2.9 %collective-permute-start.5 = (bf16[256,256]{1,0:T(8,128)(2,1)}, bf16[256,256]{1,0:T(8,128)(2,1)}, u32[]{:S(2)}, u32[]{:S(2)}) collective-permute-start(bf16[256,256]{1,0:T(8,128)(2,1)} %refs_0_.1), channel_id=1, source_target_pairs={{0,24},{4,28},{8,16},{12,20},{16,8},{20,12},{24,0},{28,4},{1,25},{... | collective-permute-start | bytes 393224 | tf_op jit(solution)/shard_map/ppermute | solution.py:21
  9.8 8.6 %collective-permute-done.3.refs_4_ = bf16[256,256]{1,0:T(8,128)(2,1)} collective-permute-done((bf16[256,256]{1,0:T(8,128)(2,1)}, bf16[256,256]{1,0:T(8,128)(2,1)}, u32[]{:S(2)}, u32[]{:S(2)}) %collective-permute-start.3) | collective-permute-done | bytes 131104 | tf_op jit(solution)/shard_map/ppermute | solution.py:21
  18.4 1.7 %collective-permute-start.13 = (bf16[512,256]{1,0:T(8,128)(2,1)S(1)}, bf16[512,256]{1,0:T(8,128)(2,1)S(1)}, u32[]{:S(2)}, u32[]{:S(2)}) collective-permute-start(bf16[512,256]{1,0:T(8,128)(2,1)S(1)} %get-tuple-element.47.refs_0_), channel_id=1, source_target_pairs={{0,16},{4,20},{8,24},{12,28},{16,0},{20,4},{24,8},{28,12},{1,17},{... | collective-permute-start | bytes 786440 | tf_op jit(solution)/shard_map/ppermute | solution.py:21
  20.1 1.5 %collective-permute-start.18 = (bf16[512,256]{1,0:T(8,128)(2,1)S(1)}, bf16[512,256]{1,0:T(8,128)(2,1)S(1)}, u32[]{:S(2)}, u32[]{:S(2)}) collective-permute-start(bf16[512,256]{1,0:T(8,128)(2,1)S(1)} %get-tuple-element.46.refs_8_), channel_id=1, source_target_pairs={{0,8},{4,12},{8,0},{12,4},{16,24},{20,28},{24,16},{28,20},{1,9},{5... | collective-permute-start | bytes 786440 | tf_op jit(solution)/shard_map/ppermute | solution.py:21
  21.6 0.7 copy-done.15
  22.8 0.7 xor_bitcast_fusion
  23.5 1.4 %collective-permute-done.13.refs_4_ = bf16[512,256]{1,0:T(8,128)(2,1)S(1)} collective-permute-done((bf16[512,256]{1,0:T(8,128)(2,1)S(1)}, bf16[512,256]{1,0:T(8,128)(2,1)S(1)}, u32[]{:S(2)}, u32[]{:S(2)}) %collective-permute-start.13) | collective-permute-done | bytes 262176 | tf_op jit(solution)/shard_map/ppermute | solution.py:21
  24.8 1.7 %collective-permute-start.15 = (bf16[512,256]{1,0:T(8,128)(2,1)S(1)}, bf16[512,256]{1,0:T(8,128)(2,1)}, u32[]{:S(2)}, u32[]{:S(2)}) collective-permute-start(bf16[512,256]{1,0:T(8,128)(2,1)S(1)} %collective-permute-done.11.refs_2_), channel_id=1, source_target_pairs={{0,16},{4,20},{8,24},{12,28},{16,0},{20,4},{24,8},{28,12},{1,17},{... | collective-permute-start | bytes 786440 | tf_op jit(solution)/shard_map/ppermute | solution.py:21
  27.4 1.4 %collective-permute-start.22 = (bf16[512,256]{1,0:T(8,128)(2,1)S(1)}, bf16[512,256]{1,0:T(8,128)(2,1)}, u32[]{:S(2)}, u32[]{:S(2)}) collective-permute-start(bf16[512,256]{1,0:T(8,128)(2,1)S(1)} %collective-permute-done.20.refs_12_), channel_id=1, source_target_pairs={{0,8},{4,12},{8,0},{12,4},{16,24},{20,28},{24,16},{28,20},{1,9},{5... | collective-permute-start | bytes 786440 | tf_op jit(solution)/shard_map/ppermute | solution.py:21
  28.9 0.7 multiply_add_fusion
  30.1 2.2 %collective-permute-done.15.refs_6_ = bf16[512,256]{1,0:T(8,128)(2,1)} collective-permute-done((bf16[512,256]{1,0:T(8,128)(2,1)S(1)}, bf16[512,256]{1,0:T(8,128)(2,1)}, u32[]{:S(2)}, u32[]{:S(2)}) %collective-permute-start.15) | collective-permute-done | bytes 262176 | tf_op jit(solution)/shard_map/ppermute | solution.py:21
  32.3 0.8 select_reduce_fusion
  33.2 3.0 %collective-permute-done.22.refs_14_ = bf16[512,256]{1,0:T(8,128)(2,1)} collective-permute-done((bf16[512,256]{1,0:T(8,128)(2,1)S(1)}, bf16[512,256]{1,0:T(8,128)(2,1)}, u32[]{:S(2)}, u32[]{:S(2)}) %collective-permute-start.22) | collective-permute-done | bytes 262176 | tf_op jit(solution)/shard_map/ppermute | solution.py:21
  36.2 0.7 copy-done.5
  37.4 2.2 %copy-done.1 = bf16[1024,2048]{1,0:T(8,128)(2,1)S(1)} copy-done((bf16[1024,2048]{1,0:T(8,128)(2,1)S(1)}, bf16[1024,2048]{1,0:T(8,128)(2,1)}, u32[]{:S(2)}) %copy-start.1) | copy-done | bytes 4194328
  39.6 0.9 copy-done.14
  40.5 0.9 copy-done.16
  41.4 3.1 %shard_map.112 = (f32[256,256]{1,0:T(8,128)S(1)}, bf16[256,256]{1,0:T(8,128)(2,1)}, bf16[256,256]{1,0:T(8,128)(2,1)}, bf16[256,256]{1,0:T(8,128)(2,1)}) custom-call(bf16[1024,2048]{1,0:T(8,128)(2,1)S(1)} %copy-done.1, bf16[256,256]{1,0:T(8,128)(2,1)S(1)} %copy-done.14, bf16[256,256]{1,0:T(8,128)(2,1)S(1)} %copy-done.16, ...), custom_call_target="tpu_custom_call" | custom-call | flops 1073741824 | bytes 6946816 | tf_op jit(solution)/shard_map/pallas_call | solution.py:30
  44.5 0.7 copy-done.7
  45.2 1.6 %collective-permute-start.7 = (bf16[256,256]{1,0:T(8,128)(2,1)}, bf16[256,256]{1,0:T(8,128)(2,1)}, u32[]{:S(2)}, u32[]{:S(2)}) collective-permute-start(bf16[256,256]{1,0:T(8,128)(2,1)} %get-tuple-element.20), channel_id=1, source_target_pairs={{0,1},{1,0},{2,3},{3,2},{4,5},{5,4},{6,7},{7,6},{8,9},{9,8},{10,11... | collective-permute-start | bytes 393224 | tf_op jit(solution)/shard_map/ppermute | solution.py:21
  46.8 0.7 copy-done.9
  47.5 2.6 %collective-permute-start.8 = (bf16[256,256]{1,0:T(8,128)(2,1)}, bf16[256,256]{1,0:T(8,128)(2,1)}, u32[]{:S(2)}, u32[]{:S(2)}) collective-permute-start(bf16[256,256]{1,0:T(8,128)(2,1)} %get-tuple-element.21), channel_id=1, source_target_pairs={{0,2},{1,3},{2,0},{3,1},{4,6},{5,7},{6,4},{7,5},{8,10},{9,11},{10,... | collective-permute-start | bytes 393224 | tf_op jit(solution)/shard_map/ppermute | solution.py:21
  50.1 0.7 copy-done.11
  51.0 1.7 %copy.24 = bf16[256,256]{0,1:T(8,128)(2,1)} copy(bf16[256,256]{1,0:T(8,128)(2,1)} %param.17) | data formatting | bytes 262144 | tf_op args[8]
  52.7 0.9 copy-done.6
  53.6 0.9 copy-done.8
  54.6 0.9 copy-done.10
  55.5 0.9 copy-done.12
  56.5 2.0 %shard_map.113 = (f32[256,256]{1,0:T(8,128)S(1)}, bf16[256,256]{1,0:T(8,128)(2,1)S(1)}, bf16[256,256]{1,0:T(8,128)(2,1)S(1)}, bf16[256,256]{1,0:T(8,128)(2,1)S(1)}) custom-call(s32[32]{0:T(128)S(1)} %get-tuple-element.43.which, s32[32]{0:T(128)S(1)} %get-tuple-element.42.slot, s32[32]{0:T(128)S(1)} %broadcast_select_fusion.target, ...), custom_call_target="tpu_custom_call" | custom-call | flops 268435456 | bytes 7078272 | tf_op jit(solution)/shard_map/pallas_call | solution.py:30
  58.6 0.7 copy-done.13
  61.2 1.0 copy.21
  62.2 0.7 collective-permute-start.24
  63.0 1.0 copy.22
  64.0 3.5 %collective-permute-start.25 = (bf16[256,256]{0,1:T(8,128)(2,1)S(1)}, bf16[256,256]{0,1:T(8,128)(2,1)S(1)}, u32[]{:S(2)}, u32[]{:S(2)}) collective-permute-start(bf16[256,256]{0,1:T(8,128)(2,1)S(1)} %copy.22), channel_id=1, source_target_pairs={{0,2},{1,3},{2,0},{3,1},{4,6},{5,7},{6,4},{7,5},{8,10},{9,11},{10,... | collective-permute-start | bytes 393224 | tf_op jit(solution)/shard_map/ppermute | solution.py:21
  67.5 1.0 copy.23
  68.8 1.4 %fusion.4 = f32[256,256]{0,1:T(8,128)S(1)} fusion(bf16[256,256]{1,0:T(8,128)(2,1)S(1)} %copy-done, bf16[256,256]{1,0:T(8,128)(2,1)} %collective-permute-done.9, bf16[256,256]{1,0:T(8,128)(2,1)} %collective-permute-done.8, f32[256,256]{1,0:T(8,128)S(1)} %get-tuple-element.19, bf16[256,256]{1,0:T(8,128)(2,1)} %collective-permute-done.7), kind=kOutput, calls=%fused_computation.19 | convolution fusion | flops 201719808 | bytes 1048576 | tf_op jit(solution)/shard_map/dot_general | solution.py:145
  70.3 1.1 copy.20
  71.3 5.2 %collective-permute-done.25 = bf16[256,256]{0,1:T(8,128)(2,1)S(1)} collective-permute-done((bf16[256,256]{0,1:T(8,128)(2,1)S(1)}, bf16[256,256]{0,1:T(8,128)(2,1)S(1)}, u32[]{:S(2)}, u32[]{:S(2)}) %collective-permute-start.25) | collective-permute-done | bytes 131104 | tf_op jit(solution)/shard_map/ppermute | solution.py:21
  76.6 1.1 multiply_convert_fusion
  77.6 1.3 %fusion.1 = f32[256,256]{1,0:T(8,128)S(1)} fusion(bf16[256,256]{0,1:T(8,128)(2,1)S(1)} %get-tuple-element.44, bf16[256,256]{1,0:T(8,128)(2,1)} %collective-permute-done.9, bf16[256,256]{1,0:T(8,128)(2,1)} %collective-permute-done.8, f32[256,256]{1,0:T(8,128)S(1)} %get-tuple-element.19, bf16[256,256]{1,0:T(8,128)(2,1)} %collective-permute-done.7), kind=kOutput, calls=%fused_computation.16 | convolution fusion | flops 34013184 | bytes 1048576 | tf_op jit(solution)/shard_map/dot_general | solution.py:168
  79.0 1.2 %collective-permute-done.37 = bf16[128,256]{1,0:T(8,128)(2,1)S(1)} collective-permute-done((bf16[128,256]{1,0:T(8,128)(2,1)S(1)}, bf16[128,256]{1,0:T(8,128)(2,1)S(1)}, u32[]{:S(2)}, u32[]{:S(2)}) %collective-permute-start.37) | collective-permute-done | bytes 65568 | tf_op jit(solution)/shard_map/ppermute | solution.py:21
  80.3 1.5 %collective-permute-start.38 = (bf16[128,256]{1,0:T(8,128)(2,1)S(1)}, bf16[128,256]{1,0:T(8,128)(2,1)S(1)}, u32[]{:S(2)}, u32[]{:S(2)}) collective-permute-start(bf16[128,256]{1,0:T(8,128)(2,1)S(1)} %fusion), channel_id=1, source_target_pairs={{0,8},{4,12},{8,0},{12,4},{16,24},{20,28},{24,16},{28,20},{1,9},{5... | collective-permute-start | bytes 196616 | tf_op jit(solution)/shard_map/ppermute | solution.py:21
  82.2 1.6 %collective-permute-start.40 = (bf16[128,256]{1,0:T(8,128)(2,1)S(1)}, bf16[128,256]{1,0:T(8,128)(2,1)S(1)}, u32[]{:S(2)}, u32[]{:S(2)}) collective-permute-start(bf16[128,256]{1,0:T(8,128)(2,1)S(1)} %fusion), channel_id=1, source_target_pairs={{0,24},{4,28},{8,16},{12,20},{16,8},{20,12},{24,0},{28,4},{1,25},{... | collective-permute-start | bytes 196616 | tf_op jit(solution)/shard_map/ppermute | solution.py:21
  83.9 2.5 %collective-permute-start.27 = (bf16[256,256]{1,0:T(8,128)(2,1)S(1)}, bf16[256,256]{1,0:T(8,128)(2,1)S(1)}, u32[]{:S(2)}, u32[]{:S(2)}) collective-permute-start(bf16[256,256]{1,0:T(8,128)(2,1)S(1)} %bitcast.15), channel_id=1, source_target_pairs={{0,1},{1,0},{2,3},{3,2},{4,5},{5,4},{6,7},{7,6},{8,9},{9,8},{10,11... | collective-permute-start | bytes 393224 | tf_op jit(solution)/shard_map/ppermute | solution.py:21
  86.3 1.0 collective-permute-start.28
  87.3 1.5 %collective-permute-start.29 = (bf16[256,256]{1,0:T(8,128)(2,1)S(1)}, bf16[256,256]{1,0:T(8,128)(2,1)S(1)}, u32[]{:S(2)}, u32[]{:S(2)}) collective-permute-start(bf16[256,256]{1,0:T(8,128)(2,1)S(1)} %bitcast.17), channel_id=1, source_target_pairs={{0,3},{1,2},{2,1},{3,0},{4,7},{5,6},{6,5},{7,4},{8,11},{9,10},{10,... | collective-permute-start | bytes 393224 | tf_op jit(solution)/shard_map/ppermute | solution.py:21
  88.8 1.2 %collective-permute-start.41 = (bf16[128,256]{1,0:T(8,128)(2,1)S(1)}, bf16[128,256]{1,0:T(8,128)(2,1)S(1)}, u32[]{:S(2)}, u32[]{:S(2)}) collective-permute-start(bf16[128,256]{1,0:T(8,128)(2,1)S(1)} %add_convert_fusion.5), channel_id=1, source_target_pairs={{0,1},{1,0},{2,3},{3,2},{4,5},{5,4},{6,7},{7,6},{8,9},{9,8},{10,11... | collective-permute-start | bytes 196616 | tf_op jit(solution)/shard_map/ppermute | solution.py:21
  90.0 1.8 %collective-permute-start.42 = (bf16[128,256]{1,0:T(8,128)(2,1)S(1)}, bf16[128,256]{1,0:T(8,128)(2,1)S(1)}, u32[]{:S(2)}, u32[]{:S(2)}) collective-permute-start(bf16[128,256]{1,0:T(8,128)(2,1)S(1)} %add_convert_fusion.5), channel_id=1, source_target_pairs={{0,2},{1,3},{2,0},{3,1},{4,6},{5,7},{6,4},{7,5},{8,10},{9,11},{10,... | collective-permute-start | bytes 196616 | tf_op jit(solution)/shard_map/ppermute | solution.py:21
  91.8 1.5 %collective-permute-start.43 = (bf16[128,256]{1,0:T(8,128)(2,1)S(1)}, bf16[128,256]{1,0:T(8,128)(2,1)S(1)}, u32[]{:S(2)}, u32[]{:S(2)}) collective-permute-start(bf16[128,256]{1,0:T(8,128)(2,1)S(1)} %add_convert_fusion.5), channel_id=1, source_target_pairs={{0,3},{1,2},{2,1},{3,0},{4,7},{5,6},{6,5},{7,4},{8,11},{9,10},{10,... | collective-permute-start | bytes 196616 | tf_op jit(solution)/shard_map/ppermute | solution.py:21
  93.3 8.3 %collective-permute-done.28.refs_2_ = bf16[256,256]{1,0:T(8,128)(2,1)S(1)} collective-permute-done((bf16[256,256]{1,0:T(8,128)(2,1)S(1)}, bf16[256,256]{1,0:T(8,128)(2,1)S(1)}, u32[]{:S(2)}, u32[]{:S(2)}) %collective-permute-start.28) | collective-permute-done | bytes 131104 | tf_op jit(solution)/shard_map/ppermute | solution.py:21
  101.6 2.2 %copy-done.2 = bf16[1024,2048]{1,0:T(8,128)(2,1)S(1)} copy-done((bf16[1024,2048]{1,0:T(8,128)(2,1)S(1)}, bf16[1024,2048]{1,0:T(8,128)(2,1)}, u32[]{:S(2)}) %copy-start.2) | copy-done | bytes 4194328
  103.7 0.8 shard_map.115
  105.1 0.8 copy-done.3
  105.9 0.8 shard_map.114
  107.6 1.5 %collective-permute-start.32 = (bf16[256,256]{1,0:T(8,128)(2,1)S(1)}, bf16[256,256]{1,0:T(8,128)(2,1)S(1)}, u32[]{:S(2)}, u32[]{:S(2)}) collective-permute-start(bf16[256,256]{1,0:T(8,128)(2,1)S(1)} %add_convert_fusion.3), channel_id=1, source_target_pairs={{0,8},{4,12},{8,0},{12,4},{16,24},{20,28},{24,16},{28,20},{1,9},{5... | collective-permute-start | bytes 393224 | tf_op jit(solution)/shard_map/ppermute | solution.py:21
  109.6 1.7 %collective-permute-start.36 = (bf16[256,256]{1,0:T(8,128)(2,1)S(1)}, bf16[256,256]{1,0:T(8,128)(2,1)S(1)}, u32[]{:S(2)}, u32[]{:S(2)}) collective-permute-start(bf16[256,256]{1,0:T(8,128)(2,1)S(1)} %add_convert_fusion.1), channel_id=1, source_target_pairs={{0,24},{4,28},{8,16},{12,20},{16,8},{20,12},{24,0},{28,4},{1,25},{... | collective-permute-start | bytes 393224 | tf_op jit(solution)/shard_map/ppermute | solution.py:21
  111.4 0.8 copy.25
  112.2 0.7 maximum_select_fusion
  112.9 0.8 collective-permute-done.32
  113.7 3.9 %collective-permute-done.34 = bf16[256,256]{1,0:T(8,128)(2,1)S(1)} collective-permute-done((bf16[256,256]{1,0:T(8,128)(2,1)S(1)}, bf16[256,256]{1,0:T(8,128)(2,1)S(1)}, u32[]{:S(2)}, u32[]{:S(2)}) %collective-permute-start.34) | collective-permute-done | bytes 131104 | tf_op jit(solution)/shard_map/ppermute | solution.py:21
  117.5 0.9 convolution_convert_fusion
  (96 shorter events, 7.9 us)
Async XLA Ops:
  0.6 68.2 %copy-start = (bf16[256,256]{1,0:T(8,128)(2,1)S(1)}, bf16[256,256]{1,0:T(8,128)(2,1)}, u32[]{:S(2)}) copy-start(bf16[256,256]{1,0:T(8,128)(2,1)} %param.10) | copy-start | bytes 393220
  0.6 52.0 %copy-start.4 = (bf16[32,128,128]{2,1,0:T(8,128)(2,1)S(1)}, bf16[32,128,128]{2,1,0:T(8,128)(2,1)}, u32[]{:S(2)}) copy-start(bf16[32,128,128]{2,1,0:T(8,128)(2,1)} %tiles.1) | copy-start | bytes 3145732
  0.7 9.1 %collective-permute-start.1 = (bf16[256,256]{1,0:T(8,128)(2,1)}, bf16[256,256]{1,0:T(8,128)(2,1)}, u32[]{:S(2)}, u32[]{:S(2)}) collective-permute-start(bf16[256,256]{1,0:T(8,128)(2,1)} %refs_0_.1), channel_id=1, source_target_pairs={{0,8},{4,12},{8,0},{12,4},{16,24},{20,28},{24,16},{28,20},{1,9},{5... | collective-permute-start | bytes 393224 | tf_op jit(solution)/shard_map/ppermute | solution.py:21
  4.7 17.5 %collective-permute-start.11 = (bf16[512,256]{1,0:T(8,128)(2,1)S(1)}, bf16[512,256]{1,0:T(8,128)(2,1)S(1)}, u32[]{:S(2)}, u32[]{:S(2)}) collective-permute-start(bf16[512,256]{1,0:T(8,128)(2,1)S(1)} %get-tuple-element.47.refs_0_), channel_id=1, source_target_pairs={{0,8},{4,12},{8,0},{12,4},{16,24},{20,28},{24,16},{28,20},{1,9},{5... | collective-permute-start | bytes 786440 | tf_op jit(solution)/shard_map/ppermute | solution.py:21
  4.9 17.8 %collective-permute-start.20 = (bf16[512,256]{1,0:T(8,128)(2,1)S(1)}, bf16[512,256]{1,0:T(8,128)(2,1)S(1)}, u32[]{:S(2)}, u32[]{:S(2)}) collective-permute-start(bf16[512,256]{1,0:T(8,128)(2,1)S(1)} %get-tuple-element.46.refs_8_), channel_id=1, source_target_pairs={{0,16},{4,20},{8,24},{12,28},{16,0},{20,4},{24,8},{28,12},{1,17},{... | collective-permute-start | bytes 786440 | tf_op jit(solution)/shard_map/ppermute | solution.py:21
  6.8 11.5 %collective-permute-start.3 = (bf16[256,256]{1,0:T(8,128)(2,1)}, bf16[256,256]{1,0:T(8,128)(2,1)}, u32[]{:S(2)}, u32[]{:S(2)}) collective-permute-start(bf16[256,256]{1,0:T(8,128)(2,1)} %refs_0_.1), channel_id=1, source_target_pairs={{0,16},{4,20},{8,24},{12,28},{16,0},{20,4},{24,8},{28,12},{1,17},{... | collective-permute-start | bytes 393224 | tf_op jit(solution)/shard_map/ppermute | solution.py:21
  6.9 13.2 %collective-permute-start.5 = (bf16[256,256]{1,0:T(8,128)(2,1)}, bf16[256,256]{1,0:T(8,128)(2,1)}, u32[]{:S(2)}, u32[]{:S(2)}) collective-permute-start(bf16[256,256]{1,0:T(8,128)(2,1)} %refs_0_.1), channel_id=1, source_target_pairs={{0,24},{4,28},{8,16},{12,20},{16,8},{20,12},{24,0},{28,4},{1,25},{... | collective-permute-start | bytes 393224 | tf_op jit(solution)/shard_map/ppermute | solution.py:21
  9.8 11.8 %collective-permute-start = (bf16[256,256]{1,0:T(8,128)(2,1)}, bf16[256,256]{1,0:T(8,128)(2,1)S(1)}, u32[]{:S(2)}, u32[]{:S(2)}) collective-permute-start(bf16[256,256]{1,0:T(8,128)(2,1)} %refs_0_.1), channel_id=1, source_target_pairs={{0,4},{4,0},{8,12},{12,8},{16,20},{20,16},{24,28},{28,24},{1,5},{5... | collective-permute-start | bytes 393224 | tf_op jit(solution)/shard_map/ppermute | solution.py:21
  18.4 6.5 %collective-permute-start.13 = (bf16[512,256]{1,0:T(8,128)(2,1)S(1)}, bf16[512,256]{1,0:T(8,128)(2,1)S(1)}, u32[]{:S(2)}, u32[]{:S(2)}) collective-permute-start(bf16[512,256]{1,0:T(8,128)(2,1)S(1)} %get-tuple-element.47.refs_0_), channel_id=1, source_target_pairs={{0,16},{4,20},{8,24},{12,28},{16,0},{20,4},{24,8},{28,12},{1,17},{... | collective-permute-start | bytes 786440 | tf_op jit(solution)/shard_map/ppermute | solution.py:21
  20.1 6.7 %collective-permute-start.18 = (bf16[512,256]{1,0:T(8,128)(2,1)S(1)}, bf16[512,256]{1,0:T(8,128)(2,1)S(1)}, u32[]{:S(2)}, u32[]{:S(2)}) collective-permute-start(bf16[512,256]{1,0:T(8,128)(2,1)S(1)} %get-tuple-element.46.refs_8_), channel_id=1, source_target_pairs={{0,8},{4,12},{8,0},{12,4},{16,24},{20,28},{24,16},{28,20},{1,9},{5... | collective-permute-start | bytes 786440 | tf_op jit(solution)/shard_map/ppermute | solution.py:21
  21.6 0.7 copy-start.15
  22.2 4.6 %collective-permute-start.10 = (bf16[512,256]{1,0:T(8,128)(2,1)S(1)}, bf16[512,256]{1,0:T(8,128)(2,1)S(1)}, u32[]{:S(2)}, u32[]{:S(2)}) collective-permute-start(bf16[512,256]{1,0:T(8,128)(2,1)S(1)} %get-tuple-element.47.refs_0_), channel_id=1, source_target_pairs={{0,4},{4,0},{8,12},{12,8},{16,20},{20,16},{24,28},{28,24},{1,5},{5... | collective-permute-start | bytes 786440 | tf_op jit(solution)/shard_map/ppermute | solution.py:21
  22.2 5.1 %collective-permute-start.17 = (bf16[512,256]{1,0:T(8,128)(2,1)S(1)}, bf16[512,256]{1,0:T(8,128)(2,1)S(1)}, u32[]{:S(2)}, u32[]{:S(2)}) collective-permute-start(bf16[512,256]{1,0:T(8,128)(2,1)S(1)} %get-tuple-element.46.refs_8_), channel_id=1, source_target_pairs={{0,4},{4,0},{8,12},{12,8},{16,20},{20,16},{24,28},{28,24},{1,5},{5... | collective-permute-start | bytes 786440 | tf_op jit(solution)/shard_map/ppermute | solution.py:21
  22.7 4.7 %collective-permute-start.2 = (bf16[256,256]{1,0:T(8,128)(2,1)}, bf16[256,256]{1,0:T(8,128)(2,1)S(1)}, u32[]{:S(2)}, u32[]{:S(2)}) collective-permute-start(bf16[256,256]{1,0:T(8,128)(2,1)} %collective-permute-done.1.refs_2_), channel_id=1, source_target_pairs={{0,4},{4,0},{8,12},{12,8},{16,20},{20,16},{24,28},{28,24},{1,5},{5... | collective-permute-start | bytes 393224 | tf_op jit(solution)/shard_map/ppermute | solution.py:21
  24.8 7.4 %collective-permute-start.15 = (bf16[512,256]{1,0:T(8,128)(2,1)S(1)}, bf16[512,256]{1,0:T(8,128)(2,1)}, u32[]{:S(2)}, u32[]{:S(2)}) collective-permute-start(bf16[512,256]{1,0:T(8,128)(2,1)S(1)} %collective-permute-done.11.refs_2_), channel_id=1, source_target_pairs={{0,16},{4,20},{8,24},{12,28},{16,0},{20,4},{24,8},{28,12},{1,17},{... | collective-permute-start | bytes 786440 | tf_op jit(solution)/shard_map/ppermute | solution.py:21
  26.8 2.8 %collective-permute-start.4 = (bf16[256,256]{1,0:T(8,128)(2,1)}, bf16[256,256]{1,0:T(8,128)(2,1)S(1)}, u32[]{:S(2)}, u32[]{:S(2)}) collective-permute-start(bf16[256,256]{1,0:T(8,128)(2,1)} %collective-permute-done.3.refs_4_), channel_id=1, source_target_pairs={{0,4},{4,0},{8,12},{12,8},{16,20},{20,16},{24,28},{28,24},{1,5},{5... | collective-permute-start | bytes 393224 | tf_op jit(solution)/shard_map/ppermute | solution.py:21
  26.9 2.9 %collective-permute-start.6 = (bf16[256,256]{1,0:T(8,128)(2,1)}, bf16[256,256]{1,0:T(8,128)(2,1)S(1)}, u32[]{:S(2)}, u32[]{:S(2)}) collective-permute-start(bf16[256,256]{1,0:T(8,128)(2,1)} %collective-permute-done.5.refs_6_), channel_id=1, source_target_pairs={{0,4},{4,0},{8,12},{12,8},{16,20},{20,16},{24,28},{28,24},{1,5},{5... | collective-permute-start | bytes 393224 | tf_op jit(solution)/shard_map/ppermute | solution.py:21
  27.4 8.9 %collective-permute-start.12 = (bf16[512,256]{1,0:T(8,128)(2,1)S(1)}, bf16[512,256]{1,0:T(8,128)(2,1)S(1)}, u32[]{:S(2)}, u32[]{:S(2)}) collective-permute-start(bf16[512,256]{1,0:T(8,128)(2,1)S(1)} %collective-permute-done.11.refs_2_), channel_id=1, source_target_pairs={{0,4},{4,0},{8,12},{12,8},{16,20},{20,16},{24,28},{28,24},{1,5},{5... | collective-permute-start | bytes 786440 | tf_op jit(solution)/shard_map/ppermute | solution.py:21
  27.4 8.8 %collective-permute-start.22 = (bf16[512,256]{1,0:T(8,128)(2,1)S(1)}, bf16[512,256]{1,0:T(8,128)(2,1)}, u32[]{:S(2)}, u32[]{:S(2)}) collective-permute-start(bf16[512,256]{1,0:T(8,128)(2,1)S(1)} %collective-permute-done.20.refs_12_), channel_id=1, source_target_pairs={{0,8},{4,12},{8,0},{12,4},{16,24},{20,28},{24,16},{28,20},{1,9},{5... | collective-permute-start | bytes 786440 | tf_op jit(solution)/shard_map/ppermute | solution.py:21
  29.5 15.0 %collective-permute-start.21 = (bf16[512,256]{1,0:T(8,128)(2,1)S(1)}, bf16[512,256]{1,0:T(8,128)(2,1)S(1)}, u32[]{:S(2)}, u32[]{:S(2)}) collective-permute-start(bf16[512,256]{1,0:T(8,128)(2,1)S(1)} %collective-permute-done.20.refs_12_), channel_id=1, source_target_pairs={{0,4},{4,0},{8,12},{12,8},{16,20},{20,16},{24,28},{28,24},{1,5},{5... | collective-permute-start | bytes 786440 | tf_op jit(solution)/shard_map/ppermute | solution.py:21
  29.7 17.1 %collective-permute-start.14 = (bf16[512,256]{1,0:T(8,128)(2,1)S(1)}, bf16[512,256]{1,0:T(8,128)(2,1)S(1)}, u32[]{:S(2)}, u32[]{:S(2)}) collective-permute-start(bf16[512,256]{1,0:T(8,128)(2,1)S(1)} %collective-permute-done.13.refs_4_), channel_id=1, source_target_pairs={{0,4},{4,0},{8,12},{12,8},{16,20},{20,16},{24,28},{28,24},{1,5},{5... | collective-permute-start | bytes 786440 | tf_op jit(solution)/shard_map/ppermute | solution.py:21
  32.2 17.9 %collective-permute-start.19 = (bf16[512,256]{1,0:T(8,128)(2,1)S(1)}, bf16[512,256]{1,0:T(8,128)(2,1)S(1)}, u32[]{:S(2)}, u32[]{:S(2)}) collective-permute-start(bf16[512,256]{1,0:T(8,128)(2,1)S(1)} %collective-permute-done.18.refs_10_), channel_id=1, source_target_pairs={{0,4},{4,0},{8,12},{12,8},{16,20},{20,16},{24,28},{28,24},{1,5},{5... | collective-permute-start | bytes 786440 | tf_op jit(solution)/shard_map/ppermute | solution.py:21
  36.2 16.5 %collective-permute-start.16 = (bf16[512,256]{1,0:T(8,128)(2,1)}, bf16[512,256]{1,0:T(8,128)(2,1)}, u32[]{:S(2)}, u32[]{:S(2)}) collective-permute-start(bf16[512,256]{1,0:T(8,128)(2,1)} %collective-permute-done.15.refs_6_), channel_id=1, source_target_pairs={{0,4},{4,0},{8,12},{12,8},{16,20},{20,16},{24,28},{28,24},{1,5},{5... | collective-permute-start | bytes 786440 | tf_op jit(solution)/shard_map/ppermute | solution.py:21
  36.2 0.7 copy-start.5
  36.9 15.8 %collective-permute-start.23 = (bf16[512,256]{1,0:T(8,128)(2,1)}, bf16[512,256]{1,0:T(8,128)(2,1)}, u32[]{:S(2)}, u32[]{:S(2)}) collective-permute-start(bf16[512,256]{1,0:T(8,128)(2,1)} %collective-permute-done.22.refs_14_), channel_id=1, source_target_pairs={{0,4},{4,0},{8,12},{12,8},{16,20},{20,16},{24,28},{28,24},{1,5},{5... | collective-permute-start | bytes 786440 | tf_op jit(solution)/shard_map/ppermute | solution.py:21
  37.4 2.2 %copy-start.1 = (bf16[1024,2048]{1,0:T(8,128)(2,1)S(1)}, bf16[1024,2048]{1,0:T(8,128)(2,1)}, u32[]{:S(2)}) copy-start(bf16[1024,2048]{1,0:T(8,128)(2,1)} %a_ref.5) | copy-start | bytes 12582916
  39.6 0.9 copy-start.14
  40.5 0.9 copy-start.16
  44.5 0.7 copy-start.7
  45.2 23.3 %collective-permute-start.7 = (bf16[256,256]{1,0:T(8,128)(2,1)}, bf16[256,256]{1,0:T(8,128)(2,1)}, u32[]{:S(2)}, u32[]{:S(2)}) collective-permute-start(bf16[256,256]{1,0:T(8,128)(2,1)} %get-tuple-element.20), channel_id=1, source_target_pairs={{0,1},{1,0},{2,3},{3,2},{4,5},{5,4},{6,7},{7,6},{8,9},{9,8},{10,11... | collective-permute-start | bytes 393224 | tf_op jit(solution)/shard_map/ppermute | solution.py:21
  46.8 0.7 copy-start.9
  47.5 21.3 %collective-permute-start.8 = (bf16[256,256]{1,0:T(8,128)(2,1)}, bf16[256,256]{1,0:T(8,128)(2,1)}, u32[]{:S(2)}, u32[]{:S(2)}) collective-permute-start(bf16[256,256]{1,0:T(8,128)(2,1)} %get-tuple-element.21), channel_id=1, source_target_pairs={{0,2},{1,3},{2,0},{3,1},{4,6},{5,7},{6,4},{7,5},{8,10},{9,11},{10,... | collective-permute-start | bytes 393224 | tf_op jit(solution)/shard_map/ppermute | solution.py:21
  50.1 0.7 copy-start.11
  50.8 18.1 %collective-permute-start.9 = (bf16[256,256]{1,0:T(8,128)(2,1)}, bf16[256,256]{1,0:T(8,128)(2,1)}, u32[]{:S(2)}, u32[]{:S(2)}) collective-permute-start(bf16[256,256]{1,0:T(8,128)(2,1)} %get-tuple-element.22), channel_id=1, source_target_pairs={{0,3},{1,2},{2,1},{3,0},{4,7},{5,6},{6,5},{7,4},{8,11},{9,10},{10,... | collective-permute-start | bytes 393224 | tf_op jit(solution)/shard_map/ppermute | solution.py:21
  52.7 1.0 copy-start.6
  53.6 0.9 copy-start.8
  54.6 0.9 copy-start.10
  55.5 0.9 copy-start.12
  58.6 0.7 copy-start.13
  59.3 0.7 copy-start.17
  59.9 0.7 copy-start.18
  62.2 9.1 %collective-permute-start.24 = (bf16[256,256]{0,1:T(8,128)(2,1)S(1)}, bf16[256,256]{0,1:T(8,128)(2,1)S(1)}, u32[]{:S(2)}, u32[]{:S(2)}) collective-permute-start(bf16[256,256]{0,1:T(8,128)(2,1)S(1)} %copy.21), channel_id=1, source_target_pairs={{0,1},{1,0},{2,3},{3,2},{4,5},{5,4},{6,7},{7,6},{8,9},{9,8},{10,11... | collective-permute-start | bytes 393224 | tf_op jit(solution)/shard_map/ppermute | solution.py:21
  64.0 12.6 %collective-permute-start.25 = (bf16[256,256]{0,1:T(8,128)(2,1)S(1)}, bf16[256,256]{0,1:T(8,128)(2,1)S(1)}, u32[]{:S(2)}, u32[]{:S(2)}) collective-permute-start(bf16[256,256]{0,1:T(8,128)(2,1)S(1)} %copy.22), channel_id=1, source_target_pairs={{0,2},{1,3},{2,0},{3,1},{4,6},{5,7},{6,4},{7,5},{8,10},{9,11},{10,... | collective-permute-start | bytes 393224 | tf_op jit(solution)/shard_map/ppermute | solution.py:21
  68.5 8.0 %collective-permute-start.26 = (bf16[256,256]{0,1:T(8,128)(2,1)S(1)}, bf16[256,256]{0,1:T(8,128)(2,1)S(1)}, u32[]{:S(2)}, u32[]{:S(2)}) collective-permute-start(bf16[256,256]{0,1:T(8,128)(2,1)S(1)} %copy.23), channel_id=1, source_target_pairs={{0,3},{1,2},{2,1},{3,0},{4,7},{5,6},{6,5},{7,4},{8,11},{9,10},{10,... | collective-permute-start | bytes 393224 | tf_op jit(solution)/shard_map/ppermute | solution.py:21
  79.0 1.3 %collective-permute-start.37 = (bf16[128,256]{1,0:T(8,128)(2,1)S(1)}, bf16[128,256]{1,0:T(8,128)(2,1)S(1)}, u32[]{:S(2)}, u32[]{:S(2)}) collective-permute-start(bf16[128,256]{1,0:T(8,128)(2,1)S(1)} %fusion.3), channel_id=1, source_target_pairs={{0,4},{4,0},{8,12},{12,8},{16,20},{20,16},{24,28},{28,24},{1,5},{5... | collective-permute-start | bytes 196616 | tf_op jit(solution)/shard_map/ppermute | solution.py:21
  80.3 7.0 %collective-permute-start.38 = (bf16[128,256]{1,0:T(8,128)(2,1)S(1)}, bf16[128,256]{1,0:T(8,128)(2,1)S(1)}, u32[]{:S(2)}, u32[]{:S(2)}) collective-permute-start(bf16[128,256]{1,0:T(8,128)(2,1)S(1)} %fusion), channel_id=1, source_target_pairs={{0,8},{4,12},{8,0},{12,4},{16,24},{20,28},{24,16},{28,20},{1,9},{5... | collective-permute-start | bytes 196616 | tf_op jit(solution)/shard_map/ppermute | solution.py:21
  81.8 6.9 %collective-permute-start.39 = (bf16[128,256]{1,0:T(8,128)(2,1)S(1)}, bf16[128,256]{1,0:T(8,128)(2,1)S(1)}, u32[]{:S(2)}, u32[]{:S(2)}) collective-permute-start(bf16[128,256]{1,0:T(8,128)(2,1)S(1)} %fusion), channel_id=1, source_target_pairs={{0,16},{4,20},{8,24},{12,28},{16,0},{20,4},{24,8},{28,12},{1,17},{... | collective-permute-start | bytes 196616 | tf_op jit(solution)/shard_map/ppermute | solution.py:21
  82.2 6.5 %collective-permute-start.40 = (bf16[128,256]{1,0:T(8,128)(2,1)S(1)}, bf16[128,256]{1,0:T(8,128)(2,1)S(1)}, u32[]{:S(2)}, u32[]{:S(2)}) collective-permute-start(bf16[128,256]{1,0:T(8,128)(2,1)S(1)} %fusion), channel_id=1, source_target_pairs={{0,24},{4,28},{8,16},{12,20},{16,8},{20,12},{24,0},{28,4},{1,25},{... | collective-permute-start | bytes 196616 | tf_op jit(solution)/shard_map/ppermute | solution.py:21
  83.9 7.9 %collective-permute-start.27 = (bf16[256,256]{1,0:T(8,128)(2,1)S(1)}, bf16[256,256]{1,0:T(8,128)(2,1)S(1)}, u32[]{:S(2)}, u32[]{:S(2)}) collective-permute-start(bf16[256,256]{1,0:T(8,128)(2,1)S(1)} %bitcast.15), channel_id=1, source_target_pairs={{0,1},{1,0},{2,3},{3,2},{4,5},{5,4},{6,7},{7,6},{8,9},{9,8},{10,11... | collective-permute-start | bytes 393224 | tf_op jit(solution)/shard_map/ppermute | solution.py:21
  86.3 15.2 %collective-permute-start.28 = (bf16[256,256]{1,0:T(8,128)(2,1)S(1)}, bf16[256,256]{1,0:T(8,128)(2,1)S(1)}, u32[]{:S(2)}, u32[]{:S(2)}) collective-permute-start(bf16[256,256]{1,0:T(8,128)(2,1)S(1)} %bitcast.16), channel_id=1, source_target_pairs={{0,2},{1,3},{2,0},{3,1},{4,6},{5,7},{6,4},{7,5},{8,10},{9,11},{10,... | collective-permute-start | bytes 393224 | tf_op jit(solution)/shard_map/ppermute | solution.py:21
  87.3 14.3 %collective-permute-start.29 = (bf16[256,256]{1,0:T(8,128)(2,1)S(1)}, bf16[256,256]{1,0:T(8,128)(2,1)S(1)}, u32[]{:S(2)}, u32[]{:S(2)}) collective-permute-start(bf16[256,256]{1,0:T(8,128)(2,1)S(1)} %bitcast.17), channel_id=1, source_target_pairs={{0,3},{1,2},{2,1},{3,0},{4,7},{5,6},{6,5},{7,4},{8,11},{9,10},{10,... | collective-permute-start | bytes 393224 | tf_op jit(solution)/shard_map/ppermute | solution.py:21
  88.8 17.9 %collective-permute-start.41 = (bf16[128,256]{1,0:T(8,128)(2,1)S(1)}, bf16[128,256]{1,0:T(8,128)(2,1)S(1)}, u32[]{:S(2)}, u32[]{:S(2)}) collective-permute-start(bf16[128,256]{1,0:T(8,128)(2,1)S(1)} %add_convert_fusion.5), channel_id=1, source_target_pairs={{0,1},{1,0},{2,3},{3,2},{4,5},{5,4},{6,7},{7,6},{8,9},{9,8},{10,11... | collective-permute-start | bytes 196616 | tf_op jit(solution)/shard_map/ppermute | solution.py:21
  90.0 16.8 %collective-permute-start.42 = (bf16[128,256]{1,0:T(8,128)(2,1)S(1)}, bf16[128,256]{1,0:T(8,128)(2,1)S(1)}, u32[]{:S(2)}, u32[]{:S(2)}) collective-permute-start(bf16[128,256]{1,0:T(8,128)(2,1)S(1)} %add_convert_fusion.5), channel_id=1, source_target_pairs={{0,2},{1,3},{2,0},{3,1},{4,6},{5,7},{6,4},{7,5},{8,10},{9,11},{10,... | collective-permute-start | bytes 196616 | tf_op jit(solution)/shard_map/ppermute | solution.py:21
  91.8 15.5 %collective-permute-start.43 = (bf16[128,256]{1,0:T(8,128)(2,1)S(1)}, bf16[128,256]{1,0:T(8,128)(2,1)S(1)}, u32[]{:S(2)}, u32[]{:S(2)}) collective-permute-start(bf16[128,256]{1,0:T(8,128)(2,1)S(1)} %add_convert_fusion.5), channel_id=1, source_target_pairs={{0,3},{1,2},{2,1},{3,0},{4,7},{5,6},{6,5},{7,4},{8,11},{9,10},{10,... | collective-permute-start | bytes 196616 | tf_op jit(solution)/shard_map/ppermute | solution.py:21
  101.6 2.2 %copy-start.2 = (bf16[1024,2048]{1,0:T(8,128)(2,1)S(1)}, bf16[1024,2048]{1,0:T(8,128)(2,1)}, u32[]{:S(2)}) copy-start(bf16[1024,2048]{1,0:T(8,128)(2,1)} %a_ref.5) | copy-start | bytes 12582916
  103.7 2.2 %copy-start.3 = (bf16[1024,2048]{1,0:T(8,128)(2,1)S(1)}, bf16[1024,2048]{1,0:T(8,128)(2,1)}, u32[]{:S(2)}) copy-start(bf16[1024,2048]{1,0:T(8,128)(2,1)} %a_ref.5) | copy-start | bytes 12582916
  104.6 3.0 %collective-permute-start.31 = (bf16[256,256]{1,0:T(8,128)(2,1)S(1)}, bf16[256,256]{1,0:T(8,128)(2,1)S(1)}, u32[]{:S(2)}, u32[]{:S(2)}) collective-permute-start(bf16[256,256]{1,0:T(8,128)(2,1)S(1)} %get-tuple-element.30), channel_id=1, source_target_pairs={{0,4},{4,0},{8,12},{12,8},{16,20},{20,16},{24,28},{28,24},{1,5},{5... | collective-permute-start | bytes 393224 | tf_op jit(solution)/shard_map/ppermute | solution.py:21
  104.6 4.4 %collective-permute-start.33 = (bf16[256,256]{1,0:T(8,128)(2,1)S(1)}, bf16[256,256]{1,0:T(8,128)(2,1)S(1)}, u32[]{:S(2)}, u32[]{:S(2)}) collective-permute-start(bf16[256,256]{1,0:T(8,128)(2,1)S(1)} %get-tuple-element.32), channel_id=1, source_target_pairs={{0,4},{4,0},{8,12},{12,8},{16,20},{20,16},{24,28},{28,24},{1,5},{5... | collective-permute-start | bytes 393224 | tf_op jit(solution)/shard_map/ppermute | solution.py:21
  106.7 2.8 %collective-permute-start.35 = (bf16[256,256]{1,0:T(8,128)(2,1)S(1)}, bf16[256,256]{1,0:T(8,128)(2,1)S(1)}, u32[]{:S(2)}, u32[]{:S(2)}) collective-permute-start(bf16[256,256]{1,0:T(8,128)(2,1)S(1)} %get-tuple-element.34), channel_id=1, source_target_pairs={{0,4},{4,0},{8,12},{12,8},{16,20},{20,16},{24,28},{28,24},{1,5},{5... | collective-permute-start | bytes 393224 | tf_op jit(solution)/shard_map/ppermute | solution.py:21
  106.8 6.0 %collective-permute-start.30 = (bf16[256,256]{1,0:T(8,128)(2,1)S(1)}, bf16[256,256]{1,0:T(8,128)(2,1)S(1)}, u32[]{:S(2)}, u32[]{:S(2)}) collective-permute-start(bf16[256,256]{1,0:T(8,128)(2,1)S(1)} %get-tuple-element.28), channel_id=1, source_target_pairs={{0,4},{4,0},{8,12},{12,8},{16,20},{20,16},{24,28},{28,24},{1,5},{5... | collective-permute-start | bytes 393224 | tf_op jit(solution)/shard_map/ppermute | solution.py:21
  107.4 4.8 %collective-permute-start.44 = (f32[128,256]{1,0:T(8,128)S(1)}, f32[128,256]{1,0:T(8,128)S(1)}, u32[]{:S(2)}, u32[]{:S(2)}) collective-permute-start(f32[128,256]{1,0:T(8,128)S(1)} %add_multiply_fusion), channel_id=1, source_target_pairs={{0,4},{4,0},{8,12},{12,8},{16,20},{20,16},{24,28},{28,24},{1,5},{5... | collective-permute-start | bytes 393224 | tf_op jit(solution)/shard_map/ppermute | solution.py:21
  107.6 6.1 %collective-permute-start.32 = (bf16[256,256]{1,0:T(8,128)(2,1)S(1)}, bf16[256,256]{1,0:T(8,128)(2,1)S(1)}, u32[]{:S(2)}, u32[]{:S(2)}) collective-permute-start(bf16[256,256]{1,0:T(8,128)(2,1)S(1)} %add_convert_fusion.3), channel_id=1, source_target_pairs={{0,8},{4,12},{8,0},{12,4},{16,24},{20,28},{24,16},{28,20},{1,9},{5... | collective-permute-start | bytes 393224 | tf_op jit(solution)/shard_map/ppermute | solution.py:21
  109.1 8.4 %collective-permute-start.34 = (bf16[256,256]{1,0:T(8,128)(2,1)S(1)}, bf16[256,256]{1,0:T(8,128)(2,1)S(1)}, u32[]{:S(2)}, u32[]{:S(2)}) collective-permute-start(bf16[256,256]{1,0:T(8,128)(2,1)S(1)} %add_convert_fusion.2), channel_id=1, source_target_pairs={{0,16},{4,20},{8,24},{12,28},{16,0},{20,4},{24,8},{28,12},{1,17},{... | collective-permute-start | bytes 393224 | tf_op jit(solution)/shard_map/ppermute | solution.py:21
  109.6 7.9 %collective-permute-start.36 = (bf16[256,256]{1,0:T(8,128)(2,1)S(1)}, bf16[256,256]{1,0:T(8,128)(2,1)S(1)}, u32[]{:S(2)}, u32[]{:S(2)}) collective-permute-start(bf16[256,256]{1,0:T(8,128)(2,1)S(1)} %add_convert_fusion.1), channel_id=1, source_target_pairs={{0,24},{4,28},{8,16},{12,20},{16,8},{20,12},{24,0},{28,4},{1,25},{... | collective-permute-start | bytes 393224 | tf_op jit(solution)/shard_map/ppermute | solution.py:21
  (1 other events, 0.6 us)

commit v2 on v0

v2 whole, which is shorter than its diff:
```python
import functools
import math

import jax
import jax.numpy as jnp
from jax import lax
from jax.experimental import pallas as pl
from jax.experimental.pallas import tpu as pltpu
from jax.sharding import PartitionSpec as P

BLK = 128
CAP = 4
BF16 = jnp.bfloat16
F32 = jnp.float32
WHOLE = pl.BlockSpec(memory_space=pltpu.VMEM)
SCALARS = pl.BlockSpec(memory_space=pltpu.SMEM)


def swap(x, axis, offset):
    size = lax.axis_size(axis)
    return lax.ppermute(x, axis, [(i, i ^ offset) for i in range(size)])


def shape(*dims, dtype=BF16):
    return jax.ShapeDtypeStruct(dims, dtype)


def nbytes(arrays):
    return sum(math.prod(a.shape) * jnp.dtype(a.dtype).itemsize for a in arrays)


def call(kernel, outs, operands, scratch=(), lists=()):
    held = nbytes(outs) + nbytes(scratch)
    operands = [pltpu.with_memory_space_constraint(x, pltpu.VMEM) for x in operands]
    return pl.pallas_call(
        kernel,
        out_shape=outs,
        in_specs=[SCALARS] * len(lists) + [WHOLE] * len(operands),
        out_specs=[WHOLE] * len(outs),
        scratch_shapes=[pltpu.VMEM(x.shape, x.dtype) for x in scratch],
        compiler_params=pltpu.CompilerParams(vmem_limit_bytes=held + (4 << 20)),
        cost_estimate=pl.CostEstimate(flops=0, bytes_accessed=0, transcendentals=0),
    )(*lists, *operands)


def part(index, size):
    return pl.ds(pl.multiple_of(index * size, size), size)


def later_kernel(x_ref, _, out):
    out[...] = x_ref[...]


def add_kernel(x_ref, y_ref, _, out):
    out[...] = (x_ref[...].astype(F32) + y_ref[...].astype(F32)).astype(out.dtype)


def stack_kernel(*refs):
    for i, ref in enumerate(refs[:-2]):
        refs[-1][i] = ref[...]


def lists_kernel(held, spare, owner, slot, target, _, which, code, which2, code2, count):
    r = lax.axis_index("row")
    for refs in ((which, code), (which2, code2)):
        for i in range(refs[0].shape[0]):
            refs[0][i] = 0
            refs[1][i] = spare * held
    for t in range(count.shape[0]):
        count[t] = 0

    def place(k, _):
        t = owner[0, k] ^ r
        i = t // 2 * CAP + count[t]
        count[t] += 1

        @pl.when(t % 2 == 0)
        def _():
            which[i] = k
            code[i] = target[k] * held + slot[k]

        @pl.when(t % 2 == 1)
        def _():
            which2[i] = k
            code2[i] = target[k] * held + slot[k]

        return 0

    lax.fori_loop(0, slot.shape[0], place, 0)


def tiles_kernel(which, tiles, out):
    for i in range(out.shape[0]):
        out[i] = tiles[which[i]]


def aggregate_kernel(n_row, n_col, _, a_ref, own, other, near, across, __, keep, send, x_ref):
    span = own.shape[0]
    r, c = lax.axis_index("row"), lax.axis_index("col")
    x_ref[part(r, span), :] = own[...]
    x_ref[part(r ^ 1, span), :] = other[...]
    for t in range(2, n_row):
        x_ref[part(r ^ t, span), :] = (across if t % 2 else near)[t // 2 - 1]
    for s in range(n_col):
        block = jnp.dot(a_ref[part(c ^ s, span), :], x_ref[...], preferred_element_type=F32)
        if s % 2:
            send[s // 2] = block.astype(BF16)
        else:
            keep[s // 2] = block


def halve_kernel(kept, received, keep, send):
    for i in range(kept.shape[0]):
        block = kept[i] + received[i].astype(F32)
        if i % 2:
            send[i // 2] = block.astype(BF16)
        else:
            keep[i // 2] = block


def project_kernel(kept, received, w_ref, projected, flipped):
    total = kept[0] + received[0].astype(F32)
    high = total.astype(BF16)
    low = (total - high.astype(F32)).astype(BF16)
    projected[...] = jnp.dot(high, w_ref[...], preferred_element_type=F32) + jnp.dot(
        low, w_ref[...], preferred_element_type=F32
    )
    flipped[...] = total.T.astype(BF16)


def add_pulls(pulls, held, code, tile_of, acc):
    for i, piece in pulls:
        block = piece[part(code[i] % held, BLK), :]
        rows = part(code[i] // held, BLK)
        acc[rows, :] += jnp.dot(tile_of(i), block, preferred_element_type=F32)


def pulls_of(chips, pieces):
    return [
        (i * CAP + m, piece)
        for i, piece in zip(chips, pieces, strict=True)
        for m in range(CAP)
    ]


def early_kernel(offsets, held, which, code, code2, projected, tiles, tiles2, *refs):
    pieces, (own, others) = refs[:-2], refs[-2:]
    pulls = pulls_of(offsets, pieces)
    span = projected.shape[0]
    own[...] = jnp.zeros_like(own)
    others[...] = jnp.zeros_like(others)
    own[part(lax.axis_index("col"), span), :] = projected[...]
    add_pulls(pulls, held, code2, lambda i: tiles2[i], others)
    add_pulls(pulls, held, code, lambda i: tiles[which[i]], own)


def others_kernel(offsets, held, code, acc_in, tiles, *refs):
    pieces, (out, acc) = refs[:-2], refs[-2:]
    acc[...] = acc_in[...]
    add_pulls(pulls_of(offsets, pieces), held, code, lambda i: tiles[i], acc)
    out[...] = acc[: out.shape[0], :].astype(BF16)


def own_kernel(offsets, held, which, code, acc_in, tiles, *refs):
    pieces, out = refs[:-1], refs[-1]
    out[...] = acc_in[...]
    add_pulls(pulls_of(offsets, pieces), held, code, lambda i: tiles[which[i]], out)


def merge_kernel(n_col, own, received, keep, *sends):
    span = keep.shape[0]
    c = lax.axis_index("col")
    for s in range(n_col):
        rows = part(c ^ s, span)
        block = own[rows, :] + received[rows, :].astype(F32)
        if s:
            sends[s - 1][...] = block.astype(BF16)
        else:
            keep[...] = block


def activate_kernel(cotangent, kept, *refs):
    parts, (activated, flipped) = refs[:-2], refs[-2:]
    mixed = kept[...]
    for ref in parts:
        mixed = mixed + ref[...].astype(F32)
    sigmoid_z = jax.nn.sigmoid(mixed)
    activated[...] = (mixed * sigmoid_z).astype(BF16)
    grad_pre = cotangent[...].astype(F32) * sigmoid_z * (1.0 + mixed * (1.0 - sigmoid_z))
    flipped[...] = grad_pre.T.astype(BF16)


def weight_kernel(x_ref, g_ref, kept, given):
    half = x_ref.shape[0] // 2
    mine = lax.axis_index("row") % 2
    for out, core in ((kept, mine), (given, 1 - mine)):
        product = lax.dot_general(
            x_ref[part(core, half), :],
            g_ref[...],
            (((1,), (1,)), ((), ())),
            preferred_element_type=F32,
        )
        out[...] = product.astype(out.dtype)


def join_kernel(kept, received, flipped, total, joined):
    total[...] = (kept[...] + received[...].astype(F32)).astype(BF16)
    joined[: flipped.shape[0], :] = flipped[...]
    joined[flipped.shape[0] :, :] = total[...]


def joined_kernel(at, kept, received, out):
    out[...] = (kept[...].astype(F32) + received[at:, :].astype(F32)).astype(BF16)


def panel_kernel(*refs):
    pieces, out = refs[:-1], refs[-1]
    span = pieces[0].shape[1]
    c = lax.axis_index("col")
    for s, piece in enumerate(pieces):
        out[:, part(c ^ s, span)] = piece[: out.shape[0], :]


def transposed_kernel(offsets, a_ref, g_ref, _, given, kept):
    span = kept.shape[2]
    r = lax.axis_index("row")
    for out, core in ((given, 1), (kept, 0)):
        for i, t in enumerate(offsets):
            columns = part(r ^ t ^ core, span)
            product = jnp.dot(g_ref[...], a_ref[:, columns], preferred_element_type=F32)
            out[i] = product.astype(out.dtype)


def tree_kernel(*refs):
    terms, out = [ref[...].astype(F32) for ref in refs[:-2]], refs[-1]
    while len(terms) > 1:
        terms = [a + b for a, b in zip(terms[::2], terms[1::2], strict=True)]
    out[...] = terms[0].astype(out.dtype)


def cores_kernel(kept, received, own, *sends):
    own[...] = kept[0] + received[0].astype(F32)
    for i, send in enumerate(sends, 1):
        send[...] = (kept[i] + received[i].astype(F32)).astype(BF16)


def reduce_columns(keep, send, span, hid):
    bit = 1
    while True:
        received = swap(send, "col", bit)
        count = keep.shape[0]
        if count == 1:
            return keep, received
        bit *= 2
        keep, send = call(
            halve_kernel,
            [shape(count // 2, span, hid, dtype=F32), shape(count // 2, span, hid)],
            [keep, received],
        )


def local(
    nodes, weight, adjacency, history, pull_owner, pull_slot, pull_target, hist_tiles, cotangent
):
    n_row, n_col = lax.axis_size("row"), lax.axis_size("col")
    span, hid = nodes.shape
    panel, columns = adjacency.shape
    row_count = panel // BLK
    chips = list(range(0, n_row, 2))

    beside = swap(nodes, "row", 1)
    near = [swap(nodes, "row", t) for t in chips[:0:-1]][::-1]
    (history,) = call(later_kernel, [shape(*history.shape)], [history, beside])
    (stacked,) = call(stack_kernel, [shape(len(near), span, hid)], [*near, history])
    across = swap(stacked, "row", 1)

    blocks_held = history.shape[0] // BLK
    places = len(chips) * CAP
    which, code, which2, code2 = pl.pallas_call(
        functools.partial(lists_kernel, blocks_held, row_count),
        out_shape=[shape(places, dtype=jnp.int32)] * 4,
        in_specs=[SCALARS] * 3 + [WHOLE],
        out_specs=[SCALARS] * 4,
        scratch_shapes=[pltpu.SMEM((n_row,), jnp.int32)],
        compiler_params=pltpu.CompilerParams(vmem_limit_bytes=4 << 20),
    )(pull_owner.T, pull_slot, pull_target, history)
    (tiles,) = call(tiles_kernel, [shape(places, BLK, BLK)], [hist_tiles], lists=[which2])
    tiles = swap(tiles, "row", 1)
    code2 = swap(code2, "row", 1)

    blocks = [shape(n_col // 2, span, hid, dtype=F32), shape(n_col // 2, span, hid)]
    keep, send = call(
        functools.partial(aggregate_kernel, n_row, n_col),
        blocks,
        [adjacency, nodes, beside, stacked, across, tiles],
        [shape(columns, hid)],
        [code2],
    )
    keep, received = reduce_columns(keep, send, span, hid)
    projected, summed = call(
        project_kernel, [shape(span, hid, dtype=F32), shape(hid, span)], [keep, received, weight]
    )

    past = [history] + [swap(history, "row", t) for t in chips[1:]]
    early = [i for i, t in enumerate(chips) if t & (t - 1) == 0]
    late = [i for i, t in enumerate(chips) if t & (t - 1)]

    spare = shape(panel + BLK, hid, dtype=F32)
    own_terms, terms = call(
        functools.partial(early_kernel, early, blocks_held),
        [spare, spare],
        [projected, hist_tiles, tiles, *[past[i] for i in early]],
        lists=[which, code, code2],
    )
    (given,) = call(
        functools.partial(others_kernel, late, blocks_held),
        [shape(panel, hid)],
        [terms, tiles, *[past[i] for i in late]],
        [spare],
        [code2],
    )
    received = swap(given, "row", 1)
    (terms,) = call(
        functools.partial(own_kernel, late, blocks_held),
        [spare],
        [own_terms, hist_tiles, *[past[i] for i in late]],
        lists=[which, code],
    )
    keep, *sends = call(
        functools.partial(merge_kernel, n_col),
        [shape(span, hid, dtype=BF16 if s else F32) for s in range(n_col)],
        [terms, received],
    )
    activated, flipped = call(
        activate_kernel,
        [shape(span, hid), shape(hid, span)],
        [cotangent, keep, *[swap(send, "col", s) for s, send in enumerate(sends, 1)]],
    )

    kept, given = call(
        weight_kernel,
        [shape(hid // 2, hid, dtype=F32), shape(hid // 2, hid)],
        [summed, flipped],
    )
    kept, joined = call(
        join_kernel,
        [shape(hid // 2, hid), shape(hid + hid // 2, span)],
        [kept, swap(given, "row", 1), flipped],
    )
    pieces = [flipped, swap(joined, "col", 1)]
    pieces += [swap(flipped, "col", s) for s in range(2, n_col)]
    (kept,) = call(
        functools.partial(joined_kernel, hid), [shape(hid // 2, hid)], [kept, pieces[1]]
    )
    gradients = call(panel_kernel, [shape(hid, panel)], pieces)[0]
    (halfway,) = call(
        tree_kernel,
        [shape(hid // 2, hid)],
        [*[swap(kept, "row", t) if t else kept for t in chips], gradients],
    )

    given, kept = call(
        functools.partial(transposed_kernel, chips),
        [shape(len(chips), hid, span, dtype=dtype) for dtype in (BF16, F32)],
        [adjacency, gradients, halfway],
    )
    received = swap(given, "row", 1)
    total, *sends = call(
        cores_kernel,
        [shape(hid, span, dtype=BF16 if t else F32) for t in chips],
        [kept, received],
    )
    arrived = [swap(send, "row", t) for t, send in zip(chips[1:], sends, strict=True)]
    for x in arrived:
        total = total + x.astype(F32)
    grad_proj = total.astype(BF16)
    grad_nodes = lax.dot_general(
        grad_proj, weight, (((0,), (1,)), ((), ())), preferred_element_type=F32
    ).astype(BF16)

    for bit in [1 << b for b in range(1, n_col.bit_length() - 1)]:
        received = swap(halfway, "col", bit)
        (halfway,) = call(add_kernel, [shape(*halfway.shape)], [halfway, received, arrived[0]])
    other = swap(halfway, "row", 1)
    even = lax.axis_index("row") % 2 == 0
    grad_weight = jnp.concatenate(
        [jnp.where(even, halfway, other), jnp.where(even, other, halfway)], axis=0
    ).astype(F32) * (1.0 / math.sqrt(span * n_row * n_col))
    return (activated, grad_nodes, grad_weight)


def solution(mesh):
    return jax.shard_map(
        local,
        mesh=mesh,
        in_specs=(
            P(("row", "col"), None),
            P(),
            P("row", "col"),
            P(("row", "col"), None),
            P(("row", "col"), None),
            P(("row", "col")),
            P(("row", "col")),
            P(("row", "col"), None, None),
            P(("row", "col"), None),
        ),
        out_specs=(P(("row", "col"), None), P(("row", "col"), None), P()),
        check_vma=False,
    )
```

time: 297 us -> 92.8 us (0.31)
  waiting for transfers between devices: 241 us -> 44.1 us
  starting transfers between devices: 0.2 us -> 31 us
  matrix products: 19.2 us -> 0.91 us
  blocking collectives: 15.9 us -> 0 us
  between operations: 13.9 us -> 0.93 us
  Pallas kernels: 0 us -> 10.3 us
    psum x1 -> x0, waiting for transfers between devices: 127 us -> none  [local(): lax.psum(partial_grad, ('row', 'col')) * (1.0 / math.sqrt(all_nodes))]
    all_gather x2 -> x0, waiting for transfers between devices: 57.3 us -> none  [the longest x1 38.8 us: local(): everything = lax.all_gather(blocks, 'row', axis=0, tiled=True)]
    reduce_scatter x2 -> x0, waiting for transfers between devices: 55.2 us -> none  [the longest x1 33.6 us: local(): lax.psum_scatter(lax.dot_general(adjacency, grad_panel, (((0,), (0,)), ((...]
    ppermute x0 -> x29, waiting for transfers between devices: none -> 44.1 us  [swap(): return lax.ppermute(x, axis, [(i, i ^ offset) for i in range(size)])]
    ppermute x0 -> x29, starting transfers between devices: none -> 31 us  [swap(): return lax.ppermute(x, axis, [(i, i ^ offset) for i in range(size)])]
    dot_general x7 -> x1, matrix products: 19.2 us -> 0.91 us  [local(): lax.dot_general(grad_proj, weight, (((0,), (1,)), ((), ())), preferred_el...]
    all_gather x1 -> x0, blocking collectives: 15.9 us -> none  [local(): grad_panel = lax.all_gather(grad_pre, 'col', axis=0, tiled=True)]
    pallas_call x0 -> x20, Pallas kernels: none -> 10.3 us  [the longest x19 8.4 us: call(): pl.pallas_call(kernel, out_shape=outs, in_specs=[SCALARS] * len(lists) +...]
  transfers between devices with their start and end apart: 5 -> 29, of which waited for: 5 -> 15; matrix products, arithmetic and copies ran while one was open for 4% -> 1% of each run, Pallas kernels for 0% -> 7%
where the time goes in v2:
time: 92.8 us; the launch traced here: 92.6 us
  waiting for transfers between devices  44.1 us (48%)
  starting transfers between devices  31 us (33%)
  Pallas kernels  10.3 us (11%)
  local copies, waits for them, and re-layouts  4.58 us (5%)
  between operations  0.93 us (1%)
    ppermute x29, waiting for transfers between devices, swap(): return lax.ppermute(x, axis, [(i, i ^ offset) for i in range(size)])  44.1 us
    ppermute x29, starting transfers between devices, swap(): return lax.ppermute(x, axis, [(i, i ^ offset) for i in range(size)])  31 us
    pallas_call x19, Pallas kernels, call(): pl.pallas_call(kernel, out_shape=outs, in_specs=[SCALARS] * len(lists) +...  8.4 us
    unnamed x20, local copies, waits for them, and re-layouts  4.58 us
    pallas_call x1, Pallas kernels, local(): pl.pallas_call(functools.partial(lists_kernel, blocks_held, row_count), o...  1.95 us
  transfers between devices with their start and end apart: 29, of which 15 were waited for; matrix products, arithmetic and copies ran while one was open for 1% of the time, Pallas kernels for 7%

profile of v2, /device:TPU:0, one launch (start us, length us, event | category | flops | bytes accessed | tf_op | source)
XLA Modules:
  0.0 92.6 jit_solution(5649989082815600221)
XLA Ops:
  0.6 0.5 collective-permute-start
  1.1 2.6 %collective-permute-start.2 = (bf16[256,256]{1,0:T(8,128)(2,1)}, bf16[256,256]{1,0:T(8,128)(2,1)S(1)}, u32[]{:S(2)}, u32[]{:S(2)}) collective-permute-start(bf16[256,256]{1,0:T(8,128)(2,1)} %own.1), channel_id=1, source_target_pairs={{0,8},{4,12},{8,0},{12,4},{16,24},{20,28},{24,16},{28,20},{1,9},{5... | collective-permute-start | bytes 393224 | tf_op jit(solution)/shard_map/ppermute | solution.py:21
  3.7 1.5 %collective-permute-start.3 = (bf16[256,256]{1,0:T(8,128)(2,1)}, bf16[256,256]{1,0:T(8,128)(2,1)S(1)}, u32[]{:S(2)}, u32[]{:S(2)}) collective-permute-start(bf16[256,256]{1,0:T(8,128)(2,1)} %own.1), channel_id=1, source_target_pairs={{0,16},{4,20},{8,24},{12,28},{16,0},{20,4},{24,8},{28,12},{1,17},{... | collective-permute-start | bytes 393224 | tf_op jit(solution)/shard_map/ppermute | solution.py:21
  5.2 0.0 collective-permute-start.4
  5.3 1.0 %copy-done.3 = bf16[1024,256]{1,0:T(8,128)(2,1)S(1)} copy-done((bf16[1024,256]{1,0:T(8,128)(2,1)S(1)}, bf16[1024,256]{1,0:T(8,128)(2,1)}, u32[]{:S(2)}) %copy-start.3) | copy-done | bytes 524312
  6.4 0.8 copy-done.7
  7.2 0.8 copy-done.8
  8.0 0.7 copy-done.9
  8.6 1.9 %shard_map.113 = (s32[16]{0:T(128)S(1)}, s32[16]{0:T(128)S(1)}, s32[16]{0:T(128)S(1)}, s32[16]{0:T(128)S(1)}) custom-call(s32[1,32]{1,0:T(1,128)S(1)} %bitcast.2, s32[32]{0:T(128)S(1)} %copy-done.8, s32[32]{0:T(128)S(1)} %copy-done.9, bf16[1024,256]{1,0:T(8,128)(2,1)S(1)} %shard_map.112._.refs_3_.refs_0_), custom_call_target="tpu_custom_call" | custom-call | tf_op jit(solution)/shard_map/pallas_call | solution.py:279
  10.6 1.2 %copy-done.1 = bf16[32,128,128]{2,1,0:T(8,128)(2,1)S(1)} copy-done((bf16[32,128,128]{2,1,0:T(8,128)(2,1)S(1)}, bf16[32,128,128]{2,1,0:T(8,128)(2,1)}, u32[]{:S(2)}) %copy-start.1) | copy-done | bytes 1048600
  11.8 0.6 shard_map.115
  12.4 0.1 collective-permute-start.6
  12.6 0.5 collective-permute-start.5
  13.1 2.0 %collective-permute-start.10 = (bf16[1024,256]{1,0:T(8,128)(2,1)S(1)}, bf16[1024,256]{1,0:T(8,128)(2,1)S(1)}, u32[]{:S(2)}, u32[]{:S(2)}) collective-permute-start(bf16[1024,256]{1,0:T(8,128)(2,1)S(1)} %shard_map.112._.refs_3_.refs_0_), channel_id=1, source_target_pairs={{0,16},{4,20},{8,24},{12,28},{16,0},{20,4},{24,8},{28,12},{1,17},{... | collective-permute-start | bytes 1572872 | tf_op jit(solution)/shard_map/ppermute | solution.py:21
  15.1 1.5 %collective-permute-start.9 = (bf16[1024,256]{1,0:T(8,128)(2,1)S(1)}, bf16[1024,256]{1,0:T(8,128)(2,1)S(1)}, u32[]{:S(2)}, u32[]{:S(2)}) collective-permute-start(bf16[1024,256]{1,0:T(8,128)(2,1)S(1)} %shard_map.112._.refs_3_.refs_0_), channel_id=1, source_target_pairs={{0,8},{4,12},{8,0},{12,4},{16,24},{20,28},{24,16},{28,20},{1,9},{5... | collective-permute-start | bytes 1572872 | tf_op jit(solution)/shard_map/ppermute | solution.py:21
  16.6 1.1 %collective-permute-done.1._.code2.code = s32[16]{0:T(128)S(1)} collective-permute-done((s32[16]{0:T(128)S(1)}, s32[16]{0:T(128)S(1)}, u32[]{:S(2)}, u32[]{:S(2)}) %collective-permute-start.1) | collective-permute-done | bytes 96 | tf_op jit(solution)/shard_map/ppermute | solution.py:21
  17.7 0.2 collective-permute-start.11
  17.9 1.9 %shard_map.116 = (f32[2,256,256]{2,1,0:T(8,128)S(1)}, bf16[2,256,256]{2,1,0:T(8,128)(2,1)S(1)}) custom-call(s32[16]{0:T(128)S(1)} %collective-permute-done.1._.code2.code, bf16[1024,2048]{1,0:T(8,128)(2,1)S(1)} %copy-done, bf16[256,256]{1,0:T(8,128)(2,1)S(1)} %copy-done.5, bf16[256,256]{1,0:T(8,128)(2,1)S(1)} %collective-permute-done._.other, ...), custom_call_target="tpu_custom_call" | custom-call | tf_op jit(solution)/shard_map/pallas_call | solution.py:35
  19.8 2.0 %collective-permute-start.7 = (bf16[2,256,256]{2,1,0:T(8,128)(2,1)S(1)}, bf16[2,256,256]{2,1,0:T(8,128)(2,1)S(1)}, u32[]{:S(2)}, u32[]{:S(2)}) collective-permute-start(bf16[2,256,256]{2,1,0:T(8,128)(2,1)S(1)} %get-tuple-element.36), channel_id=1, source_target_pairs={{0,1},{1,0},{2,3},{3,2},{4,5},{5,4},{6,7},{7,6},{8,9},{9,8},{10,11... | collective-permute-start | bytes 786440 | tf_op jit(solution)/shard_map/ppermute | solution.py:21
  21.7 6.4 %collective-permute-done.7.received = bf16[2,256,256]{2,1,0:T(8,128)(2,1)S(1)} collective-permute-done((bf16[2,256,256]{2,1,0:T(8,128)(2,1)S(1)}, bf16[2,256,256]{2,1,0:T(8,128)(2,1)S(1)}, u32[]{:S(2)}, u32[]{:S(2)}) %collective-permute-start.7) | collective-permute-done | bytes 262176 | tf_op jit(solution)/shard_map/ppermute | solution.py:21
  28.2 2.8 %collective-permute-start.8 = (bf16[1,256,256]{2,1,0:T(8,128)(2,1)S(1)}, bf16[1,256,256]{2,1,0:T(8,128)(2,1)S(1)}, u32[]{:S(2)}, u32[]{:S(2)}) collective-permute-start(bf16[1,256,256]{2,1,0:T(8,128)(2,1)S(1)} %get-tuple-element.38), channel_id=1, source_target_pairs={{0,2},{1,3},{2,0},{3,1},{4,6},{5,7},{6,4},{7,5},{8,10},{9,11},{10,... | collective-permute-start | bytes 393224 | tf_op jit(solution)/shard_map/ppermute | solution.py:21
  31.0 5.6 %collective-permute-done.8.received = bf16[1,256,256]{2,1,0:T(8,128)(2,1)S(1)} collective-permute-done((bf16[1,256,256]{2,1,0:T(8,128)(2,1)S(1)}, bf16[1,256,256]{2,1,0:T(8,128)(2,1)S(1)}, u32[]{:S(2)}, u32[]{:S(2)}) %collective-permute-start.8) | collective-permute-done | bytes 131104 | tf_op jit(solution)/shard_map/ppermute | solution.py:21
  36.6 0.2 shard_map.118
  36.9 1.3 %shard_map.119 = (f32[1152,256]{1,0:T(8,128)S(1)}, f32[1152,256]{1,0:T(8,128)S(1)}) custom-call(s32[16]{0:T(128)S(1)} %get-tuple-element.31.which, s32[16]{0:T(128)S(1)} %get-tuple-element.32.code, s32[16]{0:T(128)S(1)} %collective-permute-done.1._.code2.code, f32[256,256]{1,0:T(8,128)S(1)} %get-tuple-element.39.projected, ...), custom_call_target="tpu_custom_call" | custom-call | tf_op jit(solution)/shard_map/pallas_call | solution.py:35
  38.2 1.6 %collective-permute-done.11.refs_0_ = bf16[1024,256]{1,0:T(8,128)(2,1)S(1)} collective-permute-done((bf16[1024,256]{1,0:T(8,128)(2,1)S(1)}, bf16[1024,256]{1,0:T(8,128)(2,1)S(1)}, u32[]{:S(2)}, u32[]{:S(2)}) %collective-permute-start.11) | collective-permute-done | bytes 524320 | tf_op jit(solution)/shard_map/ppermute | solution.py:21
  39.7 0.8 shard_map.121
  40.6 0.1 collective-permute-start.12
  40.7 0.8 shard_map.120.own
  41.5 0.0 copy-start.6
  41.5 1.1 %collective-permute-done.12.received = bf16[1024,256]{1,0:T(8,128)(2,1)S(1)} collective-permute-done((bf16[1024,256]{1,0:T(8,128)(2,1)S(1)}, bf16[1024,256]{1,0:T(8,128)(2,1)S(1)}, u32[]{:S(2)}, u32[]{:S(2)}) %collective-permute-start.12) | collective-permute-done | bytes 524320 | tf_op jit(solution)/shard_map/ppermute | solution.py:21
  42.6 0.1 shard_map.122
  42.7 1.8 %collective-permute-start.13 = (bf16[256,256]{1,0:T(8,128)(2,1)S(1)}, bf16[256,256]{1,0:T(8,128)(2,1)S(1)}, u32[]{:S(2)}, u32[]{:S(2)}) collective-permute-start(bf16[256,256]{1,0:T(8,128)(2,1)S(1)} %get-tuple-element.43), channel_id=1, source_target_pairs={{0,1},{1,0},{2,3},{3,2},{4,5},{5,4},{6,7},{7,6},{8,9},{9,8},{10,11... | collective-permute-start | bytes 393224 | tf_op jit(solution)/shard_map/ppermute | solution.py:21
  44.5 2.6 %collective-permute-start.14 = (bf16[256,256]{1,0:T(8,128)(2,1)S(1)}, bf16[256,256]{1,0:T(8,128)(2,1)S(1)}, u32[]{:S(2)}, u32[]{:S(2)}) collective-permute-start(bf16[256,256]{1,0:T(8,128)(2,1)S(1)} %get-tuple-element.44), channel_id=1, source_target_pairs={{0,2},{1,3},{2,0},{3,1},{4,6},{5,7},{6,4},{7,5},{8,10},{9,11},{10,... | collective-permute-start | bytes 393224 | tf_op jit(solution)/shard_map/ppermute | solution.py:21
  47.1 0.1 collective-permute-start.15
  47.1 3.0 %collective-permute-done.13.refs_0_ = bf16[256,256]{1,0:T(8,128)(2,1)S(1)} collective-permute-done((bf16[256,256]{1,0:T(8,128)(2,1)S(1)}, bf16[256,256]{1,0:T(8,128)(2,1)S(1)}, u32[]{:S(2)}, u32[]{:S(2)}) %collective-permute-start.13) | collective-permute-done | bytes 131104 | tf_op jit(solution)/shard_map/ppermute | solution.py:21
  50.2 7.2 %collective-permute-done.14.refs_1_ = bf16[256,256]{1,0:T(8,128)(2,1)S(1)} collective-permute-done((bf16[256,256]{1,0:T(8,128)(2,1)S(1)}, bf16[256,256]{1,0:T(8,128)(2,1)S(1)}, u32[]{:S(2)}, u32[]{:S(2)}) %collective-permute-start.14) | collective-permute-done | bytes 131104 | tf_op jit(solution)/shard_map/ppermute | solution.py:21
  57.4 0.8 shard_map.123
  58.2 0.2 shard_map.124
  58.4 0.1 collective-permute-start.16
  58.5 1.2 %collective-permute-done.16.received = bf16[128,256]{1,0:T(8,128)(2,1)S(1)} collective-permute-done((bf16[128,256]{1,0:T(8,128)(2,1)S(1)}, bf16[128,256]{1,0:T(8,128)(2,1)S(1)}, u32[]{:S(2)}, u32[]{:S(2)}) %collective-permute-start.16) | collective-permute-done | bytes 65568 | tf_op jit(solution)/shard_map/ppermute | solution.py:21
  59.8 2.4 %collective-permute-start.17 = (bf16[384,256]{1,0:T(8,128)(2,1)S(1)}, bf16[384,256]{1,0:T(8,128)(2,1)S(1)}, u32[]{:S(2)}, u32[]{:S(2)}) collective-permute-start(bf16[384,256]{1,0:T(8,128)(2,1)S(1)} %get-tuple-element.51), channel_id=1, source_target_pairs={{0,1},{1,0},{2,3},{3,2},{4,5},{5,4},{6,7},{7,6},{8,9},{9,8},{10,11... | collective-permute-start | bytes 589832 | tf_op jit(solution)/shard_map/ppermute | solution.py:21
  62.1 1.1 %collective-permute-start.18 = (bf16[256,256]{1,0:T(8,128)(2,1)S(1)}, bf16[256,256]{1,0:T(8,128)(2,1)S(1)}, u32[]{:S(2)}, u32[]{:S(2)}) collective-permute-start(bf16[256,256]{1,0:T(8,128)(2,1)S(1)} %get-tuple-element.47.g_ref.flipped.refs_0_), channel_id=1, source_target_pairs={{0,2},{1,3},{2,0},{3,1},{4,6},{5,7},{6,4},{7,5},{8,10},{9,11},{10,... | collective-permute-start | bytes 393224 | tf_op jit(solution)/shard_map/ppermute | solution.py:21
  63.2 1.4 %collective-permute-start.19 = (bf16[256,256]{1,0:T(8,128)(2,1)S(1)}, bf16[256,256]{1,0:T(8,128)(2,1)S(1)}, u32[]{:S(2)}, u32[]{:S(2)}) collective-permute-start(bf16[256,256]{1,0:T(8,128)(2,1)S(1)} %get-tuple-element.47.g_ref.flipped.refs_0_), channel_id=1, source_target_pairs={{0,3},{1,2},{2,1},{3,0},{4,7},{5,6},{6,5},{7,4},{8,11},{9,10},{10,... | collective-permute-start | bytes 393224 | tf_op jit(solution)/shard_map/ppermute | solution.py:21
  64.6 5.6 %collective-permute-done.17.refs_1_.received = bf16[384,256]{1,0:T(8,128)(2,1)S(1)} collective-permute-done((bf16[384,256]{1,0:T(8,128)(2,1)S(1)}, bf16[384,256]{1,0:T(8,128)(2,1)S(1)}, u32[]{:S(2)}, u32[]{:S(2)}) %collective-permute-start.17) | collective-permute-done | bytes 196640 | tf_op jit(solution)/shard_map/ppermute | solution.py:21
  70.2 1.6 %collective-permute-start.20 = (bf16[128,256]{1,0:T(8,128)(2,1)S(1)}, bf16[128,256]{1,0:T(8,128)(2,1)S(1)}, u32[]{:S(2)}, u32[]{:S(2)}) collective-permute-start(bf16[128,256]{1,0:T(8,128)(2,1)S(1)} %shard_map.127.refs_0_), channel_id=1, source_target_pairs={{0,8},{4,12},{8,0},{12,4},{16,24},{20,28},{24,16},{28,20},{1,9},{5... | collective-permute-start | bytes 196616 | tf_op jit(solution)/shard_map/ppermute | solution.py:21
  71.7 1.5 %collective-permute-start.21 = (bf16[128,256]{1,0:T(8,128)(2,1)S(1)}, bf16[128,256]{1,0:T(8,128)(2,1)S(1)}, u32[]{:S(2)}, u32[]{:S(2)}) collective-permute-start(bf16[128,256]{1,0:T(8,128)(2,1)S(1)} %shard_map.127.refs_0_), channel_id=1, source_target_pairs={{0,16},{4,20},{8,24},{12,28},{16,0},{20,4},{24,8},{28,12},{1,17},{... | collective-permute-start | bytes 196616 | tf_op jit(solution)/shard_map/ppermute | solution.py:21
  73.2 0.5 collective-permute-start.22
  73.7 1.5 %collective-permute-done.19.refs_3_ = bf16[256,256]{1,0:T(8,128)(2,1)S(1)} collective-permute-done((bf16[256,256]{1,0:T(8,128)(2,1)S(1)}, bf16[256,256]{1,0:T(8,128)(2,1)S(1)}, u32[]{:S(2)}, u32[]{:S(2)}) %collective-permute-start.19) | collective-permute-done | bytes 131104 | tf_op jit(solution)/shard_map/ppermute | solution.py:21
  75.2 0.1 shard_map.126.refs_4_.g_ref
  75.3 1.4 %collective-permute-done.21.refs_2_ = bf16[128,256]{1,0:T(8,128)(2,1)S(1)} collective-permute-done((bf16[128,256]{1,0:T(8,128)(2,1)S(1)}, bf16[128,256]{1,0:T(8,128)(2,1)S(1)}, u32[]{:S(2)}, u32[]{:S(2)}) %collective-permute-start.21) | collective-permute-done | bytes 65568 | tf_op jit(solution)/shard_map/ppermute | solution.py:21
  76.7 1.7 %collective-permute-done.22.refs_3_ = bf16[128,256]{1,0:T(8,128)(2,1)S(1)} collective-permute-done((bf16[128,256]{1,0:T(8,128)(2,1)S(1)}, bf16[128,256]{1,0:T(8,128)(2,1)S(1)}, u32[]{:S(2)}, u32[]{:S(2)}) %collective-permute-start.22) | collective-permute-done | bytes 65568 | tf_op jit(solution)/shard_map/ppermute | solution.py:21
  78.4 1.3 %shard_map.129 = (bf16[4,256,256]{2,1,0:T(8,128)(2,1)S(1)}, f32[4,256,256]{2,1,0:T(8,128)S(1)}) custom-call(bf16[1024,2048]{1,0:T(8,128)(2,1)S(1)} %copy-done, bf16[256,1024]{1,0:T(8,128)(2,1)S(1)} %shard_map.126.refs_4_.g_ref, bf16[128,256]{1,0:T(8,128)(2,1)S(1)} %shard_map.128._.x_ref), custom_call_target="tpu_custom_call" | custom-call | tf_op jit(solution)/shard_map/pallas_call | solution.py:35
  79.8 0.1 collective-permute-start.23
  79.8 1.9 %collective-permute-done.23.received = bf16[4,256,256]{2,1,0:T(8,128)(2,1)S(1)} collective-permute-done((bf16[4,256,256]{2,1,0:T(8,128)(2,1)S(1)}, bf16[4,256,256]{2,1,0:T(8,128)(2,1)S(1)}, u32[]{:S(2)}, u32[]{:S(2)}) %collective-permute-start.23) | collective-permute-done | bytes 524320 | tf_op jit(solution)/shard_map/ppermute | solution.py:21
  81.7 0.1 shard_map.130
  81.8 0.6 collective-permute-start.24
  82.4 0.5 collective-permute-start.25
  82.9 2.5 %collective-permute-start.26 = (bf16[256,256]{1,0:T(8,128)(2,1)S(1)}, bf16[256,256]{1,0:T(8,128)(2,1)S(1)}, u32[]{:S(2)}, u32[]{:S(2)}) collective-permute-start(bf16[256,256]{1,0:T(8,128)(2,1)S(1)} %get-tuple-element.58), channel_id=1, source_target_pairs={{0,24},{4,28},{8,16},{12,20},{16,8},{20,12},{24,0},{28,4},{1,25},{... | collective-permute-start | bytes 393224 | tf_op jit(solution)/shard_map/ppermute | solution.py:21
  85.4 0.7 collective-permute-start.27
  86.1 4.4 %collective-permute-done.27.y_ref = bf16[128,256]{1,0:T(8,128)(2,1)S(1)} collective-permute-done((bf16[128,256]{1,0:T(8,128)(2,1)S(1)}, bf16[128,256]{1,0:T(8,128)(2,1)S(1)}, u32[]{:S(2)}, u32[]{:S(2)}) %collective-permute-start.27) | collective-permute-done | bytes 65568 | tf_op jit(solution)/shard_map/ppermute | solution.py:21
  90.6 0.1 collective-permute-start.28
  90.7 0.9 convolution_convert_fusion
  91.6 0.3 collective-permute-done.28
  91.9 0.7 convert_multiply_fusion
  (37 shorter events, 0.3 us)
Async XLA Ops:
  0.6 4.6 %collective-permute-start = (bf16[256,256]{1,0:T(8,128)(2,1)}, bf16[256,256]{1,0:T(8,128)(2,1)S(1)}, u32[]{:S(2)}, u32[]{:S(2)}) collective-permute-start(bf16[256,256]{1,0:T(8,128)(2,1)} %own.1), channel_id=1, source_target_pairs={{0,4},{4,0},{8,12},{12,8},{16,20},{20,16},{24,28},{28,24},{1,5},{5... | collective-permute-start | bytes 393224 | tf_op jit(solution)/shard_map/ppermute | solution.py:21
  1.1 11.4 %collective-permute-start.2 = (bf16[256,256]{1,0:T(8,128)(2,1)}, bf16[256,256]{1,0:T(8,128)(2,1)S(1)}, u32[]{:S(2)}, u32[]{:S(2)}) collective-permute-start(bf16[256,256]{1,0:T(8,128)(2,1)} %own.1), channel_id=1, source_target_pairs={{0,8},{4,12},{8,0},{12,4},{16,24},{20,28},{24,16},{28,20},{1,9},{5... | collective-permute-start | bytes 393224 | tf_op jit(solution)/shard_map/ppermute | solution.py:21
  3.7 8.8 %collective-permute-start.3 = (bf16[256,256]{1,0:T(8,128)(2,1)}, bf16[256,256]{1,0:T(8,128)(2,1)S(1)}, u32[]{:S(2)}, u32[]{:S(2)}) collective-permute-start(bf16[256,256]{1,0:T(8,128)(2,1)} %own.1), channel_id=1, source_target_pairs={{0,16},{4,20},{8,24},{12,28},{16,0},{20,4},{24,8},{28,12},{1,17},{... | collective-permute-start | bytes 393224 | tf_op jit(solution)/shard_map/ppermute | solution.py:21
  5.2 7.3 %collective-permute-start.4 = (bf16[256,256]{1,0:T(8,128)(2,1)}, bf16[256,256]{1,0:T(8,128)(2,1)S(1)}, u32[]{:S(2)}, u32[]{:S(2)}) collective-permute-start(bf16[256,256]{1,0:T(8,128)(2,1)} %own.1), channel_id=1, source_target_pairs={{0,24},{4,28},{8,16},{12,20},{16,8},{20,12},{24,0},{28,4},{1,25},{... | collective-permute-start | bytes 393224 | tf_op jit(solution)/shard_map/ppermute | solution.py:21
  5.3 1.0 %copy-start.3 = (bf16[1024,256]{1,0:T(8,128)(2,1)S(1)}, bf16[1024,256]{1,0:T(8,128)(2,1)}, u32[]{:S(2)}) copy-start(bf16[1024,256]{1,0:T(8,128)(2,1)} %x_ref.1) | copy-start | bytes 1572868
  6.3 11.6 %copy-start = (bf16[1024,2048]{1,0:T(8,128)(2,1)S(1)}, bf16[1024,2048]{1,0:T(8,128)(2,1)}, u32[]{:S(2)}) copy-start(bf16[1024,2048]{1,0:T(8,128)(2,1)} %a_ref.3) | copy-start | bytes 12582916
  6.3 0.8 copy-start.7
  7.2 0.8 copy-start.8
  8.0 0.7 copy-start.9
  10.6 1.2 %copy-start.1 = (bf16[32,128,128]{2,1,0:T(8,128)(2,1)S(1)}, bf16[32,128,128]{2,1,0:T(8,128)(2,1)}, u32[]{:S(2)}) copy-start(bf16[32,128,128]{2,1,0:T(8,128)(2,1)} %tiles.5) | copy-start | bytes 3145732
  11.8 6.0 %copy-start.5 = (bf16[256,256]{1,0:T(8,128)(2,1)S(1)}, bf16[256,256]{1,0:T(8,128)(2,1)}, u32[]{:S(2)}) copy-start(bf16[256,256]{1,0:T(8,128)(2,1)} %own.1) | copy-start | bytes 393220
  12.4 5.4 %collective-permute-start.6 = (bf16[16,128,128]{2,1,0:T(8,128)(2,1)S(1)}, bf16[16,128,128]{2,1,0:T(8,128)(2,1)S(1)}, u32[]{:S(2)}, u32[]{:S(2)}) collective-permute-start(bf16[16,128,128]{2,1,0:T(8,128)(2,1)S(1)} %shard_map.115), channel_id=1, source_target_pairs={{0,4},{4,0},{8,12},{12,8},{16,20},{20,16},{24,28},{28,24},{1,5},{5... | collective-permute-start | bytes 1572872 | tf_op jit(solution)/shard_map/ppermute | solution.py:21
  12.6 5.3 %collective-permute-start.5 = (bf16[3,256,256]{2,1,0:T(8,128)(2,1)S(1)}, bf16[3,256,256]{2,1,0:T(8,128)(2,1)S(1)}, u32[]{:S(2)}, u32[]{:S(2)}) collective-permute-start(bf16[3,256,256]{2,1,0:T(8,128)(2,1)S(1)} %shard_map.114.near), channel_id=1, source_target_pairs={{0,4},{4,0},{8,12},{12,8},{16,20},{20,16},{24,28},{28,24},{1,5},{5... | collective-permute-start | bytes 1179656 | tf_op jit(solution)/shard_map/ppermute | solution.py:21
  13.1 23.7 %collective-permute-start.10 = (bf16[1024,256]{1,0:T(8,128)(2,1)S(1)}, bf16[1024,256]{1,0:T(8,128)(2,1)S(1)}, u32[]{:S(2)}, u32[]{:S(2)}) collective-permute-start(bf16[1024,256]{1,0:T(8,128)(2,1)S(1)} %shard_map.112._.refs_3_.refs_0_), channel_id=1, source_target_pairs={{0,16},{4,20},{8,24},{12,28},{16,0},{20,4},{24,8},{28,12},{1,17},{... | collective-permute-start | bytes 1572872 | tf_op jit(solution)/shard_map/ppermute | solution.py:21
  15.1 21.8 %collective-permute-start.9 = (bf16[1024,256]{1,0:T(8,128)(2,1)S(1)}, bf16[1024,256]{1,0:T(8,128)(2,1)S(1)}, u32[]{:S(2)}, u32[]{:S(2)}) collective-permute-start(bf16[1024,256]{1,0:T(8,128)(2,1)S(1)} %shard_map.112._.refs_3_.refs_0_), channel_id=1, source_target_pairs={{0,8},{4,12},{8,0},{12,4},{16,24},{20,28},{24,16},{28,20},{1,9},{5... | collective-permute-start | bytes 1572872 | tf_op jit(solution)/shard_map/ppermute | solution.py:21
  16.6 20.0 %copy-start.4 = (bf16[256,256]{1,0:T(8,128)(2,1)S(1)}, bf16[256,256]{1,0:T(8,128)(2,1)}, u32[]{:S(2)}) copy-start(bf16[256,256]{1,0:T(8,128)(2,1)} %w_ref.1) | copy-start | bytes 393220
  16.6 1.1 %collective-permute-start.1 = (s32[16]{0:T(128)S(1)}, s32[16]{0:T(128)S(1)}, u32[]{:S(2)}, u32[]{:S(2)}) collective-permute-start(s32[16]{0:T(128)S(1)} %get-tuple-element.33), channel_id=1, source_target_pairs={{0,4},{4,0},{8,12},{12,8},{16,20},{20,16},{24,28},{28,24},{1,5},{5... | collective-permute-start | bytes 200 | tf_op jit(solution)/shard_map/ppermute | solution.py:21
  17.7 22.0 %collective-permute-start.11 = (bf16[1024,256]{1,0:T(8,128)(2,1)S(1)}, bf16[1024,256]{1,0:T(8,128)(2,1)S(1)}, u32[]{:S(2)}, u32[]{:S(2)}) collective-permute-start(bf16[1024,256]{1,0:T(8,128)(2,1)S(1)} %shard_map.112._.refs_3_.refs_0_), channel_id=1, source_target_pairs={{0,24},{4,28},{8,16},{12,20},{16,8},{20,12},{24,0},{28,4},{1,25},{... | collective-permute-start | bytes 1572872 | tf_op jit(solution)/shard_map/ppermute | solution.py:21
  19.8 17.1 %copy-start.2 = (bf16[32,128,128]{2,1,0:T(8,128)(2,1)S(1)}, bf16[32,128,128]{2,1,0:T(8,128)(2,1)}, u32[]{:S(2)}) copy-start(bf16[32,128,128]{2,1,0:T(8,128)(2,1)} %tiles.5) | copy-start | bytes 3145732
  19.8 8.4 %collective-permute-start.7 = (bf16[2,256,256]{2,1,0:T(8,128)(2,1)S(1)}, bf16[2,256,256]{2,1,0:T(8,128)(2,1)S(1)}, u32[]{:S(2)}, u32[]{:S(2)}) collective-permute-start(bf16[2,256,256]{2,1,0:T(8,128)(2,1)S(1)} %get-tuple-element.36), channel_id=1, source_target_pairs={{0,1},{1,0},{2,3},{3,2},{4,5},{5,4},{6,7},{7,6},{8,9},{9,8},{10,11... | collective-permute-start | bytes 786440 | tf_op jit(solution)/shard_map/ppermute | solution.py:21
  28.2 8.4 %collective-permute-start.8 = (bf16[1,256,256]{2,1,0:T(8,128)(2,1)S(1)}, bf16[1,256,256]{2,1,0:T(8,128)(2,1)S(1)}, u32[]{:S(2)}, u32[]{:S(2)}) collective-permute-start(bf16[1,256,256]{2,1,0:T(8,128)(2,1)S(1)} %get-tuple-element.38), channel_id=1, source_target_pairs={{0,2},{1,3},{2,0},{3,1},{4,6},{5,7},{6,4},{7,5},{8,10},{9,11},{10,... | collective-permute-start | bytes 393224 | tf_op jit(solution)/shard_map/ppermute | solution.py:21
  40.6 2.0 %collective-permute-start.12 = (bf16[1024,256]{1,0:T(8,128)(2,1)S(1)}, bf16[1024,256]{1,0:T(8,128)(2,1)S(1)}, u32[]{:S(2)}, u32[]{:S(2)}) collective-permute-start(bf16[1024,256]{1,0:T(8,128)(2,1)S(1)} %shard_map.121), channel_id=1, source_target_pairs={{0,4},{4,0},{8,12},{12,8},{16,20},{20,16},{24,28},{28,24},{1,5},{5... | collective-permute-start | bytes 1572872 | tf_op jit(solution)/shard_map/ppermute | solution.py:21
  41.5 15.9 %copy-start.6 = (bf16[256,256]{1,0:T(8,128)(2,1)S(1)}, bf16[256,256]{1,0:T(8,128)(2,1)}, u32[]{:S(2)}) copy-start(bf16[256,256]{1,0:T(8,128)(2,1)} %cotangent.1) | copy-start | bytes 393220
  42.7 7.5 %collective-permute-start.13 = (bf16[256,256]{1,0:T(8,128)(2,1)S(1)}, bf16[256,256]{1,0:T(8,128)(2,1)S(1)}, u32[]{:S(2)}, u32[]{:S(2)}) collective-permute-start(bf16[256,256]{1,0:T(8,128)(2,1)S(1)} %get-tuple-element.43), channel_id=1, source_target_pairs={{0,1},{1,0},{2,3},{3,2},{4,5},{5,4},{6,7},{7,6},{8,9},{9,8},{10,11... | collective-permute-start | bytes 393224 | tf_op jit(solution)/shard_map/ppermute | solution.py:21
  44.5 12.9 %collective-permute-start.14 = (bf16[256,256]{1,0:T(8,128)(2,1)S(1)}, bf16[256,256]{1,0:T(8,128)(2,1)S(1)}, u32[]{:S(2)}, u32[]{:S(2)}) collective-permute-start(bf16[256,256]{1,0:T(8,128)(2,1)S(1)} %get-tuple-element.44), channel_id=1, source_target_pairs={{0,2},{1,3},{2,0},{3,1},{4,6},{5,7},{6,4},{7,5},{8,10},{9,11},{10,... | collective-permute-start | bytes 393224 | tf_op jit(solution)/shard_map/ppermute | solution.py:21
  47.1 10.3 %collective-permute-start.15 = (bf16[256,256]{1,0:T(8,128)(2,1)S(1)}, bf16[256,256]{1,0:T(8,128)(2,1)S(1)}, u32[]{:S(2)}, u32[]{:S(2)}) collective-permute-start(bf16[256,256]{1,0:T(8,128)(2,1)S(1)} %get-tuple-element.45), channel_id=1, source_target_pairs={{0,3},{1,2},{2,1},{3,0},{4,7},{5,6},{6,5},{7,4},{8,11},{9,10},{10,... | collective-permute-start | bytes 393224 | tf_op jit(solution)/shard_map/ppermute | solution.py:21
  58.4 1.3 %collective-permute-start.16 = (bf16[128,256]{1,0:T(8,128)(2,1)S(1)}, bf16[128,256]{1,0:T(8,128)(2,1)S(1)}, u32[]{:S(2)}, u32[]{:S(2)}) collective-permute-start(bf16[128,256]{1,0:T(8,128)(2,1)S(1)} %get-tuple-element.50), channel_id=1, source_target_pairs={{0,4},{4,0},{8,12},{12,8},{16,20},{20,16},{24,28},{28,24},{1,5},{5... | collective-permute-start | bytes 196616 | tf_op jit(solution)/shard_map/ppermute | solution.py:21
  59.8 10.4 %collective-permute-start.17 = (bf16[384,256]{1,0:T(8,128)(2,1)S(1)}, bf16[384,256]{1,0:T(8,128)(2,1)S(1)}, u32[]{:S(2)}, u32[]{:S(2)}) collective-permute-start(bf16[384,256]{1,0:T(8,128)(2,1)S(1)} %get-tuple-element.51), channel_id=1, source_target_pairs={{0,1},{1,0},{2,3},{3,2},{4,5},{5,4},{6,7},{7,6},{8,9},{9,8},{10,11... | collective-permute-start | bytes 589832 | tf_op jit(solution)/shard_map/ppermute | solution.py:21
  62.1 11.6 %collective-permute-start.18 = (bf16[256,256]{1,0:T(8,128)(2,1)S(1)}, bf16[256,256]{1,0:T(8,128)(2,1)S(1)}, u32[]{:S(2)}, u32[]{:S(2)}) collective-permute-start(bf16[256,256]{1,0:T(8,128)(2,1)S(1)} %get-tuple-element.47.g_ref.flipped.refs_0_), channel_id=1, source_target_pairs={{0,2},{1,3},{2,0},{3,1},{4,6},{5,7},{6,4},{7,5},{8,10},{9,11},{10,... | collective-permute-start | bytes 393224 | tf_op jit(solution)/shard_map/ppermute | solution.py:21
  63.2 12.0 %collective-permute-start.19 = (bf16[256,256]{1,0:T(8,128)(2,1)S(1)}, bf16[256,256]{1,0:T(8,128)(2,1)S(1)}, u32[]{:S(2)}, u32[]{:S(2)}) collective-permute-start(bf16[256,256]{1,0:T(8,128)(2,1)S(1)} %get-tuple-element.47.g_ref.flipped.refs_0_), channel_id=1, source_target_pairs={{0,3},{1,2},{2,1},{3,0},{4,7},{5,6},{6,5},{7,4},{8,11},{9,10},{10,... | collective-permute-start | bytes 393224 | tf_op jit(solution)/shard_map/ppermute | solution.py:21
  70.2 5.2 %collective-permute-start.20 = (bf16[128,256]{1,0:T(8,128)(2,1)S(1)}, bf16[128,256]{1,0:T(8,128)(2,1)S(1)}, u32[]{:S(2)}, u32[]{:S(2)}) collective-permute-start(bf16[128,256]{1,0:T(8,128)(2,1)S(1)} %shard_map.127.refs_0_), channel_id=1, source_target_pairs={{0,8},{4,12},{8,0},{12,4},{16,24},{20,28},{24,16},{28,20},{1,9},{5... | collective-permute-start | bytes 196616 | tf_op jit(solution)/shard_map/ppermute | solution.py:21
  71.7 5.0 %collective-permute-start.21 = (bf16[128,256]{1,0:T(8,128)(2,1)S(1)}, bf16[128,256]{1,0:T(8,128)(2,1)S(1)}, u32[]{:S(2)}, u32[]{:S(2)}) collective-permute-start(bf16[128,256]{1,0:T(8,128)(2,1)S(1)} %shard_map.127.refs_0_), channel_id=1, source_target_pairs={{0,16},{4,20},{8,24},{12,28},{16,0},{20,4},{24,8},{28,12},{1,17},{... | collective-permute-start | bytes 196616 | tf_op jit(solution)/shard_map/ppermute | solution.py:21
  73.2 5.2 %collective-permute-start.22 = (bf16[128,256]{1,0:T(8,128)(2,1)S(1)}, bf16[128,256]{1,0:T(8,128)(2,1)S(1)}, u32[]{:S(2)}, u32[]{:S(2)}) collective-permute-start(bf16[128,256]{1,0:T(8,128)(2,1)S(1)} %shard_map.127.refs_0_), channel_id=1, source_target_pairs={{0,24},{4,28},{8,16},{12,20},{16,8},{20,12},{24,0},{28,4},{1,25},{... | collective-permute-start | bytes 196616 | tf_op jit(solution)/shard_map/ppermute | solution.py:21
  79.8 2.0 %collective-permute-start.23 = (bf16[4,256,256]{2,1,0:T(8,128)(2,1)S(1)}, bf16[4,256,256]{2,1,0:T(8,128)(2,1)S(1)}, u32[]{:S(2)}, u32[]{:S(2)}) collective-permute-start(bf16[4,256,256]{2,1,0:T(8,128)(2,1)S(1)} %get-tuple-element.54), channel_id=1, source_target_pairs={{0,4},{4,0},{8,12},{12,8},{16,20},{20,16},{24,28},{28,24},{1,5},{5... | collective-permute-start | bytes 1572872 | tf_op jit(solution)/shard_map/ppermute | solution.py:21
  81.8 8.7 %collective-permute-start.24 = (bf16[256,256]{1,0:T(8,128)(2,1)S(1)}, bf16[256,256]{1,0:T(8,128)(2,1)S(1)}, u32[]{:S(2)}, u32[]{:S(2)}) collective-permute-start(bf16[256,256]{1,0:T(8,128)(2,1)S(1)} %get-tuple-element.56), channel_id=1, source_target_pairs={{0,8},{4,12},{8,0},{12,4},{16,24},{20,28},{24,16},{28,20},{1,9},{5... | collective-permute-start | bytes 393224 | tf_op jit(solution)/shard_map/ppermute | solution.py:21
  82.4 8.2 %collective-permute-start.25 = (bf16[256,256]{1,0:T(8,128)(2,1)S(1)}, bf16[256,256]{1,0:T(8,128)(2,1)S(1)}, u32[]{:S(2)}, u32[]{:S(2)}) collective-permute-start(bf16[256,256]{1,0:T(8,128)(2,1)S(1)} %get-tuple-element.57), channel_id=1, source_target_pairs={{0,16},{4,20},{8,24},{12,28},{16,0},{20,4},{24,8},{28,12},{1,17},{... | collective-permute-start | bytes 393224 | tf_op jit(solution)/shard_map/ppermute | solution.py:21
  82.9 7.7 %collective-permute-start.26 = (bf16[256,256]{1,0:T(8,128)(2,1)S(1)}, bf16[256,256]{1,0:T(8,128)(2,1)S(1)}, u32[]{:S(2)}, u32[]{:S(2)}) collective-permute-start(bf16[256,256]{1,0:T(8,128)(2,1)S(1)} %get-tuple-element.58), channel_id=1, source_target_pairs={{0,24},{4,28},{8,16},{12,20},{16,8},{20,12},{24,0},{28,4},{1,25},{... | collective-permute-start | bytes 393224 | tf_op jit(solution)/shard_map/ppermute | solution.py:21
  85.4 5.2 %collective-permute-start.27 = (bf16[128,256]{1,0:T(8,128)(2,1)S(1)}, bf16[128,256]{1,0:T(8,128)(2,1)S(1)}, u32[]{:S(2)}, u32[]{:S(2)}) collective-permute-start(bf16[128,256]{1,0:T(8,128)(2,1)S(1)} %shard_map.128._.x_ref), channel_id=1, source_target_pairs={{0,2},{1,3},{2,0},{3,1},{4,6},{5,7},{6,4},{7,5},{8,10},{9,11},{10,... | collective-permute-start | bytes 196616 | tf_op jit(solution)/shard_map/ppermute | solution.py:21
  90.6 1.3 %collective-permute-start.28 = (bf16[128,256]{1,0:T(8,128)(2,1)S(1)}, bf16[128,256]{1,0:T(8,128)(2,1)S(1)}, u32[]{:S(2)}, u32[]{:S(2)}) collective-permute-start(bf16[128,256]{1,0:T(8,128)(2,1)S(1)} %shard_map.131), channel_id=1, source_target_pairs={{0,4},{4,0},{8,12},{12,8},{16,20},{20,16},{24,28},{28,24},{1,5},{5... | collective-permute-start | bytes 196616 | tf_op jit(solution)/shard_map/ppermute | solution.py:21

commit v3 on v2

--- a/solution.py
+++ b/solution.py
@@ -203,16 +203,6 @@
         out[...] = product.astype(out.dtype)
 
 
-def join_kernel(kept, received, flipped, total, joined):
-    total[...] = (kept[...] + received[...].astype(F32)).astype(BF16)
-    joined[: flipped.shape[0], :] = flipped[...]
-    joined[flipped.shape[0] :, :] = total[...]
-
-
-def joined_kernel(at, kept, received, out):
-    out[...] = (kept[...].astype(F32) + received[at:, :].astype(F32)).astype(BF16)
-
-
 def panel_kernel(*refs):
     pieces, out = refs[:-1], refs[-1]
     span = pieces[0].shape[1]
@@ -238,10 +228,9 @@
     out[...] = terms[0].astype(out.dtype)
 
 
-def cores_kernel(kept, received, own, *sends):
-    own[...] = kept[0] + received[0].astype(F32)
-    for i, send in enumerate(sends, 1):
-        send[...] = (kept[i] + received[i].astype(F32)).astype(BF16)
+def cores_kernel(places, kept, received, _, *outs):
+    for i, out in zip(places, outs, strict=True):
+        out[...] = (kept[i] + received[i].astype(F32)).astype(out.dtype)
 
 
 def reduce_columns(keep, send, span, hid):
@@ -337,21 +326,13 @@
         [cotangent, keep, *[swap(send, "col", s) for s, send in enumerate(sends, 1)]],
     )
 
+    pieces = [swap(flipped, "col", s) if s else flipped for s in range(n_col)]
     kept, given = call(
         weight_kernel,
         [shape(hid // 2, hid, dtype=F32), shape(hid // 2, hid)],
         [summed, flipped],
     )
-    kept, joined = call(
-        join_kernel,
-        [shape(hid // 2, hid), shape(hid + hid // 2, span)],
-        [kept, swap(given, "row", 1), flipped],
-    )
-    pieces = [flipped, swap(joined, "col", 1)]
-    pieces += [swap(flipped, "col", s) for s in range(2, n_col)]
-    (kept,) = call(
-        functools.partial(joined_kernel, hid), [shape(hid // 2, hid)], [kept, pieces[1]]
-    )
+    kept = (kept + swap(given, "row", 1).astype(F32)).astype(BF16)
     gradients = call(panel_kernel, [shape(hid, panel)], pieces)[0]
     (halfway,) = call(
         tree_kernel,
@@ -365,14 +346,22 @@
         [adjacency, gradients, halfway],
     )
     received = swap(given, "row", 1)
-    total, *sends = call(
-        cores_kernel,
-        [shape(hid, span, dtype=BF16 if t else F32) for t in chips],
-        [kept, received],
-    )
-    arrived = [swap(send, "row", t) for t, send in zip(chips[1:], sends, strict=True)]
-    for x in arrived:
-        total = total + x.astype(F32)
+    arrived, token = {}, given
+    for places in (list(range(2, len(chips))), [0, 1]):
+        sums = call(
+            functools.partial(cores_kernel, places),
+            [shape(hid, span, dtype=BF16 if i else F32) for i in places],
+            [kept, received, token],
+        )
+        for i, x in zip(places, sums, strict=True):
+            arrived[i] = swap(x, "row", chips[i]) if i else x
+        if token is given:
+            beside = swap(halfway, "col", 1)
+            (token,) = call(add_kernel, [shape(*halfway.shape)], [halfway, beside, sums[0]])
+    halfway = token
+    total = arrived[0]
+    for i in range(1, len(chips)):
+        total = total + arrived[i].astype(F32)
     grad_proj = total.astype(BF16)
     grad_nodes = lax.dot_general(
         grad_proj, weight, (((0,), (1,)), ((), ())), preferred_element_type=F32
@@ -380,7 +369,7 @@
 
     for bit in [1 << b for b in range(1, n_col.bit_length() - 1)]:
         received = swap(halfway, "col", bit)
-        (halfway,) = call(add_kernel, [shape(*halfway.shape)], [halfway, received, arrived[0]])
+        (halfway,) = call(add_kernel, [shape(*halfway.shape)], [halfway, received, arrived[len(chips) - 1]])
     other = swap(halfway, "row", 1)
     even = lax.axis_index("row") % 2 == 0
     grad_weight = jnp.concatenate(

time: 92.8 us -> 91.3 us (0.984)
  waiting for transfers between devices: 44.1 us -> 33.8 us
  starting transfers between devices: 31 us -> 39.7 us
    ppermute x29 -> x30, waiting for transfers between devices: 44.1 us -> 33.8 us  [swap(): return lax.ppermute(x, axis, [(i, i ^ offset) for i in range(size)])]
    ppermute x29 -> x30, starting transfers between devices: 31 us -> 39.7 us  [swap(): return lax.ppermute(x, axis, [(i, i ^ offset) for i in range(size)])]
  transfers between devices with their start and end apart: 29 -> 30, of which waited for: 15 -> 12; matrix products, arithmetic and copies ran while one was open for 1% -> 1% of each run, Pallas kernels for 7% -> 8%
where the time goes in v3:
time: 91.3 us; the launch traced here: 91.1 us
  starting transfers between devices  39.7 us (43%)
  waiting for transfers between devices  33.8 us (37%)
  Pallas kernels  10.3 us (11%)
  local copies, waits for them, and re-layouts  4.58 us (5%)
  between operations  0.96 us (1%)
    ppermute x30, starting transfers between devices, swap(): return lax.ppermute(x, axis, [(i, i ^ offset) for i in range(size)])  39.7 us
    ppermute x30, waiting for transfers between devices, swap(): return lax.ppermute(x, axis, [(i, i ^ offset) for i in range(size)])  33.8 us
    pallas_call x19, Pallas kernels, call(): pl.pallas_call(kernel, out_shape=outs, in_specs=[SCALARS] * len(lists) +...  8.37 us
    unnamed x20, local copies, waits for them, and re-layouts  4.58 us
    pallas_call x1, Pallas kernels, local(): pl.pallas_call(functools.partial(lists_kernel, blocks_held, row_count), o...  1.95 us
  transfers between devices with their start and end apart: 30, of which 12 were waited for; matrix products, arithmetic and copies ran while one was open for 1% of the time, Pallas kernels for 8%

profile of v3, /device:TPU:0, one launch (start us, length us, event | category | flops | bytes accessed | tf_op | source)
XLA Modules:
  0.0 91.1 jit_solution(12841488205084505781)
XLA Ops:
  0.6 0.5 collective-permute-start
  1.1 2.6 %collective-permute-start.2 = (bf16[256,256]{1,0:T(8,128)(2,1)}, bf16[256,256]{1,0:T(8,128)(2,1)S(1)}, u32[]{:S(2)}, u32[]{:S(2)}) collective-permute-start(bf16[256,256]{1,0:T(8,128)(2,1)} %own.1), channel_id=1, source_target_pairs={{0,8},{4,12},{8,0},{12,4},{16,24},{20,28},{24,16},{28,20},{1,9},{5... | collective-permute-start | bytes 393224 | tf_op jit(solution)/shard_map/ppermute | solution.py:21
  3.7 1.5 %collective-permute-start.3 = (bf16[256,256]{1,0:T(8,128)(2,1)}, bf16[256,256]{1,0:T(8,128)(2,1)S(1)}, u32[]{:S(2)}, u32[]{:S(2)}) collective-permute-start(bf16[256,256]{1,0:T(8,128)(2,1)} %own.1), channel_id=1, source_target_pairs={{0,16},{4,20},{8,24},{12,28},{16,0},{20,4},{24,8},{28,12},{1,17},{... | collective-permute-start | bytes 393224 | tf_op jit(solution)/shard_map/ppermute | solution.py:21
  5.2 0.0 collective-permute-start.4
  5.3 1.0 %copy-done.3 = bf16[1024,256]{1,0:T(8,128)(2,1)S(1)} copy-done((bf16[1024,256]{1,0:T(8,128)(2,1)S(1)}, bf16[1024,256]{1,0:T(8,128)(2,1)}, u32[]{:S(2)}) %copy-start.3) | copy-done | bytes 524312
  6.3 0.0 copy-start.7
  6.4 0.8 copy-done.7
  7.2 0.8 copy-done.8
  8.0 0.7 copy-done.9
  8.6 1.9 %shard_map.113 = (s32[16]{0:T(128)S(1)}, s32[16]{0:T(128)S(1)}, s32[16]{0:T(128)S(1)}, s32[16]{0:T(128)S(1)}) custom-call(s32[1,32]{1,0:T(1,128)S(1)} %bitcast.2, s32[32]{0:T(128)S(1)} %copy-done.8, s32[32]{0:T(128)S(1)} %copy-done.9, bf16[1024,256]{1,0:T(8,128)(2,1)S(1)} %shard_map.112._.refs_3_.refs_0_), custom_call_target="tpu_custom_call" | custom-call | tf_op jit(solution)/shard_map/pallas_call | solution.py:268
  10.6 0.0 copy-start.1
  10.6 1.2 %copy-done.1 = bf16[32,128,128]{2,1,0:T(8,128)(2,1)S(1)} copy-done((bf16[32,128,128]{2,1,0:T(8,128)(2,1)S(1)}, bf16[32,128,128]{2,1,0:T(8,128)(2,1)}, u32[]{:S(2)}) %copy-start.1) | copy-done | bytes 1048600
  11.8 0.6 shard_map.115
  12.4 0.1 collective-permute-start.6
  12.6 0.5 collective-permute-start.5
  13.1 2.0 %collective-permute-start.10 = (bf16[1024,256]{1,0:T(8,128)(2,1)S(1)}, bf16[1024,256]{1,0:T(8,128)(2,1)S(1)}, u32[]{:S(2)}, u32[]{:S(2)}) collective-permute-start(bf16[1024,256]{1,0:T(8,128)(2,1)S(1)} %shard_map.112._.refs_3_.refs_0_), channel_id=1, source_target_pairs={{0,16},{4,20},{8,24},{12,28},{16,0},{20,4},{24,8},{28,12},{1,17},{... | collective-permute-start | bytes 1572872 | tf_op jit(solution)/shard_map/ppermute | solution.py:21
  15.1 1.5 %collective-permute-start.9 = (bf16[1024,256]{1,0:T(8,128)(2,1)S(1)}, bf16[1024,256]{1,0:T(8,128)(2,1)S(1)}, u32[]{:S(2)}, u32[]{:S(2)}) collective-permute-start(bf16[1024,256]{1,0:T(8,128)(2,1)S(1)} %shard_map.112._.refs_3_.refs_0_), channel_id=1, source_target_pairs={{0,8},{4,12},{8,0},{12,4},{16,24},{20,28},{24,16},{28,20},{1,9},{5... | collective-permute-start | bytes 1572872 | tf_op jit(solution)/shard_map/ppermute | solution.py:21
  16.6 1.1 %collective-permute-done.1._.code2.code = s32[16]{0:T(128)S(1)} collective-permute-done((s32[16]{0:T(128)S(1)}, s32[16]{0:T(128)S(1)}, u32[]{:S(2)}, u32[]{:S(2)}) %collective-permute-start.1) | collective-permute-done | bytes 96 | tf_op jit(solution)/shard_map/ppermute | solution.py:21
  17.7 0.2 collective-permute-start.11
  17.9 1.9 %shard_map.116 = (f32[2,256,256]{2,1,0:T(8,128)S(1)}, bf16[2,256,256]{2,1,0:T(8,128)(2,1)S(1)}) custom-call(s32[16]{0:T(128)S(1)} %collective-permute-done.1._.code2.code, bf16[1024,2048]{1,0:T(8,128)(2,1)S(1)} %copy-done, bf16[256,256]{1,0:T(8,128)(2,1)S(1)} %copy-done.5, bf16[256,256]{1,0:T(8,128)(2,1)S(1)} %collective-permute-done._.other, ...), custom_call_target="tpu_custom_call" | custom-call | tf_op jit(solution)/shard_map/pallas_call | solution.py:35
  19.8 0.0 copy-start.2
  19.8 2.0 %collective-permute-start.7 = (bf16[2,256,256]{2,1,0:T(8,128)(2,1)S(1)}, bf16[2,256,256]{2,1,0:T(8,128)(2,1)S(1)}, u32[]{:S(2)}, u32[]{:S(2)}) collective-permute-start(bf16[2,256,256]{2,1,0:T(8,128)(2,1)S(1)} %get-tuple-element.34), channel_id=1, source_target_pairs={{0,1},{1,0},{2,3},{3,2},{4,5},{5,4},{6,7},{7,6},{8,9},{9,8},{10,11... | collective-permute-start | bytes 786440 | tf_op jit(solution)/shard_map/ppermute | solution.py:21
  21.7 6.4 %collective-permute-done.7.received = bf16[2,256,256]{2,1,0:T(8,128)(2,1)S(1)} collective-permute-done((bf16[2,256,256]{2,1,0:T(8,128)(2,1)S(1)}, bf16[2,256,256]{2,1,0:T(8,128)(2,1)S(1)}, u32[]{:S(2)}, u32[]{:S(2)}) %collective-permute-start.7) | collective-permute-done | bytes 262176 | tf_op jit(solution)/shard_map/ppermute | solution.py:21
  28.2 2.8 %collective-permute-start.8 = (bf16[1,256,256]{2,1,0:T(8,128)(2,1)S(1)}, bf16[1,256,256]{2,1,0:T(8,128)(2,1)S(1)}, u32[]{:S(2)}, u32[]{:S(2)}) collective-permute-start(bf16[1,256,256]{2,1,0:T(8,128)(2,1)S(1)} %get-tuple-element.36), channel_id=1, source_target_pairs={{0,2},{1,3},{2,0},{3,1},{4,6},{5,7},{6,4},{7,5},{8,10},{9,11},{10,... | collective-permute-start | bytes 393224 | tf_op jit(solution)/shard_map/ppermute | solution.py:21
  31.0 5.6 %collective-permute-done.8.received = bf16[1,256,256]{2,1,0:T(8,128)(2,1)S(1)} collective-permute-done((bf16[1,256,256]{2,1,0:T(8,128)(2,1)S(1)}, bf16[1,256,256]{2,1,0:T(8,128)(2,1)S(1)}, u32[]{:S(2)}, u32[]{:S(2)}) %collective-permute-start.8) | collective-permute-done | bytes 131104 | tf_op jit(solution)/shard_map/ppermute | solution.py:21
  36.6 0.2 shard_map.118
  36.9 1.3 %shard_map.119 = (f32[1152,256]{1,0:T(8,128)S(1)}, f32[1152,256]{1,0:T(8,128)S(1)}) custom-call(s32[16]{0:T(128)S(1)} %get-tuple-element.29.which, s32[16]{0:T(128)S(1)} %get-tuple-element.30.code, s32[16]{0:T(128)S(1)} %collective-permute-done.1._.code2.code, f32[256,256]{1,0:T(8,128)S(1)} %get-tuple-element.37.projected, ...), custom_call_target="tpu_custom_call" | custom-call | tf_op jit(solution)/shard_map/pallas_call | solution.py:35
  38.2 1.6 %collective-permute-done.11.refs_0_ = bf16[1024,256]{1,0:T(8,128)(2,1)S(1)} collective-permute-done((bf16[1024,256]{1,0:T(8,128)(2,1)S(1)}, bf16[1024,256]{1,0:T(8,128)(2,1)S(1)}, u32[]{:S(2)}, u32[]{:S(2)}) %collective-permute-start.11) | collective-permute-done | bytes 524320 | tf_op jit(solution)/shard_map/ppermute | solution.py:21
  39.7 0.8 shard_map.121
  40.6 0.1 collective-permute-start.12
  40.7 0.8 shard_map.120.own
  41.5 0.0 copy-start.6
  41.5 1.1 %collective-permute-done.12.received = bf16[1024,256]{1,0:T(8,128)(2,1)S(1)} collective-permute-done((bf16[1024,256]{1,0:T(8,128)(2,1)S(1)}, bf16[1024,256]{1,0:T(8,128)(2,1)S(1)}, u32[]{:S(2)}, u32[]{:S(2)}) %collective-permute-start.12) | collective-permute-done | bytes 524320 | tf_op jit(solution)/shard_map/ppermute | solution.py:21
  42.6 0.1 shard_map.122
  42.7 1.8 %collective-permute-start.13 = (bf16[256,256]{1,0:T(8,128)(2,1)S(1)}, bf16[256,256]{1,0:T(8,128)(2,1)S(1)}, u32[]{:S(2)}, u32[]{:S(2)}) collective-permute-start(bf16[256,256]{1,0:T(8,128)(2,1)S(1)} %get-tuple-element.41), channel_id=1, source_target_pairs={{0,1},{1,0},{2,3},{3,2},{4,5},{5,4},{6,7},{7,6},{8,9},{9,8},{10,11... | collective-permute-start | bytes 393224 | tf_op jit(solution)/shard_map/ppermute | solution.py:21
  44.5 2.6 %collective-permute-start.14 = (bf16[256,256]{1,0:T(8,128)(2,1)S(1)}, bf16[256,256]{1,0:T(8,128)(2,1)S(1)}, u32[]{:S(2)}, u32[]{:S(2)}) collective-permute-start(bf16[256,256]{1,0:T(8,128)(2,1)S(1)} %get-tuple-element.42), channel_id=1, source_target_pairs={{0,2},{1,3},{2,0},{3,1},{4,6},{5,7},{6,4},{7,5},{8,10},{9,11},{10,... | collective-permute-start | bytes 393224 | tf_op jit(solution)/shard_map/ppermute | solution.py:21
  47.1 0.1 collective-permute-start.15
  47.1 3.0 %collective-permute-done.13.refs_0_ = bf16[256,256]{1,0:T(8,128)(2,1)S(1)} collective-permute-done((bf16[256,256]{1,0:T(8,128)(2,1)S(1)}, bf16[256,256]{1,0:T(8,128)(2,1)S(1)}, u32[]{:S(2)}, u32[]{:S(2)}) %collective-permute-start.13) | collective-permute-done | bytes 131104 | tf_op jit(solution)/shard_map/ppermute | solution.py:21
  50.2 7.2 %collective-permute-done.14.refs_1_ = bf16[256,256]{1,0:T(8,128)(2,1)S(1)} collective-permute-done((bf16[256,256]{1,0:T(8,128)(2,1)S(1)}, bf16[256,256]{1,0:T(8,128)(2,1)S(1)}, u32[]{:S(2)}, u32[]{:S(2)}) %collective-permute-start.14) | collective-permute-done | bytes 131104 | tf_op jit(solution)/shard_map/ppermute | solution.py:21
  57.4 0.8 shard_map.123
  58.2 0.2 shard_map.125
  58.4 0.1 collective-permute-start.19
  58.5 2.4 %collective-permute-start.16 = (bf16[256,256]{1,0:T(8,128)(2,1)S(1)}, bf16[256,256]{1,0:T(8,128)(2,1)S(1)}, u32[]{:S(2)}, u32[]{:S(2)}) collective-permute-start(bf16[256,256]{1,0:T(8,128)(2,1)S(1)} %get-tuple-element.45.refs_0_.g_ref), channel_id=1, source_target_pairs={{0,1},{1,0},{2,3},{3,2},{4,5},{5,4},{6,7},{7,6},{8,9},{9,8},{10,11... | collective-permute-start | bytes 393224 | tf_op jit(solution)/shard_map/ppermute | solution.py:21
  60.8 1.1 %collective-permute-start.17 = (bf16[256,256]{1,0:T(8,128)(2,1)S(1)}, bf16[256,256]{1,0:T(8,128)(2,1)S(1)}, u32[]{:S(2)}, u32[]{:S(2)}) collective-permute-start(bf16[256,256]{1,0:T(8,128)(2,1)S(1)} %get-tuple-element.45.refs_0_.g_ref), channel_id=1, source_target_pairs={{0,2},{1,3},{2,0},{3,1},{4,6},{5,7},{6,4},{7,5},{8,10},{9,11},{10,... | collective-permute-start | bytes 393224 | tf_op jit(solution)/shard_map/ppermute | solution.py:21
  61.9 1.4 %collective-permute-start.18 = (bf16[256,256]{1,0:T(8,128)(2,1)S(1)}, bf16[256,256]{1,0:T(8,128)(2,1)S(1)}, u32[]{:S(2)}, u32[]{:S(2)}) collective-permute-start(bf16[256,256]{1,0:T(8,128)(2,1)S(1)} %get-tuple-element.45.refs_0_.g_ref), channel_id=1, source_target_pairs={{0,3},{1,2},{2,1},{3,0},{4,7},{5,6},{6,5},{7,4},{8,11},{9,10},{10,... | collective-permute-start | bytes 393224 | tf_op jit(solution)/shard_map/ppermute | solution.py:21
  63.3 1.6 %collective-permute-start.20 = (bf16[128,256]{1,0:T(8,128)(2,1)S(1)}, bf16[128,256]{1,0:T(8,128)(2,1)S(1)}, u32[]{:S(2)}, u32[]{:S(2)}) collective-permute-start(bf16[128,256]{1,0:T(8,128)(2,1)S(1)} %add_convert_fusion.2.refs_0_), channel_id=1, source_target_pairs={{0,8},{4,12},{8,0},{12,4},{16,24},{20,28},{24,16},{28,20},{1,9},{5... | collective-permute-start | bytes 196616 | tf_op jit(solution)/shard_map/ppermute | solution.py:21
  64.9 1.5 %collective-permute-start.21 = (bf16[128,256]{1,0:T(8,128)(2,1)S(1)}, bf16[128,256]{1,0:T(8,128)(2,1)S(1)}, u32[]{:S(2)}, u32[]{:S(2)}) collective-permute-start(bf16[128,256]{1,0:T(8,128)(2,1)S(1)} %add_convert_fusion.2.refs_0_), channel_id=1, source_target_pairs={{0,16},{4,20},{8,24},{12,28},{16,0},{20,4},{24,8},{28,12},{1,17},{... | collective-permute-start | bytes 196616 | tf_op jit(solution)/shard_map/ppermute | solution.py:21
  66.4 0.7 collective-permute-done.16.refs_1_
  67.1 2.4 %collective-permute-start.22 = (bf16[128,256]{1,0:T(8,128)(2,1)S(1)}, bf16[128,256]{1,0:T(8,128)(2,1)S(1)}, u32[]{:S(2)}, u32[]{:S(2)}) collective-permute-start(bf16[128,256]{1,0:T(8,128)(2,1)S(1)} %add_convert_fusion.2.refs_0_), channel_id=1, source_target_pairs={{0,24},{4,28},{8,16},{12,20},{16,8},{20,12},{24,0},{28,4},{1,25},{... | collective-permute-start | bytes 196616 | tf_op jit(solution)/shard_map/ppermute | solution.py:21
  69.6 4.2 %collective-permute-done.17.refs_2_ = bf16[256,256]{1,0:T(8,128)(2,1)S(1)} collective-permute-done((bf16[256,256]{1,0:T(8,128)(2,1)S(1)}, bf16[256,256]{1,0:T(8,128)(2,1)S(1)}, u32[]{:S(2)}, u32[]{:S(2)}) %collective-permute-start.17) | collective-permute-done | bytes 131104 | tf_op jit(solution)/shard_map/ppermute | solution.py:21
  73.7 0.1 shard_map.124.refs_4_.g_ref
  73.9 1.3 %shard_map.127 = (bf16[4,256,256]{2,1,0:T(8,128)(2,1)S(1)}, f32[4,256,256]{2,1,0:T(8,128)S(1)}) custom-call(bf16[1024,2048]{1,0:T(8,128)(2,1)S(1)} %copy-done, bf16[256,1024]{1,0:T(8,128)(2,1)S(1)} %shard_map.124.refs_4_.g_ref, bf16[128,256]{1,0:T(8,128)(2,1)S(1)} %shard_map.126._.x_ref), custom_call_target="tpu_custom_call" | custom-call | tf_op jit(solution)/shard_map/pallas_call | solution.py:35
  75.2 0.1 collective-permute-start.23
  75.3 2.7 %collective-permute-start.24 = (bf16[128,256]{1,0:T(8,128)(2,1)S(1)}, bf16[128,256]{1,0:T(8,128)(2,1)S(1)}, u32[]{:S(2)}, u32[]{:S(2)}) collective-permute-start(bf16[128,256]{1,0:T(8,128)(2,1)S(1)} %shard_map.126._.x_ref), channel_id=1, source_target_pairs={{0,1},{1,0},{2,3},{3,2},{4,5},{5,4},{6,7},{7,6},{8,9},{9,8},{10,11... | collective-permute-start | bytes 196616 | tf_op jit(solution)/shard_map/ppermute | solution.py:21
  78.0 2.5 %collective-permute-start.27 = (bf16[256,256]{1,0:T(8,128)(2,1)S(1)}, bf16[256,256]{1,0:T(8,128)(2,1)S(1)}, u32[]{:S(2)}, u32[]{:S(2)}) collective-permute-start(bf16[256,256]{1,0:T(8,128)(2,1)S(1)} %get-tuple-element.54), channel_id=1, source_target_pairs={{0,24},{4,28},{8,16},{12,20},{16,8},{20,12},{24,0},{28,4},{1,25},{... | collective-permute-start | bytes 393224 | tf_op jit(solution)/shard_map/ppermute | solution.py:21
  80.5 0.1 collective-permute-done.24.y_ref
  80.7 1.5 %collective-permute-start.25 = (bf16[256,256]{1,0:T(8,128)(2,1)S(1)}, bf16[256,256]{1,0:T(8,128)(2,1)S(1)}, u32[]{:S(2)}, u32[]{:S(2)}) collective-permute-start(bf16[256,256]{1,0:T(8,128)(2,1)S(1)} %get-tuple-element.53), channel_id=1, source_target_pairs={{0,8},{4,12},{8,0},{12,4},{16,24},{20,28},{24,16},{28,20},{1,9},{5... | collective-permute-start | bytes 393224 | tf_op jit(solution)/shard_map/ppermute | solution.py:21
  82.3 1.5 %collective-permute-start.26 = (bf16[256,256]{1,0:T(8,128)(2,1)S(1)}, bf16[256,256]{1,0:T(8,128)(2,1)S(1)}, u32[]{:S(2)}, u32[]{:S(2)}) collective-permute-start(bf16[256,256]{1,0:T(8,128)(2,1)S(1)} %get-tuple-element.51._), channel_id=1, source_target_pairs={{0,16},{4,20},{8,24},{12,28},{16,0},{20,4},{24,8},{28,12},{1,17},{... | collective-permute-start | bytes 393224 | tf_op jit(solution)/shard_map/ppermute | solution.py:21
  83.8 2.8 %collective-permute-start.28 = (bf16[128,256]{1,0:T(8,128)(2,1)S(1)}, bf16[128,256]{1,0:T(8,128)(2,1)S(1)}, u32[]{:S(2)}, u32[]{:S(2)}) collective-permute-start(bf16[128,256]{1,0:T(8,128)(2,1)S(1)} %shard_map.129._.x_ref), channel_id=1, source_target_pairs={{0,2},{1,3},{2,0},{3,1},{4,6},{5,7},{6,4},{7,5},{8,10},{9,11},{10,... | collective-permute-start | bytes 196616 | tf_op jit(solution)/shard_map/ppermute | solution.py:21
  86.6 2.4 %collective-permute-done.28.y_ref = bf16[128,256]{1,0:T(8,128)(2,1)S(1)} collective-permute-done((bf16[128,256]{1,0:T(8,128)(2,1)S(1)}, bf16[128,256]{1,0:T(8,128)(2,1)S(1)}, u32[]{:S(2)}, u32[]{:S(2)}) %collective-permute-start.28) | collective-permute-done | bytes 65568 | tf_op jit(solution)/shard_map/ppermute | solution.py:21
  89.0 0.1 collective-permute-start.29
  89.1 0.9 %convolution_convert_fusion = bf16[256,256]{1,0:T(8,128)(2,1)} fusion(bf16[256,256]{1,0:T(8,128)(2,1)S(1)} %copy-done.4, bf16[256,256]{1,0:T(8,128)(2,1)S(1)} %collective-permute-done.27._, bf16[256,256]{1,0:T(8,128)(2,1)S(1)} %collective-permute-done.26, f32[256,256]{1,0:T(8,128)S(1)} %get-tuple-element.52, bf16[256,256]{1,0:T(8,128)(2,1)S(1)} %collective-permute-done.25), kind=kOutput, calls=%fused_computation | convolution fusion | flops 34078720 | bytes 917504 | tf_op jit(solution)/shard_map/dot_general | solution.py:366
  90.0 0.3 collective-permute-done.29
  90.3 0.7 convert_multiply_fusion
  (40 shorter events, 0.4 us)
Async XLA Ops:
  0.6 4.6 %collective-permute-start = (bf16[256,256]{1,0:T(8,128)(2,1)}, bf16[256,256]{1,0:T(8,128)(2,1)S(1)}, u32[]{:S(2)}, u32[]{:S(2)}) collective-permute-start(bf16[256,256]{1,0:T(8,128)(2,1)} %own.1), channel_id=1, source_target_pairs={{0,4},{4,0},{8,12},{12,8},{16,20},{20,16},{24,28},{28,24},{1,5},{5... | collective-permute-start | bytes 393224 | tf_op jit(solution)/shard_map/ppermute | solution.py:21
  1.1 11.4 %collective-permute-start.2 = (bf16[256,256]{1,0:T(8,128)(2,1)}, bf16[256,256]{1,0:T(8,128)(2,1)S(1)}, u32[]{:S(2)}, u32[]{:S(2)}) collective-permute-start(bf16[256,256]{1,0:T(8,128)(2,1)} %own.1), channel_id=1, source_target_pairs={{0,8},{4,12},{8,0},{12,4},{16,24},{20,28},{24,16},{28,20},{1,9},{5... | collective-permute-start | bytes 393224 | tf_op jit(solution)/shard_map/ppermute | solution.py:21
  3.7 8.8 %collective-permute-start.3 = (bf16[256,256]{1,0:T(8,128)(2,1)}, bf16[256,256]{1,0:T(8,128)(2,1)S(1)}, u32[]{:S(2)}, u32[]{:S(2)}) collective-permute-start(bf16[256,256]{1,0:T(8,128)(2,1)} %own.1), channel_id=1, source_target_pairs={{0,16},{4,20},{8,24},{12,28},{16,0},{20,4},{24,8},{28,12},{1,17},{... | collective-permute-start | bytes 393224 | tf_op jit(solution)/shard_map/ppermute | solution.py:21
  5.2 7.3 %collective-permute-start.4 = (bf16[256,256]{1,0:T(8,128)(2,1)}, bf16[256,256]{1,0:T(8,128)(2,1)S(1)}, u32[]{:S(2)}, u32[]{:S(2)}) collective-permute-start(bf16[256,256]{1,0:T(8,128)(2,1)} %own.1), channel_id=1, source_target_pairs={{0,24},{4,28},{8,16},{12,20},{16,8},{20,12},{24,0},{28,4},{1,25},{... | collective-permute-start | bytes 393224 | tf_op jit(solution)/shard_map/ppermute | solution.py:21
  5.3 1.0 %copy-start.3 = (bf16[1024,256]{1,0:T(8,128)(2,1)S(1)}, bf16[1024,256]{1,0:T(8,128)(2,1)}, u32[]{:S(2)}) copy-start(bf16[1024,256]{1,0:T(8,128)(2,1)} %x_ref.1) | copy-start | bytes 1572868
  6.3 11.6 %copy-start = (bf16[1024,2048]{1,0:T(8,128)(2,1)S(1)}, bf16[1024,2048]{1,0:T(8,128)(2,1)}, u32[]{:S(2)}) copy-start(bf16[1024,2048]{1,0:T(8,128)(2,1)} %a_ref.3) | copy-start | bytes 12582916
  6.3 0.8 copy-start.7
  7.2 0.8 copy-start.8
  8.0 0.7 copy-start.9
  10.6 1.2 %copy-start.1 = (bf16[32,128,128]{2,1,0:T(8,128)(2,1)S(1)}, bf16[32,128,128]{2,1,0:T(8,128)(2,1)}, u32[]{:S(2)}) copy-start(bf16[32,128,128]{2,1,0:T(8,128)(2,1)} %tiles.5) | copy-start | bytes 3145732
  11.8 6.0 %copy-start.5 = (bf16[256,256]{1,0:T(8,128)(2,1)S(1)}, bf16[256,256]{1,0:T(8,128)(2,1)}, u32[]{:S(2)}) copy-start(bf16[256,256]{1,0:T(8,128)(2,1)} %own.1) | copy-start | bytes 393220
  12.4 5.4 %collective-permute-start.6 = (bf16[16,128,128]{2,1,0:T(8,128)(2,1)S(1)}, bf16[16,128,128]{2,1,0:T(8,128)(2,1)S(1)}, u32[]{:S(2)}, u32[]{:S(2)}) collective-permute-start(bf16[16,128,128]{2,1,0:T(8,128)(2,1)S(1)} %shard_map.115), channel_id=1, source_target_pairs={{0,4},{4,0},{8,12},{12,8},{16,20},{20,16},{24,28},{28,24},{1,5},{5... | collective-permute-start | bytes 1572872 | tf_op jit(solution)/shard_map/ppermute | solution.py:21
  12.6 5.3 %collective-permute-start.5 = (bf16[3,256,256]{2,1,0:T(8,128)(2,1)S(1)}, bf16[3,256,256]{2,1,0:T(8,128)(2,1)S(1)}, u32[]{:S(2)}, u32[]{:S(2)}) collective-permute-start(bf16[3,256,256]{2,1,0:T(8,128)(2,1)S(1)} %shard_map.114.near), channel_id=1, source_target_pairs={{0,4},{4,0},{8,12},{12,8},{16,20},{20,16},{24,28},{28,24},{1,5},{5... | collective-permute-start | bytes 1179656 | tf_op jit(solution)/shard_map/ppermute | solution.py:21
  13.1 23.7 %collective-permute-start.10 = (bf16[1024,256]{1,0:T(8,128)(2,1)S(1)}, bf16[1024,256]{1,0:T(8,128)(2,1)S(1)}, u32[]{:S(2)}, u32[]{:S(2)}) collective-permute-start(bf16[1024,256]{1,0:T(8,128)(2,1)S(1)} %shard_map.112._.refs_3_.refs_0_), channel_id=1, source_target_pairs={{0,16},{4,20},{8,24},{12,28},{16,0},{20,4},{24,8},{28,12},{1,17},{... | collective-permute-start | bytes 1572872 | tf_op jit(solution)/shard_map/ppermute | solution.py:21
  15.1 21.8 %collective-permute-start.9 = (bf16[1024,256]{1,0:T(8,128)(2,1)S(1)}, bf16[1024,256]{1,0:T(8,128)(2,1)S(1)}, u32[]{:S(2)}, u32[]{:S(2)}) collective-permute-start(bf16[1024,256]{1,0:T(8,128)(2,1)S(1)} %shard_map.112._.refs_3_.refs_0_), channel_id=1, source_target_pairs={{0,8},{4,12},{8,0},{12,4},{16,24},{20,28},{24,16},{28,20},{1,9},{5... | collective-permute-start | bytes 1572872 | tf_op jit(solution)/shard_map/ppermute | solution.py:21
  16.6 20.0 %copy-start.4 = (bf16[256,256]{1,0:T(8,128)(2,1)S(1)}, bf16[256,256]{1,0:T(8,128)(2,1)}, u32[]{:S(2)}) copy-start(bf16[256,256]{1,0:T(8,128)(2,1)} %w_ref.1) | copy-start | bytes 393220
  16.6 1.1 %collective-permute-start.1 = (s32[16]{0:T(128)S(1)}, s32[16]{0:T(128)S(1)}, u32[]{:S(2)}, u32[]{:S(2)}) collective-permute-start(s32[16]{0:T(128)S(1)} %get-tuple-element.31), channel_id=1, source_target_pairs={{0,4},{4,0},{8,12},{12,8},{16,20},{20,16},{24,28},{28,24},{1,5},{5... | collective-permute-start | bytes 200 | tf_op jit(solution)/shard_map/ppermute | solution.py:21
  17.7 22.0 %collective-permute-start.11 = (bf16[1024,256]{1,0:T(8,128)(2,1)S(1)}, bf16[1024,256]{1,0:T(8,128)(2,1)S(1)}, u32[]{:S(2)}, u32[]{:S(2)}) collective-permute-start(bf16[1024,256]{1,0:T(8,128)(2,1)S(1)} %shard_map.112._.refs_3_.refs_0_), channel_id=1, source_target_pairs={{0,24},{4,28},{8,16},{12,20},{16,8},{20,12},{24,0},{28,4},{1,25},{... | collective-permute-start | bytes 1572872 | tf_op jit(solution)/shard_map/ppermute | solution.py:21
  19.8 17.1 %copy-start.2 = (bf16[32,128,128]{2,1,0:T(8,128)(2,1)S(1)}, bf16[32,128,128]{2,1,0:T(8,128)(2,1)}, u32[]{:S(2)}) copy-start(bf16[32,128,128]{2,1,0:T(8,128)(2,1)} %tiles.5) | copy-start | bytes 3145732
  19.8 8.4 %collective-permute-start.7 = (bf16[2,256,256]{2,1,0:T(8,128)(2,1)S(1)}, bf16[2,256,256]{2,1,0:T(8,128)(2,1)S(1)}, u32[]{:S(2)}, u32[]{:S(2)}) collective-permute-start(bf16[2,256,256]{2,1,0:T(8,128)(2,1)S(1)} %get-tuple-element.34), channel_id=1, source_target_pairs={{0,1},{1,0},{2,3},{3,2},{4,5},{5,4},{6,7},{7,6},{8,9},{9,8},{10,11... | collective-permute-start | bytes 786440 | tf_op jit(solution)/shard_map/ppermute | solution.py:21
  28.2 8.4 %collective-permute-start.8 = (bf16[1,256,256]{2,1,0:T(8,128)(2,1)S(1)}, bf16[1,256,256]{2,1,0:T(8,128)(2,1)S(1)}, u32[]{:S(2)}, u32[]{:S(2)}) collective-permute-start(bf16[1,256,256]{2,1,0:T(8,128)(2,1)S(1)} %get-tuple-element.36), channel_id=1, source_target_pairs={{0,2},{1,3},{2,0},{3,1},{4,6},{5,7},{6,4},{7,5},{8,10},{9,11},{10,... | collective-permute-start | bytes 393224 | tf_op jit(solution)/shard_map/ppermute | solution.py:21
  40.6 2.0 %collective-permute-start.12 = (bf16[1024,256]{1,0:T(8,128)(2,1)S(1)}, bf16[1024,256]{1,0:T(8,128)(2,1)S(1)}, u32[]{:S(2)}, u32[]{:S(2)}) collective-permute-start(bf16[1024,256]{1,0:T(8,128)(2,1)S(1)} %shard_map.121), channel_id=1, source_target_pairs={{0,4},{4,0},{8,12},{12,8},{16,20},{20,16},{24,28},{28,24},{1,5},{5... | collective-permute-start | bytes 1572872 | tf_op jit(solution)/shard_map/ppermute | solution.py:21
  41.5 15.9 %copy-start.6 = (bf16[256,256]{1,0:T(8,128)(2,1)S(1)}, bf16[256,256]{1,0:T(8,128)(2,1)}, u32[]{:S(2)}) copy-start(bf16[256,256]{1,0:T(8,128)(2,1)} %cotangent.1) | copy-start | bytes 393220
  42.7 7.5 %collective-permute-start.13 = (bf16[256,256]{1,0:T(8,128)(2,1)S(1)}, bf16[256,256]{1,0:T(8,128)(2,1)S(1)}, u32[]{:S(2)}, u32[]{:S(2)}) collective-permute-start(bf16[256,256]{1,0:T(8,128)(2,1)S(1)} %get-tuple-element.41), channel_id=1, source_target_pairs={{0,1},{1,0},{2,3},{3,2},{4,5},{5,4},{6,7},{7,6},{8,9},{9,8},{10,11... | collective-permute-start | bytes 393224 | tf_op jit(solution)/shard_map/ppermute | solution.py:21
  44.5 12.9 %collective-permute-start.14 = (bf16[256,256]{1,0:T(8,128)(2,1)S(1)}, bf16[256,256]{1,0:T(8,128)(2,1)S(1)}, u32[]{:S(2)}, u32[]{:S(2)}) collective-permute-start(bf16[256,256]{1,0:T(8,128)(2,1)S(1)} %get-tuple-element.42), channel_id=1, source_target_pairs={{0,2},{1,3},{2,0},{3,1},{4,6},{5,7},{6,4},{7,5},{8,10},{9,11},{10,... | collective-permute-start | bytes 393224 | tf_op jit(solution)/shard_map/ppermute | solution.py:21
  47.1 10.3 %collective-permute-start.15 = (bf16[256,256]{1,0:T(8,128)(2,1)S(1)}, bf16[256,256]{1,0:T(8,128)(2,1)S(1)}, u32[]{:S(2)}, u32[]{:S(2)}) collective-permute-start(bf16[256,256]{1,0:T(8,128)(2,1)S(1)} %get-tuple-element.43), channel_id=1, source_target_pairs={{0,3},{1,2},{2,1},{3,0},{4,7},{5,6},{6,5},{7,4},{8,11},{9,10},{10,... | collective-permute-start | bytes 393224 | tf_op jit(solution)/shard_map/ppermute | solution.py:21
  58.4 4.9 %collective-permute-start.19 = (bf16[128,256]{1,0:T(8,128)(2,1)S(1)}, bf16[128,256]{1,0:T(8,128)(2,1)S(1)}, u32[]{:S(2)}, u32[]{:S(2)}) collective-permute-start(bf16[128,256]{1,0:T(8,128)(2,1)S(1)} %get-tuple-element.48), channel_id=1, source_target_pairs={{0,4},{4,0},{8,12},{12,8},{16,20},{20,16},{24,28},{28,24},{1,5},{5... | collective-permute-start | bytes 196616 | tf_op jit(solution)/shard_map/ppermute | solution.py:21
  58.5 8.6 %collective-permute-start.16 = (bf16[256,256]{1,0:T(8,128)(2,1)S(1)}, bf16[256,256]{1,0:T(8,128)(2,1)S(1)}, u32[]{:S(2)}, u32[]{:S(2)}) collective-permute-start(bf16[256,256]{1,0:T(8,128)(2,1)S(1)} %get-tuple-element.45.refs_0_.g_ref), channel_id=1, source_target_pairs={{0,1},{1,0},{2,3},{3,2},{4,5},{5,4},{6,7},{7,6},{8,9},{9,8},{10,11... | collective-permute-start | bytes 393224 | tf_op jit(solution)/shard_map/ppermute | solution.py:21
  60.8 12.9 %collective-permute-start.17 = (bf16[256,256]{1,0:T(8,128)(2,1)S(1)}, bf16[256,256]{1,0:T(8,128)(2,1)S(1)}, u32[]{:S(2)}, u32[]{:S(2)}) collective-permute-start(bf16[256,256]{1,0:T(8,128)(2,1)S(1)} %get-tuple-element.45.refs_0_.g_ref), channel_id=1, source_target_pairs={{0,2},{1,3},{2,0},{3,1},{4,6},{5,7},{6,4},{7,5},{8,10},{9,11},{10,... | collective-permute-start | bytes 393224 | tf_op jit(solution)/shard_map/ppermute | solution.py:21
  61.9 11.8 %collective-permute-start.18 = (bf16[256,256]{1,0:T(8,128)(2,1)S(1)}, bf16[256,256]{1,0:T(8,128)(2,1)S(1)}, u32[]{:S(2)}, u32[]{:S(2)}) collective-permute-start(bf16[256,256]{1,0:T(8,128)(2,1)S(1)} %get-tuple-element.45.refs_0_.g_ref), channel_id=1, source_target_pairs={{0,3},{1,2},{2,1},{3,0},{4,7},{5,6},{6,5},{7,4},{8,11},{9,10},{10,... | collective-permute-start | bytes 393224 | tf_op jit(solution)/shard_map/ppermute | solution.py:21
  63.3 10.5 %collective-permute-start.20 = (bf16[128,256]{1,0:T(8,128)(2,1)S(1)}, bf16[128,256]{1,0:T(8,128)(2,1)S(1)}, u32[]{:S(2)}, u32[]{:S(2)}) collective-permute-start(bf16[128,256]{1,0:T(8,128)(2,1)S(1)} %add_convert_fusion.2.refs_0_), channel_id=1, source_target_pairs={{0,8},{4,12},{8,0},{12,4},{16,24},{20,28},{24,16},{28,20},{1,9},{5... | collective-permute-start | bytes 196616 | tf_op jit(solution)/shard_map/ppermute | solution.py:21
  64.9 8.9 %collective-permute-start.21 = (bf16[128,256]{1,0:T(8,128)(2,1)S(1)}, bf16[128,256]{1,0:T(8,128)(2,1)S(1)}, u32[]{:S(2)}, u32[]{:S(2)}) collective-permute-start(bf16[128,256]{1,0:T(8,128)(2,1)S(1)} %add_convert_fusion.2.refs_0_), channel_id=1, source_target_pairs={{0,16},{4,20},{8,24},{12,28},{16,0},{20,4},{24,8},{28,12},{1,17},{... | collective-permute-start | bytes 196616 | tf_op jit(solution)/shard_map/ppermute | solution.py:21
  67.1 6.7 %collective-permute-start.22 = (bf16[128,256]{1,0:T(8,128)(2,1)S(1)}, bf16[128,256]{1,0:T(8,128)(2,1)S(1)}, u32[]{:S(2)}, u32[]{:S(2)}) collective-permute-start(bf16[128,256]{1,0:T(8,128)(2,1)S(1)} %add_convert_fusion.2.refs_0_), channel_id=1, source_target_pairs={{0,24},{4,28},{8,16},{12,20},{16,8},{20,12},{24,0},{28,4},{1,25},{... | collective-permute-start | bytes 196616 | tf_op jit(solution)/shard_map/ppermute | solution.py:21
  75.2 2.7 %collective-permute-start.23 = (bf16[4,256,256]{2,1,0:T(8,128)(2,1)S(1)}, bf16[4,256,256]{2,1,0:T(8,128)(2,1)S(1)}, u32[]{:S(2)}, u32[]{:S(2)}) collective-permute-start(bf16[4,256,256]{2,1,0:T(8,128)(2,1)S(1)} %get-tuple-element.50._), channel_id=1, source_target_pairs={{0,4},{4,0},{8,12},{12,8},{16,20},{20,16},{24,28},{28,24},{1,5},{5... | collective-permute-start | bytes 1572872 | tf_op jit(solution)/shard_map/ppermute | solution.py:21
  75.3 5.3 %collective-permute-start.24 = (bf16[128,256]{1,0:T(8,128)(2,1)S(1)}, bf16[128,256]{1,0:T(8,128)(2,1)S(1)}, u32[]{:S(2)}, u32[]{:S(2)}) collective-permute-start(bf16[128,256]{1,0:T(8,128)(2,1)S(1)} %shard_map.126._.x_ref), channel_id=1, source_target_pairs={{0,1},{1,0},{2,3},{3,2},{4,5},{5,4},{6,7},{7,6},{8,9},{9,8},{10,11... | collective-permute-start | bytes 196616 | tf_op jit(solution)/shard_map/ppermute | solution.py:21
  78.0 11.0 %collective-permute-start.27 = (bf16[256,256]{1,0:T(8,128)(2,1)S(1)}, bf16[256,256]{1,0:T(8,128)(2,1)S(1)}, u32[]{:S(2)}, u32[]{:S(2)}) collective-permute-start(bf16[256,256]{1,0:T(8,128)(2,1)S(1)} %get-tuple-element.54), channel_id=1, source_target_pairs={{0,24},{4,28},{8,16},{12,20},{16,8},{20,12},{24,0},{28,4},{1,25},{... | collective-permute-start | bytes 393224 | tf_op jit(solution)/shard_map/ppermute | solution.py:21
  80.7 8.4 %collective-permute-start.25 = (bf16[256,256]{1,0:T(8,128)(2,1)S(1)}, bf16[256,256]{1,0:T(8,128)(2,1)S(1)}, u32[]{:S(2)}, u32[]{:S(2)}) collective-permute-start(bf16[256,256]{1,0:T(8,128)(2,1)S(1)} %get-tuple-element.53), channel_id=1, source_target_pairs={{0,8},{4,12},{8,0},{12,4},{16,24},{20,28},{24,16},{28,20},{1,9},{5... | collective-permute-start | bytes 393224 | tf_op jit(solution)/shard_map/ppermute | solution.py:21
  82.3 6.8 %collective-permute-start.26 = (bf16[256,256]{1,0:T(8,128)(2,1)S(1)}, bf16[256,256]{1,0:T(8,128)(2,1)S(1)}, u32[]{:S(2)}, u32[]{:S(2)}) collective-permute-start(bf16[256,256]{1,0:T(8,128)(2,1)S(1)} %get-tuple-element.51._), channel_id=1, source_target_pairs={{0,16},{4,20},{8,24},{12,28},{16,0},{20,4},{24,8},{28,12},{1,17},{... | collective-permute-start | bytes 393224 | tf_op jit(solution)/shard_map/ppermute | solution.py:21
  83.8 5.2 %collective-permute-start.28 = (bf16[128,256]{1,0:T(8,128)(2,1)S(1)}, bf16[128,256]{1,0:T(8,128)(2,1)S(1)}, u32[]{:S(2)}, u32[]{:S(2)}) collective-permute-start(bf16[128,256]{1,0:T(8,128)(2,1)S(1)} %shard_map.129._.x_ref), channel_id=1, source_target_pairs={{0,2},{1,3},{2,0},{3,1},{4,6},{5,7},{6,4},{7,5},{8,10},{9,11},{10,... | collective-permute-start | bytes 196616 | tf_op jit(solution)/shard_map/ppermute | solution.py:21
  89.0 1.3 %collective-permute-start.29 = (bf16[128,256]{1,0:T(8,128)(2,1)S(1)}, bf16[128,256]{1,0:T(8,128)(2,1)S(1)}, u32[]{:S(2)}, u32[]{:S(2)}) collective-permute-start(bf16[128,256]{1,0:T(8,128)(2,1)S(1)} %shard_map.131), channel_id=1, source_target_pairs={{0,4},{4,0},{8,12},{12,8},{16,20},{20,16},{24,28},{28,24},{1,5},{5... | collective-permute-start | bytes 196616 | tf_op jit(solution)/shard_map/ppermute | solution.py:21

commit v4 on v3

--- a/solution.py
+++ b/solution.py
@@ -23,6 +23,10 @@
 
 def shape(*dims, dtype=BF16):
     return jax.ShapeDtypeStruct(dims, dtype)
+
+
+def column_offsets(n_col):
+    return [n_col - 1, *range(1, n_col - 1)]
 
 
 def nbytes(arrays):
@@ -56,11 +60,11 @@
 
 
 def stack_kernel(*refs):
-    for i, ref in enumerate(refs[:-2]):
+    for i, ref in enumerate(refs[:-3]):
         refs[-1][i] = ref[...]
 
 
-def lists_kernel(held, spare, owner, slot, target, _, which, code, which2, code2, count):
+def lists_kernel(held, spare, mine, theirs, _, which, code, which2, code2, count):
     r = lax.axis_index("row")
     for refs in ((which, code), (which2, code2)):
         for i in range(refs[0].shape[0]):
@@ -70,31 +74,26 @@
         count[t] = 0
 
     def place(k, _):
-        t = owner[0, k] ^ r
-        i = t // 2 * CAP + count[t]
-        count[t] += 1
-
-        @pl.when(t % 2 == 0)
-        def _():
-            which[i] = k
-            code[i] = target[k] * held + slot[k]
-
-        @pl.when(t % 2 == 1)
-        def _():
-            which2[i] = k
-            code2[i] = target[k] * held + slot[k]
+        for pulls, refs, at in (
+            (mine, (which, code), 0),
+            (theirs, (which2, code2), count.shape[0] // 2),
+        ):
+            t = pulls[0, k] ^ r
+
+            @pl.when(t % 2 == 0)
+            def _(pulls=pulls, refs=refs, at=at, t=t):
+                chip = t // 2
+                i = chip * CAP + count[at + chip]
+                count[at + chip] += 1
+                refs[0][i] = k
+                refs[1][i] = pulls[2, k] * held + pulls[1, k]
 
         return 0
 
-    lax.fori_loop(0, slot.shape[0], place, 0)
-
-
-def tiles_kernel(which, tiles, out):
-    for i in range(out.shape[0]):
-        out[i] = tiles[which[i]]
-
-
-def aggregate_kernel(n_row, n_col, _, a_ref, own, other, near, across, __, keep, send, x_ref):
+    lax.fori_loop(0, mine.shape[1], place, 0)
+
+
+def aggregate_kernel(n_row, n_col, a_ref, own, other, near, across, keep, send, x_ref):
     span = own.shape[0]
     r, c = lax.axis_index("row"), lax.axis_index("col")
     x_ref[part(r, span), :] = own[...]
@@ -143,21 +142,21 @@
     ]
 
 
-def early_kernel(offsets, held, which, code, code2, projected, tiles, tiles2, *refs):
+def early_kernel(offsets, held, which, code, which2, code2, projected, tiles, tiles2, *refs):
     pieces, (own, others) = refs[:-2], refs[-2:]
     pulls = pulls_of(offsets, pieces)
     span = projected.shape[0]
     own[...] = jnp.zeros_like(own)
     others[...] = jnp.zeros_like(others)
     own[part(lax.axis_index("col"), span), :] = projected[...]
-    add_pulls(pulls, held, code2, lambda i: tiles2[i], others)
+    add_pulls(pulls, held, code2, lambda i: tiles2[which2[i]], others)
     add_pulls(pulls, held, code, lambda i: tiles[which[i]], own)
 
 
-def others_kernel(offsets, held, code, acc_in, tiles, *refs):
+def others_kernel(offsets, held, which, code, acc_in, tiles, *refs):
     pieces, (out, acc) = refs[:-2], refs[-2:]
     acc[...] = acc_in[...]
-    add_pulls(pulls_of(offsets, pieces), held, code, lambda i: tiles[i], acc)
+    add_pulls(pulls_of(offsets, pieces), held, code, lambda i: tiles[which[i]], acc)
     out[...] = acc[: out.shape[0], :].astype(BF16)
 
 
@@ -179,15 +178,37 @@
             keep[...] = block
 
 
-def activate_kernel(cotangent, kept, *refs):
-    parts, (activated, flipped) = refs[:-2], refs[-2:]
+def gradient_kernel(cotangent, kept, *refs):
+    parts, (mixed_out, flipped) = refs[:-2], refs[-2:]
     mixed = kept[...]
     for ref in parts:
         mixed = mixed + ref[...].astype(F32)
+    mixed_out[...] = mixed
     sigmoid_z = jax.nn.sigmoid(mixed)
-    activated[...] = (mixed * sigmoid_z).astype(BF16)
     grad_pre = cotangent[...].astype(F32) * sigmoid_z * (1.0 + mixed * (1.0 - sigmoid_z))
     flipped[...] = grad_pre.T.astype(BF16)
+
+
+def activate_kernel(mixed, kept, received, activated, total):
+    activated[...] = (mixed[...] * jax.nn.sigmoid(mixed[...])).astype(BF16)
+    total[...] = (kept[...] + received[...].astype(F32)).astype(BF16)
+
+
+def scale_kernel(scale, mine, other, out):
+    half = mine.shape[0]
+    core = lax.axis_index("row") % 2
+    out[part(core, half), :] = mine[...].astype(F32) * scale
+    out[part(1 - core, half), :] = other[...].astype(F32) * scale
+
+
+def nodes_kernel(w_ref, *refs):
+    refs, out = refs[:-1], refs[-1]
+    total = refs[0][...]
+    for ref in refs[1:]:
+        total = total + ref[...].astype(F32)
+    out[...] = lax.dot_general(
+        total.T.astype(BF16), w_ref[...], (((1,), (1,)), ((), ())), preferred_element_type=F32
+    ).astype(BF16)
 
 
 def weight_kernel(x_ref, g_ref, kept, given):
@@ -203,12 +224,12 @@
         out[...] = product.astype(out.dtype)
 
 
-def panel_kernel(*refs):
+def panel_kernel(offsets, *refs):
     pieces, out = refs[:-1], refs[-1]
     span = pieces[0].shape[1]
     c = lax.axis_index("col")
-    for s, piece in enumerate(pieces):
-        out[:, part(c ^ s, span)] = piece[: out.shape[0], :]
+    for s, piece in zip(offsets, pieces, strict=True):
+        out[:, part(c ^ s, span)] = piece[...]
 
 
 def transposed_kernel(offsets, a_ref, g_ref, _, given, kept):
@@ -239,7 +260,7 @@
         received = swap(send, "col", bit)
         count = keep.shape[0]
         if count == 1:
-            return keep, received
+            return keep, received, send
         bit *= 2
         keep, send = call(
             halve_kernel,
@@ -256,39 +277,40 @@
     panel, columns = adjacency.shape
     row_count = panel // BLK
     chips = list(range(0, n_row, 2))
+    offsets = column_offsets(n_col)
+
+    pulls = jnp.stack([pull_owner[:, 0], pull_slot, pull_target])
+    their_pulls = swap(pulls, "row", 1)
+    tiles = swap(hist_tiles, "row", 1)
 
     beside = swap(nodes, "row", 1)
     near = [swap(nodes, "row", t) for t in chips[:0:-1]][::-1]
     (history,) = call(later_kernel, [shape(*history.shape)], [history, beside])
-    (stacked,) = call(stack_kernel, [shape(len(near), span, hid)], [*near, history])
+    (stacked,) = call(stack_kernel, [shape(len(near), span, hid)], [*near, history, tiles])
     across = swap(stacked, "row", 1)
+
+    blocks = [shape(n_col // 2, span, hid, dtype=F32), shape(n_col // 2, span, hid)]
+    keep, send = call(
+        functools.partial(aggregate_kernel, n_row, n_col),
+        blocks,
+        [adjacency, nodes, beside, stacked, across],
+        [shape(columns, hid)],
+    )
+    keep, received, halved = reduce_columns(keep, send, span, hid)
+    projected, summed = call(
+        project_kernel, [shape(span, hid, dtype=F32), shape(hid, span)], [keep, received, weight]
+    )
 
     blocks_held = history.shape[0] // BLK
     places = len(chips) * CAP
     which, code, which2, code2 = pl.pallas_call(
         functools.partial(lists_kernel, blocks_held, row_count),
         out_shape=[shape(places, dtype=jnp.int32)] * 4,
-        in_specs=[SCALARS] * 3 + [WHOLE],
+        in_specs=[SCALARS] * 2 + [WHOLE],
         out_specs=[SCALARS] * 4,
         scratch_shapes=[pltpu.SMEM((n_row,), jnp.int32)],
         compiler_params=pltpu.CompilerParams(vmem_limit_bytes=4 << 20),
-    )(pull_owner.T, pull_slot, pull_target, history)
-    (tiles,) = call(tiles_kernel, [shape(places, BLK, BLK)], [hist_tiles], lists=[which2])
-    tiles = swap(tiles, "row", 1)
-    code2 = swap(code2, "row", 1)
-
-    blocks = [shape(n_col // 2, span, hid, dtype=F32), shape(n_col // 2, span, hid)]
-    keep, send = call(
-        functools.partial(aggregate_kernel, n_row, n_col),
-        blocks,
-        [adjacency, nodes, beside, stacked, across, tiles],
-        [shape(columns, hid)],
-        [code2],
-    )
-    keep, received = reduce_columns(keep, send, span, hid)
-    projected, summed = call(
-        project_kernel, [shape(span, hid, dtype=F32), shape(hid, span)], [keep, received, weight]
-    )
+    )(pulls, their_pulls, halved)
 
     past = [history] + [swap(history, "row", t) for t in chips[1:]]
     early = [i for i, t in enumerate(chips) if t & (t - 1) == 0]
@@ -299,14 +321,14 @@
         functools.partial(early_kernel, early, blocks_held),
         [spare, spare],
         [projected, hist_tiles, tiles, *[past[i] for i in early]],
-        lists=[which, code, code2],
+        lists=[which, code, which2, code2],
     )
     (given,) = call(
         functools.partial(others_kernel, late, blocks_held),
         [shape(panel, hid)],
         [terms, tiles, *[past[i] for i in late]],
         [spare],
-        [code2],
+        [which2, code2],
     )
     received = swap(given, "row", 1)
     (terms,) = call(
@@ -320,20 +342,26 @@
         [shape(span, hid, dtype=BF16 if s else F32) for s in range(n_col)],
         [terms, received],
     )
-    activated, flipped = call(
-        activate_kernel,
-        [shape(span, hid), shape(hid, span)],
-        [cotangent, keep, *[swap(send, "col", s) for s, send in enumerate(sends, 1)]],
-    )
-
-    pieces = [swap(flipped, "col", s) if s else flipped for s in range(n_col)]
+    mixed, flipped = call(
+        gradient_kernel,
+        [shape(span, hid, dtype=F32), shape(hid, span)],
+        [cotangent, keep, *[swap(sends[s - 1], "col", s) for s in offsets]],
+    )
+
+    pieces = [swap(flipped, "col", s) if s else flipped for s in [*offsets, 0]]
     kept, given = call(
         weight_kernel,
         [shape(hid // 2, hid, dtype=F32), shape(hid // 2, hid)],
         [summed, flipped],
     )
-    kept = (kept + swap(given, "row", 1).astype(F32)).astype(BF16)
-    gradients = call(panel_kernel, [shape(hid, panel)], pieces)[0]
+    activated, kept = call(
+        activate_kernel,
+        [shape(span, hid), shape(hid // 2, hid)],
+        [mixed, kept, swap(given, "row", 1)],
+    )
+    gradients = call(
+        functools.partial(panel_kernel, [*offsets, 0]), [shape(hid, panel)], pieces
+    )[0]
     (halfway,) = call(
         tree_kernel,
         [shape(hid // 2, hid)],
@@ -347,7 +375,7 @@
     )
     received = swap(given, "row", 1)
     arrived, token = {}, given
-    for places in (list(range(2, len(chips))), [0, 1]):
+    for places in (list(range(1, len(chips))), [0]):
         sums = call(
             functools.partial(cores_kernel, places),
             [shape(hid, span, dtype=BF16 if i else F32) for i in places],
@@ -359,22 +387,19 @@
             beside = swap(halfway, "col", 1)
             (token,) = call(add_kernel, [shape(*halfway.shape)], [halfway, beside, sums[0]])
     halfway = token
-    total = arrived[0]
-    for i in range(1, len(chips)):
-        total = total + arrived[i].astype(F32)
-    grad_proj = total.astype(BF16)
-    grad_nodes = lax.dot_general(
-        grad_proj, weight, (((0,), (1,)), ((), ())), preferred_element_type=F32
-    ).astype(BF16)
+    (grad_nodes,) = call(
+        nodes_kernel, [shape(span, hid)], [weight, *[arrived[i] for i in range(len(chips))]]
+    )
 
     for bit in [1 << b for b in range(1, n_col.bit_length() - 1)]:
         received = swap(halfway, "col", bit)
         (halfway,) = call(add_kernel, [shape(*halfway.shape)], [halfway, received, arrived[len(chips) - 1]])
-    other = swap(halfway, "row", 1)
-    even = lax.axis_index("row") % 2 == 0
-    grad_weight = jnp.concatenate(
-        [jnp.where(even, halfway, other), jnp.where(even, other, halfway)], axis=0
-    ).astype(F32) * (1.0 / math.sqrt(span * n_row * n_col))
+    scale = 1.0 / math.sqrt(span * n_row * n_col)
+    (grad_weight,) = call(
+        functools.partial(scale_kernel, scale),
+        [shape(hid, hid, dtype=F32)],
+        [halfway, swap(halfway, "row", 1)],
+    )
     return (activated, grad_nodes, grad_weight)
 
 

time: 91.3 us -> 85.7 us (0.939)
  starting transfers between devices: 39.7 us -> 31.3 us
  waiting for transfers between devices: 33.8 us -> 38.7 us
  local copies, waits for them, and re-layouts: 4.58 us -> 3.27 us
  Pallas kernels: 10.3 us -> 11.3 us
    ppermute x30, starting transfers between devices: 39.7 us -> 31.3 us  [swap(): return lax.ppermute(x, axis, [(i, i ^ offset) for i in range(size)])]
    ppermute x30, waiting for transfers between devices: 33.8 us -> 38.7 us  [swap(): return lax.ppermute(x, axis, [(i, i ^ offset) for i in range(size)])]
    unnamed x20, local copies, waits for them, and re-layouts: 4.58 us -> 3.27 us
    pallas_call x19 -> x21, Pallas kernels: 8.37 us -> 8.91 us  [call(): pl.pallas_call(kernel, out_shape=outs, in_specs=[SCALARS] * len(lists) +...]
  transfers between devices with their start and end apart: 30 -> 30, of which waited for: 12 -> 18; matrix products, arithmetic and copies ran while one was open for 1% -> 0% of each run, Pallas kernels for 8% -> 9%
where the time goes in v4:
time: 85.7 us; the launch traced here: 85.5 us
  waiting for transfers between devices  38.7 us (45%)
  starting transfers between devices  31.3 us (37%)
  Pallas kernels  11.3 us (13%)
  local copies, waits for them, and re-layouts  3.27 us (4%)
  between operations  0.94 us (1%)
    ppermute x30, waiting for transfers between devices, swap(): return lax.ppermute(x, axis, [(i, i ^ offset) for i in range(size)])  38.7 us
    ppermute x30, starting transfers between devices, swap(): return lax.ppermute(x, axis, [(i, i ^ offset) for i in range(size)])  31.3 us
    pallas_call x21, Pallas kernels, call(): pl.pallas_call(kernel, out_shape=outs, in_specs=[SCALARS] * len(lists) +...  8.91 us
    unnamed x20, local copies, waits for them, and re-layouts  3.27 us
    pallas_call x1, Pallas kernels, local(): pl.pallas_call(functools.partial(lists_kernel, blocks_held, row_count), o...  2.38 us
  transfers between devices with their start and end apart: 30, of which 18 were waited for; matrix products, arithmetic and copies ran while one was open for 0% of the time, Pallas kernels for 9%

profile of v4, /device:TPU:0, one launch (start us, length us, event | category | flops | bytes accessed | tf_op | source)
XLA Modules:
  0.0 85.5 jit_solution(16113074344538454876)
XLA Ops:
  0.6 0.5 collective-permute-start.5
  1.1 0.1 collective-permute-start.1
  1.2 2.9 %collective-permute-start.2 = (bf16[256,256]{1,0:T(8,128)(2,1)}, bf16[256,256]{1,0:T(8,128)(2,1)S(1)}, u32[]{:S(2)}, u32[]{:S(2)}) collective-permute-start(bf16[256,256]{1,0:T(8,128)(2,1)} %own.1), channel_id=1, source_target_pairs={{0,8},{4,12},{8,0},{12,4},{16,24},{20,28},{24,16},{28,20},{1,9},{5... | collective-permute-start | bytes 393224 | tf_op jit(solution)/shard_map/ppermute | solution.py:21
  4.1 1.5 %collective-permute-start.3 = (bf16[256,256]{1,0:T(8,128)(2,1)}, bf16[256,256]{1,0:T(8,128)(2,1)S(1)}, u32[]{:S(2)}, u32[]{:S(2)}) collective-permute-start(bf16[256,256]{1,0:T(8,128)(2,1)} %own.1), channel_id=1, source_target_pairs={{0,16},{4,20},{8,24},{12,28},{16,0},{20,4},{24,8},{28,12},{1,17},{... | collective-permute-start | bytes 393224 | tf_op jit(solution)/shard_map/ppermute | solution.py:21
  5.7 1.0 %copy-done.3 = bf16[1024,256]{1,0:T(8,128)(2,1)S(1)} copy-done((bf16[1024,256]{1,0:T(8,128)(2,1)S(1)}, bf16[1024,256]{1,0:T(8,128)(2,1)}, u32[]{:S(2)}) %copy-start.3) | copy-done | bytes 524312
  6.8 1.6 %collective-permute-done.2.refs_0_ = bf16[256,256]{1,0:T(8,128)(2,1)S(1)} collective-permute-done((bf16[256,256]{1,0:T(8,128)(2,1)}, bf16[256,256]{1,0:T(8,128)(2,1)S(1)}, u32[]{:S(2)}, u32[]{:S(2)}) %collective-permute-start.2) | collective-permute-done | bytes 131104 | tf_op jit(solution)/shard_map/ppermute | solution.py:21
  8.3 4.0 %collective-permute-done.3.refs_1_ = bf16[256,256]{1,0:T(8,128)(2,1)S(1)} collective-permute-done((bf16[256,256]{1,0:T(8,128)(2,1)}, bf16[256,256]{1,0:T(8,128)(2,1)S(1)}, u32[]{:S(2)}, u32[]{:S(2)}) %collective-permute-start.3) | collective-permute-done | bytes 131104 | tf_op jit(solution)/shard_map/ppermute | solution.py:21
  12.4 0.0 copy-start.8
  12.5 0.1 collective-permute-start.6
  12.5 1.6 %collective-permute-start.10 = (bf16[1024,256]{1,0:T(8,128)(2,1)S(1)}, bf16[1024,256]{1,0:T(8,128)(2,1)S(1)}, u32[]{:S(2)}, u32[]{:S(2)}) collective-permute-start(bf16[1024,256]{1,0:T(8,128)(2,1)S(1)} %shard_map.112.refs_3_.refs_0_), channel_id=1, source_target_pairs={{0,16},{4,20},{8,24},{12,28},{16,0},{20,4},{24,8},{28,12},{1,17},{... | collective-permute-start | bytes 1572872 | tf_op jit(solution)/shard_map/ppermute | solution.py:21
  14.1 0.5 collective-permute-start.9
  14.7 1.4 %collective-permute-start.11 = (bf16[1024,256]{1,0:T(8,128)(2,1)S(1)}, bf16[1024,256]{1,0:T(8,128)(2,1)S(1)}, u32[]{:S(2)}, u32[]{:S(2)}) collective-permute-start(bf16[1024,256]{1,0:T(8,128)(2,1)S(1)} %shard_map.112.refs_3_.refs_0_), channel_id=1, source_target_pairs={{0,24},{4,28},{8,16},{12,20},{16,8},{20,12},{24,0},{28,4},{1,25},{... | collective-permute-start | bytes 1572872 | tf_op jit(solution)/shard_map/ppermute | solution.py:21
  16.1 2.2 %copy-done = bf16[1024,2048]{1,0:T(8,128)(2,1)S(1)} copy-done((bf16[1024,2048]{1,0:T(8,128)(2,1)S(1)}, bf16[1024,2048]{1,0:T(8,128)(2,1)}, u32[]{:S(2)}) %copy-start) | copy-done | bytes 4194328
  18.3 1.3 %shard_map.114 = (f32[2,256,256]{2,1,0:T(8,128)S(1)}, bf16[2,256,256]{2,1,0:T(8,128)(2,1)S(1)}) custom-call(bf16[1024,2048]{1,0:T(8,128)(2,1)S(1)} %copy-done, bf16[256,256]{1,0:T(8,128)(2,1)S(1)} %copy-done.5, bf16[256,256]{1,0:T(8,128)(2,1)S(1)} %collective-permute-done.1._.other, bf16[3,256,256]{2,1,0:T(8,128)(2,1)S(1)} %shard_map.113.near, ...), custom_call_target="tpu_custom_call" | custom-call | tf_op jit(solution)/shard_map/pallas_call | solution.py:39
  19.6 1.6 %collective-permute-start.7 = (bf16[2,256,256]{2,1,0:T(8,128)(2,1)S(1)}, bf16[2,256,256]{2,1,0:T(8,128)(2,1)S(1)}, u32[]{:S(2)}, u32[]{:S(2)}) collective-permute-start(bf16[2,256,256]{2,1,0:T(8,128)(2,1)S(1)} %get-tuple-element.31), channel_id=1, source_target_pairs={{0,1},{1,0},{2,3},{3,2},{4,5},{5,4},{6,7},{7,6},{8,9},{9,8},{10,11... | collective-permute-start | bytes 786440 | tf_op jit(solution)/shard_map/ppermute | solution.py:21
  21.3 6.2 %collective-permute-done.7.received = bf16[2,256,256]{2,1,0:T(8,128)(2,1)S(1)} collective-permute-done((bf16[2,256,256]{2,1,0:T(8,128)(2,1)S(1)}, bf16[2,256,256]{2,1,0:T(8,128)(2,1)S(1)}, u32[]{:S(2)}, u32[]{:S(2)}) %collective-permute-start.7) | collective-permute-done | bytes 262176 | tf_op jit(solution)/shard_map/ppermute | solution.py:21
  27.6 2.7 %collective-permute-start.8 = (bf16[1,256,256]{2,1,0:T(8,128)(2,1)S(1)}, bf16[1,256,256]{2,1,0:T(8,128)(2,1)S(1)}, u32[]{:S(2)}, u32[]{:S(2)}) collective-permute-start(bf16[1,256,256]{2,1,0:T(8,128)(2,1)S(1)} %get-tuple-element.32._), channel_id=1, source_target_pairs={{0,2},{1,3},{2,0},{3,1},{4,6},{5,7},{6,4},{7,5},{8,10},{9,11},{10,... | collective-permute-start | bytes 393224 | tf_op jit(solution)/shard_map/ppermute | solution.py:21
  30.2 0.1 collective-permute-start
  30.3 1.1 %collective-permute-done.theirs = s32[3,32]{1,0:T(4,128)S(1)} collective-permute-done((s32[3,32]{1,0:T(4,128)S(1)}, s32[3,32]{1,0:T(4,128)S(1)}, u32[]{:S(2)}, u32[]{:S(2)}) %collective-permute-start) | collective-permute-done | bytes 416 | tf_op jit(solution)/shard_map/ppermute | solution.py:21
  31.5 2.4 %shard_map.116 = (s32[16]{0:T(128)S(1)}, s32[16]{0:T(128)S(1)}, s32[16]{0:T(128)S(1)}, s32[16]{0:T(128)S(1)}) custom-call(s32[3,32]{1,0:T(4,128)S(1)} %pad_add_fusion.mine, s32[3,32]{1,0:T(4,128)S(1)} %collective-permute-done.theirs, bf16[1,256,256]{2,1,0:T(8,128)(2,1)S(1)} %get-tuple-element.32._), custom_call_target="tpu_custom_call" | custom-call | tf_op jit(solution)/shard_map/pallas_call | solution.py:306
  33.8 1.6 %collective-permute-done.8.received = bf16[1,256,256]{2,1,0:T(8,128)(2,1)S(1)} collective-permute-done((bf16[1,256,256]{2,1,0:T(8,128)(2,1)S(1)}, bf16[1,256,256]{2,1,0:T(8,128)(2,1)S(1)}, u32[]{:S(2)}, u32[]{:S(2)}) %collective-permute-start.8) | collective-permute-done | bytes 131104 | tf_op jit(solution)/shard_map/ppermute | solution.py:21
  35.4 0.2 shard_map.117
  35.7 1.2 %shard_map.118 = (f32[1152,256]{1,0:T(8,128)S(1)}, f32[1152,256]{1,0:T(8,128)S(1)}) custom-call(s32[16]{0:T(128)S(1)} %get-tuple-element.33.which, s32[16]{0:T(128)S(1)} %get-tuple-element.34.code, s32[16]{0:T(128)S(1)} %get-tuple-element.35.which2.which, s32[16]{0:T(128)S(1)} %get-tuple-element.36.code2.code, f32[256,256]{1,0:T(8,128)S(1)} %get-tuple-element.38.projected, ...), custom_call_target="tpu_custom_call" | custom-call | tf_op jit(solution)/shard_map/pallas_call | solution.py:39
  36.9 2.3 %collective-permute-done.11.refs_0_ = bf16[1024,256]{1,0:T(8,128)(2,1)S(1)} collective-permute-done((bf16[1024,256]{1,0:T(8,128)(2,1)S(1)}, bf16[1024,256]{1,0:T(8,128)(2,1)S(1)}, u32[]{:S(2)}, u32[]{:S(2)}) %collective-permute-start.11) | collective-permute-done | bytes 524320 | tf_op jit(solution)/shard_map/ppermute | solution.py:21
  39.3 0.8 shard_map.120
  40.1 0.1 collective-permute-start.12
  40.2 0.8 shard_map.119.own
  41.0 1.1 %collective-permute-done.12.received = bf16[1024,256]{1,0:T(8,128)(2,1)S(1)} collective-permute-done((bf16[1024,256]{1,0:T(8,128)(2,1)S(1)}, bf16[1024,256]{1,0:T(8,128)(2,1)S(1)}, u32[]{:S(2)}, u32[]{:S(2)}) %collective-permute-start.12) | collective-permute-done | bytes 524320 | tf_op jit(solution)/shard_map/ppermute | solution.py:21
  42.1 0.1 shard_map.121
  42.2 3.7 %collective-permute-start.13 = (bf16[256,256]{1,0:T(8,128)(2,1)S(1)}, bf16[256,256]{1,0:T(8,128)(2,1)S(1)}, u32[]{:S(2)}, u32[]{:S(2)}) collective-permute-start(bf16[256,256]{1,0:T(8,128)(2,1)S(1)} %get-tuple-element.42), channel_id=1, source_target_pairs={{0,3},{1,2},{2,1},{3,0},{4,7},{5,6},{6,5},{7,4},{8,11},{9,10},{10,... | collective-permute-start | bytes 393224 | tf_op jit(solution)/shard_map/ppermute | solution.py:21
  45.9 0.8 collective-permute-start.15
  46.7 3.8 %collective-permute-done.13.refs_0_ = bf16[256,256]{1,0:T(8,128)(2,1)S(1)} collective-permute-done((bf16[256,256]{1,0:T(8,128)(2,1)S(1)}, bf16[256,256]{1,0:T(8,128)(2,1)S(1)}, u32[]{:S(2)}, u32[]{:S(2)}) %collective-permute-start.13) | collective-permute-done | bytes 131104 | tf_op jit(solution)/shard_map/ppermute | solution.py:21
  50.4 3.1 %collective-permute-done.14.refs_1_ = bf16[256,256]{1,0:T(8,128)(2,1)S(1)} collective-permute-done((bf16[256,256]{1,0:T(8,128)(2,1)S(1)}, bf16[256,256]{1,0:T(8,128)(2,1)S(1)}, u32[]{:S(2)}, u32[]{:S(2)}) %collective-permute-start.14) | collective-permute-done | bytes 131104 | tf_op jit(solution)/shard_map/ppermute | solution.py:21
  53.6 3.7 %collective-permute-done.15.refs_2_ = bf16[256,256]{1,0:T(8,128)(2,1)S(1)} collective-permute-done((bf16[256,256]{1,0:T(8,128)(2,1)S(1)}, bf16[256,256]{1,0:T(8,128)(2,1)S(1)}, u32[]{:S(2)}, u32[]{:S(2)}) %collective-permute-start.15) | collective-permute-done | bytes 131104 | tf_op jit(solution)/shard_map/ppermute | solution.py:21
  57.2 0.2 shard_map.122
  57.5 2.5 %collective-permute-start.17 = (bf16[256,256]{1,0:T(8,128)(2,1)S(1)}, bf16[256,256]{1,0:T(8,128)(2,1)S(1)}, u32[]{:S(2)}, u32[]{:S(2)}) collective-permute-start(bf16[256,256]{1,0:T(8,128)(2,1)S(1)} %get-tuple-element.47.g_ref.refs_3_), channel_id=1, source_target_pairs={{0,3},{1,2},{2,1},{3,0},{4,7},{5,6},{6,5},{7,4},{8,11},{9,10},{10,... | collective-permute-start | bytes 393224 | tf_op jit(solution)/shard_map/ppermute | solution.py:21
  60.0 0.2 shard_map.123
  60.2 0.1 collective-permute-start.16
  60.3 0.1 collective-permute-start.18
  60.4 1.9 %collective-permute-start.19 = (bf16[256,256]{1,0:T(8,128)(2,1)S(1)}, bf16[256,256]{1,0:T(8,128)(2,1)S(1)}, u32[]{:S(2)}, u32[]{:S(2)}) collective-permute-start(bf16[256,256]{1,0:T(8,128)(2,1)S(1)} %get-tuple-element.47.g_ref.refs_3_), channel_id=1, source_target_pairs={{0,2},{1,3},{2,0},{3,1},{4,6},{5,7},{6,4},{7,5},{8,10},{9,11},{10,... | collective-permute-start | bytes 393224 | tf_op jit(solution)/shard_map/ppermute | solution.py:21
  62.3 0.7 shard_map.124
  63.0 1.2 %collective-permute-start.20 = (bf16[128,256]{1,0:T(8,128)(2,1)S(1)}, bf16[128,256]{1,0:T(8,128)(2,1)S(1)}, u32[]{:S(2)}, u32[]{:S(2)}) collective-permute-start(bf16[128,256]{1,0:T(8,128)(2,1)S(1)} %get-tuple-element.51.refs_0_), channel_id=1, source_target_pairs={{0,8},{4,12},{8,0},{12,4},{16,24},{20,28},{24,16},{28,20},{1,9},{5... | collective-permute-start | bytes 196616 | tf_op jit(solution)/shard_map/ppermute | solution.py:21
  64.2 0.8 collective-permute-start.21
  65.0 0.6 collective-permute-done.17.refs_0_
  65.6 1.5 %collective-permute-start.22 = (bf16[128,256]{1,0:T(8,128)(2,1)S(1)}, bf16[128,256]{1,0:T(8,128)(2,1)S(1)}, u32[]{:S(2)}, u32[]{:S(2)}) collective-permute-start(bf16[128,256]{1,0:T(8,128)(2,1)S(1)} %get-tuple-element.51.refs_0_), channel_id=1, source_target_pairs={{0,24},{4,28},{8,16},{12,20},{16,8},{20,12},{24,0},{28,4},{1,25},{... | collective-permute-start | bytes 196616 | tf_op jit(solution)/shard_map/ppermute | solution.py:21
  67.1 2.3 %collective-permute-done.18.refs_1_ = bf16[256,256]{1,0:T(8,128)(2,1)S(1)} collective-permute-done((bf16[256,256]{1,0:T(8,128)(2,1)S(1)}, bf16[256,256]{1,0:T(8,128)(2,1)S(1)}, u32[]{:S(2)}, u32[]{:S(2)}) %collective-permute-start.18) | collective-permute-done | bytes 131104 | tf_op jit(solution)/shard_map/ppermute | solution.py:21
  69.4 1.2 %collective-permute-done.19.refs_2_ = bf16[256,256]{1,0:T(8,128)(2,1)S(1)} collective-permute-done((bf16[256,256]{1,0:T(8,128)(2,1)S(1)}, bf16[256,256]{1,0:T(8,128)(2,1)S(1)}, u32[]{:S(2)}, u32[]{:S(2)}) %collective-permute-start.19) | collective-permute-done | bytes 131104 | tf_op jit(solution)/shard_map/ppermute | solution.py:21
  70.6 0.1 shard_map.125.refs_4_.g_ref
  70.7 0.1 collective-permute-done.22.refs_3_
  70.8 1.3 %shard_map.127 = (bf16[4,256,256]{2,1,0:T(8,128)(2,1)S(1)}, f32[4,256,256]{2,1,0:T(8,128)S(1)}) custom-call(bf16[1024,2048]{1,0:T(8,128)(2,1)S(1)} %copy-done.1, bf16[256,1024]{1,0:T(8,128)(2,1)S(1)} %shard_map.125.refs_4_.g_ref, bf16[128,256]{1,0:T(8,128)(2,1)S(1)} %shard_map.126._.x_ref), custom_call_target="tpu_custom_call" | custom-call | tf_op jit(solution)/shard_map/pallas_call | solution.py:39
  72.2 0.1 collective-permute-start.23
  72.2 0.1 collective-permute-start.24
  72.3 1.8 %collective-permute-done.23.received = bf16[4,256,256]{2,1,0:T(8,128)(2,1)S(1)} collective-permute-done((bf16[4,256,256]{2,1,0:T(8,128)(2,1)S(1)}, bf16[4,256,256]{2,1,0:T(8,128)(2,1)S(1)}, u32[]{:S(2)}, u32[]{:S(2)}) %collective-permute-start.23) | collective-permute-done | bytes 524320 | tf_op jit(solution)/shard_map/ppermute | solution.py:21
  74.1 0.1 shard_map.128
  74.2 1.6 %collective-permute-start.27 = (bf16[256,256]{1,0:T(8,128)(2,1)S(1)}, bf16[256,256]{1,0:T(8,128)(2,1)S(1)}, u32[]{:S(2)}, u32[]{:S(2)}) collective-permute-start(bf16[256,256]{1,0:T(8,128)(2,1)S(1)} %get-tuple-element.56), channel_id=1, source_target_pairs={{0,24},{4,28},{8,16},{12,20},{16,8},{20,12},{24,0},{28,4},{1,25},{... | collective-permute-start | bytes 393224 | tf_op jit(solution)/shard_map/ppermute | solution.py:21
  75.8 1.5 %collective-permute-start.25 = (bf16[256,256]{1,0:T(8,128)(2,1)S(1)}, bf16[256,256]{1,0:T(8,128)(2,1)S(1)}, u32[]{:S(2)}, u32[]{:S(2)}) collective-permute-start(bf16[256,256]{1,0:T(8,128)(2,1)S(1)} %get-tuple-element.54._), channel_id=1, source_target_pairs={{0,8},{4,12},{8,0},{12,4},{16,24},{20,28},{24,16},{28,20},{1,9},{5... | collective-permute-start | bytes 393224 | tf_op jit(solution)/shard_map/ppermute | solution.py:21
  77.3 1.3 %collective-permute-start.28 = (bf16[128,256]{1,0:T(8,128)(2,1)S(1)}, bf16[128,256]{1,0:T(8,128)(2,1)S(1)}, u32[]{:S(2)}, u32[]{:S(2)}) collective-permute-start(bf16[128,256]{1,0:T(8,128)(2,1)S(1)} %shard_map.129._.x_ref), channel_id=1, source_target_pairs={{0,2},{1,3},{2,0},{3,1},{4,6},{5,7},{6,4},{7,5},{8,10},{9,11},{10,... | collective-permute-start | bytes 196616 | tf_op jit(solution)/shard_map/ppermute | solution.py:21
  78.6 1.1 %collective-permute-start.26 = (bf16[256,256]{1,0:T(8,128)(2,1)S(1)}, bf16[256,256]{1,0:T(8,128)(2,1)S(1)}, u32[]{:S(2)}, u32[]{:S(2)}) collective-permute-start(bf16[256,256]{1,0:T(8,128)(2,1)S(1)} %get-tuple-element.55), channel_id=1, source_target_pairs={{0,16},{4,20},{8,24},{12,28},{16,0},{20,4},{24,8},{28,12},{1,17},{... | collective-permute-start | bytes 393224 | tf_op jit(solution)/shard_map/ppermute | solution.py:21
  79.6 3.4 %collective-permute-done.28.y_ref = bf16[128,256]{1,0:T(8,128)(2,1)S(1)} collective-permute-done((bf16[128,256]{1,0:T(8,128)(2,1)S(1)}, bf16[128,256]{1,0:T(8,128)(2,1)S(1)}, u32[]{:S(2)}, u32[]{:S(2)}) %collective-permute-start.28) | collective-permute-done | bytes 65568 | tf_op jit(solution)/shard_map/ppermute | solution.py:21
  83.1 0.1 collective-permute-start.29
  83.2 0.4 collective-permute-done.25.refs_1_
  83.6 0.2 collective-permute-done.26.refs_2_
  83.8 0.9 %shard_map.131 = bf16[256,256]{1,0:T(8,128)(2,1)} custom-call(bf16[256,256]{1,0:T(8,128)(2,1)S(1)} %copy-done.4, f32[256,256]{1,0:T(8,128)S(1)} %shard_map.130.refs_0_, bf16[256,256]{1,0:T(8,128)(2,1)S(1)} %collective-permute-done.25.refs_1_, bf16[256,256]{1,0:T(8,128)(2,1)S(1)} %collective-permute-done.26.refs_2_, ...), custom_call_target="tpu_custom_call" | custom-call | tf_op jit(solution)/shard_map/pallas_call | solution.py:39
  84.7 0.7 shard_map.133
  (39 shorter events, 0.3 us)
Async XLA Ops:
  0.6 11.7 %collective-permute-start.5 = (bf16[32,128,128]{2,1,0:T(8,128)(2,1)}, bf16[32,128,128]{2,1,0:T(8,128)(2,1)S(1)}, u32[]{:S(2)}, u32[]{:S(2)}) collective-permute-start(bf16[32,128,128]{2,1,0:T(8,128)(2,1)} %tiles.3), channel_id=1, source_target_pairs={{0,4},{4,0},{8,12},{12,8},{16,20},{20,16},{24,28},{28,24},{1,5},{5... | collective-permute-start | bytes 3145736 | tf_op jit(solution)/shard_map/ppermute | solution.py:21
  1.1 4.5 %collective-permute-start.1 = (bf16[256,256]{1,0:T(8,128)(2,1)}, bf16[256,256]{1,0:T(8,128)(2,1)S(1)}, u32[]{:S(2)}, u32[]{:S(2)}) collective-permute-start(bf16[256,256]{1,0:T(8,128)(2,1)} %own.1), channel_id=1, source_target_pairs={{0,4},{4,0},{8,12},{12,8},{16,20},{20,16},{24,28},{28,24},{1,5},{5... | collective-permute-start | bytes 393224 | tf_op jit(solution)/shard_map/ppermute | solution.py:21
  1.2 7.1 %collective-permute-start.2 = (bf16[256,256]{1,0:T(8,128)(2,1)}, bf16[256,256]{1,0:T(8,128)(2,1)S(1)}, u32[]{:S(2)}, u32[]{:S(2)}) collective-permute-start(bf16[256,256]{1,0:T(8,128)(2,1)} %own.1), channel_id=1, source_target_pairs={{0,8},{4,12},{8,0},{12,4},{16,24},{20,28},{24,16},{28,20},{1,9},{5... | collective-permute-start | bytes 393224 | tf_op jit(solution)/shard_map/ppermute | solution.py:21
  4.1 8.2 %collective-permute-start.3 = (bf16[256,256]{1,0:T(8,128)(2,1)}, bf16[256,256]{1,0:T(8,128)(2,1)S(1)}, u32[]{:S(2)}, u32[]{:S(2)}) collective-permute-start(bf16[256,256]{1,0:T(8,128)(2,1)} %own.1), channel_id=1, source_target_pairs={{0,16},{4,20},{8,24},{12,28},{16,0},{20,4},{24,8},{28,12},{1,17},{... | collective-permute-start | bytes 393224 | tf_op jit(solution)/shard_map/ppermute | solution.py:21
  5.7 6.7 %collective-permute-start.4 = (bf16[256,256]{1,0:T(8,128)(2,1)}, bf16[256,256]{1,0:T(8,128)(2,1)S(1)}, u32[]{:S(2)}, u32[]{:S(2)}) collective-permute-start(bf16[256,256]{1,0:T(8,128)(2,1)} %own.1), channel_id=1, source_target_pairs={{0,24},{4,28},{8,16},{12,20},{16,8},{20,12},{24,0},{28,4},{1,25},{... | collective-permute-start | bytes 393224 | tf_op jit(solution)/shard_map/ppermute | solution.py:21
  5.7 1.0 %copy-start.3 = (bf16[1024,256]{1,0:T(8,128)(2,1)S(1)}, bf16[1024,256]{1,0:T(8,128)(2,1)}, u32[]{:S(2)}) copy-start(bf16[1024,256]{1,0:T(8,128)(2,1)} %x_ref.1) | copy-start | bytes 1572868
  6.8 9.3 %copy-start.5 = (bf16[256,256]{1,0:T(8,128)(2,1)S(1)}, bf16[256,256]{1,0:T(8,128)(2,1)}, u32[]{:S(2)}) copy-start(bf16[256,256]{1,0:T(8,128)(2,1)} %own.1) | copy-start | bytes 393220
  12.4 17.8 %copy-start.7 = (s32[32]{0:T(128)S(1)}, s32[32]{0:T(128)}, u32[]{:S(2)}) copy-start(s32[32]{0:T(128)} %param.15) | copy-start | bytes 388
  12.4 17.8 %copy-start.8 = (s32[32]{0:T(128)S(1)}, s32[32]{0:T(128)}, u32[]{:S(2)}) copy-start(s32[32]{0:T(128)} %param.14) | copy-start | bytes 388
  12.4 17.8 %copy-start.9 = (s32[32,1]{0,1:T(1,128)S(1)}, s32[32,1]{0,1:T(1,128)}, u32[]{:S(2)}) copy-start(s32[32,1]{0,1:T(1,128)} %param.13) | copy-start | bytes 388
  12.4 23.0 %copy-start.4 = (bf16[256,256]{1,0:T(8,128)(2,1)S(1)}, bf16[256,256]{1,0:T(8,128)(2,1)}, u32[]{:S(2)}) copy-start(bf16[256,256]{1,0:T(8,128)(2,1)} %w_ref.3) | copy-start | bytes 393220
  12.5 3.6 %collective-permute-start.6 = (bf16[3,256,256]{2,1,0:T(8,128)(2,1)S(1)}, bf16[3,256,256]{2,1,0:T(8,128)(2,1)S(1)}, u32[]{:S(2)}, u32[]{:S(2)}) collective-permute-start(bf16[3,256,256]{2,1,0:T(8,128)(2,1)S(1)} %shard_map.113.near), channel_id=1, source_target_pairs={{0,4},{4,0},{8,12},{12,8},{16,20},{20,16},{24,28},{28,24},{1,5},{5... | collective-permute-start | bytes 1179656 | tf_op jit(solution)/shard_map/ppermute | solution.py:21
  12.5 23.1 %collective-permute-start.10 = (bf16[1024,256]{1,0:T(8,128)(2,1)S(1)}, bf16[1024,256]{1,0:T(8,128)(2,1)S(1)}, u32[]{:S(2)}, u32[]{:S(2)}) collective-permute-start(bf16[1024,256]{1,0:T(8,128)(2,1)S(1)} %shard_map.112.refs_3_.refs_0_), channel_id=1, source_target_pairs={{0,16},{4,20},{8,24},{12,28},{16,0},{20,4},{24,8},{28,12},{1,17},{... | collective-permute-start | bytes 1572872 | tf_op jit(solution)/shard_map/ppermute | solution.py:21
  14.1 21.6 %collective-permute-start.9 = (bf16[1024,256]{1,0:T(8,128)(2,1)S(1)}, bf16[1024,256]{1,0:T(8,128)(2,1)S(1)}, u32[]{:S(2)}, u32[]{:S(2)}) collective-permute-start(bf16[1024,256]{1,0:T(8,128)(2,1)S(1)} %shard_map.112.refs_3_.refs_0_), channel_id=1, source_target_pairs={{0,8},{4,12},{8,0},{12,4},{16,24},{20,28},{24,16},{28,20},{1,9},{5... | collective-permute-start | bytes 1572872 | tf_op jit(solution)/shard_map/ppermute | solution.py:21
  14.7 24.6 %collective-permute-start.11 = (bf16[1024,256]{1,0:T(8,128)(2,1)S(1)}, bf16[1024,256]{1,0:T(8,128)(2,1)S(1)}, u32[]{:S(2)}, u32[]{:S(2)}) collective-permute-start(bf16[1024,256]{1,0:T(8,128)(2,1)S(1)} %shard_map.112.refs_3_.refs_0_), channel_id=1, source_target_pairs={{0,24},{4,28},{8,16},{12,20},{16,8},{20,12},{24,0},{28,4},{1,25},{... | collective-permute-start | bytes 1572872 | tf_op jit(solution)/shard_map/ppermute | solution.py:21
  16.1 2.2 %copy-start = (bf16[1024,2048]{1,0:T(8,128)(2,1)S(1)}, bf16[1024,2048]{1,0:T(8,128)(2,1)}, u32[]{:S(2)}) copy-start(bf16[1024,2048]{1,0:T(8,128)(2,1)} %a_ref.3) | copy-start | bytes 12582916
  19.6 16.1 %copy-start.2 = (bf16[32,128,128]{2,1,0:T(8,128)(2,1)S(1)}, bf16[32,128,128]{2,1,0:T(8,128)(2,1)}, u32[]{:S(2)}) copy-start(bf16[32,128,128]{2,1,0:T(8,128)(2,1)} %tiles.3) | copy-start | bytes 3145732
  19.6 7.9 %collective-permute-start.7 = (bf16[2,256,256]{2,1,0:T(8,128)(2,1)S(1)}, bf16[2,256,256]{2,1,0:T(8,128)(2,1)S(1)}, u32[]{:S(2)}, u32[]{:S(2)}) collective-permute-start(bf16[2,256,256]{2,1,0:T(8,128)(2,1)S(1)} %get-tuple-element.31), channel_id=1, source_target_pairs={{0,1},{1,0},{2,3},{3,2},{4,5},{5,4},{6,7},{7,6},{8,9},{9,8},{10,11... | collective-permute-start | bytes 786440 | tf_op jit(solution)/shard_map/ppermute | solution.py:21
  27.6 7.9 %collective-permute-start.8 = (bf16[1,256,256]{2,1,0:T(8,128)(2,1)S(1)}, bf16[1,256,256]{2,1,0:T(8,128)(2,1)S(1)}, u32[]{:S(2)}, u32[]{:S(2)}) collective-permute-start(bf16[1,256,256]{2,1,0:T(8,128)(2,1)S(1)} %get-tuple-element.32._), channel_id=1, source_target_pairs={{0,2},{1,3},{2,0},{3,1},{4,6},{5,7},{6,4},{7,5},{8,10},{9,11},{10,... | collective-permute-start | bytes 393224 | tf_op jit(solution)/shard_map/ppermute | solution.py:21
  30.2 1.2 %collective-permute-start = (s32[3,32]{1,0:T(4,128)S(1)}, s32[3,32]{1,0:T(4,128)S(1)}, u32[]{:S(2)}, u32[]{:S(2)}) collective-permute-start(s32[3,32]{1,0:T(4,128)S(1)} %pad_add_fusion.mine), channel_id=1, source_target_pairs={{0,4},{4,0},{8,12},{12,8},{16,20},{20,16},{24,28},{28,24},{1,5},{5... | collective-permute-start | bytes 1160 | tf_op jit(solution)/shard_map/ppermute | solution.py:21
  40.1 2.0 %collective-permute-start.12 = (bf16[1024,256]{1,0:T(8,128)(2,1)S(1)}, bf16[1024,256]{1,0:T(8,128)(2,1)S(1)}, u32[]{:S(2)}, u32[]{:S(2)}) collective-permute-start(bf16[1024,256]{1,0:T(8,128)(2,1)S(1)} %shard_map.120), channel_id=1, source_target_pairs={{0,4},{4,0},{8,12},{12,8},{16,20},{20,16},{24,28},{28,24},{1,5},{5... | collective-permute-start | bytes 1572872 | tf_op jit(solution)/shard_map/ppermute | solution.py:21
  41.0 16.2 %copy-start.6 = (bf16[256,256]{1,0:T(8,128)(2,1)S(1)}, bf16[256,256]{1,0:T(8,128)(2,1)}, u32[]{:S(2)}) copy-start(bf16[256,256]{1,0:T(8,128)(2,1)} %cotangent.1) | copy-start | bytes 393220
  42.1 28.7 %copy-start.1 = (bf16[1024,2048]{1,0:T(8,128)(2,1)S(1)}, bf16[1024,2048]{1,0:T(8,128)(2,1)}, u32[]{:S(2)}) copy-start(bf16[1024,2048]{1,0:T(8,128)(2,1)} %a_ref.3) | copy-start | bytes 12582916
  42.2 8.2 %collective-permute-start.13 = (bf16[256,256]{1,0:T(8,128)(2,1)S(1)}, bf16[256,256]{1,0:T(8,128)(2,1)S(1)}, u32[]{:S(2)}, u32[]{:S(2)}) collective-permute-start(bf16[256,256]{1,0:T(8,128)(2,1)S(1)} %get-tuple-element.42), channel_id=1, source_target_pairs={{0,3},{1,2},{2,1},{3,0},{4,7},{5,6},{6,5},{7,4},{8,11},{9,10},{10,... | collective-permute-start | bytes 393224 | tf_op jit(solution)/shard_map/ppermute | solution.py:21
  45.9 7.7 %collective-permute-start.14 = (bf16[256,256]{1,0:T(8,128)(2,1)S(1)}, bf16[256,256]{1,0:T(8,128)(2,1)S(1)}, u32[]{:S(2)}, u32[]{:S(2)}) collective-permute-start(bf16[256,256]{1,0:T(8,128)(2,1)S(1)} %get-tuple-element.43), channel_id=1, source_target_pairs={{0,1},{1,0},{2,3},{3,2},{4,5},{5,4},{6,7},{7,6},{8,9},{9,8},{10,11... | collective-permute-start | bytes 393224 | tf_op jit(solution)/shard_map/ppermute | solution.py:21
  45.9 11.4 %collective-permute-start.15 = (bf16[256,256]{1,0:T(8,128)(2,1)S(1)}, bf16[256,256]{1,0:T(8,128)(2,1)S(1)}, u32[]{:S(2)}, u32[]{:S(2)}) collective-permute-start(bf16[256,256]{1,0:T(8,128)(2,1)S(1)} %get-tuple-element.44), channel_id=1, source_target_pairs={{0,2},{1,3},{2,0},{3,1},{4,6},{5,7},{6,4},{7,5},{8,10},{9,11},{10,... | collective-permute-start | bytes 393224 | tf_op jit(solution)/shard_map/ppermute | solution.py:21
  57.5 8.2 %collective-permute-start.17 = (bf16[256,256]{1,0:T(8,128)(2,1)S(1)}, bf16[256,256]{1,0:T(8,128)(2,1)S(1)}, u32[]{:S(2)}, u32[]{:S(2)}) collective-permute-start(bf16[256,256]{1,0:T(8,128)(2,1)S(1)} %get-tuple-element.47.g_ref.refs_3_), channel_id=1, source_target_pairs={{0,3},{1,2},{2,1},{3,0},{4,7},{5,6},{6,5},{7,4},{8,11},{9,10},{10,... | collective-permute-start | bytes 393224 | tf_op jit(solution)/shard_map/ppermute | solution.py:21
  60.2 2.1 %collective-permute-start.16 = (bf16[128,256]{1,0:T(8,128)(2,1)S(1)}, bf16[128,256]{1,0:T(8,128)(2,1)S(1)}, u32[]{:S(2)}, u32[]{:S(2)}) collective-permute-start(bf16[128,256]{1,0:T(8,128)(2,1)S(1)} %get-tuple-element.49), channel_id=1, source_target_pairs={{0,4},{4,0},{8,12},{12,8},{16,20},{20,16},{24,28},{28,24},{1,5},{5... | collective-permute-start | bytes 196616 | tf_op jit(solution)/shard_map/ppermute | solution.py:21
  60.3 9.1 %collective-permute-start.18 = (bf16[256,256]{1,0:T(8,128)(2,1)S(1)}, bf16[256,256]{1,0:T(8,128)(2,1)S(1)}, u32[]{:S(2)}, u32[]{:S(2)}) collective-permute-start(bf16[256,256]{1,0:T(8,128)(2,1)S(1)} %get-tuple-element.47.g_ref.refs_3_), channel_id=1, source_target_pairs={{0,1},{1,0},{2,3},{3,2},{4,5},{5,4},{6,7},{7,6},{8,9},{9,8},{10,11... | collective-permute-start | bytes 393224 | tf_op jit(solution)/shard_map/ppermute | solution.py:21
  60.4 10.2 %collective-permute-start.19 = (bf16[256,256]{1,0:T(8,128)(2,1)S(1)}, bf16[256,256]{1,0:T(8,128)(2,1)S(1)}, u32[]{:S(2)}, u32[]{:S(2)}) collective-permute-start(bf16[256,256]{1,0:T(8,128)(2,1)S(1)} %get-tuple-element.47.g_ref.refs_3_), channel_id=1, source_target_pairs={{0,2},{1,3},{2,0},{3,1},{4,6},{5,7},{6,4},{7,5},{8,10},{9,11},{10,... | collective-permute-start | bytes 393224 | tf_op jit(solution)/shard_map/ppermute | solution.py:21
  63.0 7.7 %collective-permute-start.20 = (bf16[128,256]{1,0:T(8,128)(2,1)S(1)}, bf16[128,256]{1,0:T(8,128)(2,1)S(1)}, u32[]{:S(2)}, u32[]{:S(2)}) collective-permute-start(bf16[128,256]{1,0:T(8,128)(2,1)S(1)} %get-tuple-element.51.refs_0_), channel_id=1, source_target_pairs={{0,8},{4,12},{8,0},{12,4},{16,24},{20,28},{24,16},{28,20},{1,9},{5... | collective-permute-start | bytes 196616 | tf_op jit(solution)/shard_map/ppermute | solution.py:21
  64.2 6.5 %collective-permute-start.21 = (bf16[128,256]{1,0:T(8,128)(2,1)S(1)}, bf16[128,256]{1,0:T(8,128)(2,1)S(1)}, u32[]{:S(2)}, u32[]{:S(2)}) collective-permute-start(bf16[128,256]{1,0:T(8,128)(2,1)S(1)} %get-tuple-element.51.refs_0_), channel_id=1, source_target_pairs={{0,16},{4,20},{8,24},{12,28},{16,0},{20,4},{24,8},{28,12},{1,17},{... | collective-permute-start | bytes 196616 | tf_op jit(solution)/shard_map/ppermute | solution.py:21
  65.6 5.2 %collective-permute-start.22 = (bf16[128,256]{1,0:T(8,128)(2,1)S(1)}, bf16[128,256]{1,0:T(8,128)(2,1)S(1)}, u32[]{:S(2)}, u32[]{:S(2)}) collective-permute-start(bf16[128,256]{1,0:T(8,128)(2,1)S(1)} %get-tuple-element.51.refs_0_), channel_id=1, source_target_pairs={{0,24},{4,28},{8,16},{12,20},{16,8},{20,12},{24,0},{28,4},{1,25},{... | collective-permute-start | bytes 196616 | tf_op jit(solution)/shard_map/ppermute | solution.py:21
  72.2 2.0 %collective-permute-start.23 = (bf16[4,256,256]{2,1,0:T(8,128)(2,1)S(1)}, bf16[4,256,256]{2,1,0:T(8,128)(2,1)S(1)}, u32[]{:S(2)}, u32[]{:S(2)}) collective-permute-start(bf16[4,256,256]{2,1,0:T(8,128)(2,1)S(1)} %get-tuple-element.53._), channel_id=1, source_target_pairs={{0,4},{4,0},{8,12},{12,8},{16,20},{20,16},{24,28},{28,24},{1,5},{5... | collective-permute-start | bytes 1572872 | tf_op jit(solution)/shard_map/ppermute | solution.py:21
  72.2 5.0 %collective-permute-start.24 = (bf16[128,256]{1,0:T(8,128)(2,1)S(1)}, bf16[128,256]{1,0:T(8,128)(2,1)S(1)}, u32[]{:S(2)}, u32[]{:S(2)}) collective-permute-start(bf16[128,256]{1,0:T(8,128)(2,1)S(1)} %shard_map.126._.x_ref), channel_id=1, source_target_pairs={{0,1},{1,0},{2,3},{3,2},{4,5},{5,4},{6,7},{7,6},{8,9},{9,8},{10,11... | collective-permute-start | bytes 196616 | tf_op jit(solution)/shard_map/ppermute | solution.py:21
  74.2 8.9 %collective-permute-start.27 = (bf16[256,256]{1,0:T(8,128)(2,1)S(1)}, bf16[256,256]{1,0:T(8,128)(2,1)S(1)}, u32[]{:S(2)}, u32[]{:S(2)}) collective-permute-start(bf16[256,256]{1,0:T(8,128)(2,1)S(1)} %get-tuple-element.56), channel_id=1, source_target_pairs={{0,24},{4,28},{8,16},{12,20},{16,8},{20,12},{24,0},{28,4},{1,25},{... | collective-permute-start | bytes 393224 | tf_op jit(solution)/shard_map/ppermute | solution.py:21
  75.8 7.8 %collective-permute-start.25 = (bf16[256,256]{1,0:T(8,128)(2,1)S(1)}, bf16[256,256]{1,0:T(8,128)(2,1)S(1)}, u32[]{:S(2)}, u32[]{:S(2)}) collective-permute-start(bf16[256,256]{1,0:T(8,128)(2,1)S(1)} %get-tuple-element.54._), channel_id=1, source_target_pairs={{0,8},{4,12},{8,0},{12,4},{16,24},{20,28},{24,16},{28,20},{1,9},{5... | collective-permute-start | bytes 393224 | tf_op jit(solution)/shard_map/ppermute | solution.py:21
  77.3 5.8 %collective-permute-start.28 = (bf16[128,256]{1,0:T(8,128)(2,1)S(1)}, bf16[128,256]{1,0:T(8,128)(2,1)S(1)}, u32[]{:S(2)}, u32[]{:S(2)}) collective-permute-start(bf16[128,256]{1,0:T(8,128)(2,1)S(1)} %shard_map.129._.x_ref), channel_id=1, source_target_pairs={{0,2},{1,3},{2,0},{3,1},{4,6},{5,7},{6,4},{7,5},{8,10},{9,11},{10,... | collective-permute-start | bytes 196616 | tf_op jit(solution)/shard_map/ppermute | solution.py:21
  78.6 5.2 %collective-permute-start.26 = (bf16[256,256]{1,0:T(8,128)(2,1)S(1)}, bf16[256,256]{1,0:T(8,128)(2,1)S(1)}, u32[]{:S(2)}, u32[]{:S(2)}) collective-permute-start(bf16[256,256]{1,0:T(8,128)(2,1)S(1)} %get-tuple-element.55), channel_id=1, source_target_pairs={{0,16},{4,20},{8,24},{12,28},{16,0},{20,4},{24,8},{28,12},{1,17},{... | collective-permute-start | bytes 393224 | tf_op jit(solution)/shard_map/ppermute | solution.py:21
  83.1 1.6 %collective-permute-start.29 = (bf16[128,256]{1,0:T(8,128)(2,1)S(1)}, bf16[128,256]{1,0:T(8,128)(2,1)S(1)}, u32[]{:S(2)}, u32[]{:S(2)}) collective-permute-start(bf16[128,256]{1,0:T(8,128)(2,1)S(1)} %shard_map.132.mine), channel_id=1, source_target_pairs={{0,4},{4,0},{8,12},{12,8},{16,20},{20,16},{24,28},{28,24},{1,5},{5... | collective-permute-start | bytes 196616 | tf_op jit(solution)/shard_map/ppermute | solution.py:21

commit v5 on v4

--- a/solution.py
+++ b/solution.py
@@ -51,17 +51,24 @@
     return pl.ds(pl.multiple_of(index * size, size), size)
 
 
-def later_kernel(x_ref, _, out):
+def later_kernel(x_ref, *refs):
+    out = refs[-1]
     out[...] = x_ref[...]
 
 
-def add_kernel(x_ref, y_ref, _, out):
-    out[...] = (x_ref[...].astype(F32) + y_ref[...].astype(F32)).astype(out.dtype)
+def add_kernel(x_ref, y_ref, _, *outs):
+    rows = outs[0].shape[0]
+    for i, out in enumerate(outs):
+        at = pl.ds(i * rows, rows)
+        out[...] = (x_ref[at, :].astype(F32) + y_ref[at, :].astype(F32)).astype(out.dtype)
 
 
 def stack_kernel(*refs):
-    for i, ref in enumerate(refs[:-3]):
-        refs[-1][i] = ref[...]
+    refs, (_, low, high) = refs[:-3], refs[-3:]
+    half = low.shape[1]
+    for i, ref in enumerate(refs):
+        low[i] = ref[:half, :]
+        high[i] = ref[half:, :]
 
 
 def lists_kernel(held, spare, mine, theirs, _, which, code, which2, code2, count):
@@ -93,32 +100,31 @@
     lax.fori_loop(0, mine.shape[1], place, 0)
 
 
-def aggregate_kernel(n_row, n_col, a_ref, own, other, near, across, keep, send, x_ref):
+def aggregate_kernel(n_row, n_col, a_ref, own, other, *refs):
+    near, (low, high), outs, x_ref = refs[: -3 - n_col], refs[-3 - n_col : -1 - n_col], refs[-1 - n_col : -1], refs[-1]
     span = own.shape[0]
+    half = span // 2
     r, c = lax.axis_index("row"), lax.axis_index("col")
     x_ref[part(r, span), :] = own[...]
     x_ref[part(r ^ 1, span), :] = other[...]
-    for t in range(2, n_row):
-        x_ref[part(r ^ t, span), :] = (across if t % 2 else near)[t // 2 - 1]
-    for s in range(n_col):
+    for i, ref in enumerate(near):
+        t = 2 * (i + 1)
+        x_ref[part(r ^ t, span), :] = ref[...]
+        x_ref[part((r ^ t ^ 1) * 2, half), :] = low[i]
+        x_ref[part((r ^ t ^ 1) * 2 + 1, half), :] = high[i]
+    for s, out in enumerate(outs):
         block = jnp.dot(a_ref[part(c ^ s, span), :], x_ref[...], preferred_element_type=F32)
-        if s % 2:
-            send[s // 2] = block.astype(BF16)
-        else:
-            keep[s // 2] = block
-
-
-def halve_kernel(kept, received, keep, send):
-    for i in range(kept.shape[0]):
-        block = kept[i] + received[i].astype(F32)
-        if i % 2:
-            send[i // 2] = block.astype(BF16)
-        else:
-            keep[i // 2] = block
-
-
-def project_kernel(kept, received, w_ref, projected, flipped):
-    total = kept[0] + received[0].astype(F32)
+        out[...] = block.astype(out.dtype)
+
+
+def halve_kernel(count, *refs):
+    kept, received, outs = refs[:count], refs[count : 2 * count], refs[2 * count :]
+    for out, x, y in zip(outs, kept, received, strict=True):
+        out[...] = (x[...] + y[...].astype(F32)).astype(out.dtype)
+
+
+def project_kernel(kept, received, w_ref, _, projected, flipped):
+    total = kept[...] + received[...].astype(F32)
     high = total.astype(BF16)
     low = (total - high.astype(F32)).astype(BF16)
     projected[...] = jnp.dot(high, w_ref[...], preferred_element_type=F32) + jnp.dot(
@@ -142,18 +148,16 @@
     ]
 
 
-def early_kernel(offsets, held, which, code, which2, code2, projected, tiles, tiles2, *refs):
+def early_kernel(offsets, held, which, code, which2, code2, tiles, tiles2, *refs):
     pieces, (own, others) = refs[:-2], refs[-2:]
     pulls = pulls_of(offsets, pieces)
-    span = projected.shape[0]
     own[...] = jnp.zeros_like(own)
     others[...] = jnp.zeros_like(others)
-    own[part(lax.axis_index("col"), span), :] = projected[...]
     add_pulls(pulls, held, code2, lambda i: tiles2[which2[i]], others)
     add_pulls(pulls, held, code, lambda i: tiles[which[i]], own)
 
 
-def others_kernel(offsets, held, which, code, acc_in, tiles, *refs):
+def others_kernel(offsets, held, which, code, acc_in, tiles, _, *refs):
     pieces, (out, acc) = refs[:-2], refs[-2:]
     acc[...] = acc_in[...]
     add_pulls(pulls_of(offsets, pieces), held, code, lambda i: tiles[which[i]], acc)
@@ -166,7 +170,7 @@
     add_pulls(pulls_of(offsets, pieces), held, code, lambda i: tiles[which[i]], out)
 
 
-def merge_kernel(n_col, own, received, keep, *sends):
+def merge_kernel(n_col, projected, own, received, keep, *sends):
     span = keep.shape[0]
     c = lax.axis_index("col")
     for s in range(n_col):
@@ -175,7 +179,7 @@
         if s:
             sends[s - 1][...] = block.astype(BF16)
         else:
-            keep[...] = block
+            keep[...] = block + projected[...]
 
 
 def gradient_kernel(cotangent, kept, *refs):
@@ -194,11 +198,13 @@
     total[...] = (kept[...] + received[...].astype(F32)).astype(BF16)
 
 
-def scale_kernel(scale, mine, other, out):
-    half = mine.shape[0]
+def scale_kernel(scale, *refs):
+    refs, out = refs[:-1], refs[-1]
+    count, rows = len(refs) // 2, refs[0].shape[0]
     core = lax.axis_index("row") % 2
-    out[part(core, half), :] = mine[...].astype(F32) * scale
-    out[part(1 - core, half), :] = other[...].astype(F32) * scale
+    for i, ref in enumerate(refs):
+        at = core if i < count else 1 - core
+        out[part(at * count + i % count, rows), :] = ref[...].astype(F32) * scale
 
 
 def nodes_kernel(w_ref, *refs):
@@ -254,19 +260,21 @@
         out[...] = (kept[i] + received[i].astype(F32)).astype(out.dtype)
 
 
-def reduce_columns(keep, send, span, hid):
-    bit = 1
+def reduce_columns(blocks, span, hid):
+    bit, halved = 1, None
     while True:
-        received = swap(send, "col", bit)
-        count = keep.shape[0]
+        keep, send = blocks[::2], blocks[1::2]
+        received = [swap(x, "col", bit) for x in send]
+        count = len(keep)
         if count == 1:
-            return keep, received, send
+            return keep[0], received[0], halved
         bit *= 2
-        keep, send = call(
-            halve_kernel,
-            [shape(count // 2, span, hid, dtype=F32), shape(count // 2, span, hid)],
-            [keep, received],
+        blocks = call(
+            functools.partial(halve_kernel, count),
+            [shape(span, hid, dtype=BF16 if s % 2 else F32) for s in range(count)],
+            [*keep, *received],
         )
+        halved = blocks[1]
 
 
 def local(
@@ -285,22 +293,19 @@
 
     beside = swap(nodes, "row", 1)
     near = [swap(nodes, "row", t) for t in chips[:0:-1]][::-1]
-    (history,) = call(later_kernel, [shape(*history.shape)], [history, beside])
-    (stacked,) = call(stack_kernel, [shape(len(near), span, hid)], [*near, history, tiles])
-    across = swap(stacked, "row", 1)
-
-    blocks = [shape(n_col // 2, span, hid, dtype=F32), shape(n_col // 2, span, hid)]
-    keep, send = call(
+    (history,) = call(later_kernel, [shape(*history.shape)], [history, beside, tiles])
+    stacked = call(
+        stack_kernel, [shape(len(near), span // 2, hid)] * 2, [*near, history]
+    )
+    across = [swap(x, "row", 1) for x in stacked]
+
+    blocks = call(
         functools.partial(aggregate_kernel, n_row, n_col),
-        blocks,
-        [adjacency, nodes, beside, stacked, across],
+        [shape(span, hid, dtype=BF16 if s % 2 else F32) for s in range(n_col)],
+        [adjacency, nodes, beside, *near, *across],
         [shape(columns, hid)],
     )
-    keep, received, halved = reduce_columns(keep, send, span, hid)
-    projected, summed = call(
-        project_kernel, [shape(span, hid, dtype=F32), shape(hid, span)], [keep, received, weight]
-    )
-
+    keep, received, halved = reduce_columns(blocks, span, hid)
     blocks_held = history.shape[0] // BLK
     places = len(chips) * CAP
     which, code, which2, code2 = pl.pallas_call(
@@ -320,13 +325,16 @@
     own_terms, terms = call(
         functools.partial(early_kernel, early, blocks_held),
         [spare, spare],
-        [projected, hist_tiles, tiles, *[past[i] for i in early]],
+        [hist_tiles, tiles, *[past[i] for i in early]],
         lists=[which, code, which2, code2],
+    )
+    projected, summed = call(
+        project_kernel, [shape(span, hid, dtype=F32), shape(hid, span)], [keep, received, weight, own_terms]
     )
     (given,) = call(
         functools.partial(others_kernel, late, blocks_held),
         [shape(panel, hid)],
-        [terms, tiles, *[past[i] for i in late]],
+        [terms, tiles, projected, *[past[i] for i in late]],
         [spare],
         [which2, code2],
     )
@@ -340,7 +348,7 @@
     keep, *sends = call(
         functools.partial(merge_kernel, n_col),
         [shape(span, hid, dtype=BF16 if s else F32) for s in range(n_col)],
-        [terms, received],
+        [projected, terms, received],
     )
     mixed, flipped = call(
         gradient_kernel,
@@ -391,14 +399,20 @@
         nodes_kernel, [shape(span, hid)], [weight, *[arrived[i] for i in range(len(chips))]]
     )
 
+    halfway = [halfway]
     for bit in [1 << b for b in range(1, n_col.bit_length() - 1)]:
-        received = swap(halfway, "col", bit)
-        (halfway,) = call(add_kernel, [shape(*halfway.shape)], [halfway, received, arrived[len(chips) - 1]])
+        received = swap(halfway[0], "col", bit)
+        count = 2 if 2 * bit == n_col else 1
+        halfway = call(
+            add_kernel,
+            [shape(hid // 2 // count, hid)] * count,
+            [halfway[0], received, arrived[len(chips) - 1]],
+        )
     scale = 1.0 / math.sqrt(span * n_row * n_col)
     (grad_weight,) = call(
         functools.partial(scale_kernel, scale),
         [shape(hid, hid, dtype=F32)],
-        [halfway, swap(halfway, "row", 1)],
+        [*halfway, *[swap(x, "row", 1) for x in halfway]],
     )
     return (activated, grad_nodes, grad_weight)
 

time: 85.7 us -> 83 us (0.968)
  waiting for transfers between devices: 38.7 us -> 32.7 us
  starting transfers between devices: 31.3 us -> 34.6 us
    ppermute x30 -> x33, waiting for transfers between devices: 38.7 us -> 32.7 us  [swap(): return lax.ppermute(x, axis, [(i, i ^ offset) for i in range(size)])]
    ppermute x30 -> x33, starting transfers between devices: 31.3 us -> 34.6 us  [swap(): return lax.ppermute(x, axis, [(i, i ^ offset) for i in range(size)])]
  transfers between devices with their start and end apart: 30 -> 33, of which waited for: 18 -> 18; matrix products, arithmetic and copies ran while one was open for 0% -> 0% of each run, Pallas kernels for 9% -> 10%
where the time goes in v5:
time: 83 us; the launch traced here: 82.8 us
  starting transfers between devices  34.6 us (42%)
  waiting for transfers between devices  32.7 us (39%)
  Pallas kernels  11.3 us (14%)
  local copies, waits for them, and re-layouts  3.26 us (4%)
  between operations  0.94 us (1%)
    ppermute x33, starting transfers between devices, swap(): return lax.ppermute(x, axis, [(i, i ^ offset) for i in range(size)])  34.6 us
    ppermute x33, waiting for transfers between devices, swap(): return lax.ppermute(x, axis, [(i, i ^ offset) for i in range(size)])  32.7 us
    pallas_call x21, Pallas kernels, call(): pl.pallas_call(kernel, out_shape=outs, in_specs=[SCALARS] * len(lists) +...  8.97 us
    unnamed x20, local copies, waits for them, and re-layouts  3.26 us
    pallas_call x1, Pallas kernels, local(): pl.pallas_call(functools.partial(lists_kernel, blocks_held, row_count), o...  2.38 us
  transfers between devices with their start and end apart: 33, of which 18 were waited for; matrix products, arithmetic and copies ran while one was open for 0% of the time, Pallas kernels for 10%

profile of v5, /device:TPU:0, one launch (start us, length us, event | category | flops | bytes accessed | tf_op | source)
XLA Modules:
  0.0 82.8 jit_solution(2081927789271034509)
XLA Ops:
  0.6 0.5 collective-permute-start.4
  1.1 0.1 collective-permute-start
  1.2 2.9 %collective-permute-start.1 = (bf16[256,256]{1,0:T(8,128)(2,1)}, bf16[256,256]{1,0:T(8,128)(2,1)S(1)}, u32[]{:S(2)}, u32[]{:S(2)}) collective-permute-start(bf16[256,256]{1,0:T(8,128)(2,1)} %own.1), channel_id=1, source_target_pairs={{0,8},{4,12},{8,0},{12,4},{16,24},{20,28},{24,16},{28,20},{1,9},{5... | collective-permute-start | bytes 393224 | tf_op jit(solution)/shard_map/ppermute | solution.py:21
  4.1 1.5 %collective-permute-start.2 = (bf16[256,256]{1,0:T(8,128)(2,1)}, bf16[256,256]{1,0:T(8,128)(2,1)S(1)}, u32[]{:S(2)}, u32[]{:S(2)}) collective-permute-start(bf16[256,256]{1,0:T(8,128)(2,1)} %own.1), channel_id=1, source_target_pairs={{0,16},{4,20},{8,24},{12,28},{16,0},{20,4},{24,8},{28,12},{1,17},{... | collective-permute-start | bytes 393224 | tf_op jit(solution)/shard_map/ppermute | solution.py:21
  5.7 1.0 %copy-done.3 = bf16[1024,256]{1,0:T(8,128)(2,1)S(1)} copy-done((bf16[1024,256]{1,0:T(8,128)(2,1)S(1)}, bf16[1024,256]{1,0:T(8,128)(2,1)}, u32[]{:S(2)}) %copy-start.3) | copy-done | bytes 524312
  6.8 2.0 %collective-permute-start.11 = (bf16[1024,256]{1,0:T(8,128)(2,1)S(1)}, bf16[1024,256]{1,0:T(8,128)(2,1)S(1)}, u32[]{:S(2)}, u32[]{:S(2)}) collective-permute-start(bf16[1024,256]{1,0:T(8,128)(2,1)S(1)} %shard_map.112.refs_3_.refs_0_), channel_id=1, source_target_pairs={{0,8},{4,12},{8,0},{12,4},{16,24},{20,28},{24,16},{28,20},{1,9},{5... | collective-permute-start | bytes 1572872 | tf_op jit(solution)/shard_map/ppermute | solution.py:21
  8.8 1.5 %collective-permute-start.12 = (bf16[1024,256]{1,0:T(8,128)(2,1)S(1)}, bf16[1024,256]{1,0:T(8,128)(2,1)S(1)}, u32[]{:S(2)}, u32[]{:S(2)}) collective-permute-start(bf16[1024,256]{1,0:T(8,128)(2,1)S(1)} %shard_map.112.refs_3_.refs_0_), channel_id=1, source_target_pairs={{0,16},{4,20},{8,24},{12,28},{16,0},{20,4},{24,8},{28,12},{1,17},{... | collective-permute-start | bytes 1572872 | tf_op jit(solution)/shard_map/ppermute | solution.py:21
  10.3 1.4 %collective-permute-start.13 = (bf16[1024,256]{1,0:T(8,128)(2,1)S(1)}, bf16[1024,256]{1,0:T(8,128)(2,1)S(1)}, u32[]{:S(2)}, u32[]{:S(2)}) collective-permute-start(bf16[1024,256]{1,0:T(8,128)(2,1)S(1)} %shard_map.112.refs_3_.refs_0_), channel_id=1, source_target_pairs={{0,24},{4,28},{8,16},{12,20},{16,8},{20,12},{24,0},{28,4},{1,25},{... | collective-permute-start | bytes 1572872 | tf_op jit(solution)/shard_map/ppermute | solution.py:21
  11.7 0.9 %collective-permute-done.2.refs_1_ = bf16[256,256]{1,0:T(8,128)(2,1)S(1)} collective-permute-done((bf16[256,256]{1,0:T(8,128)(2,1)}, bf16[256,256]{1,0:T(8,128)(2,1)S(1)}, u32[]{:S(2)}, u32[]{:S(2)}) %collective-permute-start.2) | collective-permute-done | bytes 131104 | tf_op jit(solution)/shard_map/ppermute | solution.py:21
  12.6 0.6 collective-permute-done.3.refs_2_
  13.3 0.1 collective-permute-start.5
  13.4 0.5 collective-permute-start.6
  13.9 0.9 %collective-permute-done.5.refs_3_ = bf16[3,128,256]{2,1,0:T(8,128)(2,1)S(1)} collective-permute-done((bf16[3,128,256]{2,1,0:T(8,128)(2,1)S(1)}, bf16[3,128,256]{2,1,0:T(8,128)(2,1)S(1)}, u32[]{:S(2)}, u32[]{:S(2)}) %collective-permute-start.5) | collective-permute-done | bytes 196640 | tf_op jit(solution)/shard_map/ppermute | solution.py:21
  14.8 0.3 collective-permute-done.6.refs_4_
  15.1 2.2 %copy-done = bf16[1024,2048]{1,0:T(8,128)(2,1)S(1)} copy-done((bf16[1024,2048]{1,0:T(8,128)(2,1)S(1)}, bf16[1024,2048]{1,0:T(8,128)(2,1)}, u32[]{:S(2)}) %copy-start) | copy-done | bytes 4194328
  17.3 1.3 %shard_map.114 = (f32[256,256]{1,0:T(8,128)S(1)}, bf16[256,256]{1,0:T(8,128)(2,1)S(1)}, f32[256,256]{1,0:T(8,128)S(1)}, bf16[256,256]{1,0:T(8,128)(2,1)S(1)}) custom-call(bf16[1024,2048]{1,0:T(8,128)(2,1)S(1)} %copy-done, bf16[256,256]{1,0:T(8,128)(2,1)S(1)} %copy-done.5, bf16[256,256]{1,0:T(8,128)(2,1)S(1)} %collective-permute-done.refs_0_.other, ...), custom_call_target="tpu_custom_call" | custom-call | tf_op jit(solution)/shard_map/pallas_call | solution.py:39
  18.6 1.6 %collective-permute-start.7 = (bf16[256,256]{1,0:T(8,128)(2,1)S(1)}, bf16[256,256]{1,0:T(8,128)(2,1)S(1)}, u32[]{:S(2)}, u32[]{:S(2)}) collective-permute-start(bf16[256,256]{1,0:T(8,128)(2,1)S(1)} %get-tuple-element.40), channel_id=1, source_target_pairs={{0,1},{1,0},{2,3},{3,2},{4,5},{5,4},{6,7},{7,6},{8,9},{9,8},{10,11... | collective-permute-start | bytes 393224 | tf_op jit(solution)/shard_map/ppermute | solution.py:21
  20.2 0.5 collective-permute-start.8
  20.7 4.3 %collective-permute-done.7.refs_2_ = bf16[256,256]{1,0:T(8,128)(2,1)S(1)} collective-permute-done((bf16[256,256]{1,0:T(8,128)(2,1)S(1)}, bf16[256,256]{1,0:T(8,128)(2,1)S(1)}, u32[]{:S(2)}, u32[]{:S(2)}) %collective-permute-start.7) | collective-permute-done | bytes 131104 | tf_op jit(solution)/shard_map/ppermute | solution.py:21
  25.0 2.1 %collective-permute-done.8.refs_3_ = bf16[256,256]{1,0:T(8,128)(2,1)S(1)} collective-permute-done((bf16[256,256]{1,0:T(8,128)(2,1)S(1)}, bf16[256,256]{1,0:T(8,128)(2,1)S(1)}, u32[]{:S(2)}, u32[]{:S(2)}) %collective-permute-start.8) | collective-permute-done | bytes 131104 | tf_op jit(solution)/shard_map/ppermute | solution.py:21
  27.2 2.7 %collective-permute-start.9 = (bf16[256,256]{1,0:T(8,128)(2,1)S(1)}, bf16[256,256]{1,0:T(8,128)(2,1)S(1)}, u32[]{:S(2)}, u32[]{:S(2)}) collective-permute-start(bf16[256,256]{1,0:T(8,128)(2,1)S(1)} %get-tuple-element.43._), channel_id=1, source_target_pairs={{0,2},{1,3},{2,0},{3,1},{4,6},{5,7},{6,4},{7,5},{8,10},{9,11},{10,... | collective-permute-start | bytes 393224 | tf_op jit(solution)/shard_map/ppermute | solution.py:21
  29.8 0.1 collective-permute-start.10
  29.9 1.1 %collective-permute-done.10.theirs = s32[3,32]{1,0:T(4,128)S(1)} collective-permute-done((s32[3,32]{1,0:T(4,128)S(1)}, s32[3,32]{1,0:T(4,128)S(1)}, u32[]{:S(2)}, u32[]{:S(2)}) %collective-permute-start.10) | collective-permute-done | bytes 416 | tf_op jit(solution)/shard_map/ppermute | solution.py:21
  31.1 2.4 %shard_map.116 = (s32[16]{0:T(128)S(1)}, s32[16]{0:T(128)S(1)}, s32[16]{0:T(128)S(1)}, s32[16]{0:T(128)S(1)}) custom-call(s32[3,32]{1,0:T(4,128)S(1)} %pad_add_fusion.mine, s32[3,32]{1,0:T(4,128)S(1)} %collective-permute-done.10.theirs, bf16[256,256]{1,0:T(8,128)(2,1)S(1)} %get-tuple-element.43._), custom_call_target="tpu_custom_call" | custom-call | tf_op jit(solution)/shard_map/pallas_call | solution.py:311
  33.4 1.4 %collective-permute-done.12.refs_2_ = bf16[1024,256]{1,0:T(8,128)(2,1)S(1)} collective-permute-done((bf16[1024,256]{1,0:T(8,128)(2,1)S(1)}, bf16[1024,256]{1,0:T(8,128)(2,1)S(1)}, u32[]{:S(2)}, u32[]{:S(2)}) %collective-permute-start.12) | collective-permute-done | bytes 524320 | tf_op jit(solution)/shard_map/ppermute | solution.py:21
  34.8 1.2 %shard_map.117 = (f32[1152,256]{1,0:T(8,128)S(1)}, f32[1152,256]{1,0:T(8,128)S(1)}) custom-call(s32[16]{0:T(128)S(1)} %get-tuple-element.44.which, s32[16]{0:T(128)S(1)} %get-tuple-element.45.code, s32[16]{0:T(128)S(1)} %get-tuple-element.46.which2.which, s32[16]{0:T(128)S(1)} %get-tuple-element.47.code2.code, bf16[32,128,128]{2,1,0:T(8,128)(2,1)S(1)} %copy-done.2, ...), custom_call_target="tpu_custom_call" | custom-call | tf_op jit(solution)/shard_map/pallas_call | solution.py:39
  36.1 0.2 shard_map.118
  36.3 0.8 %shard_map.120 = bf16[1024,256]{1,0:T(8,128)(2,1)S(1)} custom-call(s32[16]{0:T(128)S(1)} %get-tuple-element.46.which2.which, s32[16]{0:T(128)S(1)} %get-tuple-element.47.code2.code, f32[1152,256]{1,0:T(8,128)S(1)} %get-tuple-element.50.acc_in, bf16[32,128,128]{2,1,0:T(8,128)(2,1)S(1)} %collective-permute-done.4.refs_1_.tiles2.tiles, ...), custom_call_target="tpu_custom_call" | custom-call | tf_op jit(solution)/shard_map/pallas_call | solution.py:39
  37.2 0.1 collective-permute-start.14
  37.3 0.8 shard_map.119.own
  38.1 1.1 %collective-permute-done.14.received = bf16[1024,256]{1,0:T(8,128)(2,1)S(1)} collective-permute-done((bf16[1024,256]{1,0:T(8,128)(2,1)S(1)}, bf16[1024,256]{1,0:T(8,128)(2,1)S(1)}, u32[]{:S(2)}, u32[]{:S(2)}) %collective-permute-start.14) | collective-permute-done | bytes 524320 | tf_op jit(solution)/shard_map/ppermute | solution.py:21
  39.2 0.2 shard_map.121
  39.3 3.7 %collective-permute-start.15 = (bf16[256,256]{1,0:T(8,128)(2,1)S(1)}, bf16[256,256]{1,0:T(8,128)(2,1)S(1)}, u32[]{:S(2)}, u32[]{:S(2)}) collective-permute-start(bf16[256,256]{1,0:T(8,128)(2,1)S(1)} %get-tuple-element.52), channel_id=1, source_target_pairs={{0,3},{1,2},{2,1},{3,0},{4,7},{5,6},{6,5},{7,4},{8,11},{9,10},{10,... | collective-permute-start | bytes 393224 | tf_op jit(solution)/shard_map/ppermute | solution.py:21
  43.0 0.8 collective-permute-start.17
  43.8 3.8 %collective-permute-done.15.refs_0_ = bf16[256,256]{1,0:T(8,128)(2,1)S(1)} collective-permute-done((bf16[256,256]{1,0:T(8,128)(2,1)S(1)}, bf16[256,256]{1,0:T(8,128)(2,1)S(1)}, u32[]{:S(2)}, u32[]{:S(2)}) %collective-permute-start.15) | collective-permute-done | bytes 131104 | tf_op jit(solution)/shard_map/ppermute | solution.py:21
  47.6 3.1 %collective-permute-done.16.refs_1_ = bf16[256,256]{1,0:T(8,128)(2,1)S(1)} collective-permute-done((bf16[256,256]{1,0:T(8,128)(2,1)S(1)}, bf16[256,256]{1,0:T(8,128)(2,1)S(1)}, u32[]{:S(2)}, u32[]{:S(2)}) %collective-permute-start.16) | collective-permute-done | bytes 131104 | tf_op jit(solution)/shard_map/ppermute | solution.py:21
  50.7 3.7 %collective-permute-done.17.refs_2_ = bf16[256,256]{1,0:T(8,128)(2,1)S(1)} collective-permute-done((bf16[256,256]{1,0:T(8,128)(2,1)S(1)}, bf16[256,256]{1,0:T(8,128)(2,1)S(1)}, u32[]{:S(2)}, u32[]{:S(2)}) %collective-permute-start.17) | collective-permute-done | bytes 131104 | tf_op jit(solution)/shard_map/ppermute | solution.py:21
  54.4 0.2 shard_map.122
  54.6 2.5 %collective-permute-start.19 = (bf16[256,256]{1,0:T(8,128)(2,1)S(1)}, bf16[256,256]{1,0:T(8,128)(2,1)S(1)}, u32[]{:S(2)}, u32[]{:S(2)}) collective-permute-start(bf16[256,256]{1,0:T(8,128)(2,1)S(1)} %get-tuple-element.57.g_ref.refs_3_), channel_id=1, source_target_pairs={{0,3},{1,2},{2,1},{3,0},{4,7},{5,6},{6,5},{7,4},{8,11},{9,10},{10,... | collective-permute-start | bytes 393224 | tf_op jit(solution)/shard_map/ppermute | solution.py:21
  57.1 0.2 shard_map.123
  57.3 0.1 collective-permute-start.18
  57.4 0.1 collective-permute-start.20
  57.5 1.9 %collective-permute-start.21 = (bf16[256,256]{1,0:T(8,128)(2,1)S(1)}, bf16[256,256]{1,0:T(8,128)(2,1)S(1)}, u32[]{:S(2)}, u32[]{:S(2)}) collective-permute-start(bf16[256,256]{1,0:T(8,128)(2,1)S(1)} %get-tuple-element.57.g_ref.refs_3_), channel_id=1, source_target_pairs={{0,2},{1,3},{2,0},{3,1},{4,6},{5,7},{6,4},{7,5},{8,10},{9,11},{10,... | collective-permute-start | bytes 393224 | tf_op jit(solution)/shard_map/ppermute | solution.py:21
  59.4 0.7 shard_map.124
  60.1 2.0 %collective-permute-start.23 = (bf16[128,256]{1,0:T(8,128)(2,1)S(1)}, bf16[128,256]{1,0:T(8,128)(2,1)S(1)}, u32[]{:S(2)}, u32[]{:S(2)}) collective-permute-start(bf16[128,256]{1,0:T(8,128)(2,1)S(1)} %get-tuple-element.61.refs_0_), channel_id=1, source_target_pairs={{0,16},{4,20},{8,24},{12,28},{16,0},{20,4},{24,8},{28,12},{1,17},{... | collective-permute-start | bytes 196616 | tf_op jit(solution)/shard_map/ppermute | solution.py:21
  62.2 0.6 collective-permute-done.19.refs_0_
  62.8 1.5 %collective-permute-start.24 = (bf16[128,256]{1,0:T(8,128)(2,1)S(1)}, bf16[128,256]{1,0:T(8,128)(2,1)S(1)}, u32[]{:S(2)}, u32[]{:S(2)}) collective-permute-start(bf16[128,256]{1,0:T(8,128)(2,1)S(1)} %get-tuple-element.61.refs_0_), channel_id=1, source_target_pairs={{0,24},{4,28},{8,16},{12,20},{16,8},{20,12},{24,0},{28,4},{1,25},{... | collective-permute-start | bytes 196616 | tf_op jit(solution)/shard_map/ppermute | solution.py:21
  64.2 2.3 %collective-permute-done.20.refs_1_ = bf16[256,256]{1,0:T(8,128)(2,1)S(1)} collective-permute-done((bf16[256,256]{1,0:T(8,128)(2,1)S(1)}, bf16[256,256]{1,0:T(8,128)(2,1)S(1)}, u32[]{:S(2)}, u32[]{:S(2)}) %collective-permute-start.20) | collective-permute-done | bytes 131104 | tf_op jit(solution)/shard_map/ppermute | solution.py:21
  66.5 1.2 %collective-permute-done.21.refs_2_ = bf16[256,256]{1,0:T(8,128)(2,1)S(1)} collective-permute-done((bf16[256,256]{1,0:T(8,128)(2,1)S(1)}, bf16[256,256]{1,0:T(8,128)(2,1)S(1)}, u32[]{:S(2)}, u32[]{:S(2)}) %collective-permute-start.21) | collective-permute-done | bytes 131104 | tf_op jit(solution)/shard_map/ppermute | solution.py:21
  67.8 0.1 collective-permute-done.24.refs_3_
  68.0 1.3 %shard_map.127 = (bf16[4,256,256]{2,1,0:T(8,128)(2,1)S(1)}, f32[4,256,256]{2,1,0:T(8,128)S(1)}) custom-call(bf16[1024,2048]{1,0:T(8,128)(2,1)S(1)} %copy-done.1, bf16[256,1024]{1,0:T(8,128)(2,1)S(1)} %shard_map.125.refs_4_.g_ref, bf16[128,256]{1,0:T(8,128)(2,1)S(1)} %shard_map.126._.x_ref), custom_call_target="tpu_custom_call" | custom-call | tf_op jit(solution)/shard_map/pallas_call | solution.py:39
  69.3 0.1 collective-permute-start.25
  69.4 0.1 collective-permute-start.26
  69.4 1.8 %collective-permute-done.25.received = bf16[4,256,256]{2,1,0:T(8,128)(2,1)S(1)} collective-permute-done((bf16[4,256,256]{2,1,0:T(8,128)(2,1)S(1)}, bf16[4,256,256]{2,1,0:T(8,128)(2,1)S(1)}, u32[]{:S(2)}, u32[]{:S(2)}) %collective-permute-start.25) | collective-permute-done | bytes 524320 | tf_op jit(solution)/shard_map/ppermute | solution.py:21
  71.3 0.1 shard_map.128
  71.3 1.6 %collective-permute-start.29 = (bf16[256,256]{1,0:T(8,128)(2,1)S(1)}, bf16[256,256]{1,0:T(8,128)(2,1)S(1)}, u32[]{:S(2)}, u32[]{:S(2)}) collective-permute-start(bf16[256,256]{1,0:T(8,128)(2,1)S(1)} %get-tuple-element.66), channel_id=1, source_target_pairs={{0,24},{4,28},{8,16},{12,20},{16,8},{20,12},{24,0},{28,4},{1,25},{... | collective-permute-start | bytes 393224 | tf_op jit(solution)/shard_map/ppermute | solution.py:21
  72.9 1.5 %collective-permute-start.27 = (bf16[256,256]{1,0:T(8,128)(2,1)S(1)}, bf16[256,256]{1,0:T(8,128)(2,1)S(1)}, u32[]{:S(2)}, u32[]{:S(2)}) collective-permute-start(bf16[256,256]{1,0:T(8,128)(2,1)S(1)} %get-tuple-element.64._), channel_id=1, source_target_pairs={{0,8},{4,12},{8,0},{12,4},{16,24},{20,28},{24,16},{28,20},{1,9},{5... | collective-permute-start | bytes 393224 | tf_op jit(solution)/shard_map/ppermute | solution.py:21
  74.4 0.5 collective-permute-start.28
  74.9 2.4 %collective-permute-start.30 = (bf16[128,256]{1,0:T(8,128)(2,1)S(1)}, bf16[128,256]{1,0:T(8,128)(2,1)S(1)}, u32[]{:S(2)}, u32[]{:S(2)}) collective-permute-start(bf16[128,256]{1,0:T(8,128)(2,1)S(1)} %shard_map.129._.x_ref), channel_id=1, source_target_pairs={{0,2},{1,3},{2,0},{3,1},{4,6},{5,7},{6,4},{7,5},{8,10},{9,11},{10,... | collective-permute-start | bytes 196616 | tf_op jit(solution)/shard_map/ppermute | solution.py:21
  77.3 3.2 %collective-permute-done.30.y_ref = bf16[128,256]{1,0:T(8,128)(2,1)S(1)} collective-permute-done((bf16[128,256]{1,0:T(8,128)(2,1)S(1)}, bf16[128,256]{1,0:T(8,128)(2,1)S(1)}, u32[]{:S(2)}, u32[]{:S(2)}) %collective-permute-start.30) | collective-permute-done | bytes 65568 | tf_op jit(solution)/shard_map/ppermute | solution.py:21
  80.5 0.1 collective-permute-start.31
  80.6 0.5 collective-permute-start.32
  81.1 0.9 %shard_map.131 = bf16[256,256]{1,0:T(8,128)(2,1)} custom-call(bf16[256,256]{1,0:T(8,128)(2,1)S(1)} %copy-done.4, f32[256,256]{1,0:T(8,128)S(1)} %shard_map.130.refs_0_, bf16[256,256]{1,0:T(8,128)(2,1)S(1)} %collective-permute-done.27.refs_1_, bf16[256,256]{1,0:T(8,128)(2,1)S(1)} %collective-permute-done.28.refs_2_, ...), custom_call_target="tpu_custom_call" | custom-call | tf_op jit(solution)/shard_map/pallas_call | solution.py:39
  82.1 0.7 shard_map.133
  (45 shorter events, 0.4 us)
Async XLA Ops:
  0.6 5.0 %collective-permute-start.4 = (bf16[32,128,128]{2,1,0:T(8,128)(2,1)}, bf16[32,128,128]{2,1,0:T(8,128)(2,1)S(1)}, u32[]{:S(2)}, u32[]{:S(2)}) collective-permute-start(bf16[32,128,128]{2,1,0:T(8,128)(2,1)} %tiles.3), channel_id=1, source_target_pairs={{0,4},{4,0},{8,12},{12,8},{16,20},{20,16},{24,28},{28,24},{1,5},{5... | collective-permute-start | bytes 3145736 | tf_op jit(solution)/shard_map/ppermute | solution.py:21
  1.1 4.5 %collective-permute-start = (bf16[256,256]{1,0:T(8,128)(2,1)}, bf16[256,256]{1,0:T(8,128)(2,1)S(1)}, u32[]{:S(2)}, u32[]{:S(2)}) collective-permute-start(bf16[256,256]{1,0:T(8,128)(2,1)} %own.1), channel_id=1, source_target_pairs={{0,4},{4,0},{8,12},{12,8},{16,20},{20,16},{24,28},{28,24},{1,5},{5... | collective-permute-start | bytes 393224 | tf_op jit(solution)/shard_map/ppermute | solution.py:21
  1.2 9.1 %collective-permute-start.1 = (bf16[256,256]{1,0:T(8,128)(2,1)}, bf16[256,256]{1,0:T(8,128)(2,1)S(1)}, u32[]{:S(2)}, u32[]{:S(2)}) collective-permute-start(bf16[256,256]{1,0:T(8,128)(2,1)} %own.1), channel_id=1, source_target_pairs={{0,8},{4,12},{8,0},{12,4},{16,24},{20,28},{24,16},{28,20},{1,9},{5... | collective-permute-start | bytes 393224 | tf_op jit(solution)/shard_map/ppermute | solution.py:21
  4.1 8.5 %collective-permute-start.2 = (bf16[256,256]{1,0:T(8,128)(2,1)}, bf16[256,256]{1,0:T(8,128)(2,1)S(1)}, u32[]{:S(2)}, u32[]{:S(2)}) collective-permute-start(bf16[256,256]{1,0:T(8,128)(2,1)} %own.1), channel_id=1, source_target_pairs={{0,16},{4,20},{8,24},{12,28},{16,0},{20,4},{24,8},{28,12},{1,17},{... | collective-permute-start | bytes 393224 | tf_op jit(solution)/shard_map/ppermute | solution.py:21
  5.7 7.6 %collective-permute-start.3 = (bf16[256,256]{1,0:T(8,128)(2,1)}, bf16[256,256]{1,0:T(8,128)(2,1)S(1)}, u32[]{:S(2)}, u32[]{:S(2)}) collective-permute-start(bf16[256,256]{1,0:T(8,128)(2,1)} %own.1), channel_id=1, source_target_pairs={{0,24},{4,28},{8,16},{12,20},{16,8},{20,12},{24,0},{28,4},{1,25},{... | collective-permute-start | bytes 393224 | tf_op jit(solution)/shard_map/ppermute | solution.py:21
  5.7 1.0 %copy-start.3 = (bf16[1024,256]{1,0:T(8,128)(2,1)S(1)}, bf16[1024,256]{1,0:T(8,128)(2,1)}, u32[]{:S(2)}) copy-start(bf16[1024,256]{1,0:T(8,128)(2,1)} %x_ref.1) | copy-start | bytes 1572868
  6.7 8.4 %copy-start.5 = (bf16[256,256]{1,0:T(8,128)(2,1)S(1)}, bf16[256,256]{1,0:T(8,128)(2,1)}, u32[]{:S(2)}) copy-start(bf16[256,256]{1,0:T(8,128)(2,1)} %own.1) | copy-start | bytes 393220
  6.8 26.7 %collective-permute-start.11 = (bf16[1024,256]{1,0:T(8,128)(2,1)S(1)}, bf16[1024,256]{1,0:T(8,128)(2,1)S(1)}, u32[]{:S(2)}, u32[]{:S(2)}) collective-permute-start(bf16[1024,256]{1,0:T(8,128)(2,1)S(1)} %shard_map.112.refs_3_.refs_0_), channel_id=1, source_target_pairs={{0,8},{4,12},{8,0},{12,4},{16,24},{20,28},{24,16},{28,20},{1,9},{5... | collective-permute-start | bytes 1572872 | tf_op jit(solution)/shard_map/ppermute | solution.py:21
  8.8 26.0 %collective-permute-start.12 = (bf16[1024,256]{1,0:T(8,128)(2,1)S(1)}, bf16[1024,256]{1,0:T(8,128)(2,1)S(1)}, u32[]{:S(2)}, u32[]{:S(2)}) collective-permute-start(bf16[1024,256]{1,0:T(8,128)(2,1)S(1)} %shard_map.112.refs_3_.refs_0_), channel_id=1, source_target_pairs={{0,16},{4,20},{8,24},{12,28},{16,0},{20,4},{24,8},{28,12},{1,17},{... | collective-permute-start | bytes 1572872 | tf_op jit(solution)/shard_map/ppermute | solution.py:21
  10.3 26.0 %collective-permute-start.13 = (bf16[1024,256]{1,0:T(8,128)(2,1)S(1)}, bf16[1024,256]{1,0:T(8,128)(2,1)S(1)}, u32[]{:S(2)}, u32[]{:S(2)}) collective-permute-start(bf16[1024,256]{1,0:T(8,128)(2,1)S(1)} %shard_map.112.refs_3_.refs_0_), channel_id=1, source_target_pairs={{0,24},{4,28},{8,16},{12,20},{16,8},{20,12},{24,0},{28,4},{1,25},{... | collective-permute-start | bytes 1572872 | tf_op jit(solution)/shard_map/ppermute | solution.py:21
  13.3 1.5 %collective-permute-start.5 = (bf16[3,128,256]{2,1,0:T(8,128)(2,1)S(1)}, bf16[3,128,256]{2,1,0:T(8,128)(2,1)S(1)}, u32[]{:S(2)}, u32[]{:S(2)}) collective-permute-start(bf16[3,128,256]{2,1,0:T(8,128)(2,1)S(1)} %get-tuple-element.36), channel_id=1, source_target_pairs={{0,4},{4,0},{8,12},{12,8},{16,20},{20,16},{24,28},{28,24},{1,5},{5... | collective-permute-start | bytes 589832 | tf_op jit(solution)/shard_map/ppermute | solution.py:21
  13.4 16.5 %copy-start.7 = (s32[32]{0:T(128)S(1)}, s32[32]{0:T(128)}, u32[]{:S(2)}) copy-start(s32[32]{0:T(128)} %param.15) | copy-start | bytes 388
  13.4 16.4 %copy-start.8 = (s32[32]{0:T(128)S(1)}, s32[32]{0:T(128)}, u32[]{:S(2)}) copy-start(s32[32]{0:T(128)} %param.14) | copy-start | bytes 388
  13.4 16.4 %copy-start.9 = (s32[32,1]{0,1:T(1,128)S(1)}, s32[32,1]{0,1:T(1,128)}, u32[]{:S(2)}) copy-start(s32[32,1]{0,1:T(1,128)} %param.13) | copy-start | bytes 388
  13.4 1.7 %collective-permute-start.6 = (bf16[3,128,256]{2,1,0:T(8,128)(2,1)S(1)}, bf16[3,128,256]{2,1,0:T(8,128)(2,1)S(1)}, u32[]{:S(2)}, u32[]{:S(2)}) collective-permute-start(bf16[3,128,256]{2,1,0:T(8,128)(2,1)S(1)} %get-tuple-element.37), channel_id=1, source_target_pairs={{0,4},{4,0},{8,12},{12,8},{16,20},{20,16},{24,28},{28,24},{1,5},{5... | collective-permute-start | bytes 589832 | tf_op jit(solution)/shard_map/ppermute | solution.py:21
  15.1 2.2 %copy-start = (bf16[1024,2048]{1,0:T(8,128)(2,1)S(1)}, bf16[1024,2048]{1,0:T(8,128)(2,1)}, u32[]{:S(2)}) copy-start(bf16[1024,2048]{1,0:T(8,128)(2,1)} %a_ref.3) | copy-start | bytes 12582916
  17.3 17.6 %copy-start.2 = (bf16[32,128,128]{2,1,0:T(8,128)(2,1)S(1)}, bf16[32,128,128]{2,1,0:T(8,128)(2,1)}, u32[]{:S(2)}) copy-start(bf16[32,128,128]{2,1,0:T(8,128)(2,1)} %tiles.3) | copy-start | bytes 3145732
  18.6 6.4 %collective-permute-start.7 = (bf16[256,256]{1,0:T(8,128)(2,1)S(1)}, bf16[256,256]{1,0:T(8,128)(2,1)S(1)}, u32[]{:S(2)}, u32[]{:S(2)}) collective-permute-start(bf16[256,256]{1,0:T(8,128)(2,1)S(1)} %get-tuple-element.40), channel_id=1, source_target_pairs={{0,1},{1,0},{2,3},{3,2},{4,5},{5,4},{6,7},{7,6},{8,9},{9,8},{10,11... | collective-permute-start | bytes 393224 | tf_op jit(solution)/shard_map/ppermute | solution.py:21
  20.2 6.9 %collective-permute-start.8 = (bf16[256,256]{1,0:T(8,128)(2,1)S(1)}, bf16[256,256]{1,0:T(8,128)(2,1)S(1)}, u32[]{:S(2)}, u32[]{:S(2)}) collective-permute-start(bf16[256,256]{1,0:T(8,128)(2,1)S(1)} %get-tuple-element.41), channel_id=1, source_target_pairs={{0,1},{1,0},{2,3},{3,2},{4,5},{5,4},{6,7},{7,6},{8,9},{9,8},{10,11... | collective-permute-start | bytes 393224 | tf_op jit(solution)/shard_map/ppermute | solution.py:21
  27.2 8.9 %collective-permute-start.9 = (bf16[256,256]{1,0:T(8,128)(2,1)S(1)}, bf16[256,256]{1,0:T(8,128)(2,1)S(1)}, u32[]{:S(2)}, u32[]{:S(2)}) collective-permute-start(bf16[256,256]{1,0:T(8,128)(2,1)S(1)} %get-tuple-element.43._), channel_id=1, source_target_pairs={{0,2},{1,3},{2,0},{3,1},{4,6},{5,7},{6,4},{7,5},{8,10},{9,11},{10,... | collective-permute-start | bytes 393224 | tf_op jit(solution)/shard_map/ppermute | solution.py:21
  29.8 1.2 %collective-permute-start.10 = (s32[3,32]{1,0:T(4,128)S(1)}, s32[3,32]{1,0:T(4,128)S(1)}, u32[]{:S(2)}, u32[]{:S(2)}) collective-permute-start(s32[3,32]{1,0:T(4,128)S(1)} %pad_add_fusion.mine), channel_id=1, source_target_pairs={{0,4},{4,0},{8,12},{12,8},{16,20},{20,16},{24,28},{28,24},{1,5},{5... | collective-permute-start | bytes 1160 | tf_op jit(solution)/shard_map/ppermute | solution.py:21
  34.8 1.2 %copy-start.4 = (bf16[256,256]{1,0:T(8,128)(2,1)S(1)}, bf16[256,256]{1,0:T(8,128)(2,1)}, u32[]{:S(2)}) copy-start(bf16[256,256]{1,0:T(8,128)(2,1)} %w_ref.3) | copy-start | bytes 393220
  37.2 2.0 %collective-permute-start.14 = (bf16[1024,256]{1,0:T(8,128)(2,1)S(1)}, bf16[1024,256]{1,0:T(8,128)(2,1)S(1)}, u32[]{:S(2)}, u32[]{:S(2)}) collective-permute-start(bf16[1024,256]{1,0:T(8,128)(2,1)S(1)} %shard_map.120), channel_id=1, source_target_pairs={{0,4},{4,0},{8,12},{12,8},{16,20},{20,16},{24,28},{28,24},{1,5},{5... | collective-permute-start | bytes 1572872 | tf_op jit(solution)/shard_map/ppermute | solution.py:21
  38.1 16.3 %copy-start.6 = (bf16[256,256]{1,0:T(8,128)(2,1)S(1)}, bf16[256,256]{1,0:T(8,128)(2,1)}, u32[]{:S(2)}) copy-start(bf16[256,256]{1,0:T(8,128)(2,1)} %cotangent.1) | copy-start | bytes 393220
  39.2 28.8 %copy-start.1 = (bf16[1024,2048]{1,0:T(8,128)(2,1)S(1)}, bf16[1024,2048]{1,0:T(8,128)(2,1)}, u32[]{:S(2)}) copy-start(bf16[1024,2048]{1,0:T(8,128)(2,1)} %a_ref.3) | copy-start | bytes 12582916
  39.3 8.2 %collective-permute-start.15 = (bf16[256,256]{1,0:T(8,128)(2,1)S(1)}, bf16[256,256]{1,0:T(8,128)(2,1)S(1)}, u32[]{:S(2)}, u32[]{:S(2)}) collective-permute-start(bf16[256,256]{1,0:T(8,128)(2,1)S(1)} %get-tuple-element.52), channel_id=1, source_target_pairs={{0,3},{1,2},{2,1},{3,0},{4,7},{5,6},{6,5},{7,4},{8,11},{9,10},{10,... | collective-permute-start | bytes 393224 | tf_op jit(solution)/shard_map/ppermute | solution.py:21
  43.0 7.7 %collective-permute-start.16 = (bf16[256,256]{1,0:T(8,128)(2,1)S(1)}, bf16[256,256]{1,0:T(8,128)(2,1)S(1)}, u32[]{:S(2)}, u32[]{:S(2)}) collective-permute-start(bf16[256,256]{1,0:T(8,128)(2,1)S(1)} %get-tuple-element.53), channel_id=1, source_target_pairs={{0,1},{1,0},{2,3},{3,2},{4,5},{5,4},{6,7},{7,6},{8,9},{9,8},{10,11... | collective-permute-start | bytes 393224 | tf_op jit(solution)/shard_map/ppermute | solution.py:21
  43.0 11.4 %collective-permute-start.17 = (bf16[256,256]{1,0:T(8,128)(2,1)S(1)}, bf16[256,256]{1,0:T(8,128)(2,1)S(1)}, u32[]{:S(2)}, u32[]{:S(2)}) collective-permute-start(bf16[256,256]{1,0:T(8,128)(2,1)S(1)} %get-tuple-element.54), channel_id=1, source_target_pairs={{0,2},{1,3},{2,0},{3,1},{4,6},{5,7},{6,4},{7,5},{8,10},{9,11},{10,... | collective-permute-start | bytes 393224 | tf_op jit(solution)/shard_map/ppermute | solution.py:21
  54.6 8.2 %collective-permute-start.19 = (bf16[256,256]{1,0:T(8,128)(2,1)S(1)}, bf16[256,256]{1,0:T(8,128)(2,1)S(1)}, u32[]{:S(2)}, u32[]{:S(2)}) collective-permute-start(bf16[256,256]{1,0:T(8,128)(2,1)S(1)} %get-tuple-element.57.g_ref.refs_3_), channel_id=1, source_target_pairs={{0,3},{1,2},{2,1},{3,0},{4,7},{5,6},{6,5},{7,4},{8,11},{9,10},{10,... | collective-permute-start | bytes 393224 | tf_op jit(solution)/shard_map/ppermute | solution.py:21
  57.3 2.1 %collective-permute-start.18 = (bf16[128,256]{1,0:T(8,128)(2,1)S(1)}, bf16[128,256]{1,0:T(8,128)(2,1)S(1)}, u32[]{:S(2)}, u32[]{:S(2)}) collective-permute-start(bf16[128,256]{1,0:T(8,128)(2,1)S(1)} %get-tuple-element.59), channel_id=1, source_target_pairs={{0,4},{4,0},{8,12},{12,8},{16,20},{20,16},{24,28},{28,24},{1,5},{5... | collective-permute-start | bytes 196616 | tf_op jit(solution)/shard_map/ppermute | solution.py:21
  57.4 9.1 %collective-permute-start.20 = (bf16[256,256]{1,0:T(8,128)(2,1)S(1)}, bf16[256,256]{1,0:T(8,128)(2,1)S(1)}, u32[]{:S(2)}, u32[]{:S(2)}) collective-permute-start(bf16[256,256]{1,0:T(8,128)(2,1)S(1)} %get-tuple-element.57.g_ref.refs_3_), channel_id=1, source_target_pairs={{0,1},{1,0},{2,3},{3,2},{4,5},{5,4},{6,7},{7,6},{8,9},{9,8},{10,11... | collective-permute-start | bytes 393224 | tf_op jit(solution)/shard_map/ppermute | solution.py:21
  57.5 10.2 %collective-permute-start.21 = (bf16[256,256]{1,0:T(8,128)(2,1)S(1)}, bf16[256,256]{1,0:T(8,128)(2,1)S(1)}, u32[]{:S(2)}, u32[]{:S(2)}) collective-permute-start(bf16[256,256]{1,0:T(8,128)(2,1)S(1)} %get-tuple-element.57.g_ref.refs_3_), channel_id=1, source_target_pairs={{0,2},{1,3},{2,0},{3,1},{4,6},{5,7},{6,4},{7,5},{8,10},{9,11},{10,... | collective-permute-start | bytes 393224 | tf_op jit(solution)/shard_map/ppermute | solution.py:21
  60.1 7.7 %collective-permute-start.22 = (bf16[128,256]{1,0:T(8,128)(2,1)S(1)}, bf16[128,256]{1,0:T(8,128)(2,1)S(1)}, u32[]{:S(2)}, u32[]{:S(2)}) collective-permute-start(bf16[128,256]{1,0:T(8,128)(2,1)S(1)} %get-tuple-element.61.refs_0_), channel_id=1, source_target_pairs={{0,8},{4,12},{8,0},{12,4},{16,24},{20,28},{24,16},{28,20},{1,9},{5... | collective-permute-start | bytes 196616 | tf_op jit(solution)/shard_map/ppermute | solution.py:21
  60.1 7.7 %collective-permute-start.23 = (bf16[128,256]{1,0:T(8,128)(2,1)S(1)}, bf16[128,256]{1,0:T(8,128)(2,1)S(1)}, u32[]{:S(2)}, u32[]{:S(2)}) collective-permute-start(bf16[128,256]{1,0:T(8,128)(2,1)S(1)} %get-tuple-element.61.refs_0_), channel_id=1, source_target_pairs={{0,16},{4,20},{8,24},{12,28},{16,0},{20,4},{24,8},{28,12},{1,17},{... | collective-permute-start | bytes 196616 | tf_op jit(solution)/shard_map/ppermute | solution.py:21
  62.8 5.2 %collective-permute-start.24 = (bf16[128,256]{1,0:T(8,128)(2,1)S(1)}, bf16[128,256]{1,0:T(8,128)(2,1)S(1)}, u32[]{:S(2)}, u32[]{:S(2)}) collective-permute-start(bf16[128,256]{1,0:T(8,128)(2,1)S(1)} %get-tuple-element.61.refs_0_), channel_id=1, source_target_pairs={{0,24},{4,28},{8,16},{12,20},{16,8},{20,12},{24,0},{28,4},{1,25},{... | collective-permute-start | bytes 196616 | tf_op jit(solution)/shard_map/ppermute | solution.py:21
  69.3 2.0 %collective-permute-start.25 = (bf16[4,256,256]{2,1,0:T(8,128)(2,1)S(1)}, bf16[4,256,256]{2,1,0:T(8,128)(2,1)S(1)}, u32[]{:S(2)}, u32[]{:S(2)}) collective-permute-start(bf16[4,256,256]{2,1,0:T(8,128)(2,1)S(1)} %get-tuple-element.63._), channel_id=1, source_target_pairs={{0,4},{4,0},{8,12},{12,8},{16,20},{20,16},{24,28},{28,24},{1,5},{5... | collective-permute-start | bytes 1572872 | tf_op jit(solution)/shard_map/ppermute | solution.py:21
  69.4 5.5 %collective-permute-start.26 = (bf16[128,256]{1,0:T(8,128)(2,1)S(1)}, bf16[128,256]{1,0:T(8,128)(2,1)S(1)}, u32[]{:S(2)}, u32[]{:S(2)}) collective-permute-start(bf16[128,256]{1,0:T(8,128)(2,1)S(1)} %shard_map.126._.x_ref), channel_id=1, source_target_pairs={{0,1},{1,0},{2,3},{3,2},{4,5},{5,4},{6,7},{7,6},{8,9},{9,8},{10,11... | collective-permute-start | bytes 196616 | tf_op jit(solution)/shard_map/ppermute | solution.py:21
  71.3 9.1 %collective-permute-start.29 = (bf16[256,256]{1,0:T(8,128)(2,1)S(1)}, bf16[256,256]{1,0:T(8,128)(2,1)S(1)}, u32[]{:S(2)}, u32[]{:S(2)}) collective-permute-start(bf16[256,256]{1,0:T(8,128)(2,1)S(1)} %get-tuple-element.66), channel_id=1, source_target_pairs={{0,24},{4,28},{8,16},{12,20},{16,8},{20,12},{24,0},{28,4},{1,25},{... | collective-permute-start | bytes 393224 | tf_op jit(solution)/shard_map/ppermute | solution.py:21
  72.9 8.2 %collective-permute-start.27 = (bf16[256,256]{1,0:T(8,128)(2,1)S(1)}, bf16[256,256]{1,0:T(8,128)(2,1)S(1)}, u32[]{:S(2)}, u32[]{:S(2)}) collective-permute-start(bf16[256,256]{1,0:T(8,128)(2,1)S(1)} %get-tuple-element.64._), channel_id=1, source_target_pairs={{0,8},{4,12},{8,0},{12,4},{16,24},{20,28},{24,16},{28,20},{1,9},{5... | collective-permute-start | bytes 393224 | tf_op jit(solution)/shard_map/ppermute | solution.py:21
  74.4 6.7 %collective-permute-start.28 = (bf16[256,256]{1,0:T(8,128)(2,1)S(1)}, bf16[256,256]{1,0:T(8,128)(2,1)S(1)}, u32[]{:S(2)}, u32[]{:S(2)}) collective-permute-start(bf16[256,256]{1,0:T(8,128)(2,1)S(1)} %get-tuple-element.65), channel_id=1, source_target_pairs={{0,16},{4,20},{8,24},{12,28},{16,0},{20,4},{24,8},{28,12},{1,17},{... | collective-permute-start | bytes 393224 | tf_op jit(solution)/shard_map/ppermute | solution.py:21
  74.9 5.6 %collective-permute-start.30 = (bf16[128,256]{1,0:T(8,128)(2,1)S(1)}, bf16[128,256]{1,0:T(8,128)(2,1)S(1)}, u32[]{:S(2)}, u32[]{:S(2)}) collective-permute-start(bf16[128,256]{1,0:T(8,128)(2,1)S(1)} %shard_map.129._.x_ref), channel_id=1, source_target_pairs={{0,2},{1,3},{2,0},{3,1},{4,6},{5,7},{6,4},{7,5},{8,10},{9,11},{10,... | collective-permute-start | bytes 196616 | tf_op jit(solution)/shard_map/ppermute | solution.py:21
  80.5 1.5 %collective-permute-start.31 = (bf16[64,256]{1,0:T(8,128)(2,1)S(1)}, bf16[64,256]{1,0:T(8,128)(2,1)S(1)}, u32[]{:S(2)}, u32[]{:S(2)}) collective-permute-start(bf16[64,256]{1,0:T(8,128)(2,1)S(1)} %get-tuple-element.67.refs_0_), channel_id=1, source_target_pairs={{0,4},{4,0},{8,12},{12,8},{16,20},{20,16},{24,28},{28,24},{1,5},{5... | collective-permute-start | bytes 98312 | tf_op jit(solution)/shard_map/ppermute | solution.py:21
  80.6 1.5 %collective-permute-start.32 = (bf16[64,256]{1,0:T(8,128)(2,1)S(1)}, bf16[64,256]{1,0:T(8,128)(2,1)S(1)}, u32[]{:S(2)}, u32[]{:S(2)}) collective-permute-start(bf16[64,256]{1,0:T(8,128)(2,1)S(1)} %get-tuple-element.68.refs_1_), channel_id=1, source_target_pairs={{0,4},{4,0},{8,12},{12,8},{16,20},{20,16},{24,28},{28,24},{1,5},{5... | collective-permute-start | bytes 98312 | tf_op jit(solution)/shard_map/ppermute | solution.py:21

commit v6 on v5

--- a/solution.py
+++ b/solution.py
@@ -63,12 +63,13 @@
         out[...] = (x_ref[at, :].astype(F32) + y_ref[at, :].astype(F32)).astype(out.dtype)
 
 
-def stack_kernel(*refs):
-    refs, (_, low, high) = refs[:-3], refs[-3:]
-    half = low.shape[1]
+def stack_kernel(own, *refs):
+    refs, (_, out) = refs[:-2], refs[-2:]
+    span = own.shape[0]
+    half = span // 2
+    out[:half, :] = own[half:, :]
     for i, ref in enumerate(refs):
-        low[i] = ref[:half, :]
-        high[i] = ref[half:, :]
+        out[pl.ds(half + i * span, span), :] = ref[...]
 
 
 def lists_kernel(held, spare, mine, theirs, _, which, code, which2, code2, count):
@@ -101,7 +102,7 @@
 
 
 def aggregate_kernel(n_row, n_col, a_ref, own, other, *refs):
-    near, (low, high), outs, x_ref = refs[: -3 - n_col], refs[-3 - n_col : -1 - n_col], refs[-1 - n_col : -1], refs[-1]
+    near, (across, keep, send, x_ref) = refs[:-4], refs[-4:]
     span = own.shape[0]
     half = span // 2
     r, c = lax.axis_index("row"), lax.axis_index("col")
@@ -110,21 +111,26 @@
     for i, ref in enumerate(near):
         t = 2 * (i + 1)
         x_ref[part(r ^ t, span), :] = ref[...]
-        x_ref[part((r ^ t ^ 1) * 2, half), :] = low[i]
-        x_ref[part((r ^ t ^ 1) * 2 + 1, half), :] = high[i]
-    for s, out in enumerate(outs):
+        x_ref[part(r ^ t ^ 1, span), :] = across[pl.ds(half + i * span, span), :]
+    for s in range(n_col):
         block = jnp.dot(a_ref[part(c ^ s, span), :], x_ref[...], preferred_element_type=F32)
-        out[...] = block.astype(out.dtype)
-
-
-def halve_kernel(count, *refs):
-    kept, received, outs = refs[:count], refs[count : 2 * count], refs[2 * count :]
-    for out, x, y in zip(outs, kept, received, strict=True):
-        out[...] = (x[...] + y[...].astype(F32)).astype(out.dtype)
+        if s % 2:
+            send[s // 2] = block.astype(BF16)
+        else:
+            keep[s // 2] = block
+
+
+def halve_kernel(kept, received, keep, send):
+    for i in range(kept.shape[0]):
+        block = kept[i] + received[i].astype(F32)
+        if i % 2:
+            send[i // 2] = block.astype(BF16)
+        else:
+            keep[i // 2] = block
 
 
 def project_kernel(kept, received, w_ref, _, projected, flipped):
-    total = kept[...] + received[...].astype(F32)
+    total = kept[0] + received[0].astype(F32)
     high = total.astype(BF16)
     low = (total - high.astype(F32)).astype(BF16)
     projected[...] = jnp.dot(high, w_ref[...], preferred_element_type=F32) + jnp.dot(
@@ -134,10 +140,20 @@
 
 
 def add_pulls(pulls, held, code, tile_of, acc):
+    half = held // 2
     for i, piece in pulls:
-        block = piece[part(code[i] % held, BLK), :]
+        slot = code[i] % held
+        if len(piece) == 1:
+            block = piece[0][part(slot, BLK), :]
+        else:
+            inside = part(slot % half, BLK)
+            block = jnp.where(slot < half, piece[0][inside, :], piece[1][inside, :])
         rows = part(code[i] // held, BLK)
         acc[rows, :] += jnp.dot(tile_of(i), block, preferred_element_type=F32)
+
+
+def slice_kernel(at, x_ref, out):
+    out[...] = x_ref[pl.ds(at, out.shape[0]), :]
 
 
 def pulls_of(chips, pieces):
@@ -149,7 +165,7 @@
 
 
 def early_kernel(offsets, held, which, code, which2, code2, tiles, tiles2, *refs):
-    pieces, (own, others) = refs[:-2], refs[-2:]
+    pieces, (own, others) = [(ref,) for ref in refs[:-2]], refs[-2:]
     pulls = pulls_of(offsets, pieces)
     own[...] = jnp.zeros_like(own)
     others[...] = jnp.zeros_like(others)
@@ -157,29 +173,32 @@
     add_pulls(pulls, held, code, lambda i: tiles[which[i]], own)
 
 
-def others_kernel(offsets, held, which, code, acc_in, tiles, _, *refs):
-    pieces, (out, acc) = refs[:-2], refs[-2:]
+def others_kernel(offsets, held, count, which, code, acc_in, tiles, *refs):
+    refs, outs, acc = refs[: -1 - count], refs[-1 - count : -1], refs[-1]
+    pieces = list(zip(refs[::2], refs[1::2], strict=True))
     acc[...] = acc_in[...]
     add_pulls(pulls_of(offsets, pieces), held, code, lambda i: tiles[which[i]], acc)
-    out[...] = acc[: out.shape[0], :].astype(BF16)
+    rows = outs[0].shape[0]
+    for i, out in enumerate(outs):
+        out[...] = acc[pl.ds(i * rows, rows), :].astype(BF16)
 
 
 def own_kernel(offsets, held, which, code, acc_in, tiles, *refs):
-    pieces, out = refs[:-1], refs[-1]
+    pieces, out = list(zip(refs[:-1:2], refs[1:-1:2], strict=True)), refs[-1]
     out[...] = acc_in[...]
     add_pulls(pulls_of(offsets, pieces), held, code, lambda i: tiles[which[i]], out)
 
 
-def merge_kernel(n_col, projected, own, received, keep, *sends):
-    span = keep.shape[0]
+def merge_kernel(n_col, projected, own, *refs):
+    received, outs, acc = refs[:n_col], refs[n_col:-1], refs[-1]
+    span = outs[0].shape[0]
     c = lax.axis_index("col")
-    for s in range(n_col):
-        rows = part(c ^ s, span)
-        block = own[rows, :] + received[rows, :].astype(F32)
-        if s:
-            sends[s - 1][...] = block.astype(BF16)
-        else:
-            keep[...] = block + projected[...]
+    for i, ref in enumerate(received):
+        rows = pl.ds(i * span, span)
+        acc[rows, :] = own[rows, :] + ref[...].astype(F32)
+    for s, out in enumerate(outs):
+        block = acc[part(c ^ s, span), :]
+        out[...] = block.astype(out.dtype) if s else block + projected[...]
 
 
 def gradient_kernel(cotangent, kept, *refs):
@@ -260,21 +279,19 @@
         out[...] = (kept[i] + received[i].astype(F32)).astype(out.dtype)
 
 
-def reduce_columns(blocks, span, hid):
-    bit, halved = 1, None
+def reduce_columns(keep, send):
+    bit = 1
     while True:
-        keep, send = blocks[::2], blocks[1::2]
-        received = [swap(x, "col", bit) for x in send]
-        count = len(keep)
+        received = swap(send, "col", bit)
+        count, span, hid = keep.shape
         if count == 1:
-            return keep[0], received[0], halved
+            return keep, received, send
         bit *= 2
-        blocks = call(
-            functools.partial(halve_kernel, count),
-            [shape(span, hid, dtype=BF16 if s % 2 else F32) for s in range(count)],
-            [*keep, *received],
+        keep, send = call(
+            halve_kernel,
+            [shape(count // 2, span, hid, dtype=F32), shape(count // 2, span, hid)],
+            [keep, received],
         )
-        halved = blocks[1]
 
 
 def local(
@@ -294,18 +311,21 @@
     beside = swap(nodes, "row", 1)
     near = [swap(nodes, "row", t) for t in chips[:0:-1]][::-1]
     (history,) = call(later_kernel, [shape(*history.shape)], [history, beside, tiles])
-    stacked = call(
-        stack_kernel, [shape(len(near), span // 2, hid)] * 2, [*near, history]
-    )
-    across = [swap(x, "row", 1) for x in stacked]
-
-    blocks = call(
+    (stacked,) = call(
+        stack_kernel,
+        [shape(span // 2 + len(near) * span, hid)],
+        [nodes, *near, history],
+    )
+    across = swap(stacked, "row", 1)
+
+    keep, send = call(
         functools.partial(aggregate_kernel, n_row, n_col),
-        [shape(span, hid, dtype=BF16 if s % 2 else F32) for s in range(n_col)],
-        [adjacency, nodes, beside, *near, *across],
+        [shape(n_col // 2, span, hid, dtype=F32), shape(n_col // 2, span, hid)],
+        [adjacency, nodes, beside, *near, across],
         [shape(columns, hid)],
     )
-    keep, received, halved = reduce_columns(blocks, span, hid)
+    keep, received, halved = reduce_columns(keep, send)
+
     blocks_held = history.shape[0] // BLK
     places = len(chips) * CAP
     which, code, which2, code2 = pl.pallas_call(
@@ -317,38 +337,51 @@
         compiler_params=pltpu.CompilerParams(vmem_limit_bytes=4 << 20),
     )(pulls, their_pulls, halved)
 
-    past = [history] + [swap(history, "row", t) for t in chips[1:]]
+    middle = history.shape[0] // 2
+    bits = [1 << b for b in range(1, n_row.bit_length() - 1)]
+    past = {0: history, **{bit: swap(history, "row", bit) for bit in bits}}
+    halves = []
+    for at, order in ((0, bits), (middle, bits[::-1])):
+        held = {}
+        for bit in order:
+            held.update({t ^ bit: swap(x, "row", bit) for t, x in list(held.items())})
+            (held[bit],) = call(
+                functools.partial(slice_kernel, at), [shape(middle, hid)], [past[bit]]
+            )
+        halves.append(held)
     early = [i for i, t in enumerate(chips) if t & (t - 1) == 0]
     late = [i for i, t in enumerate(chips) if t & (t - 1)]
+    forwarded = [held[chips[i]] for i in late for held in halves]
 
     spare = shape(panel + BLK, hid, dtype=F32)
     own_terms, terms = call(
         functools.partial(early_kernel, early, blocks_held),
         [spare, spare],
-        [hist_tiles, tiles, *[past[i] for i in early]],
+        [hist_tiles, tiles, *[past[chips[i]] for i in early]],
         lists=[which, code, which2, code2],
     )
     projected, summed = call(
         project_kernel, [shape(span, hid, dtype=F32), shape(hid, span)], [keep, received, weight, own_terms]
     )
-    (given,) = call(
-        functools.partial(others_kernel, late, blocks_held),
-        [shape(panel, hid)],
-        [terms, tiles, projected, *[past[i] for i in late]],
+    given = call(
+        functools.partial(others_kernel, late, blocks_held, n_col),
+        [shape(span, hid)] * n_col,
+        [terms, tiles, *forwarded],
         [spare],
         [which2, code2],
     )
-    received = swap(given, "row", 1)
+    received = [swap(x, "row", 1) for x in given]
     (terms,) = call(
         functools.partial(own_kernel, late, blocks_held),
         [spare],
-        [own_terms, hist_tiles, *[past[i] for i in late]],
+        [own_terms, hist_tiles, *forwarded],
         lists=[which, code],
     )
     keep, *sends = call(
         functools.partial(merge_kernel, n_col),
         [shape(span, hid, dtype=BF16 if s else F32) for s in range(n_col)],
-        [projected, terms, received],
+        [projected, terms, *received],
+        [shape(panel, hid, dtype=F32)],
     )
     mixed, flipped = call(
         gradient_kernel,

time: 83 us -> 80.5 us (0.970)
  waiting for transfers between devices: 32.7 us -> 30.6 us
    ppermute x33 -> x35, waiting for transfers between devices: 32.7 us -> 30.6 us  [swap(): return lax.ppermute(x, axis, [(i, i ^ offset) for i in range(size)])]
    ppermute x33 -> x35, starting transfers between devices: 34.6 us -> 33.9 us  [swap(): return lax.ppermute(x, axis, [(i, i ^ offset) for i in range(size)])]
    pallas_call x21 -> x23, Pallas kernels: 8.97 us -> 9.02 us  [call(): pl.pallas_call(kernel, out_shape=outs, in_specs=[SCALARS] * len(lists) +...]
  transfers between devices with their start and end apart: 33 -> 35, of which waited for: 18 -> 14; matrix products, arithmetic and copies ran while one was open for 0% -> 0% of each run, Pallas kernels for 10% -> 11%
where the time goes in v6:
time: 80.5 us; the launch traced here: 80.3 us
  starting transfers between devices  33.9 us (42%)
  waiting for transfers between devices  30.6 us (38%)
  Pallas kernels  11.4 us (14%)
  local copies, waits for them, and re-layouts  3.35 us (4%)
  between operations  1 us (1%)
    ppermute x35, starting transfers between devices, swap(): return lax.ppermute(x, axis, [(i, i ^ offset) for i in range(size)])  33.9 us
    ppermute x35, waiting for transfers between devices, swap(): return lax.ppermute(x, axis, [(i, i ^ offset) for i in range(size)])  30.6 us
    pallas_call x23, Pallas kernels, call(): pl.pallas_call(kernel, out_shape=outs, in_specs=[SCALARS] * len(lists) +...  9.02 us
    unnamed x20, local copies, waits for them, and re-layouts  3.35 us
    pallas_call x1, Pallas kernels, local(): pl.pallas_call(functools.partial(lists_kernel, blocks_held, row_count), o...  2.38 us
  transfers between devices with their start and end apart: 35, of which 14 were waited for; matrix products, arithmetic and copies ran while one was open for 0% of the time, Pallas kernels for 11%

profile of v6, /device:TPU:0, one launch (start us, length us, event | category | flops | bytes accessed | tf_op | source)
XLA Modules:
  0.0 80.3 jit_solution(7729977249391980673)
XLA Ops:
  0.6 0.5 collective-permute-start.4
  1.1 0.1 collective-permute-start
  1.2 2.9 %collective-permute-start.1 = (bf16[256,256]{1,0:T(8,128)(2,1)}, bf16[256,256]{1,0:T(8,128)(2,1)S(1)}, u32[]{:S(2)}, u32[]{:S(2)}) collective-permute-start(bf16[256,256]{1,0:T(8,128)(2,1)} %own.3), channel_id=1, source_target_pairs={{0,8},{4,12},{8,0},{12,4},{16,24},{20,28},{24,16},{28,20},{1,9},{5... | collective-permute-start | bytes 393224 | tf_op jit(solution)/shard_map/ppermute | solution.py:21
  4.1 1.5 %collective-permute-start.2 = (bf16[256,256]{1,0:T(8,128)(2,1)}, bf16[256,256]{1,0:T(8,128)(2,1)S(1)}, u32[]{:S(2)}, u32[]{:S(2)}) collective-permute-start(bf16[256,256]{1,0:T(8,128)(2,1)} %own.3), channel_id=1, source_target_pairs={{0,16},{4,20},{8,24},{12,28},{16,0},{20,4},{24,8},{28,12},{1,17},{... | collective-permute-start | bytes 393224 | tf_op jit(solution)/shard_map/ppermute | solution.py:21
  5.7 1.0 %copy-done.3 = bf16[1024,256]{1,0:T(8,128)(2,1)S(1)} copy-done((bf16[1024,256]{1,0:T(8,128)(2,1)S(1)}, bf16[1024,256]{1,0:T(8,128)(2,1)}, u32[]{:S(2)}) %copy-start.3) | copy-done | bytes 524312
  6.8 2.0 %collective-permute-start.9 = (bf16[1024,256]{1,0:T(8,128)(2,1)S(1)}, bf16[1024,256]{1,0:T(8,128)(2,1)S(1)}, u32[]{:S(2)}, u32[]{:S(2)}) collective-permute-start(bf16[1024,256]{1,0:T(8,128)(2,1)S(1)} %shard_map.112.refs_3_.refs_0_), channel_id=1, source_target_pairs={{0,8},{4,12},{8,0},{12,4},{16,24},{20,28},{24,16},{28,20},{1,9},{5... | collective-permute-start | bytes 1572872 | tf_op jit(solution)/shard_map/ppermute | solution.py:21
  8.8 1.5 %collective-permute-start.10 = (bf16[1024,256]{1,0:T(8,128)(2,1)S(1)}, bf16[1024,256]{1,0:T(8,128)(2,1)S(1)}, u32[]{:S(2)}, u32[]{:S(2)}) collective-permute-start(bf16[1024,256]{1,0:T(8,128)(2,1)S(1)} %shard_map.112.refs_3_.refs_0_), channel_id=1, source_target_pairs={{0,16},{4,20},{8,24},{12,28},{16,0},{20,4},{24,8},{28,12},{1,17},{... | collective-permute-start | bytes 1572872 | tf_op jit(solution)/shard_map/ppermute | solution.py:21
  10.3 2.3 %collective-permute-done.2.refs_1_ = bf16[256,256]{1,0:T(8,128)(2,1)S(1)} collective-permute-done((bf16[256,256]{1,0:T(8,128)(2,1)}, bf16[256,256]{1,0:T(8,128)(2,1)S(1)}, u32[]{:S(2)}, u32[]{:S(2)}) %collective-permute-start.2) | collective-permute-done | bytes 131104 | tf_op jit(solution)/shard_map/ppermute | solution.py:21
  12.6 0.6 collective-permute-done.3.refs_2_
  13.3 0.1 collective-permute-start.5
  13.4 1.8 %collective-permute-done.5.refs_3_ = bf16[896,256]{1,0:T(8,128)(2,1)S(1)} collective-permute-done((bf16[896,256]{1,0:T(8,128)(2,1)S(1)}, bf16[896,256]{1,0:T(8,128)(2,1)S(1)}, u32[]{:S(2)}, u32[]{:S(2)}) %collective-permute-start.5) | collective-permute-done | bytes 458784 | tf_op jit(solution)/shard_map/ppermute | solution.py:21
  15.2 2.2 %copy-done = bf16[1024,2048]{1,0:T(8,128)(2,1)S(1)} copy-done((bf16[1024,2048]{1,0:T(8,128)(2,1)S(1)}, bf16[1024,2048]{1,0:T(8,128)(2,1)}, u32[]{:S(2)}) %copy-start) | copy-done | bytes 4194328
  17.4 1.3 %shard_map.114 = (f32[2,256,256]{2,1,0:T(8,128)S(1)}, bf16[2,256,256]{2,1,0:T(8,128)(2,1)S(1)}) custom-call(bf16[1024,2048]{1,0:T(8,128)(2,1)S(1)} %copy-done, bf16[256,256]{1,0:T(8,128)(2,1)S(1)} %copy-done.5, bf16[256,256]{1,0:T(8,128)(2,1)S(1)} %collective-permute-done.refs_0_.other, bf16[256,256]{1,0:T(8,128)(2,1)S(1)} %collective-permute-done.1.refs_0_, ...), custom_call_target="tpu_custom_call" | custom-call | tf_op jit(solution)/shard_map/pallas_call | solution.py:39
  18.7 1.6 %collective-permute-start.6 = (bf16[2,256,256]{2,1,0:T(8,128)(2,1)S(1)}, bf16[2,256,256]{2,1,0:T(8,128)(2,1)S(1)}, u32[]{:S(2)}, u32[]{:S(2)}) collective-permute-start(bf16[2,256,256]{2,1,0:T(8,128)(2,1)S(1)} %get-tuple-element.37), channel_id=1, source_target_pairs={{0,1},{1,0},{2,3},{3,2},{4,5},{5,4},{6,7},{7,6},{8,9},{9,8},{10,11... | collective-permute-start | bytes 786440 | tf_op jit(solution)/shard_map/ppermute | solution.py:21
  20.4 1.8 %collective-permute-done.9.refs_1_.x_ref = bf16[1024,256]{1,0:T(8,128)(2,1)S(1)} collective-permute-done((bf16[1024,256]{1,0:T(8,128)(2,1)S(1)}, bf16[1024,256]{1,0:T(8,128)(2,1)S(1)}, u32[]{:S(2)}, u32[]{:S(2)}) %collective-permute-start.9) | collective-permute-done | bytes 524320 | tf_op jit(solution)/shard_map/ppermute | solution.py:21
  22.2 1.8 %collective-permute-start.11 = (bf16[512,256]{1,0:T(8,128)(2,1)S(1)}, bf16[512,256]{1,0:T(8,128)(2,1)S(1)}, u32[]{:S(2)}, u32[]{:S(2)}) collective-permute-start(bf16[512,256]{1,0:T(8,128)(2,1)S(1)} %shard_map.119), channel_id=1, source_target_pairs={{0,16},{4,20},{8,24},{12,28},{16,0},{20,4},{24,8},{28,12},{1,17},{... | collective-permute-start | bytes 786440 | tf_op jit(solution)/shard_map/ppermute | solution.py:21
  24.1 1.6 %collective-permute-start.12 = (bf16[512,256]{1,0:T(8,128)(2,1)S(1)}, bf16[512,256]{1,0:T(8,128)(2,1)S(1)}, u32[]{:S(2)}, u32[]{:S(2)}) collective-permute-start(bf16[512,256]{1,0:T(8,128)(2,1)S(1)} %shard_map.120), channel_id=1, source_target_pairs={{0,8},{4,12},{8,0},{12,4},{16,24},{20,28},{24,16},{28,20},{1,9},{5... | collective-permute-start | bytes 786440 | tf_op jit(solution)/shard_map/ppermute | solution.py:21
  25.6 0.1 collective-permute-start.8
  25.7 1.4 %collective-permute-done.6.received = bf16[2,256,256]{2,1,0:T(8,128)(2,1)S(1)} collective-permute-done((bf16[2,256,256]{2,1,0:T(8,128)(2,1)S(1)}, bf16[2,256,256]{2,1,0:T(8,128)(2,1)S(1)}, u32[]{:S(2)}, u32[]{:S(2)}) %collective-permute-start.6) | collective-permute-done | bytes 262176 | tf_op jit(solution)/shard_map/ppermute | solution.py:21
  27.2 2.6 %collective-permute-start.7 = (bf16[1,256,256]{2,1,0:T(8,128)(2,1)S(1)}, bf16[1,256,256]{2,1,0:T(8,128)(2,1)S(1)}, u32[]{:S(2)}, u32[]{:S(2)}) collective-permute-start(bf16[1,256,256]{2,1,0:T(8,128)(2,1)S(1)} %get-tuple-element.39._), channel_id=1, source_target_pairs={{0,2},{1,3},{2,0},{3,1},{4,6},{5,7},{6,4},{7,5},{8,10},{9,11},{10,... | collective-permute-start | bytes 393224 | tf_op jit(solution)/shard_map/ppermute | solution.py:21
  29.9 2.4 %shard_map.116 = (s32[16]{0:T(128)S(1)}, s32[16]{0:T(128)S(1)}, s32[16]{0:T(128)S(1)}, s32[16]{0:T(128)S(1)}) custom-call(s32[3,32]{1,0:T(4,128)S(1)} %pad_add_fusion.mine, s32[3,32]{1,0:T(4,128)S(1)} %collective-permute-done.8.theirs, bf16[1,256,256]{2,1,0:T(8,128)(2,1)S(1)} %get-tuple-element.39._), custom_call_target="tpu_custom_call" | custom-call | tf_op jit(solution)/shard_map/pallas_call | solution.py:331
  32.3 1.2 %shard_map.117 = (f32[1152,256]{1,0:T(8,128)S(1)}, f32[1152,256]{1,0:T(8,128)S(1)}) custom-call(s32[16]{0:T(128)S(1)} %get-tuple-element.40.which, s32[16]{0:T(128)S(1)} %get-tuple-element.41.code, s32[16]{0:T(128)S(1)} %get-tuple-element.42.which2.which, s32[16]{0:T(128)S(1)} %get-tuple-element.43.code2.code, bf16[32,128,128]{2,1,0:T(8,128)(2,1)S(1)} %copy-done.2, ...), custom_call_target="tpu_custom_call" | custom-call | tf_op jit(solution)/shard_map/pallas_call | solution.py:39
  33.5 0.8 %shard_map.122 = (bf16[256,256]{1,0:T(8,128)(2,1)S(1)}, bf16[256,256]{1,0:T(8,128)(2,1)S(1)}, bf16[256,256]{1,0:T(8,128)(2,1)S(1)}, bf16[256,256]{1,0:T(8,128)(2,1)S(1)}) custom-call(s32[16]{0:T(128)S(1)} %get-tuple-element.42.which2.which, s32[16]{0:T(128)S(1)} %get-tuple-element.43.code2.code, f32[1152,256]{1,0:T(8,128)S(1)} %get-tuple-element.46.acc_in, ...), custom_call_target="tpu_custom_call" | custom-call | tf_op jit(solution)/shard_map/pallas_call | solution.py:39
  34.4 0.1 collective-permute-start.13
  34.4 0.5 collective-permute-start.14
  34.9 0.1 collective-permute-start.15
  35.0 0.4 collective-permute-start.16
  35.4 0.8 shard_map.121.own
  36.3 0.1 copy-done.4
  36.4 0.2 shard_map.118
  36.7 0.2 shard_map.123
  36.8 2.9 %collective-permute-start.17 = (bf16[256,256]{1,0:T(8,128)(2,1)S(1)}, bf16[256,256]{1,0:T(8,128)(2,1)S(1)}, u32[]{:S(2)}, u32[]{:S(2)}) collective-permute-start(bf16[256,256]{1,0:T(8,128)(2,1)S(1)} %get-tuple-element.52), channel_id=1, source_target_pairs={{0,3},{1,2},{2,1},{3,0},{4,7},{5,6},{6,5},{7,4},{8,11},{9,10},{10,... | collective-permute-start | bytes 393224 | tf_op jit(solution)/shard_map/ppermute | solution.py:21
  39.7 1.6 %collective-permute-start.19 = (bf16[256,256]{1,0:T(8,128)(2,1)S(1)}, bf16[256,256]{1,0:T(8,128)(2,1)S(1)}, u32[]{:S(2)}, u32[]{:S(2)}) collective-permute-start(bf16[256,256]{1,0:T(8,128)(2,1)S(1)} %get-tuple-element.54), channel_id=1, source_target_pairs={{0,2},{1,3},{2,0},{3,1},{4,6},{5,7},{6,4},{7,5},{8,10},{9,11},{10,... | collective-permute-start | bytes 393224 | tf_op jit(solution)/shard_map/ppermute | solution.py:21
  41.3 3.8 %collective-permute-done.17.refs_0_ = bf16[256,256]{1,0:T(8,128)(2,1)S(1)} collective-permute-done((bf16[256,256]{1,0:T(8,128)(2,1)S(1)}, bf16[256,256]{1,0:T(8,128)(2,1)S(1)}, u32[]{:S(2)}, u32[]{:S(2)}) %collective-permute-start.17) | collective-permute-done | bytes 131104 | tf_op jit(solution)/shard_map/ppermute | solution.py:21
  45.1 3.0 %collective-permute-done.18.refs_1_ = bf16[256,256]{1,0:T(8,128)(2,1)S(1)} collective-permute-done((bf16[256,256]{1,0:T(8,128)(2,1)S(1)}, bf16[256,256]{1,0:T(8,128)(2,1)S(1)}, u32[]{:S(2)}, u32[]{:S(2)}) %collective-permute-start.18) | collective-permute-done | bytes 131104 | tf_op jit(solution)/shard_map/ppermute | solution.py:21
  48.1 3.8 %collective-permute-done.19.refs_2_ = bf16[256,256]{1,0:T(8,128)(2,1)S(1)} collective-permute-done((bf16[256,256]{1,0:T(8,128)(2,1)S(1)}, bf16[256,256]{1,0:T(8,128)(2,1)S(1)}, u32[]{:S(2)}, u32[]{:S(2)}) %collective-permute-start.19) | collective-permute-done | bytes 131104 | tf_op jit(solution)/shard_map/ppermute | solution.py:21
  51.9 0.2 shard_map.124
  52.1 1.2 %collective-permute-start.21 = (bf16[256,256]{1,0:T(8,128)(2,1)S(1)}, bf16[256,256]{1,0:T(8,128)(2,1)S(1)}, u32[]{:S(2)}, u32[]{:S(2)}) collective-permute-start(bf16[256,256]{1,0:T(8,128)(2,1)S(1)} %get-tuple-element.57.g_ref.refs_3_), channel_id=1, source_target_pairs={{0,3},{1,2},{2,1},{3,0},{4,7},{5,6},{6,5},{7,4},{8,11},{9,10},{10,... | collective-permute-start | bytes 393224 | tf_op jit(solution)/shard_map/ppermute | solution.py:21
  53.3 0.2 shard_map.125
  53.6 0.1 collective-permute-start.20
  53.6 0.1 collective-permute-start.22
  53.7 3.2 %collective-permute-start.23 = (bf16[256,256]{1,0:T(8,128)(2,1)S(1)}, bf16[256,256]{1,0:T(8,128)(2,1)S(1)}, u32[]{:S(2)}, u32[]{:S(2)}) collective-permute-start(bf16[256,256]{1,0:T(8,128)(2,1)S(1)} %get-tuple-element.57.g_ref.refs_3_), channel_id=1, source_target_pairs={{0,2},{1,3},{2,0},{3,1},{4,6},{5,7},{6,4},{7,5},{8,10},{9,11},{10,... | collective-permute-start | bytes 393224 | tf_op jit(solution)/shard_map/ppermute | solution.py:21
  56.9 0.7 shard_map.126
  57.6 1.3 %collective-permute-start.24 = (bf16[128,256]{1,0:T(8,128)(2,1)S(1)}, bf16[128,256]{1,0:T(8,128)(2,1)S(1)}, u32[]{:S(2)}, u32[]{:S(2)}) collective-permute-start(bf16[128,256]{1,0:T(8,128)(2,1)S(1)} %get-tuple-element.61.refs_0_), channel_id=1, source_target_pairs={{0,8},{4,12},{8,0},{12,4},{16,24},{20,28},{24,16},{28,20},{1,9},{5... | collective-permute-start | bytes 196616 | tf_op jit(solution)/shard_map/ppermute | solution.py:21
  58.9 0.5 collective-permute-start.25
  59.4 0.9 %collective-permute-done.21.refs_0_ = bf16[256,256]{1,0:T(8,128)(2,1)S(1)} collective-permute-done((bf16[256,256]{1,0:T(8,128)(2,1)S(1)}, bf16[256,256]{1,0:T(8,128)(2,1)S(1)}, u32[]{:S(2)}, u32[]{:S(2)}) %collective-permute-start.21) | collective-permute-done | bytes 131104 | tf_op jit(solution)/shard_map/ppermute | solution.py:21
  60.3 1.2 %collective-permute-start.26 = (bf16[128,256]{1,0:T(8,128)(2,1)S(1)}, bf16[128,256]{1,0:T(8,128)(2,1)S(1)}, u32[]{:S(2)}, u32[]{:S(2)}) collective-permute-start(bf16[128,256]{1,0:T(8,128)(2,1)S(1)} %get-tuple-element.61.refs_0_), channel_id=1, source_target_pairs={{0,24},{4,28},{8,16},{12,20},{16,8},{20,12},{24,0},{28,4},{1,25},{... | collective-permute-start | bytes 196616 | tf_op jit(solution)/shard_map/ppermute | solution.py:21
  61.5 2.7 %collective-permute-done.22.refs_1_ = bf16[256,256]{1,0:T(8,128)(2,1)S(1)} collective-permute-done((bf16[256,256]{1,0:T(8,128)(2,1)S(1)}, bf16[256,256]{1,0:T(8,128)(2,1)S(1)}, u32[]{:S(2)}, u32[]{:S(2)}) %collective-permute-start.22) | collective-permute-done | bytes 131104 | tf_op jit(solution)/shard_map/ppermute | solution.py:21
  64.2 0.4 collective-permute-done.23.refs_2_
  64.8 0.7 collective-permute-done.26.refs_3_
  65.5 1.3 %shard_map.129 = (bf16[4,256,256]{2,1,0:T(8,128)(2,1)S(1)}, f32[4,256,256]{2,1,0:T(8,128)S(1)}) custom-call(bf16[1024,2048]{1,0:T(8,128)(2,1)S(1)} %copy-done.1, bf16[256,1024]{1,0:T(8,128)(2,1)S(1)} %shard_map.127.refs_4_.g_ref, bf16[128,256]{1,0:T(8,128)(2,1)S(1)} %shard_map.128._.x_ref), custom_call_target="tpu_custom_call" | custom-call | tf_op jit(solution)/shard_map/pallas_call | solution.py:39
  66.8 0.1 collective-permute-start.27
  66.9 0.1 collective-permute-start.28
  66.9 1.8 %collective-permute-done.27.received = bf16[4,256,256]{2,1,0:T(8,128)(2,1)S(1)} collective-permute-done((bf16[4,256,256]{2,1,0:T(8,128)(2,1)S(1)}, bf16[4,256,256]{2,1,0:T(8,128)(2,1)S(1)}, u32[]{:S(2)}, u32[]{:S(2)}) %collective-permute-start.27) | collective-permute-done | bytes 524320 | tf_op jit(solution)/shard_map/ppermute | solution.py:21
  68.8 0.1 shard_map.130
  68.8 1.3 %collective-permute-start.31 = (bf16[256,256]{1,0:T(8,128)(2,1)S(1)}, bf16[256,256]{1,0:T(8,128)(2,1)S(1)}, u32[]{:S(2)}, u32[]{:S(2)}) collective-permute-start(bf16[256,256]{1,0:T(8,128)(2,1)S(1)} %get-tuple-element.66), channel_id=1, source_target_pairs={{0,24},{4,28},{8,16},{12,20},{16,8},{20,12},{24,0},{28,4},{1,25},{... | collective-permute-start | bytes 393224 | tf_op jit(solution)/shard_map/ppermute | solution.py:21
  70.1 2.0 %collective-permute-start.29 = (bf16[256,256]{1,0:T(8,128)(2,1)S(1)}, bf16[256,256]{1,0:T(8,128)(2,1)S(1)}, u32[]{:S(2)}, u32[]{:S(2)}) collective-permute-start(bf16[256,256]{1,0:T(8,128)(2,1)S(1)} %get-tuple-element.64._), channel_id=1, source_target_pairs={{0,8},{4,12},{8,0},{12,4},{16,24},{20,28},{24,16},{28,20},{1,9},{5... | collective-permute-start | bytes 393224 | tf_op jit(solution)/shard_map/ppermute | solution.py:21
  72.1 0.3 collective-permute-start.30
  72.4 0.1 collective-permute-start.32
  72.6 5.4 %collective-permute-done.32.y_ref = bf16[128,256]{1,0:T(8,128)(2,1)S(1)} collective-permute-done((bf16[128,256]{1,0:T(8,128)(2,1)S(1)}, bf16[128,256]{1,0:T(8,128)(2,1)S(1)}, u32[]{:S(2)}, u32[]{:S(2)}) %collective-permute-start.32) | collective-permute-done | bytes 65568 | tf_op jit(solution)/shard_map/ppermute | solution.py:21
  78.0 0.1 collective-permute-start.33
  78.1 0.5 collective-permute-start.34
  78.6 0.9 %shard_map.133 = bf16[256,256]{1,0:T(8,128)(2,1)} custom-call(bf16[256,256]{1,0:T(8,128)(2,1)S(1)} %copy-done.4, f32[256,256]{1,0:T(8,128)S(1)} %shard_map.132.refs_0_, bf16[256,256]{1,0:T(8,128)(2,1)S(1)} %collective-permute-done.29.refs_1_, bf16[256,256]{1,0:T(8,128)(2,1)S(1)} %collective-permute-done.30.refs_2_, ...), custom_call_target="tpu_custom_call" | custom-call | tf_op jit(solution)/shard_map/pallas_call | solution.py:39
  79.5 0.7 shard_map.135
  (51 shorter events, 0.4 us)
Async XLA Ops:
  0.6 5.0 %collective-permute-start.4 = (bf16[32,128,128]{2,1,0:T(8,128)(2,1)}, bf16[32,128,128]{2,1,0:T(8,128)(2,1)S(1)}, u32[]{:S(2)}, u32[]{:S(2)}) collective-permute-start(bf16[32,128,128]{2,1,0:T(8,128)(2,1)} %tiles.3), channel_id=1, source_target_pairs={{0,4},{4,0},{8,12},{12,8},{16,20},{20,16},{24,28},{28,24},{1,5},{5... | collective-permute-start | bytes 3145736 | tf_op jit(solution)/shard_map/ppermute | solution.py:21
  1.1 4.5 %collective-permute-start = (bf16[256,256]{1,0:T(8,128)(2,1)}, bf16[256,256]{1,0:T(8,128)(2,1)S(1)}, u32[]{:S(2)}, u32[]{:S(2)}) collective-permute-start(bf16[256,256]{1,0:T(8,128)(2,1)} %own.3), channel_id=1, source_target_pairs={{0,4},{4,0},{8,12},{12,8},{16,20},{20,16},{24,28},{28,24},{1,5},{5... | collective-permute-start | bytes 393224 | tf_op jit(solution)/shard_map/ppermute | solution.py:21
  1.2 9.1 %collective-permute-start.1 = (bf16[256,256]{1,0:T(8,128)(2,1)}, bf16[256,256]{1,0:T(8,128)(2,1)S(1)}, u32[]{:S(2)}, u32[]{:S(2)}) collective-permute-start(bf16[256,256]{1,0:T(8,128)(2,1)} %own.3), channel_id=1, source_target_pairs={{0,8},{4,12},{8,0},{12,4},{16,24},{20,28},{24,16},{28,20},{1,9},{5... | collective-permute-start | bytes 393224 | tf_op jit(solution)/shard_map/ppermute | solution.py:21
  4.1 8.5 %collective-permute-start.2 = (bf16[256,256]{1,0:T(8,128)(2,1)}, bf16[256,256]{1,0:T(8,128)(2,1)S(1)}, u32[]{:S(2)}, u32[]{:S(2)}) collective-permute-start(bf16[256,256]{1,0:T(8,128)(2,1)} %own.3), channel_id=1, source_target_pairs={{0,16},{4,20},{8,24},{12,28},{16,0},{20,4},{24,8},{28,12},{1,17},{... | collective-permute-start | bytes 393224 | tf_op jit(solution)/shard_map/ppermute | solution.py:21
  5.7 7.6 %collective-permute-start.3 = (bf16[256,256]{1,0:T(8,128)(2,1)}, bf16[256,256]{1,0:T(8,128)(2,1)S(1)}, u32[]{:S(2)}, u32[]{:S(2)}) collective-permute-start(bf16[256,256]{1,0:T(8,128)(2,1)} %own.3), channel_id=1, source_target_pairs={{0,24},{4,28},{8,16},{12,20},{16,8},{20,12},{24,0},{28,4},{1,25},{... | collective-permute-start | bytes 393224 | tf_op jit(solution)/shard_map/ppermute | solution.py:21
  5.7 1.0 %copy-start.3 = (bf16[1024,256]{1,0:T(8,128)(2,1)S(1)}, bf16[1024,256]{1,0:T(8,128)(2,1)}, u32[]{:S(2)}) copy-start(bf16[1024,256]{1,0:T(8,128)(2,1)} %x_ref.1) | copy-start | bytes 1572868
  6.7 6.5 %copy-start.5 = (bf16[256,256]{1,0:T(8,128)(2,1)S(1)}, bf16[256,256]{1,0:T(8,128)(2,1)}, u32[]{:S(2)}) copy-start(bf16[256,256]{1,0:T(8,128)(2,1)} %own.3) | copy-start | bytes 393220
  6.8 15.4 %collective-permute-start.9 = (bf16[1024,256]{1,0:T(8,128)(2,1)S(1)}, bf16[1024,256]{1,0:T(8,128)(2,1)S(1)}, u32[]{:S(2)}, u32[]{:S(2)}) collective-permute-start(bf16[1024,256]{1,0:T(8,128)(2,1)S(1)} %shard_map.112.refs_3_.refs_0_), channel_id=1, source_target_pairs={{0,8},{4,12},{8,0},{12,4},{16,24},{20,28},{24,16},{28,20},{1,9},{5... | collective-permute-start | bytes 1572872 | tf_op jit(solution)/shard_map/ppermute | solution.py:21
  8.8 15.3 %collective-permute-start.10 = (bf16[1024,256]{1,0:T(8,128)(2,1)S(1)}, bf16[1024,256]{1,0:T(8,128)(2,1)S(1)}, u32[]{:S(2)}, u32[]{:S(2)}) collective-permute-start(bf16[1024,256]{1,0:T(8,128)(2,1)S(1)} %shard_map.112.refs_3_.refs_0_), channel_id=1, source_target_pairs={{0,16},{4,20},{8,24},{12,28},{16,0},{20,4},{24,8},{28,12},{1,17},{... | collective-permute-start | bytes 1572872 | tf_op jit(solution)/shard_map/ppermute | solution.py:21
  13.3 1.9 %collective-permute-start.5 = (bf16[896,256]{1,0:T(8,128)(2,1)S(1)}, bf16[896,256]{1,0:T(8,128)(2,1)S(1)}, u32[]{:S(2)}, u32[]{:S(2)}) collective-permute-start(bf16[896,256]{1,0:T(8,128)(2,1)S(1)} %shard_map.113), channel_id=1, source_target_pairs={{0,4},{4,0},{8,12},{12,8},{16,20},{20,16},{24,28},{28,24},{1,5},{5... | collective-permute-start | bytes 1376264 | tf_op jit(solution)/shard_map/ppermute | solution.py:21
  15.2 2.2 %copy-start = (bf16[1024,2048]{1,0:T(8,128)(2,1)S(1)}, bf16[1024,2048]{1,0:T(8,128)(2,1)}, u32[]{:S(2)}) copy-start(bf16[1024,2048]{1,0:T(8,128)(2,1)} %a_ref.3) | copy-start | bytes 12582916
  18.7 6.9 %copy-start.7 = (s32[32]{0:T(128)S(1)}, s32[32]{0:T(128)}, u32[]{:S(2)}) copy-start(s32[32]{0:T(128)} %param.15) | copy-start | bytes 388
  18.7 6.9 %copy-start.8 = (s32[32]{0:T(128)S(1)}, s32[32]{0:T(128)}, u32[]{:S(2)}) copy-start(s32[32]{0:T(128)} %param.14) | copy-start | bytes 388
  18.7 6.9 %copy-start.9 = (s32[32,1]{0,1:T(1,128)S(1)}, s32[32,1]{0,1:T(1,128)}, u32[]{:S(2)}) copy-start(s32[32,1]{0,1:T(1,128)} %param.13) | copy-start | bytes 388
  18.7 13.5 %copy-start.2 = (bf16[32,128,128]{2,1,0:T(8,128)(2,1)S(1)}, bf16[32,128,128]{2,1,0:T(8,128)(2,1)}, u32[]{:S(2)}) copy-start(bf16[32,128,128]{2,1,0:T(8,128)(2,1)} %tiles.3) | copy-start | bytes 3145732
  18.7 8.4 %collective-permute-start.6 = (bf16[2,256,256]{2,1,0:T(8,128)(2,1)S(1)}, bf16[2,256,256]{2,1,0:T(8,128)(2,1)S(1)}, u32[]{:S(2)}, u32[]{:S(2)}) collective-permute-start(bf16[2,256,256]{2,1,0:T(8,128)(2,1)S(1)} %get-tuple-element.37), channel_id=1, source_target_pairs={{0,1},{1,0},{2,3},{3,2},{4,5},{5,4},{6,7},{7,6},{8,9},{9,8},{10,11... | collective-permute-start | bytes 786440 | tf_op jit(solution)/shard_map/ppermute | solution.py:21
  22.2 11.3 %collective-permute-start.11 = (bf16[512,256]{1,0:T(8,128)(2,1)S(1)}, bf16[512,256]{1,0:T(8,128)(2,1)S(1)}, u32[]{:S(2)}, u32[]{:S(2)}) collective-permute-start(bf16[512,256]{1,0:T(8,128)(2,1)S(1)} %shard_map.119), channel_id=1, source_target_pairs={{0,16},{4,20},{8,24},{12,28},{16,0},{20,4},{24,8},{28,12},{1,17},{... | collective-permute-start | bytes 786440 | tf_op jit(solution)/shard_map/ppermute | solution.py:21
  24.1 9.4 %collective-permute-start.12 = (bf16[512,256]{1,0:T(8,128)(2,1)S(1)}, bf16[512,256]{1,0:T(8,128)(2,1)S(1)}, u32[]{:S(2)}, u32[]{:S(2)}) collective-permute-start(bf16[512,256]{1,0:T(8,128)(2,1)S(1)} %shard_map.120), channel_id=1, source_target_pairs={{0,8},{4,12},{8,0},{12,4},{16,24},{20,28},{24,16},{28,20},{1,9},{5... | collective-permute-start | bytes 786440 | tf_op jit(solution)/shard_map/ppermute | solution.py:21
  25.6 4.2 %collective-permute-start.8 = (s32[3,32]{1,0:T(4,128)S(1)}, s32[3,32]{1,0:T(4,128)S(1)}, u32[]{:S(2)}, u32[]{:S(2)}) collective-permute-start(s32[3,32]{1,0:T(4,128)S(1)} %pad_add_fusion.mine), channel_id=1, source_target_pairs={{0,4},{4,0},{8,12},{12,8},{16,20},{20,16},{24,28},{28,24},{1,5},{5... | collective-permute-start | bytes 1160 | tf_op jit(solution)/shard_map/ppermute | solution.py:21
  27.2 9.0 %collective-permute-start.7 = (bf16[1,256,256]{2,1,0:T(8,128)(2,1)S(1)}, bf16[1,256,256]{2,1,0:T(8,128)(2,1)S(1)}, u32[]{:S(2)}, u32[]{:S(2)}) collective-permute-start(bf16[1,256,256]{2,1,0:T(8,128)(2,1)S(1)} %get-tuple-element.39._), channel_id=1, source_target_pairs={{0,2},{1,3},{2,0},{3,1},{4,6},{5,7},{6,4},{7,5},{8,10},{9,11},{10,... | collective-permute-start | bytes 393224 | tf_op jit(solution)/shard_map/ppermute | solution.py:21
  34.4 2.2 %collective-permute-start.13 = (bf16[256,256]{1,0:T(8,128)(2,1)S(1)}, bf16[256,256]{1,0:T(8,128)(2,1)S(1)}, u32[]{:S(2)}, u32[]{:S(2)}) collective-permute-start(bf16[256,256]{1,0:T(8,128)(2,1)S(1)} %get-tuple-element.47), channel_id=1, source_target_pairs={{0,4},{4,0},{8,12},{12,8},{16,20},{20,16},{24,28},{28,24},{1,5},{5... | collective-permute-start | bytes 393224 | tf_op jit(solution)/shard_map/ppermute | solution.py:21
  34.4 2.2 %collective-permute-start.14 = (bf16[256,256]{1,0:T(8,128)(2,1)S(1)}, bf16[256,256]{1,0:T(8,128)(2,1)S(1)}, u32[]{:S(2)}, u32[]{:S(2)}) collective-permute-start(bf16[256,256]{1,0:T(8,128)(2,1)S(1)} %get-tuple-element.48), channel_id=1, source_target_pairs={{0,4},{4,0},{8,12},{12,8},{16,20},{20,16},{24,28},{28,24},{1,5},{5... | collective-permute-start | bytes 393224 | tf_op jit(solution)/shard_map/ppermute | solution.py:21
  34.9 1.7 %collective-permute-start.15 = (bf16[256,256]{1,0:T(8,128)(2,1)S(1)}, bf16[256,256]{1,0:T(8,128)(2,1)S(1)}, u32[]{:S(2)}, u32[]{:S(2)}) collective-permute-start(bf16[256,256]{1,0:T(8,128)(2,1)S(1)} %get-tuple-element.49), channel_id=1, source_target_pairs={{0,4},{4,0},{8,12},{12,8},{16,20},{20,16},{24,28},{28,24},{1,5},{5... | collective-permute-start | bytes 393224 | tf_op jit(solution)/shard_map/ppermute | solution.py:21
  35.0 1.6 %collective-permute-start.16 = (bf16[256,256]{1,0:T(8,128)(2,1)S(1)}, bf16[256,256]{1,0:T(8,128)(2,1)S(1)}, u32[]{:S(2)}, u32[]{:S(2)}) collective-permute-start(bf16[256,256]{1,0:T(8,128)(2,1)S(1)} %get-tuple-element.50), channel_id=1, source_target_pairs={{0,4},{4,0},{8,12},{12,8},{16,20},{20,16},{24,28},{28,24},{1,5},{5... | collective-permute-start | bytes 393224 | tf_op jit(solution)/shard_map/ppermute | solution.py:21
  35.4 0.9 %copy-start.4 = (bf16[256,256]{1,0:T(8,128)(2,1)S(1)}, bf16[256,256]{1,0:T(8,128)(2,1)}, u32[]{:S(2)}) copy-start(bf16[256,256]{1,0:T(8,128)(2,1)} %w_ref.3) | copy-start | bytes 393220
  36.6 15.3 %copy-start.6 = (bf16[256,256]{1,0:T(8,128)(2,1)S(1)}, bf16[256,256]{1,0:T(8,128)(2,1)}, u32[]{:S(2)}) copy-start(bf16[256,256]{1,0:T(8,128)(2,1)} %cotangent.1) | copy-start | bytes 393220
  36.6 28.8 %copy-start.1 = (bf16[1024,2048]{1,0:T(8,128)(2,1)S(1)}, bf16[1024,2048]{1,0:T(8,128)(2,1)}, u32[]{:S(2)}) copy-start(bf16[1024,2048]{1,0:T(8,128)(2,1)} %a_ref.3) | copy-start | bytes 12582916
  36.8 8.3 %collective-permute-start.17 = (bf16[256,256]{1,0:T(8,128)(2,1)S(1)}, bf16[256,256]{1,0:T(8,128)(2,1)S(1)}, u32[]{:S(2)}, u32[]{:S(2)}) collective-permute-start(bf16[256,256]{1,0:T(8,128)(2,1)S(1)} %get-tuple-element.52), channel_id=1, source_target_pairs={{0,3},{1,2},{2,1},{3,0},{4,7},{5,6},{6,5},{7,4},{8,11},{9,10},{10,... | collective-permute-start | bytes 393224 | tf_op jit(solution)/shard_map/ppermute | solution.py:21
  39.7 8.4 %collective-permute-start.18 = (bf16[256,256]{1,0:T(8,128)(2,1)S(1)}, bf16[256,256]{1,0:T(8,128)(2,1)S(1)}, u32[]{:S(2)}, u32[]{:S(2)}) collective-permute-start(bf16[256,256]{1,0:T(8,128)(2,1)S(1)} %get-tuple-element.53), channel_id=1, source_target_pairs={{0,1},{1,0},{2,3},{3,2},{4,5},{5,4},{6,7},{7,6},{8,9},{9,8},{10,11... | collective-permute-start | bytes 393224 | tf_op jit(solution)/shard_map/ppermute | solution.py:21
  39.7 12.1 %collective-permute-start.19 = (bf16[256,256]{1,0:T(8,128)(2,1)S(1)}, bf16[256,256]{1,0:T(8,128)(2,1)S(1)}, u32[]{:S(2)}, u32[]{:S(2)}) collective-permute-start(bf16[256,256]{1,0:T(8,128)(2,1)S(1)} %get-tuple-element.54), channel_id=1, source_target_pairs={{0,2},{1,3},{2,0},{3,1},{4,6},{5,7},{6,4},{7,5},{8,10},{9,11},{10,... | collective-permute-start | bytes 393224 | tf_op jit(solution)/shard_map/ppermute | solution.py:21
  52.1 8.2 %collective-permute-start.21 = (bf16[256,256]{1,0:T(8,128)(2,1)S(1)}, bf16[256,256]{1,0:T(8,128)(2,1)S(1)}, u32[]{:S(2)}, u32[]{:S(2)}) collective-permute-start(bf16[256,256]{1,0:T(8,128)(2,1)S(1)} %get-tuple-element.57.g_ref.refs_3_), channel_id=1, source_target_pairs={{0,3},{1,2},{2,1},{3,0},{4,7},{5,6},{6,5},{7,4},{8,11},{9,10},{10,... | collective-permute-start | bytes 393224 | tf_op jit(solution)/shard_map/ppermute | solution.py:21
  53.6 3.4 %collective-permute-start.20 = (bf16[128,256]{1,0:T(8,128)(2,1)S(1)}, bf16[128,256]{1,0:T(8,128)(2,1)S(1)}, u32[]{:S(2)}, u32[]{:S(2)}) collective-permute-start(bf16[128,256]{1,0:T(8,128)(2,1)S(1)} %get-tuple-element.59), channel_id=1, source_target_pairs={{0,4},{4,0},{8,12},{12,8},{16,20},{20,16},{24,28},{28,24},{1,5},{5... | collective-permute-start | bytes 196616 | tf_op jit(solution)/shard_map/ppermute | solution.py:21
  53.6 10.6 %collective-permute-start.22 = (bf16[256,256]{1,0:T(8,128)(2,1)S(1)}, bf16[256,256]{1,0:T(8,128)(2,1)S(1)}, u32[]{:S(2)}, u32[]{:S(2)}) collective-permute-start(bf16[256,256]{1,0:T(8,128)(2,1)S(1)} %get-tuple-element.57.g_ref.refs_3_), channel_id=1, source_target_pairs={{0,1},{1,0},{2,3},{3,2},{4,5},{5,4},{6,7},{7,6},{8,9},{9,8},{10,11... | collective-permute-start | bytes 393224 | tf_op jit(solution)/shard_map/ppermute | solution.py:21
  53.7 11.0 %collective-permute-start.23 = (bf16[256,256]{1,0:T(8,128)(2,1)S(1)}, bf16[256,256]{1,0:T(8,128)(2,1)S(1)}, u32[]{:S(2)}, u32[]{:S(2)}) collective-permute-start(bf16[256,256]{1,0:T(8,128)(2,1)S(1)} %get-tuple-element.57.g_ref.refs_3_), channel_id=1, source_target_pairs={{0,2},{1,3},{2,0},{3,1},{4,6},{5,7},{6,4},{7,5},{8,10},{9,11},{10,... | collective-permute-start | bytes 393224 | tf_op jit(solution)/shard_map/ppermute | solution.py:21
  57.6 7.1 %collective-permute-start.24 = (bf16[128,256]{1,0:T(8,128)(2,1)S(1)}, bf16[128,256]{1,0:T(8,128)(2,1)S(1)}, u32[]{:S(2)}, u32[]{:S(2)}) collective-permute-start(bf16[128,256]{1,0:T(8,128)(2,1)S(1)} %get-tuple-element.61.refs_0_), channel_id=1, source_target_pairs={{0,8},{4,12},{8,0},{12,4},{16,24},{20,28},{24,16},{28,20},{1,9},{5... | collective-permute-start | bytes 196616 | tf_op jit(solution)/shard_map/ppermute | solution.py:21
  58.9 5.9 %collective-permute-start.25 = (bf16[128,256]{1,0:T(8,128)(2,1)S(1)}, bf16[128,256]{1,0:T(8,128)(2,1)S(1)}, u32[]{:S(2)}, u32[]{:S(2)}) collective-permute-start(bf16[128,256]{1,0:T(8,128)(2,1)S(1)} %get-tuple-element.61.refs_0_), channel_id=1, source_target_pairs={{0,16},{4,20},{8,24},{12,28},{16,0},{20,4},{24,8},{28,12},{1,17},{... | collective-permute-start | bytes 196616 | tf_op jit(solution)/shard_map/ppermute | solution.py:21
  60.3 5.2 %collective-permute-start.26 = (bf16[128,256]{1,0:T(8,128)(2,1)S(1)}, bf16[128,256]{1,0:T(8,128)(2,1)S(1)}, u32[]{:S(2)}, u32[]{:S(2)}) collective-permute-start(bf16[128,256]{1,0:T(8,128)(2,1)S(1)} %get-tuple-element.61.refs_0_), channel_id=1, source_target_pairs={{0,24},{4,28},{8,16},{12,20},{16,8},{20,12},{24,0},{28,4},{1,25},{... | collective-permute-start | bytes 196616 | tf_op jit(solution)/shard_map/ppermute | solution.py:21
  66.8 2.0 %collective-permute-start.27 = (bf16[4,256,256]{2,1,0:T(8,128)(2,1)S(1)}, bf16[4,256,256]{2,1,0:T(8,128)(2,1)S(1)}, u32[]{:S(2)}, u32[]{:S(2)}) collective-permute-start(bf16[4,256,256]{2,1,0:T(8,128)(2,1)S(1)} %get-tuple-element.63._), channel_id=1, source_target_pairs={{0,4},{4,0},{8,12},{12,8},{16,20},{20,16},{24,28},{28,24},{1,5},{5... | collective-permute-start | bytes 1572872 | tf_op jit(solution)/shard_map/ppermute | solution.py:21
  66.9 5.5 %collective-permute-start.28 = (bf16[128,256]{1,0:T(8,128)(2,1)S(1)}, bf16[128,256]{1,0:T(8,128)(2,1)S(1)}, u32[]{:S(2)}, u32[]{:S(2)}) collective-permute-start(bf16[128,256]{1,0:T(8,128)(2,1)S(1)} %shard_map.128._.x_ref), channel_id=1, source_target_pairs={{0,1},{1,0},{2,3},{3,2},{4,5},{5,4},{6,7},{7,6},{8,9},{9,8},{10,11... | collective-permute-start | bytes 196616 | tf_op jit(solution)/shard_map/ppermute | solution.py:21
  68.8 9.1 %collective-permute-start.31 = (bf16[256,256]{1,0:T(8,128)(2,1)S(1)}, bf16[256,256]{1,0:T(8,128)(2,1)S(1)}, u32[]{:S(2)}, u32[]{:S(2)}) collective-permute-start(bf16[256,256]{1,0:T(8,128)(2,1)S(1)} %get-tuple-element.66), channel_id=1, source_target_pairs={{0,24},{4,28},{8,16},{12,20},{16,8},{20,12},{24,0},{28,4},{1,25},{... | collective-permute-start | bytes 393224 | tf_op jit(solution)/shard_map/ppermute | solution.py:21
  70.1 8.5 %collective-permute-start.29 = (bf16[256,256]{1,0:T(8,128)(2,1)S(1)}, bf16[256,256]{1,0:T(8,128)(2,1)S(1)}, u32[]{:S(2)}, u32[]{:S(2)}) collective-permute-start(bf16[256,256]{1,0:T(8,128)(2,1)S(1)} %get-tuple-element.64._), channel_id=1, source_target_pairs={{0,8},{4,12},{8,0},{12,4},{16,24},{20,28},{24,16},{28,20},{1,9},{5... | collective-permute-start | bytes 393224 | tf_op jit(solution)/shard_map/ppermute | solution.py:21
  72.1 6.5 %collective-permute-start.30 = (bf16[256,256]{1,0:T(8,128)(2,1)S(1)}, bf16[256,256]{1,0:T(8,128)(2,1)S(1)}, u32[]{:S(2)}, u32[]{:S(2)}) collective-permute-start(bf16[256,256]{1,0:T(8,128)(2,1)S(1)} %get-tuple-element.65), channel_id=1, source_target_pairs={{0,16},{4,20},{8,24},{12,28},{16,0},{20,4},{24,8},{28,12},{1,17},{... | collective-permute-start | bytes 393224 | tf_op jit(solution)/shard_map/ppermute | solution.py:21
  72.4 5.6 %collective-permute-start.32 = (bf16[128,256]{1,0:T(8,128)(2,1)S(1)}, bf16[128,256]{1,0:T(8,128)(2,1)S(1)}, u32[]{:S(2)}, u32[]{:S(2)}) collective-permute-start(bf16[128,256]{1,0:T(8,128)(2,1)S(1)} %shard_map.131._.x_ref), channel_id=1, source_target_pairs={{0,2},{1,3},{2,0},{3,1},{4,6},{5,7},{6,4},{7,5},{8,10},{9,11},{10,... | collective-permute-start | bytes 196616 | tf_op jit(solution)/shard_map/ppermute | solution.py:21
  78.0 1.5 %collective-permute-start.33 = (bf16[64,256]{1,0:T(8,128)(2,1)S(1)}, bf16[64,256]{1,0:T(8,128)(2,1)S(1)}, u32[]{:S(2)}, u32[]{:S(2)}) collective-permute-start(bf16[64,256]{1,0:T(8,128)(2,1)S(1)} %get-tuple-element.67.refs_0_), channel_id=1, source_target_pairs={{0,4},{4,0},{8,12},{12,8},{16,20},{20,16},{24,28},{28,24},{1,5},{5... | collective-permute-start | bytes 98312 | tf_op jit(solution)/shard_map/ppermute | solution.py:21
  78.1 1.5 %collective-permute-start.34 = (bf16[64,256]{1,0:T(8,128)(2,1)S(1)}, bf16[64,256]{1,0:T(8,128)(2,1)S(1)}, u32[]{:S(2)}, u32[]{:S(2)}) collective-permute-start(bf16[64,256]{1,0:T(8,128)(2,1)S(1)} %get-tuple-element.68.refs_1_), channel_id=1, source_target_pairs={{0,4},{4,0},{8,12},{12,8},{16,20},{20,16},{24,28},{28,24},{1,5},{5... | collective-permute-start | bytes 98312 | tf_op jit(solution)/shard_map/ppermute | solution.py:21

commit v7 on v6

--- a/solution.py
+++ b/solution.py
@@ -52,8 +52,7 @@
 
 
 def later_kernel(x_ref, *refs):
-    out = refs[-1]
-    out[...] = x_ref[...]
+    refs[-1][...] = x_ref[...]
 
 
 def add_kernel(x_ref, y_ref, _, *outs):
@@ -64,7 +63,7 @@
 
 
 def stack_kernel(own, *refs):
-    refs, (_, out) = refs[:-2], refs[-2:]
+    refs, out = refs[:-3], refs[-1]
     span = own.shape[0]
     half = span // 2
     out[:half, :] = own[half:, :]
@@ -72,8 +71,9 @@
         out[pl.ds(half + i * span, span), :] = ref[...]
 
 
-def lists_kernel(held, spare, mine, theirs, _, which, code, which2, code2, count):
+def lists_kernel(held, spare, mine, theirs, _, which, code, which2, code2, made, count):
     r = lax.axis_index("row")
+    made[...] = jnp.zeros_like(made)
     for refs in ((which, code), (which2, code2)):
         for i in range(refs[0].shape[0]):
             refs[0][i] = 0
@@ -98,7 +98,7 @@
 
         return 0
 
-    lax.fori_loop(0, mine.shape[1], place, 0)
+    lax.fori_loop(0, mine.shape[1], place, 0, unroll=True)
 
 
 def aggregate_kernel(n_row, n_col, a_ref, own, other, *refs):
@@ -311,10 +311,21 @@
     beside = swap(nodes, "row", 1)
     near = [swap(nodes, "row", t) for t in chips[:0:-1]][::-1]
     (history,) = call(later_kernel, [shape(*history.shape)], [history, beside, tiles])
+    blocks_held = history.shape[0] // BLK
+    places = len(chips) * CAP
+    which, code, which2, code2, made = pl.pallas_call(
+        functools.partial(lists_kernel, blocks_held, row_count),
+        out_shape=[shape(places, dtype=jnp.int32)] * 4 + [shape(8, 128, dtype=F32)],
+        in_specs=[SCALARS] * 2 + [WHOLE],
+        out_specs=[SCALARS] * 4 + [WHOLE],
+        scratch_shapes=[pltpu.SMEM((n_row,), jnp.int32)],
+        compiler_params=pltpu.CompilerParams(vmem_limit_bytes=4 << 20),
+    )(pulls, their_pulls, history)
+
     (stacked,) = call(
         stack_kernel,
         [shape(span // 2 + len(near) * span, hid)],
-        [nodes, *near, history],
+        [nodes, *near, history, made],
     )
     across = swap(stacked, "row", 1)
 
@@ -325,17 +336,6 @@
         [shape(columns, hid)],
     )
     keep, received, halved = reduce_columns(keep, send)
-
-    blocks_held = history.shape[0] // BLK
-    places = len(chips) * CAP
-    which, code, which2, code2 = pl.pallas_call(
-        functools.partial(lists_kernel, blocks_held, row_count),
-        out_shape=[shape(places, dtype=jnp.int32)] * 4,
-        in_specs=[SCALARS] * 2 + [WHOLE],
-        out_specs=[SCALARS] * 4,
-        scratch_shapes=[pltpu.SMEM((n_row,), jnp.int32)],
-        compiler_params=pltpu.CompilerParams(vmem_limit_bytes=4 << 20),
-    )(pulls, their_pulls, halved)
 
     middle = history.shape[0] // 2
     bits = [1 << b for b in range(1, n_row.bit_length() - 1)]

time: 80.5 us -> 78.8 us (0.979)
  waiting for transfers between devices: 30.6 us -> 27.5 us
  starting transfers between devices: 33.9 us -> 35.5 us
    ppermute x35, waiting for transfers between devices: 30.6 us -> 27.5 us  [swap(): return lax.ppermute(x, axis, [(i, i ^ offset) for i in range(size)])]
    ppermute x35, starting transfers between devices: 33.9 us -> 35.5 us  [swap(): return lax.ppermute(x, axis, [(i, i ^ offset) for i in range(size)])]
    unnamed x20 -> x14, local copies, waits for them, and re-layouts: 3.35 us -> 2.86 us
  transfers between devices with their start and end apart: 35 -> 35, of which waited for: 14 -> 14; matrix products, arithmetic and copies ran while one was open for 0% -> 1% of each run, Pallas kernels for 11% -> 11%
where the time goes in v7:
time: 78.8 us; the launch traced here: 78.6 us
  starting transfers between devices  35.5 us (45%)
  waiting for transfers between devices  27.5 us (35%)
  Pallas kernels  11.1 us (14%)
  local copies, waits for them, and re-layouts  2.86 us (4%)
  between operations  0.97 us (1%)
    ppermute x35, starting transfers between devices, swap(): return lax.ppermute(x, axis, [(i, i ^ offset) for i in range(size)])  35.5 us
    ppermute x35, waiting for transfers between devices, swap(): return lax.ppermute(x, axis, [(i, i ^ offset) for i in range(size)])  27.5 us
    pallas_call x23, Pallas kernels, call(): pl.pallas_call(kernel, out_shape=outs, in_specs=[SCALARS] * len(lists) +...  9.06 us
    unnamed x14, local copies, waits for them, and re-layouts  2.86 us
    pallas_call x1, Pallas kernels, local(): pl.pallas_call(functools.partial(lists_kernel, blocks_held, row_count), o...  2.03 us
  transfers between devices with their start and end apart: 35, of which 14 were waited for; matrix products, arithmetic and copies ran while one was open for 1% of the time, Pallas kernels for 11%

profile of v7, /device:TPU:0, one launch (start us, length us, event | category | flops | bytes accessed | tf_op | source)
XLA Modules:
  0.0 78.6 jit_solution(5251021673506118184)
XLA Ops:
  0.6 0.5 collective-permute-start.4
  1.1 0.1 collective-permute-start
  1.2 2.9 %collective-permute-start.1 = (bf16[256,256]{1,0:T(8,128)(2,1)}, bf16[256,256]{1,0:T(8,128)(2,1)S(1)}, u32[]{:S(2)}, u32[]{:S(2)}) collective-permute-start(bf16[256,256]{1,0:T(8,128)(2,1)} %own.3), channel_id=1, source_target_pairs={{0,8},{4,12},{8,0},{12,4},{16,24},{20,28},{24,16},{28,20},{1,9},{5... | collective-permute-start | bytes 393224 | tf_op jit(solution)/shard_map/ppermute | solution.py:21
  4.1 1.5 %collective-permute-start.2 = (bf16[256,256]{1,0:T(8,128)(2,1)}, bf16[256,256]{1,0:T(8,128)(2,1)S(1)}, u32[]{:S(2)}, u32[]{:S(2)}) collective-permute-start(bf16[256,256]{1,0:T(8,128)(2,1)} %own.3), channel_id=1, source_target_pairs={{0,16},{4,20},{8,24},{12,28},{16,0},{20,4},{24,8},{28,12},{1,17},{... | collective-permute-start | bytes 393224 | tf_op jit(solution)/shard_map/ppermute | solution.py:21
  5.7 0.7 pad_add_fusion.mine
  6.4 0.1 collective-permute-start.5
  6.5 1.0 %copy-done.2 = bf16[1024,256]{1,0:T(8,128)(2,1)S(1)} copy-done((bf16[1024,256]{1,0:T(8,128)(2,1)S(1)}, bf16[1024,256]{1,0:T(8,128)(2,1)}, u32[]{:S(2)}) %copy-start.2) | copy-done | bytes 524312
  7.5 2.0 %collective-permute-start.9 = (bf16[1024,256]{1,0:T(8,128)(2,1)S(1)}, bf16[1024,256]{1,0:T(8,128)(2,1)S(1)}, u32[]{:S(2)}, u32[]{:S(2)}) collective-permute-start(bf16[1024,256]{1,0:T(8,128)(2,1)S(1)} %shard_map.112._.refs_3_.refs_0_), channel_id=1, source_target_pairs={{0,8},{4,12},{8,0},{12,4},{16,24},{20,28},{24,16},{28,20},{1,9},{5... | collective-permute-start | bytes 1572872 | tf_op jit(solution)/shard_map/ppermute | solution.py:21
  9.6 1.5 %collective-permute-start.10 = (bf16[1024,256]{1,0:T(8,128)(2,1)S(1)}, bf16[1024,256]{1,0:T(8,128)(2,1)S(1)}, u32[]{:S(2)}, u32[]{:S(2)}) collective-permute-start(bf16[1024,256]{1,0:T(8,128)(2,1)S(1)} %shard_map.112._.refs_3_.refs_0_), channel_id=1, source_target_pairs={{0,16},{4,20},{8,24},{12,28},{16,0},{20,4},{24,8},{28,12},{1,17},{... | collective-permute-start | bytes 1572872 | tf_op jit(solution)/shard_map/ppermute | solution.py:21
  11.1 2.0 %shard_map.113 = (s32[16]{0:T(128)S(1)}, s32[16]{0:T(128)S(1)}, s32[16]{0:T(128)S(1)}, s32[16]{0:T(128)S(1)}, f32[8,128]{1,0:T(8,128)S(1)}) custom-call(s32[3,32]{1,0:T(4,128)S(1)} %pad_add_fusion.mine, s32[3,32]{1,0:T(4,128)S(1)} %collective-permute-done.5.theirs, bf16[1024,256]{1,0:T(8,128)(2,1)S(1)} %shard_map.112._.refs_3_.refs_0_), custom_call_target="tpu_custom_call" | custom-call | tf_op jit(solution)/shard_map/pallas_call | solution.py:316
  13.2 0.9 %copy-done.4 = bf16[256,256]{1,0:T(8,128)(2,1)S(1)} copy-done((bf16[256,256]{1,0:T(8,128)(2,1)S(1)}, bf16[256,256]{1,0:T(8,128)(2,1)}, u32[]{:S(2)}) %copy-start.4) | copy-done | bytes 131096
  14.1 0.1 collective-permute-start.6
  14.2 1.8 %collective-permute-done.6.refs_3_ = bf16[896,256]{1,0:T(8,128)(2,1)S(1)} collective-permute-done((bf16[896,256]{1,0:T(8,128)(2,1)S(1)}, bf16[896,256]{1,0:T(8,128)(2,1)S(1)}, u32[]{:S(2)}, u32[]{:S(2)}) %collective-permute-start.6) | collective-permute-done | bytes 458784 | tf_op jit(solution)/shard_map/ppermute | solution.py:21
  16.0 0.9 %copy-done.5 = bf16[256,256]{1,0:T(8,128)(2,1)S(1)} copy-done((bf16[256,256]{1,0:T(8,128)(2,1)S(1)}, bf16[256,256]{1,0:T(8,128)(2,1)}, u32[]{:S(2)}) %copy-start.5) | copy-done | bytes 131096
  16.9 1.3 %shard_map.115 = (f32[2,256,256]{2,1,0:T(8,128)S(1)}, bf16[2,256,256]{2,1,0:T(8,128)(2,1)S(1)}) custom-call(bf16[1024,2048]{1,0:T(8,128)(2,1)S(1)} %copy-done, bf16[256,256]{1,0:T(8,128)(2,1)S(1)} %copy-done.5, bf16[256,256]{1,0:T(8,128)(2,1)S(1)} %collective-permute-done.refs_0_.other, bf16[256,256]{1,0:T(8,128)(2,1)S(1)} %collective-permute-done.1.refs_0_, ...), custom_call_target="tpu_custom_call" | custom-call | tf_op jit(solution)/shard_map/pallas_call | solution.py:39
  18.2 1.6 %collective-permute-start.7 = (bf16[2,256,256]{2,1,0:T(8,128)(2,1)S(1)}, bf16[2,256,256]{2,1,0:T(8,128)(2,1)S(1)}, u32[]{:S(2)}, u32[]{:S(2)}) collective-permute-start(bf16[2,256,256]{2,1,0:T(8,128)(2,1)S(1)} %get-tuple-element.39), channel_id=1, source_target_pairs={{0,1},{1,0},{2,3},{3,2},{4,5},{5,4},{6,7},{7,6},{8,9},{9,8},{10,11... | collective-permute-start | bytes 786440 | tf_op jit(solution)/shard_map/ppermute | solution.py:21
  19.9 2.3 %collective-permute-done.9.refs_1_.x_ref = bf16[1024,256]{1,0:T(8,128)(2,1)S(1)} collective-permute-done((bf16[1024,256]{1,0:T(8,128)(2,1)S(1)}, bf16[1024,256]{1,0:T(8,128)(2,1)S(1)}, u32[]{:S(2)}, u32[]{:S(2)}) %collective-permute-start.9) | collective-permute-done | bytes 524320 | tf_op jit(solution)/shard_map/ppermute | solution.py:21
  22.2 1.8 %collective-permute-start.11 = (bf16[512,256]{1,0:T(8,128)(2,1)S(1)}, bf16[512,256]{1,0:T(8,128)(2,1)S(1)}, u32[]{:S(2)}, u32[]{:S(2)}) collective-permute-start(bf16[512,256]{1,0:T(8,128)(2,1)S(1)} %shard_map.119), channel_id=1, source_target_pairs={{0,16},{4,20},{8,24},{12,28},{16,0},{20,4},{24,8},{28,12},{1,17},{... | collective-permute-start | bytes 786440 | tf_op jit(solution)/shard_map/ppermute | solution.py:21
  24.1 1.5 %collective-permute-start.12 = (bf16[512,256]{1,0:T(8,128)(2,1)S(1)}, bf16[512,256]{1,0:T(8,128)(2,1)S(1)}, u32[]{:S(2)}, u32[]{:S(2)}) collective-permute-start(bf16[512,256]{1,0:T(8,128)(2,1)S(1)} %shard_map.120), channel_id=1, source_target_pairs={{0,8},{4,12},{8,0},{12,4},{16,24},{20,28},{24,16},{28,20},{1,9},{5... | collective-permute-start | bytes 786440 | tf_op jit(solution)/shard_map/ppermute | solution.py:21
  25.6 1.2 %shard_map.117 = (f32[1152,256]{1,0:T(8,128)S(1)}, f32[1152,256]{1,0:T(8,128)S(1)}) custom-call(s32[16]{0:T(128)S(1)} %get-tuple-element.42.which, s32[16]{0:T(128)S(1)} %get-tuple-element.43.code, s32[16]{0:T(128)S(1)} %get-tuple-element.44.which2.which, s32[16]{0:T(128)S(1)} %get-tuple-element.45.code2.code, bf16[32,128,128]{2,1,0:T(8,128)(2,1)S(1)} %copy-done.1, ...), custom_call_target="tpu_custom_call" | custom-call | tf_op jit(solution)/shard_map/pallas_call | solution.py:39
  26.9 2.7 %collective-permute-start.8 = (bf16[1,256,256]{2,1,0:T(8,128)(2,1)S(1)}, bf16[1,256,256]{2,1,0:T(8,128)(2,1)S(1)}, u32[]{:S(2)}, u32[]{:S(2)}) collective-permute-start(bf16[1,256,256]{2,1,0:T(8,128)(2,1)S(1)} %get-tuple-element.41), channel_id=1, source_target_pairs={{0,2},{1,3},{2,0},{3,1},{4,6},{5,7},{6,4},{7,5},{8,10},{9,11},{10,... | collective-permute-start | bytes 393224 | tf_op jit(solution)/shard_map/ppermute | solution.py:21
  29.6 0.8 %collective-permute-done.11.refs_0_ = bf16[512,256]{1,0:T(8,128)(2,1)S(1)} collective-permute-done((bf16[512,256]{1,0:T(8,128)(2,1)S(1)}, bf16[512,256]{1,0:T(8,128)(2,1)S(1)}, u32[]{:S(2)}, u32[]{:S(2)}) %collective-permute-start.11) | collective-permute-done | bytes 262176 | tf_op jit(solution)/shard_map/ppermute | solution.py:21
  30.4 1.4 %collective-permute-done.12.refs_1_ = bf16[512,256]{1,0:T(8,128)(2,1)S(1)} collective-permute-done((bf16[512,256]{1,0:T(8,128)(2,1)S(1)}, bf16[512,256]{1,0:T(8,128)(2,1)S(1)}, u32[]{:S(2)}, u32[]{:S(2)}) %collective-permute-start.12) | collective-permute-done | bytes 262176 | tf_op jit(solution)/shard_map/ppermute | solution.py:21
  31.8 0.8 %shard_map.122 = (bf16[256,256]{1,0:T(8,128)(2,1)S(1)}, bf16[256,256]{1,0:T(8,128)(2,1)S(1)}, bf16[256,256]{1,0:T(8,128)(2,1)S(1)}, bf16[256,256]{1,0:T(8,128)(2,1)S(1)}) custom-call(s32[16]{0:T(128)S(1)} %get-tuple-element.44.which2.which, s32[16]{0:T(128)S(1)} %get-tuple-element.45.code2.code, f32[1152,256]{1,0:T(8,128)S(1)} %get-tuple-element.48.acc_in, ...), custom_call_target="tpu_custom_call" | custom-call | tf_op jit(solution)/shard_map/pallas_call | solution.py:39
  32.7 0.1 collective-permute-start.13
  32.7 0.5 collective-permute-start.14
  33.2 0.1 collective-permute-start.15
  33.3 0.4 collective-permute-start.16
  33.8 0.8 %shard_map.121.own = f32[1152,256]{1,0:T(8,128)S(1)} custom-call(s32[16]{0:T(128)S(1)} %get-tuple-element.42.which, s32[16]{0:T(128)S(1)} %get-tuple-element.43.code, f32[1152,256]{1,0:T(8,128)S(1)} %get-tuple-element.46._.acc_in, bf16[32,128,128]{2,1,0:T(8,128)(2,1)S(1)} %copy-done.1, bf16[512,256]{1,0:T(8,128)(2,1)S(1)} %collective-permute-done.11.refs_0_, ...), custom_call_target="tpu_custom_call" | custom-call | tf_op jit(solution)/shard_map/pallas_call | solution.py:39
  34.6 0.7 collective-permute-done.8.received
  35.2 0.2 shard_map.118
  35.5 0.2 shard_map.123
  35.7 3.6 %collective-permute-start.17 = (bf16[256,256]{1,0:T(8,128)(2,1)S(1)}, bf16[256,256]{1,0:T(8,128)(2,1)S(1)}, u32[]{:S(2)}, u32[]{:S(2)}) collective-permute-start(bf16[256,256]{1,0:T(8,128)(2,1)S(1)} %get-tuple-element.54), channel_id=1, source_target_pairs={{0,3},{1,2},{2,1},{3,0},{4,7},{5,6},{6,5},{7,4},{8,11},{9,10},{10,... | collective-permute-start | bytes 393224 | tf_op jit(solution)/shard_map/ppermute | solution.py:21
  39.3 0.9 %collective-permute-start.19 = (bf16[256,256]{1,0:T(8,128)(2,1)S(1)}, bf16[256,256]{1,0:T(8,128)(2,1)S(1)}, u32[]{:S(2)}, u32[]{:S(2)}) collective-permute-start(bf16[256,256]{1,0:T(8,128)(2,1)S(1)} %get-tuple-element.56), channel_id=1, source_target_pairs={{0,2},{1,3},{2,0},{3,1},{4,6},{5,7},{6,4},{7,5},{8,10},{9,11},{10,... | collective-permute-start | bytes 393224 | tf_op jit(solution)/shard_map/ppermute | solution.py:21
  40.2 3.8 %collective-permute-done.17.refs_0_ = bf16[256,256]{1,0:T(8,128)(2,1)S(1)} collective-permute-done((bf16[256,256]{1,0:T(8,128)(2,1)S(1)}, bf16[256,256]{1,0:T(8,128)(2,1)S(1)}, u32[]{:S(2)}, u32[]{:S(2)}) %collective-permute-start.17) | collective-permute-done | bytes 131104 | tf_op jit(solution)/shard_map/ppermute | solution.py:21
  44.0 2.2 %collective-permute-done.18.refs_1_ = bf16[256,256]{1,0:T(8,128)(2,1)S(1)} collective-permute-done((bf16[256,256]{1,0:T(8,128)(2,1)S(1)}, bf16[256,256]{1,0:T(8,128)(2,1)S(1)}, u32[]{:S(2)}, u32[]{:S(2)}) %collective-permute-start.18) | collective-permute-done | bytes 131104 | tf_op jit(solution)/shard_map/ppermute | solution.py:21
  46.2 4.0 %collective-permute-done.19.refs_2_ = bf16[256,256]{1,0:T(8,128)(2,1)S(1)} collective-permute-done((bf16[256,256]{1,0:T(8,128)(2,1)S(1)}, bf16[256,256]{1,0:T(8,128)(2,1)S(1)}, u32[]{:S(2)}, u32[]{:S(2)}) %collective-permute-start.19) | collective-permute-done | bytes 131104 | tf_op jit(solution)/shard_map/ppermute | solution.py:21
  50.2 0.2 shard_map.124
  50.4 2.5 %collective-permute-start.21 = (bf16[256,256]{1,0:T(8,128)(2,1)S(1)}, bf16[256,256]{1,0:T(8,128)(2,1)S(1)}, u32[]{:S(2)}, u32[]{:S(2)}) collective-permute-start(bf16[256,256]{1,0:T(8,128)(2,1)S(1)} %get-tuple-element.59.g_ref.refs_3_), channel_id=1, source_target_pairs={{0,3},{1,2},{2,1},{3,0},{4,7},{5,6},{6,5},{7,4},{8,11},{9,10},{10,... | collective-permute-start | bytes 393224 | tf_op jit(solution)/shard_map/ppermute | solution.py:21
  52.9 0.2 shard_map.125
  53.2 0.1 collective-permute-start.20
  53.2 0.1 collective-permute-start.22
  53.3 1.9 %collective-permute-start.23 = (bf16[256,256]{1,0:T(8,128)(2,1)S(1)}, bf16[256,256]{1,0:T(8,128)(2,1)S(1)}, u32[]{:S(2)}, u32[]{:S(2)}) collective-permute-start(bf16[256,256]{1,0:T(8,128)(2,1)S(1)} %get-tuple-element.59.g_ref.refs_3_), channel_id=1, source_target_pairs={{0,2},{1,3},{2,0},{3,1},{4,6},{5,7},{6,4},{7,5},{8,10},{9,11},{10,... | collective-permute-start | bytes 393224 | tf_op jit(solution)/shard_map/ppermute | solution.py:21
  55.2 0.7 shard_map.126
  55.9 1.4 %collective-permute-start.24 = (bf16[128,256]{1,0:T(8,128)(2,1)S(1)}, bf16[128,256]{1,0:T(8,128)(2,1)S(1)}, u32[]{:S(2)}, u32[]{:S(2)}) collective-permute-start(bf16[128,256]{1,0:T(8,128)(2,1)S(1)} %get-tuple-element.63.refs_0_), channel_id=1, source_target_pairs={{0,8},{4,12},{8,0},{12,4},{16,24},{20,28},{24,16},{28,20},{1,9},{5... | collective-permute-start | bytes 196616 | tf_op jit(solution)/shard_map/ppermute | solution.py:21
  57.3 0.6 collective-permute-start.25
  57.9 0.6 collective-permute-done.21.refs_0_
  58.6 1.4 %collective-permute-start.26 = (bf16[128,256]{1,0:T(8,128)(2,1)S(1)}, bf16[128,256]{1,0:T(8,128)(2,1)S(1)}, u32[]{:S(2)}, u32[]{:S(2)}) collective-permute-start(bf16[128,256]{1,0:T(8,128)(2,1)S(1)} %get-tuple-element.63.refs_0_), channel_id=1, source_target_pairs={{0,24},{4,28},{8,16},{12,20},{16,8},{20,12},{24,0},{28,4},{1,25},{... | collective-permute-start | bytes 196616 | tf_op jit(solution)/shard_map/ppermute | solution.py:21
  60.0 2.3 %collective-permute-done.22.refs_1_ = bf16[256,256]{1,0:T(8,128)(2,1)S(1)} collective-permute-done((bf16[256,256]{1,0:T(8,128)(2,1)S(1)}, bf16[256,256]{1,0:T(8,128)(2,1)S(1)}, u32[]{:S(2)}, u32[]{:S(2)}) %collective-permute-start.22) | collective-permute-done | bytes 131104 | tf_op jit(solution)/shard_map/ppermute | solution.py:21
  62.4 1.2 %collective-permute-done.23.refs_2_ = bf16[256,256]{1,0:T(8,128)(2,1)S(1)} collective-permute-done((bf16[256,256]{1,0:T(8,128)(2,1)S(1)}, bf16[256,256]{1,0:T(8,128)(2,1)S(1)}, u32[]{:S(2)}, u32[]{:S(2)}) %collective-permute-start.23) | collective-permute-done | bytes 131104 | tf_op jit(solution)/shard_map/ppermute | solution.py:21
  63.6 0.1 collective-permute-done.26.refs_3_
  63.8 1.3 %shard_map.129 = (bf16[4,256,256]{2,1,0:T(8,128)(2,1)S(1)}, f32[4,256,256]{2,1,0:T(8,128)S(1)}) custom-call(bf16[1024,2048]{1,0:T(8,128)(2,1)S(1)} %copy-done, bf16[256,1024]{1,0:T(8,128)(2,1)S(1)} %shard_map.127.refs_4_.g_ref, bf16[128,256]{1,0:T(8,128)(2,1)S(1)} %shard_map.128._.x_ref), custom_call_target="tpu_custom_call" | custom-call | tf_op jit(solution)/shard_map/pallas_call | solution.py:39
  65.1 0.1 collective-permute-start.27
  65.2 0.1 collective-permute-start.28
  65.2 1.8 %collective-permute-done.27.received = bf16[4,256,256]{2,1,0:T(8,128)(2,1)S(1)} collective-permute-done((bf16[4,256,256]{2,1,0:T(8,128)(2,1)S(1)}, bf16[4,256,256]{2,1,0:T(8,128)(2,1)S(1)}, u32[]{:S(2)}, u32[]{:S(2)}) %collective-permute-start.27) | collective-permute-done | bytes 524320 | tf_op jit(solution)/shard_map/ppermute | solution.py:21
  67.1 1.5 %collective-permute-start.31 = (bf16[256,256]{1,0:T(8,128)(2,1)S(1)}, bf16[256,256]{1,0:T(8,128)(2,1)S(1)}, u32[]{:S(2)}, u32[]{:S(2)}) collective-permute-start(bf16[256,256]{1,0:T(8,128)(2,1)S(1)} %get-tuple-element.68), channel_id=1, source_target_pairs={{0,24},{4,28},{8,16},{12,20},{16,8},{20,12},{24,0},{28,4},{1,25},{... | collective-permute-start | bytes 393224 | tf_op jit(solution)/shard_map/ppermute | solution.py:21
  68.6 1.0 %collective-permute-start.29 = (bf16[256,256]{1,0:T(8,128)(2,1)S(1)}, bf16[256,256]{1,0:T(8,128)(2,1)S(1)}, u32[]{:S(2)}, u32[]{:S(2)}) collective-permute-start(bf16[256,256]{1,0:T(8,128)(2,1)S(1)} %get-tuple-element.66._), channel_id=1, source_target_pairs={{0,8},{4,12},{8,0},{12,4},{16,24},{20,28},{24,16},{28,20},{1,9},{5... | collective-permute-start | bytes 393224 | tf_op jit(solution)/shard_map/ppermute | solution.py:21
  69.7 1.0 %collective-permute-start.30 = (bf16[256,256]{1,0:T(8,128)(2,1)S(1)}, bf16[256,256]{1,0:T(8,128)(2,1)S(1)}, u32[]{:S(2)}, u32[]{:S(2)}) collective-permute-start(bf16[256,256]{1,0:T(8,128)(2,1)S(1)} %get-tuple-element.67), channel_id=1, source_target_pairs={{0,16},{4,20},{8,24},{12,28},{16,0},{20,4},{24,8},{28,12},{1,17},{... | collective-permute-start | bytes 393224 | tf_op jit(solution)/shard_map/ppermute | solution.py:21
  70.7 1.3 %collective-permute-start.32 = (bf16[128,256]{1,0:T(8,128)(2,1)S(1)}, bf16[128,256]{1,0:T(8,128)(2,1)S(1)}, u32[]{:S(2)}, u32[]{:S(2)}) collective-permute-start(bf16[128,256]{1,0:T(8,128)(2,1)S(1)} %shard_map.131._.x_ref), channel_id=1, source_target_pairs={{0,2},{1,3},{2,0},{3,1},{4,6},{5,7},{6,4},{7,5},{8,10},{9,11},{10,... | collective-permute-start | bytes 196616 | tf_op jit(solution)/shard_map/ppermute | solution.py:21
  72.0 4.3 %collective-permute-done.32.y_ref = bf16[128,256]{1,0:T(8,128)(2,1)S(1)} collective-permute-done((bf16[128,256]{1,0:T(8,128)(2,1)S(1)}, bf16[128,256]{1,0:T(8,128)(2,1)S(1)}, u32[]{:S(2)}, u32[]{:S(2)}) %collective-permute-start.32) | collective-permute-done | bytes 65568 | tf_op jit(solution)/shard_map/ppermute | solution.py:21
  76.3 0.1 collective-permute-start.33
  76.4 0.5 collective-permute-start.34
  76.9 0.9 %shard_map.133 = bf16[256,256]{1,0:T(8,128)(2,1)} custom-call(bf16[256,256]{1,0:T(8,128)(2,1)S(1)} %copy-done.3, f32[256,256]{1,0:T(8,128)S(1)} %shard_map.132.refs_0_, bf16[256,256]{1,0:T(8,128)(2,1)S(1)} %collective-permute-done.29.refs_1_, bf16[256,256]{1,0:T(8,128)(2,1)S(1)} %collective-permute-done.30.refs_2_, ...), custom_call_target="tpu_custom_call" | custom-call | tf_op jit(solution)/shard_map/pallas_call | solution.py:39
  77.8 0.7 shard_map.135
  (45 shorter events, 0.5 us)
Async XLA Ops:
  0.6 5.8 %collective-permute-start.4 = (bf16[32,128,128]{2,1,0:T(8,128)(2,1)}, bf16[32,128,128]{2,1,0:T(8,128)(2,1)S(1)}, u32[]{:S(2)}, u32[]{:S(2)}) collective-permute-start(bf16[32,128,128]{2,1,0:T(8,128)(2,1)} %tiles.3), channel_id=1, source_target_pairs={{0,4},{4,0},{8,12},{12,8},{16,20},{20,16},{24,28},{28,24},{1,5},{5... | collective-permute-start | bytes 3145736 | tf_op jit(solution)/shard_map/ppermute | solution.py:21
  1.1 5.2 %collective-permute-start = (bf16[256,256]{1,0:T(8,128)(2,1)}, bf16[256,256]{1,0:T(8,128)(2,1)S(1)}, u32[]{:S(2)}, u32[]{:S(2)}) collective-permute-start(bf16[256,256]{1,0:T(8,128)(2,1)} %own.3), channel_id=1, source_target_pairs={{0,4},{4,0},{8,12},{12,8},{16,20},{20,16},{24,28},{28,24},{1,5},{5... | collective-permute-start | bytes 393224 | tf_op jit(solution)/shard_map/ppermute | solution.py:21
  1.2 11.9 %collective-permute-start.1 = (bf16[256,256]{1,0:T(8,128)(2,1)}, bf16[256,256]{1,0:T(8,128)(2,1)S(1)}, u32[]{:S(2)}, u32[]{:S(2)}) collective-permute-start(bf16[256,256]{1,0:T(8,128)(2,1)} %own.3), channel_id=1, source_target_pairs={{0,8},{4,12},{8,0},{12,4},{16,24},{20,28},{24,16},{28,20},{1,9},{5... | collective-permute-start | bytes 393224 | tf_op jit(solution)/shard_map/ppermute | solution.py:21
  4.1 9.0 %collective-permute-start.2 = (bf16[256,256]{1,0:T(8,128)(2,1)}, bf16[256,256]{1,0:T(8,128)(2,1)S(1)}, u32[]{:S(2)}, u32[]{:S(2)}) collective-permute-start(bf16[256,256]{1,0:T(8,128)(2,1)} %own.3), channel_id=1, source_target_pairs={{0,16},{4,20},{8,24},{12,28},{16,0},{20,4},{24,8},{28,12},{1,17},{... | collective-permute-start | bytes 393224 | tf_op jit(solution)/shard_map/ppermute | solution.py:21
  5.7 7.5 %collective-permute-start.3 = (bf16[256,256]{1,0:T(8,128)(2,1)}, bf16[256,256]{1,0:T(8,128)(2,1)S(1)}, u32[]{:S(2)}, u32[]{:S(2)}) collective-permute-start(bf16[256,256]{1,0:T(8,128)(2,1)} %own.3), channel_id=1, source_target_pairs={{0,24},{4,28},{8,16},{12,20},{16,8},{20,12},{24,0},{28,4},{1,25},{... | collective-permute-start | bytes 393224 | tf_op jit(solution)/shard_map/ppermute | solution.py:21
  6.4 3.2 %collective-permute-start.5 = (s32[3,32]{1,0:T(4,128)S(1)}, s32[3,32]{1,0:T(4,128)S(1)}, u32[]{:S(2)}, u32[]{:S(2)}) collective-permute-start(s32[3,32]{1,0:T(4,128)S(1)} %pad_add_fusion.mine), channel_id=1, source_target_pairs={{0,4},{4,0},{8,12},{12,8},{16,20},{20,16},{24,28},{28,24},{1,5},{5... | collective-permute-start | bytes 1160 | tf_op jit(solution)/shard_map/ppermute | solution.py:21
  6.5 1.0 %copy-start.2 = (bf16[1024,256]{1,0:T(8,128)(2,1)S(1)}, bf16[1024,256]{1,0:T(8,128)(2,1)}, u32[]{:S(2)}) copy-start(bf16[1024,256]{1,0:T(8,128)(2,1)} %x_ref.1) | copy-start | bytes 1572868
  7.5 8.5 %copy-start = (bf16[1024,2048]{1,0:T(8,128)(2,1)S(1)}, bf16[1024,2048]{1,0:T(8,128)(2,1)}, u32[]{:S(2)}) copy-start(bf16[1024,2048]{1,0:T(8,128)(2,1)} %a_ref.3) | copy-start | bytes 12582916
  7.5 14.6 %collective-permute-start.9 = (bf16[1024,256]{1,0:T(8,128)(2,1)S(1)}, bf16[1024,256]{1,0:T(8,128)(2,1)S(1)}, u32[]{:S(2)}, u32[]{:S(2)}) collective-permute-start(bf16[1024,256]{1,0:T(8,128)(2,1)S(1)} %shard_map.112._.refs_3_.refs_0_), channel_id=1, source_target_pairs={{0,8},{4,12},{8,0},{12,4},{16,24},{20,28},{24,16},{28,20},{1,9},{5... | collective-permute-start | bytes 1572872 | tf_op jit(solution)/shard_map/ppermute | solution.py:21
  9.6 14.5 %collective-permute-start.10 = (bf16[1024,256]{1,0:T(8,128)(2,1)S(1)}, bf16[1024,256]{1,0:T(8,128)(2,1)S(1)}, u32[]{:S(2)}, u32[]{:S(2)}) collective-permute-start(bf16[1024,256]{1,0:T(8,128)(2,1)S(1)} %shard_map.112._.refs_3_.refs_0_), channel_id=1, source_target_pairs={{0,16},{4,20},{8,24},{12,28},{16,0},{20,4},{24,8},{28,12},{1,17},{... | collective-permute-start | bytes 1572872 | tf_op jit(solution)/shard_map/ppermute | solution.py:21
  13.2 0.9 %copy-start.4 = (bf16[256,256]{1,0:T(8,128)(2,1)S(1)}, bf16[256,256]{1,0:T(8,128)(2,1)}, u32[]{:S(2)}) copy-start(bf16[256,256]{1,0:T(8,128)(2,1)} %own.3) | copy-start | bytes 393220
  14.1 1.9 %collective-permute-start.6 = (bf16[896,256]{1,0:T(8,128)(2,1)S(1)}, bf16[896,256]{1,0:T(8,128)(2,1)S(1)}, u32[]{:S(2)}, u32[]{:S(2)}) collective-permute-start(bf16[896,256]{1,0:T(8,128)(2,1)S(1)} %shard_map.114), channel_id=1, source_target_pairs={{0,4},{4,0},{8,12},{12,8},{16,20},{20,16},{24,28},{28,24},{1,5},{5... | collective-permute-start | bytes 1376264 | tf_op jit(solution)/shard_map/ppermute | solution.py:21
  16.0 0.9 %copy-start.5 = (bf16[256,256]{1,0:T(8,128)(2,1)S(1)}, bf16[256,256]{1,0:T(8,128)(2,1)}, u32[]{:S(2)}) copy-start(bf16[256,256]{1,0:T(8,128)(2,1)} %own.3) | copy-start | bytes 393220
  18.2 7.4 %copy-start.1 = (bf16[32,128,128]{2,1,0:T(8,128)(2,1)S(1)}, bf16[32,128,128]{2,1,0:T(8,128)(2,1)}, u32[]{:S(2)}) copy-start(bf16[32,128,128]{2,1,0:T(8,128)(2,1)} %tiles.3) | copy-start | bytes 3145732
  18.2 8.6 %collective-permute-start.7 = (bf16[2,256,256]{2,1,0:T(8,128)(2,1)S(1)}, bf16[2,256,256]{2,1,0:T(8,128)(2,1)S(1)}, u32[]{:S(2)}, u32[]{:S(2)}) collective-permute-start(bf16[2,256,256]{2,1,0:T(8,128)(2,1)S(1)} %get-tuple-element.39), channel_id=1, source_target_pairs={{0,1},{1,0},{2,3},{3,2},{4,5},{5,4},{6,7},{7,6},{8,9},{9,8},{10,11... | collective-permute-start | bytes 786440 | tf_op jit(solution)/shard_map/ppermute | solution.py:21
  22.2 8.2 %collective-permute-start.11 = (bf16[512,256]{1,0:T(8,128)(2,1)S(1)}, bf16[512,256]{1,0:T(8,128)(2,1)S(1)}, u32[]{:S(2)}, u32[]{:S(2)}) collective-permute-start(bf16[512,256]{1,0:T(8,128)(2,1)S(1)} %shard_map.119), channel_id=1, source_target_pairs={{0,16},{4,20},{8,24},{12,28},{16,0},{20,4},{24,8},{28,12},{1,17},{... | collective-permute-start | bytes 786440 | tf_op jit(solution)/shard_map/ppermute | solution.py:21
  24.1 7.7 %collective-permute-start.12 = (bf16[512,256]{1,0:T(8,128)(2,1)S(1)}, bf16[512,256]{1,0:T(8,128)(2,1)S(1)}, u32[]{:S(2)}, u32[]{:S(2)}) collective-permute-start(bf16[512,256]{1,0:T(8,128)(2,1)S(1)} %shard_map.120), channel_id=1, source_target_pairs={{0,8},{4,12},{8,0},{12,4},{16,24},{20,28},{24,16},{28,20},{1,9},{5... | collective-permute-start | bytes 786440 | tf_op jit(solution)/shard_map/ppermute | solution.py:21
  26.9 8.3 %collective-permute-start.8 = (bf16[1,256,256]{2,1,0:T(8,128)(2,1)S(1)}, bf16[1,256,256]{2,1,0:T(8,128)(2,1)S(1)}, u32[]{:S(2)}, u32[]{:S(2)}) collective-permute-start(bf16[1,256,256]{2,1,0:T(8,128)(2,1)S(1)} %get-tuple-element.41), channel_id=1, source_target_pairs={{0,2},{1,3},{2,0},{3,1},{4,6},{5,7},{6,4},{7,5},{8,10},{9,11},{10,... | collective-permute-start | bytes 393224 | tf_op jit(solution)/shard_map/ppermute | solution.py:21
  32.7 2.8 %collective-permute-start.13 = (bf16[256,256]{1,0:T(8,128)(2,1)S(1)}, bf16[256,256]{1,0:T(8,128)(2,1)S(1)}, u32[]{:S(2)}, u32[]{:S(2)}) collective-permute-start(bf16[256,256]{1,0:T(8,128)(2,1)S(1)} %get-tuple-element.49), channel_id=1, source_target_pairs={{0,4},{4,0},{8,12},{12,8},{16,20},{20,16},{24,28},{28,24},{1,5},{5... | collective-permute-start | bytes 393224 | tf_op jit(solution)/shard_map/ppermute | solution.py:21
  32.7 2.8 %collective-permute-start.14 = (bf16[256,256]{1,0:T(8,128)(2,1)S(1)}, bf16[256,256]{1,0:T(8,128)(2,1)S(1)}, u32[]{:S(2)}, u32[]{:S(2)}) collective-permute-start(bf16[256,256]{1,0:T(8,128)(2,1)S(1)} %get-tuple-element.50), channel_id=1, source_target_pairs={{0,4},{4,0},{8,12},{12,8},{16,20},{20,16},{24,28},{28,24},{1,5},{5... | collective-permute-start | bytes 393224 | tf_op jit(solution)/shard_map/ppermute | solution.py:21
  33.2 2.3 %collective-permute-start.15 = (bf16[256,256]{1,0:T(8,128)(2,1)S(1)}, bf16[256,256]{1,0:T(8,128)(2,1)S(1)}, u32[]{:S(2)}, u32[]{:S(2)}) collective-permute-start(bf16[256,256]{1,0:T(8,128)(2,1)S(1)} %get-tuple-element.51), channel_id=1, source_target_pairs={{0,4},{4,0},{8,12},{12,8},{16,20},{20,16},{24,28},{28,24},{1,5},{5... | collective-permute-start | bytes 393224 | tf_op jit(solution)/shard_map/ppermute | solution.py:21
  33.3 2.2 %collective-permute-start.16 = (bf16[256,256]{1,0:T(8,128)(2,1)S(1)}, bf16[256,256]{1,0:T(8,128)(2,1)S(1)}, u32[]{:S(2)}, u32[]{:S(2)}) collective-permute-start(bf16[256,256]{1,0:T(8,128)(2,1)S(1)} %get-tuple-element.52), channel_id=1, source_target_pairs={{0,4},{4,0},{8,12},{12,8},{16,20},{20,16},{24,28},{28,24},{1,5},{5... | collective-permute-start | bytes 393224 | tf_op jit(solution)/shard_map/ppermute | solution.py:21
  33.8 1.5 %copy-start.3 = (bf16[256,256]{1,0:T(8,128)(2,1)S(1)}, bf16[256,256]{1,0:T(8,128)(2,1)}, u32[]{:S(2)}) copy-start(bf16[256,256]{1,0:T(8,128)(2,1)} %w_ref.3) | copy-start | bytes 393220
  35.5 14.7 %copy-start.6 = (bf16[256,256]{1,0:T(8,128)(2,1)S(1)}, bf16[256,256]{1,0:T(8,128)(2,1)}, u32[]{:S(2)}) copy-start(bf16[256,256]{1,0:T(8,128)(2,1)} %cotangent.1) | copy-start | bytes 393220
  35.7 8.3 %collective-permute-start.17 = (bf16[256,256]{1,0:T(8,128)(2,1)S(1)}, bf16[256,256]{1,0:T(8,128)(2,1)S(1)}, u32[]{:S(2)}, u32[]{:S(2)}) collective-permute-start(bf16[256,256]{1,0:T(8,128)(2,1)S(1)} %get-tuple-element.54), channel_id=1, source_target_pairs={{0,3},{1,2},{2,1},{3,0},{4,7},{5,6},{6,5},{7,4},{8,11},{9,10},{10,... | collective-permute-start | bytes 393224 | tf_op jit(solution)/shard_map/ppermute | solution.py:21
  39.3 7.0 %collective-permute-start.18 = (bf16[256,256]{1,0:T(8,128)(2,1)S(1)}, bf16[256,256]{1,0:T(8,128)(2,1)S(1)}, u32[]{:S(2)}, u32[]{:S(2)}) collective-permute-start(bf16[256,256]{1,0:T(8,128)(2,1)S(1)} %get-tuple-element.55), channel_id=1, source_target_pairs={{0,1},{1,0},{2,3},{3,2},{4,5},{5,4},{6,7},{7,6},{8,9},{9,8},{10,11... | collective-permute-start | bytes 393224 | tf_op jit(solution)/shard_map/ppermute | solution.py:21
  39.3 10.9 %collective-permute-start.19 = (bf16[256,256]{1,0:T(8,128)(2,1)S(1)}, bf16[256,256]{1,0:T(8,128)(2,1)S(1)}, u32[]{:S(2)}, u32[]{:S(2)}) collective-permute-start(bf16[256,256]{1,0:T(8,128)(2,1)S(1)} %get-tuple-element.56), channel_id=1, source_target_pairs={{0,2},{1,3},{2,0},{3,1},{4,6},{5,7},{6,4},{7,5},{8,10},{9,11},{10,... | collective-permute-start | bytes 393224 | tf_op jit(solution)/shard_map/ppermute | solution.py:21
  50.4 8.2 %collective-permute-start.21 = (bf16[256,256]{1,0:T(8,128)(2,1)S(1)}, bf16[256,256]{1,0:T(8,128)(2,1)S(1)}, u32[]{:S(2)}, u32[]{:S(2)}) collective-permute-start(bf16[256,256]{1,0:T(8,128)(2,1)S(1)} %get-tuple-element.59.g_ref.refs_3_), channel_id=1, source_target_pairs={{0,3},{1,2},{2,1},{3,0},{4,7},{5,6},{6,5},{7,4},{8,11},{9,10},{10,... | collective-permute-start | bytes 393224 | tf_op jit(solution)/shard_map/ppermute | solution.py:21
  53.2 2.1 %collective-permute-start.20 = (bf16[128,256]{1,0:T(8,128)(2,1)S(1)}, bf16[128,256]{1,0:T(8,128)(2,1)S(1)}, u32[]{:S(2)}, u32[]{:S(2)}) collective-permute-start(bf16[128,256]{1,0:T(8,128)(2,1)S(1)} %get-tuple-element.61), channel_id=1, source_target_pairs={{0,4},{4,0},{8,12},{12,8},{16,20},{20,16},{24,28},{28,24},{1,5},{5... | collective-permute-start | bytes 196616 | tf_op jit(solution)/shard_map/ppermute | solution.py:21
  53.2 9.1 %collective-permute-start.22 = (bf16[256,256]{1,0:T(8,128)(2,1)S(1)}, bf16[256,256]{1,0:T(8,128)(2,1)S(1)}, u32[]{:S(2)}, u32[]{:S(2)}) collective-permute-start(bf16[256,256]{1,0:T(8,128)(2,1)S(1)} %get-tuple-element.59.g_ref.refs_3_), channel_id=1, source_target_pairs={{0,1},{1,0},{2,3},{3,2},{4,5},{5,4},{6,7},{7,6},{8,9},{9,8},{10,11... | collective-permute-start | bytes 393224 | tf_op jit(solution)/shard_map/ppermute | solution.py:21
  53.3 10.2 %collective-permute-start.23 = (bf16[256,256]{1,0:T(8,128)(2,1)S(1)}, bf16[256,256]{1,0:T(8,128)(2,1)S(1)}, u32[]{:S(2)}, u32[]{:S(2)}) collective-permute-start(bf16[256,256]{1,0:T(8,128)(2,1)S(1)} %get-tuple-element.59.g_ref.refs_3_), channel_id=1, source_target_pairs={{0,2},{1,3},{2,0},{3,1},{4,6},{5,7},{6,4},{7,5},{8,10},{9,11},{10,... | collective-permute-start | bytes 393224 | tf_op jit(solution)/shard_map/ppermute | solution.py:21
  55.9 7.7 %collective-permute-start.24 = (bf16[128,256]{1,0:T(8,128)(2,1)S(1)}, bf16[128,256]{1,0:T(8,128)(2,1)S(1)}, u32[]{:S(2)}, u32[]{:S(2)}) collective-permute-start(bf16[128,256]{1,0:T(8,128)(2,1)S(1)} %get-tuple-element.63.refs_0_), channel_id=1, source_target_pairs={{0,8},{4,12},{8,0},{12,4},{16,24},{20,28},{24,16},{28,20},{1,9},{5... | collective-permute-start | bytes 196616 | tf_op jit(solution)/shard_map/ppermute | solution.py:21
  57.3 6.3 %collective-permute-start.25 = (bf16[128,256]{1,0:T(8,128)(2,1)S(1)}, bf16[128,256]{1,0:T(8,128)(2,1)S(1)}, u32[]{:S(2)}, u32[]{:S(2)}) collective-permute-start(bf16[128,256]{1,0:T(8,128)(2,1)S(1)} %get-tuple-element.63.refs_0_), channel_id=1, source_target_pairs={{0,16},{4,20},{8,24},{12,28},{16,0},{20,4},{24,8},{28,12},{1,17},{... | collective-permute-start | bytes 196616 | tf_op jit(solution)/shard_map/ppermute | solution.py:21
  58.6 5.2 %collective-permute-start.26 = (bf16[128,256]{1,0:T(8,128)(2,1)S(1)}, bf16[128,256]{1,0:T(8,128)(2,1)S(1)}, u32[]{:S(2)}, u32[]{:S(2)}) collective-permute-start(bf16[128,256]{1,0:T(8,128)(2,1)S(1)} %get-tuple-element.63.refs_0_), channel_id=1, source_target_pairs={{0,24},{4,28},{8,16},{12,20},{16,8},{20,12},{24,0},{28,4},{1,25},{... | collective-permute-start | bytes 196616 | tf_op jit(solution)/shard_map/ppermute | solution.py:21
  65.1 2.0 %collective-permute-start.27 = (bf16[4,256,256]{2,1,0:T(8,128)(2,1)S(1)}, bf16[4,256,256]{2,1,0:T(8,128)(2,1)S(1)}, u32[]{:S(2)}, u32[]{:S(2)}) collective-permute-start(bf16[4,256,256]{2,1,0:T(8,128)(2,1)S(1)} %get-tuple-element.65._), channel_id=1, source_target_pairs={{0,4},{4,0},{8,12},{12,8},{16,20},{20,16},{24,28},{28,24},{1,5},{5... | collective-permute-start | bytes 1572872 | tf_op jit(solution)/shard_map/ppermute | solution.py:21
  65.2 5.5 %collective-permute-start.28 = (bf16[128,256]{1,0:T(8,128)(2,1)S(1)}, bf16[128,256]{1,0:T(8,128)(2,1)S(1)}, u32[]{:S(2)}, u32[]{:S(2)}) collective-permute-start(bf16[128,256]{1,0:T(8,128)(2,1)S(1)} %shard_map.128._.x_ref), channel_id=1, source_target_pairs={{0,1},{1,0},{2,3},{3,2},{4,5},{5,4},{6,7},{7,6},{8,9},{9,8},{10,11... | collective-permute-start | bytes 196616 | tf_op jit(solution)/shard_map/ppermute | solution.py:21
  67.1 9.1 %collective-permute-start.31 = (bf16[256,256]{1,0:T(8,128)(2,1)S(1)}, bf16[256,256]{1,0:T(8,128)(2,1)S(1)}, u32[]{:S(2)}, u32[]{:S(2)}) collective-permute-start(bf16[256,256]{1,0:T(8,128)(2,1)S(1)} %get-tuple-element.68), channel_id=1, source_target_pairs={{0,24},{4,28},{8,16},{12,20},{16,8},{20,12},{24,0},{28,4},{1,25},{... | collective-permute-start | bytes 393224 | tf_op jit(solution)/shard_map/ppermute | solution.py:21
  68.6 8.3 %collective-permute-start.29 = (bf16[256,256]{1,0:T(8,128)(2,1)S(1)}, bf16[256,256]{1,0:T(8,128)(2,1)S(1)}, u32[]{:S(2)}, u32[]{:S(2)}) collective-permute-start(bf16[256,256]{1,0:T(8,128)(2,1)S(1)} %get-tuple-element.66._), channel_id=1, source_target_pairs={{0,8},{4,12},{8,0},{12,4},{16,24},{20,28},{24,16},{28,20},{1,9},{5... | collective-permute-start | bytes 393224 | tf_op jit(solution)/shard_map/ppermute | solution.py:21
  69.7 7.3 %collective-permute-start.30 = (bf16[256,256]{1,0:T(8,128)(2,1)S(1)}, bf16[256,256]{1,0:T(8,128)(2,1)S(1)}, u32[]{:S(2)}, u32[]{:S(2)}) collective-permute-start(bf16[256,256]{1,0:T(8,128)(2,1)S(1)} %get-tuple-element.67), channel_id=1, source_target_pairs={{0,16},{4,20},{8,24},{12,28},{16,0},{20,4},{24,8},{28,12},{1,17},{... | collective-permute-start | bytes 393224 | tf_op jit(solution)/shard_map/ppermute | solution.py:21
  70.7 5.6 %collective-permute-start.32 = (bf16[128,256]{1,0:T(8,128)(2,1)S(1)}, bf16[128,256]{1,0:T(8,128)(2,1)S(1)}, u32[]{:S(2)}, u32[]{:S(2)}) collective-permute-start(bf16[128,256]{1,0:T(8,128)(2,1)S(1)} %shard_map.131._.x_ref), channel_id=1, source_target_pairs={{0,2},{1,3},{2,0},{3,1},{4,6},{5,7},{6,4},{7,5},{8,10},{9,11},{10,... | collective-permute-start | bytes 196616 | tf_op jit(solution)/shard_map/ppermute | solution.py:21
  76.3 1.5 %collective-permute-start.33 = (bf16[64,256]{1,0:T(8,128)(2,1)S(1)}, bf16[64,256]{1,0:T(8,128)(2,1)S(1)}, u32[]{:S(2)}, u32[]{:S(2)}) collective-permute-start(bf16[64,256]{1,0:T(8,128)(2,1)S(1)} %get-tuple-element.69.refs_0_), channel_id=1, source_target_pairs={{0,4},{4,0},{8,12},{12,8},{16,20},{20,16},{24,28},{28,24},{1,5},{5... | collective-permute-start | bytes 98312 | tf_op jit(solution)/shard_map/ppermute | solution.py:21
  76.4 1.5 %collective-permute-start.34 = (bf16[64,256]{1,0:T(8,128)(2,1)S(1)}, bf16[64,256]{1,0:T(8,128)(2,1)S(1)}, u32[]{:S(2)}, u32[]{:S(2)}) collective-permute-start(bf16[64,256]{1,0:T(8,128)(2,1)S(1)} %get-tuple-element.70.refs_1_), channel_id=1, source_target_pairs={{0,4},{4,0},{8,12},{12,8},{16,20},{20,16},{24,28},{28,24},{1,5},{5... | collective-permute-start | bytes 98312 | tf_op jit(solution)/shard_map/ppermute | solution.py:21

commit v8 on v7

--- a/solution.py
+++ b/solution.py
@@ -71,30 +71,29 @@
         out[pl.ds(half + i * span, span), :] = ref[...]
 
 
-def lists_kernel(held, spare, mine, theirs, _, which, code, which2, code2, made, count):
+def lists_kernel(held, spare, mine, theirs, _, code, code2, made, count):
+    pulls_held = mine.shape[1]
     r = lax.axis_index("row")
     made[...] = jnp.zeros_like(made)
-    for refs in ((which, code), (which2, code2)):
-        for i in range(refs[0].shape[0]):
-            refs[0][i] = 0
-            refs[1][i] = spare * held
+    for ref in (code, code2):
+        for i in range(ref.shape[0]):
+            ref[i] = spare * held * pulls_held
     for t in range(count.shape[0]):
         count[t] = 0
 
     def place(k, _):
-        for pulls, refs, at in (
-            (mine, (which, code), 0),
-            (theirs, (which2, code2), count.shape[0] // 2),
+        for pulls, ref, at in (
+            (mine, code, 0),
+            (theirs, code2, count.shape[0] // 2),
         ):
             t = pulls[0, k] ^ r
 
             @pl.when(t % 2 == 0)
-            def _(pulls=pulls, refs=refs, at=at, t=t):
+            def _(pulls=pulls, ref=ref, at=at, t=t):
                 chip = t // 2
                 i = chip * CAP + count[at + chip]
                 count[at + chip] += 1
-                refs[0][i] = k
-                refs[1][i] = pulls[2, k] * held + pulls[1, k]
+                ref[i] = (pulls[2, k] * held + pulls[1, k]) * pulls_held + k
 
         return 0
 
@@ -129,27 +128,18 @@
             keep[i // 2] = block
 
 
-def project_kernel(kept, received, w_ref, _, projected, flipped):
-    total = kept[0] + received[0].astype(F32)
-    high = total.astype(BF16)
-    low = (total - high.astype(F32)).astype(BF16)
-    projected[...] = jnp.dot(high, w_ref[...], preferred_element_type=F32) + jnp.dot(
-        low, w_ref[...], preferred_element_type=F32
-    )
-    flipped[...] = total.T.astype(BF16)
-
-
-def add_pulls(pulls, held, code, tile_of, acc):
-    half = held // 2
+def add_pulls(pulls, held, code, tiles, acc):
+    half, pulls_held = held // 2, tiles.shape[0]
     for i, piece in pulls:
-        slot = code[i] % held
+        k, where = code[i] % pulls_held, code[i] // pulls_held
+        slot = where % held
         if len(piece) == 1:
             block = piece[0][part(slot, BLK), :]
         else:
             inside = part(slot % half, BLK)
             block = jnp.where(slot < half, piece[0][inside, :], piece[1][inside, :])
-        rows = part(code[i] // held, BLK)
-        acc[rows, :] += jnp.dot(tile_of(i), block, preferred_element_type=F32)
+        rows = part(where // held, BLK)
+        acc[rows, :] += jnp.dot(tiles[k], block, preferred_element_type=F32)
 
 
 def slice_kernel(at, x_ref, out):
@@ -164,41 +154,49 @@
     ]
 
 
-def early_kernel(offsets, held, which, code, which2, code2, tiles, tiles2, *refs):
+def early_kernel(offsets, held, code, code2, tiles, tiles2, *refs):
     pieces, (own, others) = [(ref,) for ref in refs[:-2]], refs[-2:]
     pulls = pulls_of(offsets, pieces)
     own[...] = jnp.zeros_like(own)
     others[...] = jnp.zeros_like(others)
-    add_pulls(pulls, held, code2, lambda i: tiles2[which2[i]], others)
-    add_pulls(pulls, held, code, lambda i: tiles[which[i]], own)
-
-
-def others_kernel(offsets, held, count, which, code, acc_in, tiles, *refs):
+    add_pulls(pulls, held, code2, tiles2, others)
+    add_pulls(pulls, held, code, tiles, own)
+
+
+def others_kernel(offsets, held, count, code, acc_in, tiles, *refs):
     refs, outs, acc = refs[: -1 - count], refs[-1 - count : -1], refs[-1]
     pieces = list(zip(refs[::2], refs[1::2], strict=True))
     acc[...] = acc_in[...]
-    add_pulls(pulls_of(offsets, pieces), held, code, lambda i: tiles[which[i]], acc)
+    add_pulls(pulls_of(offsets, pieces), held, code, tiles, acc)
     rows = outs[0].shape[0]
     for i, out in enumerate(outs):
         out[...] = acc[pl.ds(i * rows, rows), :].astype(BF16)
 
 
-def own_kernel(offsets, held, which, code, acc_in, tiles, *refs):
+def own_kernel(offsets, held, code, acc_in, tiles, *refs):
     pieces, out = list(zip(refs[:-1:2], refs[1:-1:2], strict=True)), refs[-1]
     out[...] = acc_in[...]
-    add_pulls(pulls_of(offsets, pieces), held, code, lambda i: tiles[which[i]], out)
-
-
-def merge_kernel(n_col, projected, own, *refs):
-    received, outs, acc = refs[:n_col], refs[n_col:-1], refs[-1]
+    add_pulls(pulls_of(offsets, pieces), held, code, tiles, out)
+
+
+def merge_kernel(n_col, kept, summed, w_ref, own, *refs):
+    received, outs, (flipped, acc) = refs[:n_col], refs[n_col:-2], refs[-2:]
     span = outs[0].shape[0]
     c = lax.axis_index("col")
     for i, ref in enumerate(received):
         rows = pl.ds(i * span, span)
         acc[rows, :] = own[rows, :] + ref[...].astype(F32)
-    for s, out in enumerate(outs):
-        block = acc[part(c ^ s, span), :]
-        out[...] = block.astype(out.dtype) if s else block + projected[...]
+    for s, out in enumerate(outs[1:], 1):
+        out[...] = acc[part(c ^ s, span), :].astype(out.dtype)
+    total = kept[0] + summed[0].astype(F32)
+    high = total.astype(BF16)
+    low = (total - high.astype(F32)).astype(BF16)
+    outs[0][...] = (
+        acc[part(c, span), :]
+        + jnp.dot(high, w_ref[...], preferred_element_type=F32)
+        + jnp.dot(low, w_ref[...], preferred_element_type=F32)
+    )
+    flipped[...] = total.T.astype(BF16)
 
 
 def gradient_kernel(cotangent, kept, *refs):
@@ -313,11 +311,11 @@
     (history,) = call(later_kernel, [shape(*history.shape)], [history, beside, tiles])
     blocks_held = history.shape[0] // BLK
     places = len(chips) * CAP
-    which, code, which2, code2, made = pl.pallas_call(
+    code, code2, made = pl.pallas_call(
         functools.partial(lists_kernel, blocks_held, row_count),
-        out_shape=[shape(places, dtype=jnp.int32)] * 4 + [shape(8, 128, dtype=F32)],
+        out_shape=[shape(places, dtype=jnp.int32)] * 2 + [shape(8, 128, dtype=F32)],
         in_specs=[SCALARS] * 2 + [WHOLE],
-        out_specs=[SCALARS] * 4 + [WHOLE],
+        out_specs=[SCALARS] * 2 + [WHOLE],
         scratch_shapes=[pltpu.SMEM((n_row,), jnp.int32)],
         compiler_params=pltpu.CompilerParams(vmem_limit_bytes=4 << 20),
     )(pulls, their_pulls, history)
@@ -335,7 +333,7 @@
         [adjacency, nodes, beside, *near, across],
         [shape(columns, hid)],
     )
-    keep, received, halved = reduce_columns(keep, send)
+    keep, summed, halved = reduce_columns(keep, send)
 
     middle = history.shape[0] // 2
     bits = [1 << b for b in range(1, n_row.bit_length() - 1)]
@@ -358,31 +356,29 @@
         functools.partial(early_kernel, early, blocks_held),
         [spare, spare],
         [hist_tiles, tiles, *[past[chips[i]] for i in early]],
-        lists=[which, code, which2, code2],
-    )
-    projected, summed = call(
-        project_kernel, [shape(span, hid, dtype=F32), shape(hid, span)], [keep, received, weight, own_terms]
+        lists=[code, code2],
     )
     given = call(
         functools.partial(others_kernel, late, blocks_held, n_col),
         [shape(span, hid)] * n_col,
         [terms, tiles, *forwarded],
         [spare],
-        [which2, code2],
+        [code2],
     )
     received = [swap(x, "row", 1) for x in given]
     (terms,) = call(
         functools.partial(own_kernel, late, blocks_held),
         [spare],
         [own_terms, hist_tiles, *forwarded],
-        lists=[which, code],
-    )
-    keep, *sends = call(
+        lists=[code],
+    )
+    *blocks, summed = call(
         functools.partial(merge_kernel, n_col),
-        [shape(span, hid, dtype=BF16 if s else F32) for s in range(n_col)],
-        [projected, terms, *received],
+        [shape(span, hid, dtype=BF16 if s else F32) for s in range(n_col)] + [shape(hid, span)],
+        [keep, summed, weight, terms, *received],
         [shape(panel, hid, dtype=F32)],
     )
+    keep, *sends = blocks
     mixed, flipped = call(
         gradient_kernel,
         [shape(span, hid, dtype=F32), shape(hid, span)],
@@ -425,7 +421,7 @@
         for i, x in zip(places, sums, strict=True):
             arrived[i] = swap(x, "row", chips[i]) if i else x
         if token is given:
-            beside = swap(halfway, "col", 1)
+            beside = swap(halfway, "col", n_col // 2)
             (token,) = call(add_kernel, [shape(*halfway.shape)], [halfway, beside, sums[0]])
     halfway = token
     (grad_nodes,) = call(
@@ -433,9 +429,9 @@
     )
 
     halfway = [halfway]
-    for bit in [1 << b for b in range(1, n_col.bit_length() - 1)]:
+    for bit in [1 << b for b in range(n_col.bit_length() - 2)][::-1]:
         received = swap(halfway[0], "col", bit)
-        count = 2 if 2 * bit == n_col else 1
+        count = 2 if bit == 1 else 1
         halfway = call(
             add_kernel,
             [shape(hid // 2 // count, hid)] * count,

time: 78.8 us -> 78.8 us (level)
    pallas_call x23 -> x22, Pallas kernels: 9.06 us -> 9.03 us  [call(): pl.pallas_call(kernel, out_shape=outs, in_specs=[SCALARS] * len(lists) +...]
  transfers between devices with their start and end apart: 35 -> 35, of which waited for: 14 -> 15; matrix products, arithmetic and copies ran while one was open for 1% -> 1% of each run, Pallas kernels for 11% -> 11%
where the time goes in v8:
time: 78.8 us; the launch traced here: 78.6 us
  starting transfers between devices  35.2 us (45%)
  waiting for transfers between devices  27.9 us (35%)
  Pallas kernels  11 us (14%)
  local copies, waits for them, and re-layouts  2.86 us (4%)
  between operations  0.95 us (1%)
    ppermute x35, starting transfers between devices, swap(): return lax.ppermute(x, axis, [(i, i ^ offset) for i in range(size)])  35.2 us
    ppermute x35, waiting for transfers between devices, swap(): return lax.ppermute(x, axis, [(i, i ^ offset) for i in range(size)])  27.9 us
    pallas_call x22, Pallas kernels, call(): pl.pallas_call(kernel, out_shape=outs, in_specs=[SCALARS] * len(lists) +...  9.03 us
    unnamed x14, local copies, waits for them, and re-layouts  2.86 us
    pallas_call x1, Pallas kernels, local(): pl.pallas_call(functools.partial(lists_kernel, blocks_held, row_count), o...  1.94 us
  transfers between devices with their start and end apart: 35, of which 15 were waited for; matrix products, arithmetic and copies ran while one was open for 1% of the time, Pallas kernels for 11%

profile of v8, /device:TPU:0, one launch (start us, length us, event | category | flops | bytes accessed | tf_op | source)
XLA Modules:
  0.0 78.6 jit_solution(6512394095497841033)
XLA Ops:
  0.6 0.5 collective-permute-start.4
  1.1 0.1 collective-permute-start
  1.2 2.9 %collective-permute-start.1 = (bf16[256,256]{1,0:T(8,128)(2,1)}, bf16[256,256]{1,0:T(8,128)(2,1)S(1)}, u32[]{:S(2)}, u32[]{:S(2)}) collective-permute-start(bf16[256,256]{1,0:T(8,128)(2,1)} %own.3), channel_id=1, source_target_pairs={{0,8},{4,12},{8,0},{12,4},{16,24},{20,28},{24,16},{28,20},{1,9},{5... | collective-permute-start | bytes 393224 | tf_op jit(solution)/shard_map/ppermute | solution.py:21
  4.1 1.5 %collective-permute-start.2 = (bf16[256,256]{1,0:T(8,128)(2,1)}, bf16[256,256]{1,0:T(8,128)(2,1)S(1)}, u32[]{:S(2)}, u32[]{:S(2)}) collective-permute-start(bf16[256,256]{1,0:T(8,128)(2,1)} %own.3), channel_id=1, source_target_pairs={{0,16},{4,20},{8,24},{12,28},{16,0},{20,4},{24,8},{28,12},{1,17},{... | collective-permute-start | bytes 393224 | tf_op jit(solution)/shard_map/ppermute | solution.py:21
  5.7 0.7 pad_add_fusion.mine
  6.4 0.1 collective-permute-start.5
  6.5 1.0 %copy-done.2 = bf16[1024,256]{1,0:T(8,128)(2,1)S(1)} copy-done((bf16[1024,256]{1,0:T(8,128)(2,1)S(1)}, bf16[1024,256]{1,0:T(8,128)(2,1)}, u32[]{:S(2)}) %copy-start.2) | copy-done | bytes 524312
  7.5 2.0 %collective-permute-start.9 = (bf16[1024,256]{1,0:T(8,128)(2,1)S(1)}, bf16[1024,256]{1,0:T(8,128)(2,1)S(1)}, u32[]{:S(2)}, u32[]{:S(2)}) collective-permute-start(bf16[1024,256]{1,0:T(8,128)(2,1)S(1)} %shard_map.112._.refs_3_.refs_0_), channel_id=1, source_target_pairs={{0,8},{4,12},{8,0},{12,4},{16,24},{20,28},{24,16},{28,20},{1,9},{5... | collective-permute-start | bytes 1572872 | tf_op jit(solution)/shard_map/ppermute | solution.py:21
  9.6 1.5 %collective-permute-start.10 = (bf16[1024,256]{1,0:T(8,128)(2,1)S(1)}, bf16[1024,256]{1,0:T(8,128)(2,1)S(1)}, u32[]{:S(2)}, u32[]{:S(2)}) collective-permute-start(bf16[1024,256]{1,0:T(8,128)(2,1)S(1)} %shard_map.112._.refs_3_.refs_0_), channel_id=1, source_target_pairs={{0,16},{4,20},{8,24},{12,28},{16,0},{20,4},{24,8},{28,12},{1,17},{... | collective-permute-start | bytes 1572872 | tf_op jit(solution)/shard_map/ppermute | solution.py:21
  11.1 1.9 %shard_map.113 = (s32[16]{0:T(128)S(1)}, s32[16]{0:T(128)S(1)}, f32[8,128]{1,0:T(8,128)S(1)}) custom-call(s32[3,32]{1,0:T(4,128)S(1)} %pad_add_fusion.mine, s32[3,32]{1,0:T(4,128)S(1)} %collective-permute-done.5.theirs, bf16[1024,256]{1,0:T(8,128)(2,1)S(1)} %shard_map.112._.refs_3_.refs_0_), custom_call_target="tpu_custom_call" | custom-call | tf_op jit(solution)/shard_map/pallas_call | solution.py:314
  13.1 0.9 %copy-done.4 = bf16[256,256]{1,0:T(8,128)(2,1)S(1)} copy-done((bf16[256,256]{1,0:T(8,128)(2,1)S(1)}, bf16[256,256]{1,0:T(8,128)(2,1)}, u32[]{:S(2)}) %copy-start.4) | copy-done | bytes 131096
  14.0 0.1 collective-permute-start.6
  14.1 1.8 %collective-permute-done.6.refs_3_ = bf16[896,256]{1,0:T(8,128)(2,1)S(1)} collective-permute-done((bf16[896,256]{1,0:T(8,128)(2,1)S(1)}, bf16[896,256]{1,0:T(8,128)(2,1)S(1)}, u32[]{:S(2)}, u32[]{:S(2)}) %collective-permute-start.6) | collective-permute-done | bytes 458784 | tf_op jit(solution)/shard_map/ppermute | solution.py:21
  15.9 0.9 %copy-done.5 = bf16[256,256]{1,0:T(8,128)(2,1)S(1)} copy-done((bf16[256,256]{1,0:T(8,128)(2,1)S(1)}, bf16[256,256]{1,0:T(8,128)(2,1)}, u32[]{:S(2)}) %copy-start.5) | copy-done | bytes 131096
  16.8 1.4 %shard_map.115 = (f32[2,256,256]{2,1,0:T(8,128)S(1)}, bf16[2,256,256]{2,1,0:T(8,128)(2,1)S(1)}) custom-call(bf16[1024,2048]{1,0:T(8,128)(2,1)S(1)} %copy-done, bf16[256,256]{1,0:T(8,128)(2,1)S(1)} %copy-done.5, bf16[256,256]{1,0:T(8,128)(2,1)S(1)} %collective-permute-done.refs_0_.other, bf16[256,256]{1,0:T(8,128)(2,1)S(1)} %collective-permute-done.1.refs_0_, ...), custom_call_target="tpu_custom_call" | custom-call | tf_op jit(solution)/shard_map/pallas_call | solution.py:39
  18.2 1.6 %collective-permute-start.7 = (bf16[2,256,256]{2,1,0:T(8,128)(2,1)S(1)}, bf16[2,256,256]{2,1,0:T(8,128)(2,1)S(1)}, u32[]{:S(2)}, u32[]{:S(2)}) collective-permute-start(bf16[2,256,256]{2,1,0:T(8,128)(2,1)S(1)} %get-tuple-element.36), channel_id=1, source_target_pairs={{0,1},{1,0},{2,3},{3,2},{4,5},{5,4},{6,7},{7,6},{8,9},{9,8},{10,11... | collective-permute-start | bytes 786440 | tf_op jit(solution)/shard_map/ppermute | solution.py:21
  19.8 2.4 %collective-permute-done.9.refs_1_.x_ref = bf16[1024,256]{1,0:T(8,128)(2,1)S(1)} collective-permute-done((bf16[1024,256]{1,0:T(8,128)(2,1)S(1)}, bf16[1024,256]{1,0:T(8,128)(2,1)S(1)}, u32[]{:S(2)}, u32[]{:S(2)}) %collective-permute-start.9) | collective-permute-done | bytes 524320 | tf_op jit(solution)/shard_map/ppermute | solution.py:21
  22.2 1.8 %collective-permute-start.11 = (bf16[512,256]{1,0:T(8,128)(2,1)S(1)}, bf16[512,256]{1,0:T(8,128)(2,1)S(1)}, u32[]{:S(2)}, u32[]{:S(2)}) collective-permute-start(bf16[512,256]{1,0:T(8,128)(2,1)S(1)} %shard_map.118), channel_id=1, source_target_pairs={{0,16},{4,20},{8,24},{12,28},{16,0},{20,4},{24,8},{28,12},{1,17},{... | collective-permute-start | bytes 786440 | tf_op jit(solution)/shard_map/ppermute | solution.py:21
  24.1 1.5 %collective-permute-start.12 = (bf16[512,256]{1,0:T(8,128)(2,1)S(1)}, bf16[512,256]{1,0:T(8,128)(2,1)S(1)}, u32[]{:S(2)}, u32[]{:S(2)}) collective-permute-start(bf16[512,256]{1,0:T(8,128)(2,1)S(1)} %shard_map.119), channel_id=1, source_target_pairs={{0,8},{4,12},{8,0},{12,4},{16,24},{20,28},{24,16},{28,20},{1,9},{5... | collective-permute-start | bytes 786440 | tf_op jit(solution)/shard_map/ppermute | solution.py:21
  25.6 1.3 %shard_map.117 = (f32[1152,256]{1,0:T(8,128)S(1)}, f32[1152,256]{1,0:T(8,128)S(1)}) custom-call(s32[16]{0:T(128)S(1)} %get-tuple-element.39.code, s32[16]{0:T(128)S(1)} %get-tuple-element.40.code2.code, bf16[32,128,128]{2,1,0:T(8,128)(2,1)S(1)} %copy-done.1, bf16[32,128,128]{2,1,0:T(8,128)(2,1)S(1)} %collective-permute-done.4.refs_1_.tiles2.tiles, ...), custom_call_target="tpu_custom_call" | custom-call | tf_op jit(solution)/shard_map/pallas_call | solution.py:39
  27.0 2.7 %collective-permute-start.8 = (bf16[1,256,256]{2,1,0:T(8,128)(2,1)S(1)}, bf16[1,256,256]{2,1,0:T(8,128)(2,1)S(1)}, u32[]{:S(2)}, u32[]{:S(2)}) collective-permute-start(bf16[1,256,256]{2,1,0:T(8,128)(2,1)S(1)} %get-tuple-element.38), channel_id=1, source_target_pairs={{0,2},{1,3},{2,0},{3,1},{4,6},{5,7},{6,4},{7,5},{8,10},{9,11},{10,... | collective-permute-start | bytes 393224 | tf_op jit(solution)/shard_map/ppermute | solution.py:21
  29.6 0.8 collective-permute-done.11.refs_0_
  30.4 1.4 %collective-permute-done.12.refs_1_ = bf16[512,256]{1,0:T(8,128)(2,1)S(1)} collective-permute-done((bf16[512,256]{1,0:T(8,128)(2,1)S(1)}, bf16[512,256]{1,0:T(8,128)(2,1)S(1)}, u32[]{:S(2)}, u32[]{:S(2)}) %collective-permute-start.12) | collective-permute-done | bytes 262176 | tf_op jit(solution)/shard_map/ppermute | solution.py:21
  31.8 0.8 %shard_map.121 = (bf16[256,256]{1,0:T(8,128)(2,1)S(1)}, bf16[256,256]{1,0:T(8,128)(2,1)S(1)}, bf16[256,256]{1,0:T(8,128)(2,1)S(1)}, bf16[256,256]{1,0:T(8,128)(2,1)S(1)}) custom-call(s32[16]{0:T(128)S(1)} %get-tuple-element.40.code2.code, f32[1152,256]{1,0:T(8,128)S(1)} %get-tuple-element.42.acc_in, ...), custom_call_target="tpu_custom_call" | custom-call | tf_op jit(solution)/shard_map/pallas_call | solution.py:39
  32.7 0.1 collective-permute-start.13
  32.7 0.5 collective-permute-start.14
  33.2 0.1 collective-permute-start.15
  33.3 0.4 collective-permute-start.16
  33.8 0.8 %shard_map.120.own = f32[1152,256]{1,0:T(8,128)S(1)} custom-call(s32[16]{0:T(128)S(1)} %get-tuple-element.39.code, f32[1152,256]{1,0:T(8,128)S(1)} %get-tuple-element.41.acc_in, bf16[32,128,128]{2,1,0:T(8,128)(2,1)S(1)} %copy-done.1, bf16[512,256]{1,0:T(8,128)(2,1)S(1)} %collective-permute-done.11.refs_0_, bf16[512,256]{1,0:T(8,128)(2,1)S(1)} %collective-permute-done.12.refs_1_), custom_call_target="tpu_custom_call" | custom-call | tf_op jit(solution)/shard_map/pallas_call | solution.py:39
  34.6 0.7 collective-permute-done.8.summed
  35.3 0.3 shard_map.122
  35.6 3.6 %collective-permute-start.17 = (bf16[256,256]{1,0:T(8,128)(2,1)S(1)}, bf16[256,256]{1,0:T(8,128)(2,1)S(1)}, u32[]{:S(2)}, u32[]{:S(2)}) collective-permute-start(bf16[256,256]{1,0:T(8,128)(2,1)S(1)} %get-tuple-element.48), channel_id=1, source_target_pairs={{0,3},{1,2},{2,1},{3,0},{4,7},{5,6},{6,5},{7,4},{8,11},{9,10},{10,... | collective-permute-start | bytes 393224 | tf_op jit(solution)/shard_map/ppermute | solution.py:21
  39.2 0.9 %collective-permute-start.19 = (bf16[256,256]{1,0:T(8,128)(2,1)S(1)}, bf16[256,256]{1,0:T(8,128)(2,1)S(1)}, u32[]{:S(2)}, u32[]{:S(2)}) collective-permute-start(bf16[256,256]{1,0:T(8,128)(2,1)S(1)} %get-tuple-element.50), channel_id=1, source_target_pairs={{0,2},{1,3},{2,0},{3,1},{4,6},{5,7},{6,4},{7,5},{8,10},{9,11},{10,... | collective-permute-start | bytes 393224 | tf_op jit(solution)/shard_map/ppermute | solution.py:21
  40.1 3.8 %collective-permute-done.17.refs_0_ = bf16[256,256]{1,0:T(8,128)(2,1)S(1)} collective-permute-done((bf16[256,256]{1,0:T(8,128)(2,1)S(1)}, bf16[256,256]{1,0:T(8,128)(2,1)S(1)}, u32[]{:S(2)}, u32[]{:S(2)}) %collective-permute-start.17) | collective-permute-done | bytes 131104 | tf_op jit(solution)/shard_map/ppermute | solution.py:21
  43.9 2.6 %collective-permute-done.18.refs_1_ = bf16[256,256]{1,0:T(8,128)(2,1)S(1)} collective-permute-done((bf16[256,256]{1,0:T(8,128)(2,1)S(1)}, bf16[256,256]{1,0:T(8,128)(2,1)S(1)}, u32[]{:S(2)}, u32[]{:S(2)}) %collective-permute-start.18) | collective-permute-done | bytes 131104 | tf_op jit(solution)/shard_map/ppermute | solution.py:21
  46.4 3.9 %collective-permute-done.19.refs_2_ = bf16[256,256]{1,0:T(8,128)(2,1)S(1)} collective-permute-done((bf16[256,256]{1,0:T(8,128)(2,1)S(1)}, bf16[256,256]{1,0:T(8,128)(2,1)S(1)}, u32[]{:S(2)}, u32[]{:S(2)}) %collective-permute-start.19) | collective-permute-done | bytes 131104 | tf_op jit(solution)/shard_map/ppermute | solution.py:21
  50.3 0.2 shard_map.123
  50.5 2.5 %collective-permute-start.21 = (bf16[256,256]{1,0:T(8,128)(2,1)S(1)}, bf16[256,256]{1,0:T(8,128)(2,1)S(1)}, u32[]{:S(2)}, u32[]{:S(2)}) collective-permute-start(bf16[256,256]{1,0:T(8,128)(2,1)S(1)} %get-tuple-element.53.g_ref.refs_3_), channel_id=1, source_target_pairs={{0,3},{1,2},{2,1},{3,0},{4,7},{5,6},{6,5},{7,4},{8,11},{9,10},{10,... | collective-permute-start | bytes 393224 | tf_op jit(solution)/shard_map/ppermute | solution.py:21
  53.1 0.2 shard_map.124
  53.3 0.1 collective-permute-start.20
  53.4 0.1 collective-permute-start.22
  53.4 1.9 %collective-permute-start.23 = (bf16[256,256]{1,0:T(8,128)(2,1)S(1)}, bf16[256,256]{1,0:T(8,128)(2,1)S(1)}, u32[]{:S(2)}, u32[]{:S(2)}) collective-permute-start(bf16[256,256]{1,0:T(8,128)(2,1)S(1)} %get-tuple-element.53.g_ref.refs_3_), channel_id=1, source_target_pairs={{0,2},{1,3},{2,0},{3,1},{4,6},{5,7},{6,4},{7,5},{8,10},{9,11},{10,... | collective-permute-start | bytes 393224 | tf_op jit(solution)/shard_map/ppermute | solution.py:21
  55.4 0.7 shard_map.125
  56.0 1.4 %collective-permute-start.24 = (bf16[128,256]{1,0:T(8,128)(2,1)S(1)}, bf16[128,256]{1,0:T(8,128)(2,1)S(1)}, u32[]{:S(2)}, u32[]{:S(2)}) collective-permute-start(bf16[128,256]{1,0:T(8,128)(2,1)S(1)} %get-tuple-element.57.refs_0_), channel_id=1, source_target_pairs={{0,8},{4,12},{8,0},{12,4},{16,24},{20,28},{24,16},{28,20},{1,9},{5... | collective-permute-start | bytes 196616 | tf_op jit(solution)/shard_map/ppermute | solution.py:21
  57.5 0.6 collective-permute-start.25
  58.1 0.6 collective-permute-done.21.refs_0_
  58.7 1.4 %collective-permute-start.26 = (bf16[128,256]{1,0:T(8,128)(2,1)S(1)}, bf16[128,256]{1,0:T(8,128)(2,1)S(1)}, u32[]{:S(2)}, u32[]{:S(2)}) collective-permute-start(bf16[128,256]{1,0:T(8,128)(2,1)S(1)} %get-tuple-element.57.refs_0_), channel_id=1, source_target_pairs={{0,24},{4,28},{8,16},{12,20},{16,8},{20,12},{24,0},{28,4},{1,25},{... | collective-permute-start | bytes 196616 | tf_op jit(solution)/shard_map/ppermute | solution.py:21
  60.1 2.3 %collective-permute-done.22.refs_1_ = bf16[256,256]{1,0:T(8,128)(2,1)S(1)} collective-permute-done((bf16[256,256]{1,0:T(8,128)(2,1)S(1)}, bf16[256,256]{1,0:T(8,128)(2,1)S(1)}, u32[]{:S(2)}, u32[]{:S(2)}) %collective-permute-start.22) | collective-permute-done | bytes 131104 | tf_op jit(solution)/shard_map/ppermute | solution.py:21
  62.5 1.2 %collective-permute-done.23.refs_2_ = bf16[256,256]{1,0:T(8,128)(2,1)S(1)} collective-permute-done((bf16[256,256]{1,0:T(8,128)(2,1)S(1)}, bf16[256,256]{1,0:T(8,128)(2,1)S(1)}, u32[]{:S(2)}, u32[]{:S(2)}) %collective-permute-start.23) | collective-permute-done | bytes 131104 | tf_op jit(solution)/shard_map/ppermute | solution.py:21
  63.8 0.1 collective-permute-done.26.refs_3_
  63.9 1.3 %shard_map.128 = (bf16[4,256,256]{2,1,0:T(8,128)(2,1)S(1)}, f32[4,256,256]{2,1,0:T(8,128)S(1)}) custom-call(bf16[1024,2048]{1,0:T(8,128)(2,1)S(1)} %copy-done, bf16[256,1024]{1,0:T(8,128)(2,1)S(1)} %shard_map.126.refs_4_.g_ref, bf16[128,256]{1,0:T(8,128)(2,1)S(1)} %shard_map.127._.x_ref), custom_call_target="tpu_custom_call" | custom-call | tf_op jit(solution)/shard_map/pallas_call | solution.py:39
  65.2 0.1 collective-permute-start.27
  65.3 0.9 %collective-permute-start.28 = (bf16[128,256]{1,0:T(8,128)(2,1)S(1)}, bf16[128,256]{1,0:T(8,128)(2,1)S(1)}, u32[]{:S(2)}, u32[]{:S(2)}) collective-permute-start(bf16[128,256]{1,0:T(8,128)(2,1)S(1)} %shard_map.127._.x_ref), channel_id=1, source_target_pairs={{0,2},{1,3},{2,0},{3,1},{4,6},{5,7},{6,4},{7,5},{8,10},{9,11},{10,... | collective-permute-start | bytes 196616 | tf_op jit(solution)/shard_map/ppermute | solution.py:21
  66.2 1.0 %collective-permute-done.27.received = bf16[4,256,256]{2,1,0:T(8,128)(2,1)S(1)} collective-permute-done((bf16[4,256,256]{2,1,0:T(8,128)(2,1)S(1)}, bf16[4,256,256]{2,1,0:T(8,128)(2,1)S(1)}, u32[]{:S(2)}, u32[]{:S(2)}) %collective-permute-start.27) | collective-permute-done | bytes 524320 | tf_op jit(solution)/shard_map/ppermute | solution.py:21
  67.3 1.5 %collective-permute-start.31 = (bf16[256,256]{1,0:T(8,128)(2,1)S(1)}, bf16[256,256]{1,0:T(8,128)(2,1)S(1)}, u32[]{:S(2)}, u32[]{:S(2)}) collective-permute-start(bf16[256,256]{1,0:T(8,128)(2,1)S(1)} %get-tuple-element.62), channel_id=1, source_target_pairs={{0,24},{4,28},{8,16},{12,20},{16,8},{20,12},{24,0},{28,4},{1,25},{... | collective-permute-start | bytes 393224 | tf_op jit(solution)/shard_map/ppermute | solution.py:21
  68.8 1.0 %collective-permute-start.29 = (bf16[256,256]{1,0:T(8,128)(2,1)S(1)}, bf16[256,256]{1,0:T(8,128)(2,1)S(1)}, u32[]{:S(2)}, u32[]{:S(2)}) collective-permute-start(bf16[256,256]{1,0:T(8,128)(2,1)S(1)} %get-tuple-element.60._), channel_id=1, source_target_pairs={{0,8},{4,12},{8,0},{12,4},{16,24},{20,28},{24,16},{28,20},{1,9},{5... | collective-permute-start | bytes 393224 | tf_op jit(solution)/shard_map/ppermute | solution.py:21
  69.8 1.0 %collective-permute-start.30 = (bf16[256,256]{1,0:T(8,128)(2,1)S(1)}, bf16[256,256]{1,0:T(8,128)(2,1)S(1)}, u32[]{:S(2)}, u32[]{:S(2)}) collective-permute-start(bf16[256,256]{1,0:T(8,128)(2,1)S(1)} %get-tuple-element.61), channel_id=1, source_target_pairs={{0,16},{4,20},{8,24},{12,28},{16,0},{20,4},{24,8},{28,12},{1,17},{... | collective-permute-start | bytes 393224 | tf_op jit(solution)/shard_map/ppermute | solution.py:21
  70.8 1.1 %collective-permute-done.28.y_ref = bf16[128,256]{1,0:T(8,128)(2,1)S(1)} collective-permute-done((bf16[128,256]{1,0:T(8,128)(2,1)S(1)}, bf16[128,256]{1,0:T(8,128)(2,1)S(1)}, u32[]{:S(2)}, u32[]{:S(2)}) %collective-permute-start.28) | collective-permute-done | bytes 65568 | tf_op jit(solution)/shard_map/ppermute | solution.py:21
  71.9 0.2 collective-permute-start.32
  72.1 4.2 %collective-permute-done.32.y_ref = bf16[128,256]{1,0:T(8,128)(2,1)S(1)} collective-permute-done((bf16[128,256]{1,0:T(8,128)(2,1)S(1)}, bf16[128,256]{1,0:T(8,128)(2,1)S(1)}, u32[]{:S(2)}, u32[]{:S(2)}) %collective-permute-start.32) | collective-permute-done | bytes 65568 | tf_op jit(solution)/shard_map/ppermute | solution.py:21
  76.3 0.1 collective-permute-start.33
  76.4 0.5 collective-permute-start.34
  76.9 0.9 %shard_map.132 = bf16[256,256]{1,0:T(8,128)(2,1)} custom-call(bf16[256,256]{1,0:T(8,128)(2,1)S(1)} %copy-done.3, f32[256,256]{1,0:T(8,128)S(1)} %shard_map.131.refs_0_, bf16[256,256]{1,0:T(8,128)(2,1)S(1)} %collective-permute-done.29.refs_1_, bf16[256,256]{1,0:T(8,128)(2,1)S(1)} %collective-permute-done.30.refs_2_, ...), custom_call_target="tpu_custom_call" | custom-call | tf_op jit(solution)/shard_map/pallas_call | solution.py:39
  77.8 0.7 shard_map.134
  (44 shorter events, 0.5 us)
Async XLA Ops:
  0.6 5.8 %collective-permute-start.4 = (bf16[32,128,128]{2,1,0:T(8,128)(2,1)}, bf16[32,128,128]{2,1,0:T(8,128)(2,1)S(1)}, u32[]{:S(2)}, u32[]{:S(2)}) collective-permute-start(bf16[32,128,128]{2,1,0:T(8,128)(2,1)} %tiles.3), channel_id=1, source_target_pairs={{0,4},{4,0},{8,12},{12,8},{16,20},{20,16},{24,28},{28,24},{1,5},{5... | collective-permute-start | bytes 3145736 | tf_op jit(solution)/shard_map/ppermute | solution.py:21
  1.1 5.2 %collective-permute-start = (bf16[256,256]{1,0:T(8,128)(2,1)}, bf16[256,256]{1,0:T(8,128)(2,1)S(1)}, u32[]{:S(2)}, u32[]{:S(2)}) collective-permute-start(bf16[256,256]{1,0:T(8,128)(2,1)} %own.3), channel_id=1, source_target_pairs={{0,4},{4,0},{8,12},{12,8},{16,20},{20,16},{24,28},{28,24},{1,5},{5... | collective-permute-start | bytes 393224 | tf_op jit(solution)/shard_map/ppermute | solution.py:21
  1.2 11.8 %collective-permute-start.1 = (bf16[256,256]{1,0:T(8,128)(2,1)}, bf16[256,256]{1,0:T(8,128)(2,1)S(1)}, u32[]{:S(2)}, u32[]{:S(2)}) collective-permute-start(bf16[256,256]{1,0:T(8,128)(2,1)} %own.3), channel_id=1, source_target_pairs={{0,8},{4,12},{8,0},{12,4},{16,24},{20,28},{24,16},{28,20},{1,9},{5... | collective-permute-start | bytes 393224 | tf_op jit(solution)/shard_map/ppermute | solution.py:21
  4.1 8.9 %collective-permute-start.2 = (bf16[256,256]{1,0:T(8,128)(2,1)}, bf16[256,256]{1,0:T(8,128)(2,1)S(1)}, u32[]{:S(2)}, u32[]{:S(2)}) collective-permute-start(bf16[256,256]{1,0:T(8,128)(2,1)} %own.3), channel_id=1, source_target_pairs={{0,16},{4,20},{8,24},{12,28},{16,0},{20,4},{24,8},{28,12},{1,17},{... | collective-permute-start | bytes 393224 | tf_op jit(solution)/shard_map/ppermute | solution.py:21
  5.7 7.4 %collective-permute-start.3 = (bf16[256,256]{1,0:T(8,128)(2,1)}, bf16[256,256]{1,0:T(8,128)(2,1)S(1)}, u32[]{:S(2)}, u32[]{:S(2)}) collective-permute-start(bf16[256,256]{1,0:T(8,128)(2,1)} %own.3), channel_id=1, source_target_pairs={{0,24},{4,28},{8,16},{12,20},{16,8},{20,12},{24,0},{28,4},{1,25},{... | collective-permute-start | bytes 393224 | tf_op jit(solution)/shard_map/ppermute | solution.py:21
  6.4 3.2 %collective-permute-start.5 = (s32[3,32]{1,0:T(4,128)S(1)}, s32[3,32]{1,0:T(4,128)S(1)}, u32[]{:S(2)}, u32[]{:S(2)}) collective-permute-start(s32[3,32]{1,0:T(4,128)S(1)} %pad_add_fusion.mine), channel_id=1, source_target_pairs={{0,4},{4,0},{8,12},{12,8},{16,20},{20,16},{24,28},{28,24},{1,5},{5... | collective-permute-start | bytes 1160 | tf_op jit(solution)/shard_map/ppermute | solution.py:21
  6.5 1.0 %copy-start.2 = (bf16[1024,256]{1,0:T(8,128)(2,1)S(1)}, bf16[1024,256]{1,0:T(8,128)(2,1)}, u32[]{:S(2)}) copy-start(bf16[1024,256]{1,0:T(8,128)(2,1)} %x_ref.1) | copy-start | bytes 1572868
  7.5 8.4 %copy-start = (bf16[1024,2048]{1,0:T(8,128)(2,1)S(1)}, bf16[1024,2048]{1,0:T(8,128)(2,1)}, u32[]{:S(2)}) copy-start(bf16[1024,2048]{1,0:T(8,128)(2,1)} %a_ref.3) | copy-start | bytes 12582916
  7.5 14.6 %collective-permute-start.9 = (bf16[1024,256]{1,0:T(8,128)(2,1)S(1)}, bf16[1024,256]{1,0:T(8,128)(2,1)S(1)}, u32[]{:S(2)}, u32[]{:S(2)}) collective-permute-start(bf16[1024,256]{1,0:T(8,128)(2,1)S(1)} %shard_map.112._.refs_3_.refs_0_), channel_id=1, source_target_pairs={{0,8},{4,12},{8,0},{12,4},{16,24},{20,28},{24,16},{28,20},{1,9},{5... | collective-permute-start | bytes 1572872 | tf_op jit(solution)/shard_map/ppermute | solution.py:21
  9.6 14.5 %collective-permute-start.10 = (bf16[1024,256]{1,0:T(8,128)(2,1)S(1)}, bf16[1024,256]{1,0:T(8,128)(2,1)S(1)}, u32[]{:S(2)}, u32[]{:S(2)}) collective-permute-start(bf16[1024,256]{1,0:T(8,128)(2,1)S(1)} %shard_map.112._.refs_3_.refs_0_), channel_id=1, source_target_pairs={{0,16},{4,20},{8,24},{12,28},{16,0},{20,4},{24,8},{28,12},{1,17},{... | collective-permute-start | bytes 1572872 | tf_op jit(solution)/shard_map/ppermute | solution.py:21
  13.1 0.9 %copy-start.4 = (bf16[256,256]{1,0:T(8,128)(2,1)S(1)}, bf16[256,256]{1,0:T(8,128)(2,1)}, u32[]{:S(2)}) copy-start(bf16[256,256]{1,0:T(8,128)(2,1)} %own.3) | copy-start | bytes 393220
  14.0 1.9 %collective-permute-start.6 = (bf16[896,256]{1,0:T(8,128)(2,1)S(1)}, bf16[896,256]{1,0:T(8,128)(2,1)S(1)}, u32[]{:S(2)}, u32[]{:S(2)}) collective-permute-start(bf16[896,256]{1,0:T(8,128)(2,1)S(1)} %shard_map.114), channel_id=1, source_target_pairs={{0,4},{4,0},{8,12},{12,8},{16,20},{20,16},{24,28},{28,24},{1,5},{5... | collective-permute-start | bytes 1376264 | tf_op jit(solution)/shard_map/ppermute | solution.py:21
  15.9 0.9 %copy-start.5 = (bf16[256,256]{1,0:T(8,128)(2,1)S(1)}, bf16[256,256]{1,0:T(8,128)(2,1)}, u32[]{:S(2)}) copy-start(bf16[256,256]{1,0:T(8,128)(2,1)} %own.3) | copy-start | bytes 393220
  18.2 7.4 %copy-start.1 = (bf16[32,128,128]{2,1,0:T(8,128)(2,1)S(1)}, bf16[32,128,128]{2,1,0:T(8,128)(2,1)}, u32[]{:S(2)}) copy-start(bf16[32,128,128]{2,1,0:T(8,128)(2,1)} %tiles.3) | copy-start | bytes 3145732
  18.2 8.7 %collective-permute-start.7 = (bf16[2,256,256]{2,1,0:T(8,128)(2,1)S(1)}, bf16[2,256,256]{2,1,0:T(8,128)(2,1)S(1)}, u32[]{:S(2)}, u32[]{:S(2)}) collective-permute-start(bf16[2,256,256]{2,1,0:T(8,128)(2,1)S(1)} %get-tuple-element.36), channel_id=1, source_target_pairs={{0,1},{1,0},{2,3},{3,2},{4,5},{5,4},{6,7},{7,6},{8,9},{9,8},{10,11... | collective-permute-start | bytes 786440 | tf_op jit(solution)/shard_map/ppermute | solution.py:21
  22.2 8.2 %collective-permute-start.11 = (bf16[512,256]{1,0:T(8,128)(2,1)S(1)}, bf16[512,256]{1,0:T(8,128)(2,1)S(1)}, u32[]{:S(2)}, u32[]{:S(2)}) collective-permute-start(bf16[512,256]{1,0:T(8,128)(2,1)S(1)} %shard_map.118), channel_id=1, source_target_pairs={{0,16},{4,20},{8,24},{12,28},{16,0},{20,4},{24,8},{28,12},{1,17},{... | collective-permute-start | bytes 786440 | tf_op jit(solution)/shard_map/ppermute | solution.py:21
  24.1 7.7 %collective-permute-start.12 = (bf16[512,256]{1,0:T(8,128)(2,1)S(1)}, bf16[512,256]{1,0:T(8,128)(2,1)S(1)}, u32[]{:S(2)}, u32[]{:S(2)}) collective-permute-start(bf16[512,256]{1,0:T(8,128)(2,1)S(1)} %shard_map.119), channel_id=1, source_target_pairs={{0,8},{4,12},{8,0},{12,4},{16,24},{20,28},{24,16},{28,20},{1,9},{5... | collective-permute-start | bytes 786440 | tf_op jit(solution)/shard_map/ppermute | solution.py:21
  27.0 8.3 %collective-permute-start.8 = (bf16[1,256,256]{2,1,0:T(8,128)(2,1)S(1)}, bf16[1,256,256]{2,1,0:T(8,128)(2,1)S(1)}, u32[]{:S(2)}, u32[]{:S(2)}) collective-permute-start(bf16[1,256,256]{2,1,0:T(8,128)(2,1)S(1)} %get-tuple-element.38), channel_id=1, source_target_pairs={{0,2},{1,3},{2,0},{3,1},{4,6},{5,7},{6,4},{7,5},{8,10},{9,11},{10,... | collective-permute-start | bytes 393224 | tf_op jit(solution)/shard_map/ppermute | solution.py:21
  32.7 2.6 %collective-permute-start.13 = (bf16[256,256]{1,0:T(8,128)(2,1)S(1)}, bf16[256,256]{1,0:T(8,128)(2,1)S(1)}, u32[]{:S(2)}, u32[]{:S(2)}) collective-permute-start(bf16[256,256]{1,0:T(8,128)(2,1)S(1)} %get-tuple-element.43), channel_id=1, source_target_pairs={{0,4},{4,0},{8,12},{12,8},{16,20},{20,16},{24,28},{28,24},{1,5},{5... | collective-permute-start | bytes 393224 | tf_op jit(solution)/shard_map/ppermute | solution.py:21
  32.7 2.5 %collective-permute-start.14 = (bf16[256,256]{1,0:T(8,128)(2,1)S(1)}, bf16[256,256]{1,0:T(8,128)(2,1)S(1)}, u32[]{:S(2)}, u32[]{:S(2)}) collective-permute-start(bf16[256,256]{1,0:T(8,128)(2,1)S(1)} %get-tuple-element.44), channel_id=1, source_target_pairs={{0,4},{4,0},{8,12},{12,8},{16,20},{20,16},{24,28},{28,24},{1,5},{5... | collective-permute-start | bytes 393224 | tf_op jit(solution)/shard_map/ppermute | solution.py:21
  33.2 2.0 %collective-permute-start.15 = (bf16[256,256]{1,0:T(8,128)(2,1)S(1)}, bf16[256,256]{1,0:T(8,128)(2,1)S(1)}, u32[]{:S(2)}, u32[]{:S(2)}) collective-permute-start(bf16[256,256]{1,0:T(8,128)(2,1)S(1)} %get-tuple-element.45), channel_id=1, source_target_pairs={{0,4},{4,0},{8,12},{12,8},{16,20},{20,16},{24,28},{28,24},{1,5},{5... | collective-permute-start | bytes 393224 | tf_op jit(solution)/shard_map/ppermute | solution.py:21
  33.3 2.0 %collective-permute-start.16 = (bf16[256,256]{1,0:T(8,128)(2,1)S(1)}, bf16[256,256]{1,0:T(8,128)(2,1)S(1)}, u32[]{:S(2)}, u32[]{:S(2)}) collective-permute-start(bf16[256,256]{1,0:T(8,128)(2,1)S(1)} %get-tuple-element.46), channel_id=1, source_target_pairs={{0,4},{4,0},{8,12},{12,8},{16,20},{20,16},{24,28},{28,24},{1,5},{5... | collective-permute-start | bytes 393224 | tf_op jit(solution)/shard_map/ppermute | solution.py:21
  33.8 1.5 %copy-start.3 = (bf16[256,256]{1,0:T(8,128)(2,1)S(1)}, bf16[256,256]{1,0:T(8,128)(2,1)}, u32[]{:S(2)}) copy-start(bf16[256,256]{1,0:T(8,128)(2,1)} %w_ref.3) | copy-start | bytes 393220
  34.6 15.8 %copy-start.6 = (bf16[256,256]{1,0:T(8,128)(2,1)S(1)}, bf16[256,256]{1,0:T(8,128)(2,1)}, u32[]{:S(2)}) copy-start(bf16[256,256]{1,0:T(8,128)(2,1)} %cotangent.1) | copy-start | bytes 393220
  35.6 8.2 %collective-permute-start.17 = (bf16[256,256]{1,0:T(8,128)(2,1)S(1)}, bf16[256,256]{1,0:T(8,128)(2,1)S(1)}, u32[]{:S(2)}, u32[]{:S(2)}) collective-permute-start(bf16[256,256]{1,0:T(8,128)(2,1)S(1)} %get-tuple-element.48), channel_id=1, source_target_pairs={{0,3},{1,2},{2,1},{3,0},{4,7},{5,6},{6,5},{7,4},{8,11},{9,10},{10,... | collective-permute-start | bytes 393224 | tf_op jit(solution)/shard_map/ppermute | solution.py:21
  39.2 7.2 %collective-permute-start.18 = (bf16[256,256]{1,0:T(8,128)(2,1)S(1)}, bf16[256,256]{1,0:T(8,128)(2,1)S(1)}, u32[]{:S(2)}, u32[]{:S(2)}) collective-permute-start(bf16[256,256]{1,0:T(8,128)(2,1)S(1)} %get-tuple-element.49), channel_id=1, source_target_pairs={{0,1},{1,0},{2,3},{3,2},{4,5},{5,4},{6,7},{7,6},{8,9},{9,8},{10,11... | collective-permute-start | bytes 393224 | tf_op jit(solution)/shard_map/ppermute | solution.py:21
  39.2 11.1 %collective-permute-start.19 = (bf16[256,256]{1,0:T(8,128)(2,1)S(1)}, bf16[256,256]{1,0:T(8,128)(2,1)S(1)}, u32[]{:S(2)}, u32[]{:S(2)}) collective-permute-start(bf16[256,256]{1,0:T(8,128)(2,1)S(1)} %get-tuple-element.50), channel_id=1, source_target_pairs={{0,2},{1,3},{2,0},{3,1},{4,6},{5,7},{6,4},{7,5},{8,10},{9,11},{10,... | collective-permute-start | bytes 393224 | tf_op jit(solution)/shard_map/ppermute | solution.py:21
  50.5 8.2 %collective-permute-start.21 = (bf16[256,256]{1,0:T(8,128)(2,1)S(1)}, bf16[256,256]{1,0:T(8,128)(2,1)S(1)}, u32[]{:S(2)}, u32[]{:S(2)}) collective-permute-start(bf16[256,256]{1,0:T(8,128)(2,1)S(1)} %get-tuple-element.53.g_ref.refs_3_), channel_id=1, source_target_pairs={{0,3},{1,2},{2,1},{3,0},{4,7},{5,6},{6,5},{7,4},{8,11},{9,10},{10,... | collective-permute-start | bytes 393224 | tf_op jit(solution)/shard_map/ppermute | solution.py:21
  53.3 2.1 %collective-permute-start.20 = (bf16[128,256]{1,0:T(8,128)(2,1)S(1)}, bf16[128,256]{1,0:T(8,128)(2,1)S(1)}, u32[]{:S(2)}, u32[]{:S(2)}) collective-permute-start(bf16[128,256]{1,0:T(8,128)(2,1)S(1)} %get-tuple-element.55), channel_id=1, source_target_pairs={{0,4},{4,0},{8,12},{12,8},{16,20},{20,16},{24,28},{28,24},{1,5},{5... | collective-permute-start | bytes 196616 | tf_op jit(solution)/shard_map/ppermute | solution.py:21
  53.4 9.1 %collective-permute-start.22 = (bf16[256,256]{1,0:T(8,128)(2,1)S(1)}, bf16[256,256]{1,0:T(8,128)(2,1)S(1)}, u32[]{:S(2)}, u32[]{:S(2)}) collective-permute-start(bf16[256,256]{1,0:T(8,128)(2,1)S(1)} %get-tuple-element.53.g_ref.refs_3_), channel_id=1, source_target_pairs={{0,1},{1,0},{2,3},{3,2},{4,5},{5,4},{6,7},{7,6},{8,9},{9,8},{10,11... | collective-permute-start | bytes 393224 | tf_op jit(solution)/shard_map/ppermute | solution.py:21
  53.4 10.2 %collective-permute-start.23 = (bf16[256,256]{1,0:T(8,128)(2,1)S(1)}, bf16[256,256]{1,0:T(8,128)(2,1)S(1)}, u32[]{:S(2)}, u32[]{:S(2)}) collective-permute-start(bf16[256,256]{1,0:T(8,128)(2,1)S(1)} %get-tuple-element.53.g_ref.refs_3_), channel_id=1, source_target_pairs={{0,2},{1,3},{2,0},{3,1},{4,6},{5,7},{6,4},{7,5},{8,10},{9,11},{10,... | collective-permute-start | bytes 393224 | tf_op jit(solution)/shard_map/ppermute | solution.py:21
  56.0 7.7 %collective-permute-start.24 = (bf16[128,256]{1,0:T(8,128)(2,1)S(1)}, bf16[128,256]{1,0:T(8,128)(2,1)S(1)}, u32[]{:S(2)}, u32[]{:S(2)}) collective-permute-start(bf16[128,256]{1,0:T(8,128)(2,1)S(1)} %get-tuple-element.57.refs_0_), channel_id=1, source_target_pairs={{0,8},{4,12},{8,0},{12,4},{16,24},{20,28},{24,16},{28,20},{1,9},{5... | collective-permute-start | bytes 196616 | tf_op jit(solution)/shard_map/ppermute | solution.py:21
  57.5 6.3 %collective-permute-start.25 = (bf16[128,256]{1,0:T(8,128)(2,1)S(1)}, bf16[128,256]{1,0:T(8,128)(2,1)S(1)}, u32[]{:S(2)}, u32[]{:S(2)}) collective-permute-start(bf16[128,256]{1,0:T(8,128)(2,1)S(1)} %get-tuple-element.57.refs_0_), channel_id=1, source_target_pairs={{0,16},{4,20},{8,24},{12,28},{16,0},{20,4},{24,8},{28,12},{1,17},{... | collective-permute-start | bytes 196616 | tf_op jit(solution)/shard_map/ppermute | solution.py:21
  58.7 5.2 %collective-permute-start.26 = (bf16[128,256]{1,0:T(8,128)(2,1)S(1)}, bf16[128,256]{1,0:T(8,128)(2,1)S(1)}, u32[]{:S(2)}, u32[]{:S(2)}) collective-permute-start(bf16[128,256]{1,0:T(8,128)(2,1)S(1)} %get-tuple-element.57.refs_0_), channel_id=1, source_target_pairs={{0,24},{4,28},{8,16},{12,20},{16,8},{20,12},{24,0},{28,4},{1,25},{... | collective-permute-start | bytes 196616 | tf_op jit(solution)/shard_map/ppermute | solution.py:21
  65.2 2.0 %collective-permute-start.27 = (bf16[4,256,256]{2,1,0:T(8,128)(2,1)S(1)}, bf16[4,256,256]{2,1,0:T(8,128)(2,1)S(1)}, u32[]{:S(2)}, u32[]{:S(2)}) collective-permute-start(bf16[4,256,256]{2,1,0:T(8,128)(2,1)S(1)} %get-tuple-element.59._), channel_id=1, source_target_pairs={{0,4},{4,0},{8,12},{12,8},{16,20},{20,16},{24,28},{28,24},{1,5},{5... | collective-permute-start | bytes 1572872 | tf_op jit(solution)/shard_map/ppermute | solution.py:21
  65.3 6.6 %collective-permute-start.28 = (bf16[128,256]{1,0:T(8,128)(2,1)S(1)}, bf16[128,256]{1,0:T(8,128)(2,1)S(1)}, u32[]{:S(2)}, u32[]{:S(2)}) collective-permute-start(bf16[128,256]{1,0:T(8,128)(2,1)S(1)} %shard_map.127._.x_ref), channel_id=1, source_target_pairs={{0,2},{1,3},{2,0},{3,1},{4,6},{5,7},{6,4},{7,5},{8,10},{9,11},{10,... | collective-permute-start | bytes 196616 | tf_op jit(solution)/shard_map/ppermute | solution.py:21
  67.3 9.0 %collective-permute-start.31 = (bf16[256,256]{1,0:T(8,128)(2,1)S(1)}, bf16[256,256]{1,0:T(8,128)(2,1)S(1)}, u32[]{:S(2)}, u32[]{:S(2)}) collective-permute-start(bf16[256,256]{1,0:T(8,128)(2,1)S(1)} %get-tuple-element.62), channel_id=1, source_target_pairs={{0,24},{4,28},{8,16},{12,20},{16,8},{20,12},{24,0},{28,4},{1,25},{... | collective-permute-start | bytes 393224 | tf_op jit(solution)/shard_map/ppermute | solution.py:21
  68.8 8.1 %collective-permute-start.29 = (bf16[256,256]{1,0:T(8,128)(2,1)S(1)}, bf16[256,256]{1,0:T(8,128)(2,1)S(1)}, u32[]{:S(2)}, u32[]{:S(2)}) collective-permute-start(bf16[256,256]{1,0:T(8,128)(2,1)S(1)} %get-tuple-element.60._), channel_id=1, source_target_pairs={{0,8},{4,12},{8,0},{12,4},{16,24},{20,28},{24,16},{28,20},{1,9},{5... | collective-permute-start | bytes 393224 | tf_op jit(solution)/shard_map/ppermute | solution.py:21
  69.8 7.1 %collective-permute-start.30 = (bf16[256,256]{1,0:T(8,128)(2,1)S(1)}, bf16[256,256]{1,0:T(8,128)(2,1)S(1)}, u32[]{:S(2)}, u32[]{:S(2)}) collective-permute-start(bf16[256,256]{1,0:T(8,128)(2,1)S(1)} %get-tuple-element.61), channel_id=1, source_target_pairs={{0,16},{4,20},{8,24},{12,28},{16,0},{20,4},{24,8},{28,12},{1,17},{... | collective-permute-start | bytes 393224 | tf_op jit(solution)/shard_map/ppermute | solution.py:21
  71.9 4.3 %collective-permute-start.32 = (bf16[128,256]{1,0:T(8,128)(2,1)S(1)}, bf16[128,256]{1,0:T(8,128)(2,1)S(1)}, u32[]{:S(2)}, u32[]{:S(2)}) collective-permute-start(bf16[128,256]{1,0:T(8,128)(2,1)S(1)} %shard_map.130._.x_ref), channel_id=1, source_target_pairs={{0,1},{1,0},{2,3},{3,2},{4,5},{5,4},{6,7},{7,6},{8,9},{9,8},{10,11... | collective-permute-start | bytes 196616 | tf_op jit(solution)/shard_map/ppermute | solution.py:21
  76.3 1.5 %collective-permute-start.33 = (bf16[64,256]{1,0:T(8,128)(2,1)S(1)}, bf16[64,256]{1,0:T(8,128)(2,1)S(1)}, u32[]{:S(2)}, u32[]{:S(2)}) collective-permute-start(bf16[64,256]{1,0:T(8,128)(2,1)S(1)} %get-tuple-element.63.refs_0_), channel_id=1, source_target_pairs={{0,4},{4,0},{8,12},{12,8},{16,20},{20,16},{24,28},{28,24},{1,5},{5... | collective-permute-start | bytes 98312 | tf_op jit(solution)/shard_map/ppermute | solution.py:21
  76.4 1.5 %collective-permute-start.34 = (bf16[64,256]{1,0:T(8,128)(2,1)S(1)}, bf16[64,256]{1,0:T(8,128)(2,1)S(1)}, u32[]{:S(2)}, u32[]{:S(2)}) collective-permute-start(bf16[64,256]{1,0:T(8,128)(2,1)S(1)} %get-tuple-element.64.refs_1_), channel_id=1, source_target_pairs={{0,4},{4,0},{8,12},{12,8},{16,20},{20,16},{24,28},{28,24},{1,5},{5... | collective-permute-start | bytes 98312 | tf_op jit(solution)/shard_map/ppermute | solution.py:21

commit v9 on v7

--- a/solution.py
+++ b/solution.py
@@ -350,6 +350,7 @@
             )
         halves.append(held)
     early = [i for i, t in enumerate(chips) if t & (t - 1) == 0]
+    early = [early[0], *early[:0:-1]]
     late = [i for i, t in enumerate(chips) if t & (t - 1)]
     forwarded = [held[chips[i]] for i in late for held in halves]
 

time: 78.8 us -> 78.8 us (level)
  no operation moved by 1% of the time
where the time goes in v9:
time: 78.8 us; the launch traced here: 78.6 us
  starting transfers between devices  35.5 us (45%)
  waiting for transfers between devices  27.5 us (35%)
  Pallas kernels  11.1 us (14%)
  local copies, waits for them, and re-layouts  2.86 us (4%)
  between operations  0.97 us (1%)
    ppermute x35, starting transfers between devices, swap(): return lax.ppermute(x, axis, [(i, i ^ offset) for i in range(size)])  35.5 us
    ppermute x35, waiting for transfers between devices, swap(): return lax.ppermute(x, axis, [(i, i ^ offset) for i in range(size)])  27.5 us
    pallas_call x23, Pallas kernels, call(): pl.pallas_call(kernel, out_shape=outs, in_specs=[SCALARS] * len(lists) +...  9.04 us
    unnamed x14, local copies, waits for them, and re-layouts  2.86 us
    pallas_call x1, Pallas kernels, local(): pl.pallas_call(functools.partial(lists_kernel, blocks_held, row_count), o...  2.03 us
  transfers between devices with their start and end apart: 35, of which 14 were waited for; matrix products, arithmetic and copies ran while one was open for 1% of the time, Pallas kernels for 11%

profile of v9, /device:TPU:0, one launch (start us, length us, event | category | flops | bytes accessed | tf_op | source)
XLA Modules:
  0.0 78.6 jit_solution(13816586418934918220)
XLA Ops:
  0.6 0.5 collective-permute-start.4
  1.1 0.1 collective-permute-start
  1.2 2.9 %collective-permute-start.1 = (bf16[256,256]{1,0:T(8,128)(2,1)}, bf16[256,256]{1,0:T(8,128)(2,1)S(1)}, u32[]{:S(2)}, u32[]{:S(2)}) collective-permute-start(bf16[256,256]{1,0:T(8,128)(2,1)} %own.3), channel_id=1, source_target_pairs={{0,8},{4,12},{8,0},{12,4},{16,24},{20,28},{24,16},{28,20},{1,9},{5... | collective-permute-start | bytes 393224 | tf_op jit(solution)/shard_map/ppermute | solution.py:21
  4.1 1.5 %collective-permute-start.2 = (bf16[256,256]{1,0:T(8,128)(2,1)}, bf16[256,256]{1,0:T(8,128)(2,1)S(1)}, u32[]{:S(2)}, u32[]{:S(2)}) collective-permute-start(bf16[256,256]{1,0:T(8,128)(2,1)} %own.3), channel_id=1, source_target_pairs={{0,16},{4,20},{8,24},{12,28},{16,0},{20,4},{24,8},{28,12},{1,17},{... | collective-permute-start | bytes 393224 | tf_op jit(solution)/shard_map/ppermute | solution.py:21
  5.7 0.7 pad_add_fusion.mine
  6.4 0.1 collective-permute-start.5
  6.5 1.0 %copy-done.2 = bf16[1024,256]{1,0:T(8,128)(2,1)S(1)} copy-done((bf16[1024,256]{1,0:T(8,128)(2,1)S(1)}, bf16[1024,256]{1,0:T(8,128)(2,1)}, u32[]{:S(2)}) %copy-start.2) | copy-done | bytes 524312
  7.5 2.0 %collective-permute-start.10 = (bf16[1024,256]{1,0:T(8,128)(2,1)S(1)}, bf16[1024,256]{1,0:T(8,128)(2,1)S(1)}, u32[]{:S(2)}, u32[]{:S(2)}) collective-permute-start(bf16[1024,256]{1,0:T(8,128)(2,1)S(1)} %shard_map.112._.refs_3_.refs_0_), channel_id=1, source_target_pairs={{0,8},{4,12},{8,0},{12,4},{16,24},{20,28},{24,16},{28,20},{1,9},{5... | collective-permute-start | bytes 1572872 | tf_op jit(solution)/shard_map/ppermute | solution.py:21
  9.6 1.5 %collective-permute-start.9 = (bf16[1024,256]{1,0:T(8,128)(2,1)S(1)}, bf16[1024,256]{1,0:T(8,128)(2,1)S(1)}, u32[]{:S(2)}, u32[]{:S(2)}) collective-permute-start(bf16[1024,256]{1,0:T(8,128)(2,1)S(1)} %shard_map.112._.refs_3_.refs_0_), channel_id=1, source_target_pairs={{0,16},{4,20},{8,24},{12,28},{16,0},{20,4},{24,8},{28,12},{1,17},{... | collective-permute-start | bytes 1572872 | tf_op jit(solution)/shard_map/ppermute | solution.py:21
  11.1 2.0 %shard_map.113 = (s32[16]{0:T(128)S(1)}, s32[16]{0:T(128)S(1)}, s32[16]{0:T(128)S(1)}, s32[16]{0:T(128)S(1)}, f32[8,128]{1,0:T(8,128)S(1)}) custom-call(s32[3,32]{1,0:T(4,128)S(1)} %pad_add_fusion.mine, s32[3,32]{1,0:T(4,128)S(1)} %collective-permute-done.5.theirs, bf16[1024,256]{1,0:T(8,128)(2,1)S(1)} %shard_map.112._.refs_3_.refs_0_), custom_call_target="tpu_custom_call" | custom-call | tf_op jit(solution)/shard_map/pallas_call | solution.py:316
  13.2 0.9 %copy-done.4 = bf16[256,256]{1,0:T(8,128)(2,1)S(1)} copy-done((bf16[256,256]{1,0:T(8,128)(2,1)S(1)}, bf16[256,256]{1,0:T(8,128)(2,1)}, u32[]{:S(2)}) %copy-start.4) | copy-done | bytes 131096
  14.1 0.1 collective-permute-start.6
  14.2 1.8 %collective-permute-done.6.refs_3_ = bf16[896,256]{1,0:T(8,128)(2,1)S(1)} collective-permute-done((bf16[896,256]{1,0:T(8,128)(2,1)S(1)}, bf16[896,256]{1,0:T(8,128)(2,1)S(1)}, u32[]{:S(2)}, u32[]{:S(2)}) %collective-permute-start.6) | collective-permute-done | bytes 458784 | tf_op jit(solution)/shard_map/ppermute | solution.py:21
  16.0 0.9 %copy-done.5 = bf16[256,256]{1,0:T(8,128)(2,1)S(1)} copy-done((bf16[256,256]{1,0:T(8,128)(2,1)S(1)}, bf16[256,256]{1,0:T(8,128)(2,1)}, u32[]{:S(2)}) %copy-start.5) | copy-done | bytes 131096
  16.9 1.3 %shard_map.115 = (f32[2,256,256]{2,1,0:T(8,128)S(1)}, bf16[2,256,256]{2,1,0:T(8,128)(2,1)S(1)}) custom-call(bf16[1024,2048]{1,0:T(8,128)(2,1)S(1)} %copy-done, bf16[256,256]{1,0:T(8,128)(2,1)S(1)} %copy-done.5, bf16[256,256]{1,0:T(8,128)(2,1)S(1)} %collective-permute-done.refs_0_.other, bf16[256,256]{1,0:T(8,128)(2,1)S(1)} %collective-permute-done.1.refs_0_, ...), custom_call_target="tpu_custom_call" | custom-call | tf_op jit(solution)/shard_map/pallas_call | solution.py:39
  18.2 1.6 %collective-permute-start.7 = (bf16[2,256,256]{2,1,0:T(8,128)(2,1)S(1)}, bf16[2,256,256]{2,1,0:T(8,128)(2,1)S(1)}, u32[]{:S(2)}, u32[]{:S(2)}) collective-permute-start(bf16[2,256,256]{2,1,0:T(8,128)(2,1)S(1)} %get-tuple-element.39), channel_id=1, source_target_pairs={{0,1},{1,0},{2,3},{3,2},{4,5},{5,4},{6,7},{7,6},{8,9},{9,8},{10,11... | collective-permute-start | bytes 786440 | tf_op jit(solution)/shard_map/ppermute | solution.py:21
  19.9 2.3 %collective-permute-done.10.refs_2_.x_ref = bf16[1024,256]{1,0:T(8,128)(2,1)S(1)} collective-permute-done((bf16[1024,256]{1,0:T(8,128)(2,1)S(1)}, bf16[1024,256]{1,0:T(8,128)(2,1)S(1)}, u32[]{:S(2)}, u32[]{:S(2)}) %collective-permute-start.10) | collective-permute-done | bytes 524320 | tf_op jit(solution)/shard_map/ppermute | solution.py:21
  22.2 1.8 %collective-permute-start.11 = (bf16[512,256]{1,0:T(8,128)(2,1)S(1)}, bf16[512,256]{1,0:T(8,128)(2,1)S(1)}, u32[]{:S(2)}, u32[]{:S(2)}) collective-permute-start(bf16[512,256]{1,0:T(8,128)(2,1)S(1)} %shard_map.119), channel_id=1, source_target_pairs={{0,16},{4,20},{8,24},{12,28},{16,0},{20,4},{24,8},{28,12},{1,17},{... | collective-permute-start | bytes 786440 | tf_op jit(solution)/shard_map/ppermute | solution.py:21
  24.1 1.5 %collective-permute-start.12 = (bf16[512,256]{1,0:T(8,128)(2,1)S(1)}, bf16[512,256]{1,0:T(8,128)(2,1)S(1)}, u32[]{:S(2)}, u32[]{:S(2)}) collective-permute-start(bf16[512,256]{1,0:T(8,128)(2,1)S(1)} %shard_map.120), channel_id=1, source_target_pairs={{0,8},{4,12},{8,0},{12,4},{16,24},{20,28},{24,16},{28,20},{1,9},{5... | collective-permute-start | bytes 786440 | tf_op jit(solution)/shard_map/ppermute | solution.py:21
  25.6 1.2 %shard_map.117 = (f32[1152,256]{1,0:T(8,128)S(1)}, f32[1152,256]{1,0:T(8,128)S(1)}) custom-call(s32[16]{0:T(128)S(1)} %get-tuple-element.42.which, s32[16]{0:T(128)S(1)} %get-tuple-element.43.code, s32[16]{0:T(128)S(1)} %get-tuple-element.44.which2.which, s32[16]{0:T(128)S(1)} %get-tuple-element.45.code2.code, bf16[32,128,128]{2,1,0:T(8,128)(2,1)S(1)} %copy-done.1, ...), custom_call_target="tpu_custom_call" | custom-call | tf_op jit(solution)/shard_map/pallas_call | solution.py:39
  26.9 2.7 %collective-permute-start.8 = (bf16[1,256,256]{2,1,0:T(8,128)(2,1)S(1)}, bf16[1,256,256]{2,1,0:T(8,128)(2,1)S(1)}, u32[]{:S(2)}, u32[]{:S(2)}) collective-permute-start(bf16[1,256,256]{2,1,0:T(8,128)(2,1)S(1)} %get-tuple-element.41), channel_id=1, source_target_pairs={{0,2},{1,3},{2,0},{3,1},{4,6},{5,7},{6,4},{7,5},{8,10},{9,11},{10,... | collective-permute-start | bytes 393224 | tf_op jit(solution)/shard_map/ppermute | solution.py:21
  29.5 0.8 %collective-permute-done.11.refs_0_ = bf16[512,256]{1,0:T(8,128)(2,1)S(1)} collective-permute-done((bf16[512,256]{1,0:T(8,128)(2,1)S(1)}, bf16[512,256]{1,0:T(8,128)(2,1)S(1)}, u32[]{:S(2)}, u32[]{:S(2)}) %collective-permute-start.11) | collective-permute-done | bytes 262176 | tf_op jit(solution)/shard_map/ppermute | solution.py:21
  30.4 1.4 %collective-permute-done.12.refs_1_ = bf16[512,256]{1,0:T(8,128)(2,1)S(1)} collective-permute-done((bf16[512,256]{1,0:T(8,128)(2,1)S(1)}, bf16[512,256]{1,0:T(8,128)(2,1)S(1)}, u32[]{:S(2)}, u32[]{:S(2)}) %collective-permute-start.12) | collective-permute-done | bytes 262176 | tf_op jit(solution)/shard_map/ppermute | solution.py:21
  31.8 0.8 %shard_map.122 = (bf16[256,256]{1,0:T(8,128)(2,1)S(1)}, bf16[256,256]{1,0:T(8,128)(2,1)S(1)}, bf16[256,256]{1,0:T(8,128)(2,1)S(1)}, bf16[256,256]{1,0:T(8,128)(2,1)S(1)}) custom-call(s32[16]{0:T(128)S(1)} %get-tuple-element.44.which2.which, s32[16]{0:T(128)S(1)} %get-tuple-element.45.code2.code, f32[1152,256]{1,0:T(8,128)S(1)} %get-tuple-element.48.acc_in, ...), custom_call_target="tpu_custom_call" | custom-call | tf_op jit(solution)/shard_map/pallas_call | solution.py:39
  32.7 0.1 collective-permute-start.13
  32.7 0.5 collective-permute-start.14
  33.2 0.1 collective-permute-start.15
  33.3 0.4 collective-permute-start.16
  33.8 0.8 %shard_map.121.own = f32[1152,256]{1,0:T(8,128)S(1)} custom-call(s32[16]{0:T(128)S(1)} %get-tuple-element.42.which, s32[16]{0:T(128)S(1)} %get-tuple-element.43.code, f32[1152,256]{1,0:T(8,128)S(1)} %get-tuple-element.46._.acc_in, bf16[32,128,128]{2,1,0:T(8,128)(2,1)S(1)} %copy-done.1, bf16[512,256]{1,0:T(8,128)(2,1)S(1)} %collective-permute-done.11.refs_0_, ...), custom_call_target="tpu_custom_call" | custom-call | tf_op jit(solution)/shard_map/pallas_call | solution.py:39
  34.6 0.7 collective-permute-done.8.received
  35.2 0.2 shard_map.118
  35.5 0.2 shard_map.123
  35.7 3.6 %collective-permute-start.17 = (bf16[256,256]{1,0:T(8,128)(2,1)S(1)}, bf16[256,256]{1,0:T(8,128)(2,1)S(1)}, u32[]{:S(2)}, u32[]{:S(2)}) collective-permute-start(bf16[256,256]{1,0:T(8,128)(2,1)S(1)} %get-tuple-element.54), channel_id=1, source_target_pairs={{0,3},{1,2},{2,1},{3,0},{4,7},{5,6},{6,5},{7,4},{8,11},{9,10},{10,... | collective-permute-start | bytes 393224 | tf_op jit(solution)/shard_map/ppermute | solution.py:21
  39.2 0.9 %collective-permute-start.19 = (bf16[256,256]{1,0:T(8,128)(2,1)S(1)}, bf16[256,256]{1,0:T(8,128)(2,1)S(1)}, u32[]{:S(2)}, u32[]{:S(2)}) collective-permute-start(bf16[256,256]{1,0:T(8,128)(2,1)S(1)} %get-tuple-element.56), channel_id=1, source_target_pairs={{0,2},{1,3},{2,0},{3,1},{4,6},{5,7},{6,4},{7,5},{8,10},{9,11},{10,... | collective-permute-start | bytes 393224 | tf_op jit(solution)/shard_map/ppermute | solution.py:21
  40.1 3.8 %collective-permute-done.17.refs_0_ = bf16[256,256]{1,0:T(8,128)(2,1)S(1)} collective-permute-done((bf16[256,256]{1,0:T(8,128)(2,1)S(1)}, bf16[256,256]{1,0:T(8,128)(2,1)S(1)}, u32[]{:S(2)}, u32[]{:S(2)}) %collective-permute-start.17) | collective-permute-done | bytes 131104 | tf_op jit(solution)/shard_map/ppermute | solution.py:21
  44.0 2.3 %collective-permute-done.18.refs_1_ = bf16[256,256]{1,0:T(8,128)(2,1)S(1)} collective-permute-done((bf16[256,256]{1,0:T(8,128)(2,1)S(1)}, bf16[256,256]{1,0:T(8,128)(2,1)S(1)}, u32[]{:S(2)}, u32[]{:S(2)}) %collective-permute-start.18) | collective-permute-done | bytes 131104 | tf_op jit(solution)/shard_map/ppermute | solution.py:21
  46.2 3.9 %collective-permute-done.19.refs_2_ = bf16[256,256]{1,0:T(8,128)(2,1)S(1)} collective-permute-done((bf16[256,256]{1,0:T(8,128)(2,1)S(1)}, bf16[256,256]{1,0:T(8,128)(2,1)S(1)}, u32[]{:S(2)}, u32[]{:S(2)}) %collective-permute-start.19) | collective-permute-done | bytes 131104 | tf_op jit(solution)/shard_map/ppermute | solution.py:21
  50.2 0.2 shard_map.124
  50.4 2.5 %collective-permute-start.21 = (bf16[256,256]{1,0:T(8,128)(2,1)S(1)}, bf16[256,256]{1,0:T(8,128)(2,1)S(1)}, u32[]{:S(2)}, u32[]{:S(2)}) collective-permute-start(bf16[256,256]{1,0:T(8,128)(2,1)S(1)} %get-tuple-element.59.g_ref.refs_3_), channel_id=1, source_target_pairs={{0,3},{1,2},{2,1},{3,0},{4,7},{5,6},{6,5},{7,4},{8,11},{9,10},{10,... | collective-permute-start | bytes 393224 | tf_op jit(solution)/shard_map/ppermute | solution.py:21
  52.9 0.2 shard_map.125
  53.2 0.1 collective-permute-start.20
  53.2 0.1 collective-permute-start.22
  53.3 1.9 %collective-permute-start.23 = (bf16[256,256]{1,0:T(8,128)(2,1)S(1)}, bf16[256,256]{1,0:T(8,128)(2,1)S(1)}, u32[]{:S(2)}, u32[]{:S(2)}) collective-permute-start(bf16[256,256]{1,0:T(8,128)(2,1)S(1)} %get-tuple-element.59.g_ref.refs_3_), channel_id=1, source_target_pairs={{0,2},{1,3},{2,0},{3,1},{4,6},{5,7},{6,4},{7,5},{8,10},{9,11},{10,... | collective-permute-start | bytes 393224 | tf_op jit(solution)/shard_map/ppermute | solution.py:21
  55.2 0.7 shard_map.126
  55.9 1.4 %collective-permute-start.24 = (bf16[128,256]{1,0:T(8,128)(2,1)S(1)}, bf16[128,256]{1,0:T(8,128)(2,1)S(1)}, u32[]{:S(2)}, u32[]{:S(2)}) collective-permute-start(bf16[128,256]{1,0:T(8,128)(2,1)S(1)} %get-tuple-element.63.refs_0_), channel_id=1, source_target_pairs={{0,8},{4,12},{8,0},{12,4},{16,24},{20,28},{24,16},{28,20},{1,9},{5... | collective-permute-start | bytes 196616 | tf_op jit(solution)/shard_map/ppermute | solution.py:21
  57.3 0.6 collective-permute-start.25
  57.9 0.6 collective-permute-done.21.refs_0_
  58.6 1.4 %collective-permute-start.26 = (bf16[128,256]{1,0:T(8,128)(2,1)S(1)}, bf16[128,256]{1,0:T(8,128)(2,1)S(1)}, u32[]{:S(2)}, u32[]{:S(2)}) collective-permute-start(bf16[128,256]{1,0:T(8,128)(2,1)S(1)} %get-tuple-element.63.refs_0_), channel_id=1, source_target_pairs={{0,24},{4,28},{8,16},{12,20},{16,8},{20,12},{24,0},{28,4},{1,25},{... | collective-permute-start | bytes 196616 | tf_op jit(solution)/shard_map/ppermute | solution.py:21
  60.0 2.3 %collective-permute-done.22.refs_1_ = bf16[256,256]{1,0:T(8,128)(2,1)S(1)} collective-permute-done((bf16[256,256]{1,0:T(8,128)(2,1)S(1)}, bf16[256,256]{1,0:T(8,128)(2,1)S(1)}, u32[]{:S(2)}, u32[]{:S(2)}) %collective-permute-start.22) | collective-permute-done | bytes 131104 | tf_op jit(solution)/shard_map/ppermute | solution.py:21
  62.4 1.2 %collective-permute-done.23.refs_2_ = bf16[256,256]{1,0:T(8,128)(2,1)S(1)} collective-permute-done((bf16[256,256]{1,0:T(8,128)(2,1)S(1)}, bf16[256,256]{1,0:T(8,128)(2,1)S(1)}, u32[]{:S(2)}, u32[]{:S(2)}) %collective-permute-start.23) | collective-permute-done | bytes 131104 | tf_op jit(solution)/shard_map/ppermute | solution.py:21
  63.6 0.1 collective-permute-done.26.refs_3_
  63.8 1.3 %shard_map.129 = (bf16[4,256,256]{2,1,0:T(8,128)(2,1)S(1)}, f32[4,256,256]{2,1,0:T(8,128)S(1)}) custom-call(bf16[1024,2048]{1,0:T(8,128)(2,1)S(1)} %copy-done, bf16[256,1024]{1,0:T(8,128)(2,1)S(1)} %shard_map.127.refs_4_.g_ref, bf16[128,256]{1,0:T(8,128)(2,1)S(1)} %shard_map.128._.x_ref), custom_call_target="tpu_custom_call" | custom-call | tf_op jit(solution)/shard_map/pallas_call | solution.py:39
  65.1 0.1 collective-permute-start.27
  65.2 0.1 collective-permute-start.28
  65.2 1.8 %collective-permute-done.27.received = bf16[4,256,256]{2,1,0:T(8,128)(2,1)S(1)} collective-permute-done((bf16[4,256,256]{2,1,0:T(8,128)(2,1)S(1)}, bf16[4,256,256]{2,1,0:T(8,128)(2,1)S(1)}, u32[]{:S(2)}, u32[]{:S(2)}) %collective-permute-start.27) | collective-permute-done | bytes 524320 | tf_op jit(solution)/shard_map/ppermute | solution.py:21
  67.1 1.5 %collective-permute-start.31 = (bf16[256,256]{1,0:T(8,128)(2,1)S(1)}, bf16[256,256]{1,0:T(8,128)(2,1)S(1)}, u32[]{:S(2)}, u32[]{:S(2)}) collective-permute-start(bf16[256,256]{1,0:T(8,128)(2,1)S(1)} %get-tuple-element.68), channel_id=1, source_target_pairs={{0,24},{4,28},{8,16},{12,20},{16,8},{20,12},{24,0},{28,4},{1,25},{... | collective-permute-start | bytes 393224 | tf_op jit(solution)/shard_map/ppermute | solution.py:21
  68.6 1.0 %collective-permute-start.29 = (bf16[256,256]{1,0:T(8,128)(2,1)S(1)}, bf16[256,256]{1,0:T(8,128)(2,1)S(1)}, u32[]{:S(2)}, u32[]{:S(2)}) collective-permute-start(bf16[256,256]{1,0:T(8,128)(2,1)S(1)} %get-tuple-element.66._), channel_id=1, source_target_pairs={{0,8},{4,12},{8,0},{12,4},{16,24},{20,28},{24,16},{28,20},{1,9},{5... | collective-permute-start | bytes 393224 | tf_op jit(solution)/shard_map/ppermute | solution.py:21
  69.7 1.0 %collective-permute-start.30 = (bf16[256,256]{1,0:T(8,128)(2,1)S(1)}, bf16[256,256]{1,0:T(8,128)(2,1)S(1)}, u32[]{:S(2)}, u32[]{:S(2)}) collective-permute-start(bf16[256,256]{1,0:T(8,128)(2,1)S(1)} %get-tuple-element.67), channel_id=1, source_target_pairs={{0,16},{4,20},{8,24},{12,28},{16,0},{20,4},{24,8},{28,12},{1,17},{... | collective-permute-start | bytes 393224 | tf_op jit(solution)/shard_map/ppermute | solution.py:21
  70.7 1.3 %collective-permute-start.32 = (bf16[128,256]{1,0:T(8,128)(2,1)S(1)}, bf16[128,256]{1,0:T(8,128)(2,1)S(1)}, u32[]{:S(2)}, u32[]{:S(2)}) collective-permute-start(bf16[128,256]{1,0:T(8,128)(2,1)S(1)} %shard_map.131._.x_ref), channel_id=1, source_target_pairs={{0,2},{1,3},{2,0},{3,1},{4,6},{5,7},{6,4},{7,5},{8,10},{9,11},{10,... | collective-permute-start | bytes 196616 | tf_op jit(solution)/shard_map/ppermute | solution.py:21
  72.0 4.3 %collective-permute-done.32.y_ref = bf16[128,256]{1,0:T(8,128)(2,1)S(1)} collective-permute-done((bf16[128,256]{1,0:T(8,128)(2,1)S(1)}, bf16[128,256]{1,0:T(8,128)(2,1)S(1)}, u32[]{:S(2)}, u32[]{:S(2)}) %collective-permute-start.32) | collective-permute-done | bytes 65568 | tf_op jit(solution)/shard_map/ppermute | solution.py:21
  76.3 0.1 collective-permute-start.33
  76.4 0.5 collective-permute-start.34
  76.9 0.9 %shard_map.133 = bf16[256,256]{1,0:T(8,128)(2,1)} custom-call(bf16[256,256]{1,0:T(8,128)(2,1)S(1)} %copy-done.3, f32[256,256]{1,0:T(8,128)S(1)} %shard_map.132.refs_0_, bf16[256,256]{1,0:T(8,128)(2,1)S(1)} %collective-permute-done.29.refs_1_, bf16[256,256]{1,0:T(8,128)(2,1)S(1)} %collective-permute-done.30.refs_2_, ...), custom_call_target="tpu_custom_call" | custom-call | tf_op jit(solution)/shard_map/pallas_call | solution.py:39
  77.8 0.7 shard_map.135
  (45 shorter events, 0.5 us)
Async XLA Ops:
  0.6 5.8 %collective-permute-start.4 = (bf16[32,128,128]{2,1,0:T(8,128)(2,1)}, bf16[32,128,128]{2,1,0:T(8,128)(2,1)S(1)}, u32[]{:S(2)}, u32[]{:S(2)}) collective-permute-start(bf16[32,128,128]{2,1,0:T(8,128)(2,1)} %tiles.3), channel_id=1, source_target_pairs={{0,4},{4,0},{8,12},{12,8},{16,20},{20,16},{24,28},{28,24},{1,5},{5... | collective-permute-start | bytes 3145736 | tf_op jit(solution)/shard_map/ppermute | solution.py:21
  1.1 5.2 %collective-permute-start = (bf16[256,256]{1,0:T(8,128)(2,1)}, bf16[256,256]{1,0:T(8,128)(2,1)S(1)}, u32[]{:S(2)}, u32[]{:S(2)}) collective-permute-start(bf16[256,256]{1,0:T(8,128)(2,1)} %own.3), channel_id=1, source_target_pairs={{0,4},{4,0},{8,12},{12,8},{16,20},{20,16},{24,28},{28,24},{1,5},{5... | collective-permute-start | bytes 393224 | tf_op jit(solution)/shard_map/ppermute | solution.py:21
  1.2 11.9 %collective-permute-start.1 = (bf16[256,256]{1,0:T(8,128)(2,1)}, bf16[256,256]{1,0:T(8,128)(2,1)S(1)}, u32[]{:S(2)}, u32[]{:S(2)}) collective-permute-start(bf16[256,256]{1,0:T(8,128)(2,1)} %own.3), channel_id=1, source_target_pairs={{0,8},{4,12},{8,0},{12,4},{16,24},{20,28},{24,16},{28,20},{1,9},{5... | collective-permute-start | bytes 393224 | tf_op jit(solution)/shard_map/ppermute | solution.py:21
  4.1 9.0 %collective-permute-start.2 = (bf16[256,256]{1,0:T(8,128)(2,1)}, bf16[256,256]{1,0:T(8,128)(2,1)S(1)}, u32[]{:S(2)}, u32[]{:S(2)}) collective-permute-start(bf16[256,256]{1,0:T(8,128)(2,1)} %own.3), channel_id=1, source_target_pairs={{0,16},{4,20},{8,24},{12,28},{16,0},{20,4},{24,8},{28,12},{1,17},{... | collective-permute-start | bytes 393224 | tf_op jit(solution)/shard_map/ppermute | solution.py:21
  5.7 7.5 %collective-permute-start.3 = (bf16[256,256]{1,0:T(8,128)(2,1)}, bf16[256,256]{1,0:T(8,128)(2,1)S(1)}, u32[]{:S(2)}, u32[]{:S(2)}) collective-permute-start(bf16[256,256]{1,0:T(8,128)(2,1)} %own.3), channel_id=1, source_target_pairs={{0,24},{4,28},{8,16},{12,20},{16,8},{20,12},{24,0},{28,4},{1,25},{... | collective-permute-start | bytes 393224 | tf_op jit(solution)/shard_map/ppermute | solution.py:21
  6.4 3.2 %collective-permute-start.5 = (s32[3,32]{1,0:T(4,128)S(1)}, s32[3,32]{1,0:T(4,128)S(1)}, u32[]{:S(2)}, u32[]{:S(2)}) collective-permute-start(s32[3,32]{1,0:T(4,128)S(1)} %pad_add_fusion.mine), channel_id=1, source_target_pairs={{0,4},{4,0},{8,12},{12,8},{16,20},{20,16},{24,28},{28,24},{1,5},{5... | collective-permute-start | bytes 1160 | tf_op jit(solution)/shard_map/ppermute | solution.py:21
  6.5 1.0 %copy-start.2 = (bf16[1024,256]{1,0:T(8,128)(2,1)S(1)}, bf16[1024,256]{1,0:T(8,128)(2,1)}, u32[]{:S(2)}) copy-start(bf16[1024,256]{1,0:T(8,128)(2,1)} %x_ref.1) | copy-start | bytes 1572868
  7.5 8.5 %copy-start = (bf16[1024,2048]{1,0:T(8,128)(2,1)S(1)}, bf16[1024,2048]{1,0:T(8,128)(2,1)}, u32[]{:S(2)}) copy-start(bf16[1024,2048]{1,0:T(8,128)(2,1)} %a_ref.3) | copy-start | bytes 12582916
  7.5 14.6 %collective-permute-start.10 = (bf16[1024,256]{1,0:T(8,128)(2,1)S(1)}, bf16[1024,256]{1,0:T(8,128)(2,1)S(1)}, u32[]{:S(2)}, u32[]{:S(2)}) collective-permute-start(bf16[1024,256]{1,0:T(8,128)(2,1)S(1)} %shard_map.112._.refs_3_.refs_0_), channel_id=1, source_target_pairs={{0,8},{4,12},{8,0},{12,4},{16,24},{20,28},{24,16},{28,20},{1,9},{5... | collective-permute-start | bytes 1572872 | tf_op jit(solution)/shard_map/ppermute | solution.py:21
  9.6 14.5 %collective-permute-start.9 = (bf16[1024,256]{1,0:T(8,128)(2,1)S(1)}, bf16[1024,256]{1,0:T(8,128)(2,1)S(1)}, u32[]{:S(2)}, u32[]{:S(2)}) collective-permute-start(bf16[1024,256]{1,0:T(8,128)(2,1)S(1)} %shard_map.112._.refs_3_.refs_0_), channel_id=1, source_target_pairs={{0,16},{4,20},{8,24},{12,28},{16,0},{20,4},{24,8},{28,12},{1,17},{... | collective-permute-start | bytes 1572872 | tf_op jit(solution)/shard_map/ppermute | solution.py:21
  13.2 0.9 %copy-start.4 = (bf16[256,256]{1,0:T(8,128)(2,1)S(1)}, bf16[256,256]{1,0:T(8,128)(2,1)}, u32[]{:S(2)}) copy-start(bf16[256,256]{1,0:T(8,128)(2,1)} %own.3) | copy-start | bytes 393220
  14.1 1.9 %collective-permute-start.6 = (bf16[896,256]{1,0:T(8,128)(2,1)S(1)}, bf16[896,256]{1,0:T(8,128)(2,1)S(1)}, u32[]{:S(2)}, u32[]{:S(2)}) collective-permute-start(bf16[896,256]{1,0:T(8,128)(2,1)S(1)} %shard_map.114), channel_id=1, source_target_pairs={{0,4},{4,0},{8,12},{12,8},{16,20},{20,16},{24,28},{28,24},{1,5},{5... | collective-permute-start | bytes 1376264 | tf_op jit(solution)/shard_map/ppermute | solution.py:21
  16.0 0.9 %copy-start.5 = (bf16[256,256]{1,0:T(8,128)(2,1)S(1)}, bf16[256,256]{1,0:T(8,128)(2,1)}, u32[]{:S(2)}) copy-start(bf16[256,256]{1,0:T(8,128)(2,1)} %own.3) | copy-start | bytes 393220
  18.2 7.4 %copy-start.1 = (bf16[32,128,128]{2,1,0:T(8,128)(2,1)S(1)}, bf16[32,128,128]{2,1,0:T(8,128)(2,1)}, u32[]{:S(2)}) copy-start(bf16[32,128,128]{2,1,0:T(8,128)(2,1)} %tiles.3) | copy-start | bytes 3145732
  18.2 8.6 %collective-permute-start.7 = (bf16[2,256,256]{2,1,0:T(8,128)(2,1)S(1)}, bf16[2,256,256]{2,1,0:T(8,128)(2,1)S(1)}, u32[]{:S(2)}, u32[]{:S(2)}) collective-permute-start(bf16[2,256,256]{2,1,0:T(8,128)(2,1)S(1)} %get-tuple-element.39), channel_id=1, source_target_pairs={{0,1},{1,0},{2,3},{3,2},{4,5},{5,4},{6,7},{7,6},{8,9},{9,8},{10,11... | collective-permute-start | bytes 786440 | tf_op jit(solution)/shard_map/ppermute | solution.py:21
  22.2 8.2 %collective-permute-start.11 = (bf16[512,256]{1,0:T(8,128)(2,1)S(1)}, bf16[512,256]{1,0:T(8,128)(2,1)S(1)}, u32[]{:S(2)}, u32[]{:S(2)}) collective-permute-start(bf16[512,256]{1,0:T(8,128)(2,1)S(1)} %shard_map.119), channel_id=1, source_target_pairs={{0,16},{4,20},{8,24},{12,28},{16,0},{20,4},{24,8},{28,12},{1,17},{... | collective-permute-start | bytes 786440 | tf_op jit(solution)/shard_map/ppermute | solution.py:21
  24.1 7.7 %collective-permute-start.12 = (bf16[512,256]{1,0:T(8,128)(2,1)S(1)}, bf16[512,256]{1,0:T(8,128)(2,1)S(1)}, u32[]{:S(2)}, u32[]{:S(2)}) collective-permute-start(bf16[512,256]{1,0:T(8,128)(2,1)S(1)} %shard_map.120), channel_id=1, source_target_pairs={{0,8},{4,12},{8,0},{12,4},{16,24},{20,28},{24,16},{28,20},{1,9},{5... | collective-permute-start | bytes 786440 | tf_op jit(solution)/shard_map/ppermute | solution.py:21
  26.9 8.3 %collective-permute-start.8 = (bf16[1,256,256]{2,1,0:T(8,128)(2,1)S(1)}, bf16[1,256,256]{2,1,0:T(8,128)(2,1)S(1)}, u32[]{:S(2)}, u32[]{:S(2)}) collective-permute-start(bf16[1,256,256]{2,1,0:T(8,128)(2,1)S(1)} %get-tuple-element.41), channel_id=1, source_target_pairs={{0,2},{1,3},{2,0},{3,1},{4,6},{5,7},{6,4},{7,5},{8,10},{9,11},{10,... | collective-permute-start | bytes 393224 | tf_op jit(solution)/shard_map/ppermute | solution.py:21
  32.7 2.8 %collective-permute-start.13 = (bf16[256,256]{1,0:T(8,128)(2,1)S(1)}, bf16[256,256]{1,0:T(8,128)(2,1)S(1)}, u32[]{:S(2)}, u32[]{:S(2)}) collective-permute-start(bf16[256,256]{1,0:T(8,128)(2,1)S(1)} %get-tuple-element.49), channel_id=1, source_target_pairs={{0,4},{4,0},{8,12},{12,8},{16,20},{20,16},{24,28},{28,24},{1,5},{5... | collective-permute-start | bytes 393224 | tf_op jit(solution)/shard_map/ppermute | solution.py:21
  32.7 2.7 %collective-permute-start.14 = (bf16[256,256]{1,0:T(8,128)(2,1)S(1)}, bf16[256,256]{1,0:T(8,128)(2,1)S(1)}, u32[]{:S(2)}, u32[]{:S(2)}) collective-permute-start(bf16[256,256]{1,0:T(8,128)(2,1)S(1)} %get-tuple-element.50), channel_id=1, source_target_pairs={{0,4},{4,0},{8,12},{12,8},{16,20},{20,16},{24,28},{28,24},{1,5},{5... | collective-permute-start | bytes 393224 | tf_op jit(solution)/shard_map/ppermute | solution.py:21
  33.2 2.2 %collective-permute-start.15 = (bf16[256,256]{1,0:T(8,128)(2,1)S(1)}, bf16[256,256]{1,0:T(8,128)(2,1)S(1)}, u32[]{:S(2)}, u32[]{:S(2)}) collective-permute-start(bf16[256,256]{1,0:T(8,128)(2,1)S(1)} %get-tuple-element.51), channel_id=1, source_target_pairs={{0,4},{4,0},{8,12},{12,8},{16,20},{20,16},{24,28},{28,24},{1,5},{5... | collective-permute-start | bytes 393224 | tf_op jit(solution)/shard_map/ppermute | solution.py:21
  33.3 2.2 %collective-permute-start.16 = (bf16[256,256]{1,0:T(8,128)(2,1)S(1)}, bf16[256,256]{1,0:T(8,128)(2,1)S(1)}, u32[]{:S(2)}, u32[]{:S(2)}) collective-permute-start(bf16[256,256]{1,0:T(8,128)(2,1)S(1)} %get-tuple-element.52), channel_id=1, source_target_pairs={{0,4},{4,0},{8,12},{12,8},{16,20},{20,16},{24,28},{28,24},{1,5},{5... | collective-permute-start | bytes 393224 | tf_op jit(solution)/shard_map/ppermute | solution.py:21
  33.8 1.5 %copy-start.3 = (bf16[256,256]{1,0:T(8,128)(2,1)S(1)}, bf16[256,256]{1,0:T(8,128)(2,1)}, u32[]{:S(2)}) copy-start(bf16[256,256]{1,0:T(8,128)(2,1)} %w_ref.3) | copy-start | bytes 393220
  35.5 14.7 %copy-start.6 = (bf16[256,256]{1,0:T(8,128)(2,1)S(1)}, bf16[256,256]{1,0:T(8,128)(2,1)}, u32[]{:S(2)}) copy-start(bf16[256,256]{1,0:T(8,128)(2,1)} %cotangent.1) | copy-start | bytes 393220
  35.7 8.3 %collective-permute-start.17 = (bf16[256,256]{1,0:T(8,128)(2,1)S(1)}, bf16[256,256]{1,0:T(8,128)(2,1)S(1)}, u32[]{:S(2)}, u32[]{:S(2)}) collective-permute-start(bf16[256,256]{1,0:T(8,128)(2,1)S(1)} %get-tuple-element.54), channel_id=1, source_target_pairs={{0,3},{1,2},{2,1},{3,0},{4,7},{5,6},{6,5},{7,4},{8,11},{9,10},{10,... | collective-permute-start | bytes 393224 | tf_op jit(solution)/shard_map/ppermute | solution.py:21
  39.2 7.0 %collective-permute-start.18 = (bf16[256,256]{1,0:T(8,128)(2,1)S(1)}, bf16[256,256]{1,0:T(8,128)(2,1)S(1)}, u32[]{:S(2)}, u32[]{:S(2)}) collective-permute-start(bf16[256,256]{1,0:T(8,128)(2,1)S(1)} %get-tuple-element.55), channel_id=1, source_target_pairs={{0,1},{1,0},{2,3},{3,2},{4,5},{5,4},{6,7},{7,6},{8,9},{9,8},{10,11... | collective-permute-start | bytes 393224 | tf_op jit(solution)/shard_map/ppermute | solution.py:21
  39.2 10.9 %collective-permute-start.19 = (bf16[256,256]{1,0:T(8,128)(2,1)S(1)}, bf16[256,256]{1,0:T(8,128)(2,1)S(1)}, u32[]{:S(2)}, u32[]{:S(2)}) collective-permute-start(bf16[256,256]{1,0:T(8,128)(2,1)S(1)} %get-tuple-element.56), channel_id=1, source_target_pairs={{0,2},{1,3},{2,0},{3,1},{4,6},{5,7},{6,4},{7,5},{8,10},{9,11},{10,... | collective-permute-start | bytes 393224 | tf_op jit(solution)/shard_map/ppermute | solution.py:21
  50.4 8.2 %collective-permute-start.21 = (bf16[256,256]{1,0:T(8,128)(2,1)S(1)}, bf16[256,256]{1,0:T(8,128)(2,1)S(1)}, u32[]{:S(2)}, u32[]{:S(2)}) collective-permute-start(bf16[256,256]{1,0:T(8,128)(2,1)S(1)} %get-tuple-element.59.g_ref.refs_3_), channel_id=1, source_target_pairs={{0,3},{1,2},{2,1},{3,0},{4,7},{5,6},{6,5},{7,4},{8,11},{9,10},{10,... | collective-permute-start | bytes 393224 | tf_op jit(solution)/shard_map/ppermute | solution.py:21
  53.2 2.1 %collective-permute-start.20 = (bf16[128,256]{1,0:T(8,128)(2,1)S(1)}, bf16[128,256]{1,0:T(8,128)(2,1)S(1)}, u32[]{:S(2)}, u32[]{:S(2)}) collective-permute-start(bf16[128,256]{1,0:T(8,128)(2,1)S(1)} %get-tuple-element.61), channel_id=1, source_target_pairs={{0,4},{4,0},{8,12},{12,8},{16,20},{20,16},{24,28},{28,24},{1,5},{5... | collective-permute-start | bytes 196616 | tf_op jit(solution)/shard_map/ppermute | solution.py:21
  53.2 9.1 %collective-permute-start.22 = (bf16[256,256]{1,0:T(8,128)(2,1)S(1)}, bf16[256,256]{1,0:T(8,128)(2,1)S(1)}, u32[]{:S(2)}, u32[]{:S(2)}) collective-permute-start(bf16[256,256]{1,0:T(8,128)(2,1)S(1)} %get-tuple-element.59.g_ref.refs_3_), channel_id=1, source_target_pairs={{0,1},{1,0},{2,3},{3,2},{4,5},{5,4},{6,7},{7,6},{8,9},{9,8},{10,11... | collective-permute-start | bytes 393224 | tf_op jit(solution)/shard_map/ppermute | solution.py:21
  53.3 10.2 %collective-permute-start.23 = (bf16[256,256]{1,0:T(8,128)(2,1)S(1)}, bf16[256,256]{1,0:T(8,128)(2,1)S(1)}, u32[]{:S(2)}, u32[]{:S(2)}) collective-permute-start(bf16[256,256]{1,0:T(8,128)(2,1)S(1)} %get-tuple-element.59.g_ref.refs_3_), channel_id=1, source_target_pairs={{0,2},{1,3},{2,0},{3,1},{4,6},{5,7},{6,4},{7,5},{8,10},{9,11},{10,... | collective-permute-start | bytes 393224 | tf_op jit(solution)/shard_map/ppermute | solution.py:21
  55.9 7.7 %collective-permute-start.24 = (bf16[128,256]{1,0:T(8,128)(2,1)S(1)}, bf16[128,256]{1,0:T(8,128)(2,1)S(1)}, u32[]{:S(2)}, u32[]{:S(2)}) collective-permute-start(bf16[128,256]{1,0:T(8,128)(2,1)S(1)} %get-tuple-element.63.refs_0_), channel_id=1, source_target_pairs={{0,8},{4,12},{8,0},{12,4},{16,24},{20,28},{24,16},{28,20},{1,9},{5... | collective-permute-start | bytes 196616 | tf_op jit(solution)/shard_map/ppermute | solution.py:21
  57.3 6.3 %collective-permute-start.25 = (bf16[128,256]{1,0:T(8,128)(2,1)S(1)}, bf16[128,256]{1,0:T(8,128)(2,1)S(1)}, u32[]{:S(2)}, u32[]{:S(2)}) collective-permute-start(bf16[128,256]{1,0:T(8,128)(2,1)S(1)} %get-tuple-element.63.refs_0_), channel_id=1, source_target_pairs={{0,16},{4,20},{8,24},{12,28},{16,0},{20,4},{24,8},{28,12},{1,17},{... | collective-permute-start | bytes 196616 | tf_op jit(solution)/shard_map/ppermute | solution.py:21
  58.6 5.2 %collective-permute-start.26 = (bf16[128,256]{1,0:T(8,128)(2,1)S(1)}, bf16[128,256]{1,0:T(8,128)(2,1)S(1)}, u32[]{:S(2)}, u32[]{:S(2)}) collective-permute-start(bf16[128,256]{1,0:T(8,128)(2,1)S(1)} %get-tuple-element.63.refs_0_), channel_id=1, source_target_pairs={{0,24},{4,28},{8,16},{12,20},{16,8},{20,12},{24,0},{28,4},{1,25},{... | collective-permute-start | bytes 196616 | tf_op jit(solution)/shard_map/ppermute | solution.py:21
  65.1 2.0 %collective-permute-start.27 = (bf16[4,256,256]{2,1,0:T(8,128)(2,1)S(1)}, bf16[4,256,256]{2,1,0:T(8,128)(2,1)S(1)}, u32[]{:S(2)}, u32[]{:S(2)}) collective-permute-start(bf16[4,256,256]{2,1,0:T(8,128)(2,1)S(1)} %get-tuple-element.65._), channel_id=1, source_target_pairs={{0,4},{4,0},{8,12},{12,8},{16,20},{20,16},{24,28},{28,24},{1,5},{5... | collective-permute-start | bytes 1572872 | tf_op jit(solution)/shard_map/ppermute | solution.py:21
  65.2 5.5 %collective-permute-start.28 = (bf16[128,256]{1,0:T(8,128)(2,1)S(1)}, bf16[128,256]{1,0:T(8,128)(2,1)S(1)}, u32[]{:S(2)}, u32[]{:S(2)}) collective-permute-start(bf16[128,256]{1,0:T(8,128)(2,1)S(1)} %shard_map.128._.x_ref), channel_id=1, source_target_pairs={{0,1},{1,0},{2,3},{3,2},{4,5},{5,4},{6,7},{7,6},{8,9},{9,8},{10,11... | collective-permute-start | bytes 196616 | tf_op jit(solution)/shard_map/ppermute | solution.py:21
  67.1 9.1 %collective-permute-start.31 = (bf16[256,256]{1,0:T(8,128)(2,1)S(1)}, bf16[256,256]{1,0:T(8,128)(2,1)S(1)}, u32[]{:S(2)}, u32[]{:S(2)}) collective-permute-start(bf16[256,256]{1,0:T(8,128)(2,1)S(1)} %get-tuple-element.68), channel_id=1, source_target_pairs={{0,24},{4,28},{8,16},{12,20},{16,8},{20,12},{24,0},{28,4},{1,25},{... | collective-permute-start | bytes 393224 | tf_op jit(solution)/shard_map/ppermute | solution.py:21
  68.6 8.3 %collective-permute-start.29 = (bf16[256,256]{1,0:T(8,128)(2,1)S(1)}, bf16[256,256]{1,0:T(8,128)(2,1)S(1)}, u32[]{:S(2)}, u32[]{:S(2)}) collective-permute-start(bf16[256,256]{1,0:T(8,128)(2,1)S(1)} %get-tuple-element.66._), channel_id=1, source_target_pairs={{0,8},{4,12},{8,0},{12,4},{16,24},{20,28},{24,16},{28,20},{1,9},{5... | collective-permute-start | bytes 393224 | tf_op jit(solution)/shard_map/ppermute | solution.py:21
  69.7 7.3 %collective-permute-start.30 = (bf16[256,256]{1,0:T(8,128)(2,1)S(1)}, bf16[256,256]{1,0:T(8,128)(2,1)S(1)}, u32[]{:S(2)}, u32[]{:S(2)}) collective-permute-start(bf16[256,256]{1,0:T(8,128)(2,1)S(1)} %get-tuple-element.67), channel_id=1, source_target_pairs={{0,16},{4,20},{8,24},{12,28},{16,0},{20,4},{24,8},{28,12},{1,17},{... | collective-permute-start | bytes 393224 | tf_op jit(solution)/shard_map/ppermute | solution.py:21
  70.7 5.6 %collective-permute-start.32 = (bf16[128,256]{1,0:T(8,128)(2,1)S(1)}, bf16[128,256]{1,0:T(8,128)(2,1)S(1)}, u32[]{:S(2)}, u32[]{:S(2)}) collective-permute-start(bf16[128,256]{1,0:T(8,128)(2,1)S(1)} %shard_map.131._.x_ref), channel_id=1, source_target_pairs={{0,2},{1,3},{2,0},{3,1},{4,6},{5,7},{6,4},{7,5},{8,10},{9,11},{10,... | collective-permute-start | bytes 196616 | tf_op jit(solution)/shard_map/ppermute | solution.py:21
  76.3 1.5 %collective-permute-start.33 = (bf16[64,256]{1,0:T(8,128)(2,1)S(1)}, bf16[64,256]{1,0:T(8,128)(2,1)S(1)}, u32[]{:S(2)}, u32[]{:S(2)}) collective-permute-start(bf16[64,256]{1,0:T(8,128)(2,1)S(1)} %get-tuple-element.69.refs_0_), channel_id=1, source_target_pairs={{0,4},{4,0},{8,12},{12,8},{16,20},{20,16},{24,28},{28,24},{1,5},{5... | collective-permute-start | bytes 98312 | tf_op jit(solution)/shard_map/ppermute | solution.py:21
  76.4 1.5 %collective-permute-start.34 = (bf16[64,256]{1,0:T(8,128)(2,1)S(1)}, bf16[64,256]{1,0:T(8,128)(2,1)S(1)}, u32[]{:S(2)}, u32[]{:S(2)}) collective-permute-start(bf16[64,256]{1,0:T(8,128)(2,1)S(1)} %get-tuple-element.70.refs_1_), channel_id=1, source_target_pairs={{0,4},{4,0},{8,12},{12,8},{16,20},{20,16},{24,28},{28,24},{1,5},{5... | collective-permute-start | bytes 98312 | tf_op jit(solution)/shard_map/ppermute | solution.py:21
